TPU v7x, 32 devices: a whole 2x2x4 slice. The times are simulated.
32 devices in a mesh: dp: 4 (over y, x), tensor: 8 (over z, core).
Axes of the slice: x: 2, y: 2, z: 4, core: 2. Of those that a mesh axis runs over, the one named last changes fastest.
Arguments:
- tokens: bfloat16 [512, 3072], P(('dp', 'tensor')), may hold values from -6 to 6
- tangent_in: bfloat16 [512, 3072], P(('dp', 'tensor')), may hold values from -6 to 6
- cotangent: bfloat16 [512, 3072], P(('dp', 'tensor')), may hold values from -6 to 6
- w_in: bfloat16 [3072, 12288], P('dp', 'tensor'), may hold values from -0.109375 to 0.109375
- w_out: bfloat16 [12288, 3072], P('tensor', 'dp'), may hold values from -0.0546875 to 0.0546875
- clip_len: int32 [16], replicated, may hold values from 1 to 56, as said below
- clip_dev: int32 [16], replicated, may hold values from 0 to 3, as said below
Outputs:
- block_out: bfloat16 [512, 3072], P(('dp', 'tensor'))
- tangent_out: bfloat16 [512, 3072], P(('dp', 'tensor'))
- grad_w_in: float32 [3072, 12288], P('dp', 'tensor')
Inputs may be any that keep to these rules, and one draw needn't show every extreme that they name: `clip_len`: the clips of each index of dp have lengths that sum to at most 128; one index reaches 128 in every draw. `clip_dev`: each index of dp holds exactly 4 clips.
All inputs are finite; a program needn't handle non-finite values.
Results may differ from a plain program's by a relative error of at most 0.014.
Values may be sent and summed in bfloat16 or wider, within the bound.
A program may use at most 128 MiB of HBM per device.

v0:
```python
import math

import jax
import jax.numpy as jnp
from jax import lax
from jax.sharding import PartitionSpec as P

row_block = 32
tanh_coef = math.sqrt(2.0 / math.pi)
cubic_coef = 0.044715


def gelu_pair(pre_act):
    inner_arg = tanh_coef * (pre_act + cubic_coef * pre_act * pre_act * pre_act)
    tanh_val = jnp.tanh(inner_arg)
    act_val = 0.5 * pre_act * (1.0 + tanh_val)
    slope_val = 0.5 * (1.0 + tanh_val) + 0.5 * pre_act * (1.0 - tanh_val * tanh_val) * tanh_coef * (
        1.0 + 3.0 * cubic_coef * pre_act * pre_act
    )
    return (act_val, slope_val)


def block_pass(rows_x, rows_t, rows_g, live_rows, whole_in, whole_out):
    total_rows, model_cols = rows_x.shape
    hidden_cols = whole_in.shape[1]
    block_count = (live_rows + row_block - 1) // row_block

    def one_block(step_idx, buffers):
        out_buf, tan_buf, grad_buf = buffers
        row_start = step_idx * row_block
        tok_block = lax.dynamic_slice_in_dim(rows_x, row_start, row_block, 0)
        tan_block = lax.dynamic_slice_in_dim(rows_t, row_start, row_block, 0)
        cot_block = lax.dynamic_slice_in_dim(rows_g, row_start, row_block, 0)
        keep_row = (row_start + jnp.arange(row_block, dtype=jnp.int32) < live_rows)[:, None]
        pre_act = jnp.dot(tok_block, whole_in, preferred_element_type=jnp.float32)
        pre_tan = jnp.dot(tan_block, whole_in, preferred_element_type=jnp.float32)
        act_val, slope_val = gelu_pair(pre_act)
        act_half = act_val.astype(jnp.bfloat16)
        dact_half = (slope_val * pre_tan).astype(jnp.bfloat16)
        out_part = jnp.where(
            keep_row, jnp.dot(act_half, whole_out, preferred_element_type=jnp.float32), 0.0
        ).astype(jnp.bfloat16)
        tan_part = jnp.where(
            keep_row, jnp.dot(dact_half, whole_out, preferred_element_type=jnp.float32), 0.0
        ).astype(jnp.bfloat16)
        back_grad = lax.dot_general(
            cot_block, whole_out, (((1,), (1,)), ((), ())), preferred_element_type=jnp.float32
        )
        grad_pre = jnp.where(keep_row, slope_val * back_grad, 0.0).astype(jnp.bfloat16)
        out_buf = lax.dynamic_update_slice_in_dim(out_buf, out_part, row_start, 0)
        tan_buf = lax.dynamic_update_slice_in_dim(tan_buf, tan_part, row_start, 0)
        grad_buf = lax.dynamic_update_slice_in_dim(grad_buf, grad_pre, row_start, 0)
        return (out_buf, tan_buf, grad_buf)

    start_bufs = (
        jnp.zeros((total_rows, model_cols), jnp.bfloat16),
        jnp.zeros((total_rows, model_cols), jnp.bfloat16),
        jnp.zeros((total_rows, hidden_cols), jnp.bfloat16),
    )
    return lax.fori_loop(0, block_count, one_block, start_bufs)


def local(tokens, tangent_in, cotangent, w_in, w_out, clip_len, clip_dev):
    dp_count = lax.axis_size("dp")
    owners = jnp.arange(dp_count, dtype=jnp.int32)
    row_loads = jnp.sum(
        jnp.where(clip_dev[None, :] == owners[:, None], clip_len[None, :], 0), axis=1
    )
    whole_in, whole_out = (
        lax.all_gather(w_in, "dp", axis=0, tiled=True),
        lax.all_gather(w_out, "dp", axis=1, tiled=True),
    )
    rows_x, rows_t, rows_g = (
        lax.all_gather(tokens, "tensor", axis=0, tiled=True),
        lax.all_gather(tangent_in, "tensor", axis=0, tiled=True),
        lax.all_gather(cotangent, "tensor", axis=0, tiled=True),
    )
    total_rows, model_cols = rows_x.shape
    hidden_cols = whole_in.shape[1]
    my_index = lax.axis_index("dp")
    live_rows = jnp.take(row_loads, my_index)
    out_part, tan_part, grad_pre = block_pass(
        rows_x, rows_t, rows_g, live_rows, whole_in, whole_out
    )
    own_cols = model_cols // dp_count
    split_rows = rows_x.reshape(total_rows, dp_count, own_cols)
    tok_cols = lax.all_to_all(split_rows, "dp", split_axis=1, concat_axis=0, tiled=True).reshape(
        dp_count * total_rows, own_cols
    )
    piece = lax.all_gather(grad_pre, "dp", axis=0, tiled=True)
    group_count = piece.shape[0] // total_rows
    tok_piece = tok_cols.reshape(group_count, total_rows, own_cols)
    grad_piece = piece.reshape(group_count, total_rows, hidden_cols)
    terms = jnp.einsum(
        "gra,grb->gab", tok_piece, grad_piece, preferred_element_type=jnp.float32
    ).astype(jnp.bfloat16)
    terms = lax.optimization_barrier(terms)
    grad_w_in = jnp.sum(terms.astype(jnp.float32), axis=0)
    out_sum, tan_sum = (
        lax.psum_scatter(
            out_part.astype(jnp.float32).astype(jnp.bfloat16),
            "tensor",
            scatter_dimension=0,
            tiled=True,
        ).astype(jnp.float32),
        lax.psum_scatter(
            tan_part.astype(jnp.float32).astype(jnp.bfloat16),
            "tensor",
            scatter_dimension=0,
            tiled=True,
        ).astype(jnp.float32),
    )
    return (out_sum.astype(jnp.bfloat16), tan_sum.astype(jnp.bfloat16), grad_w_in)


def solution(mesh):
    return jax.shard_map(
        local,
        mesh=mesh,
        in_specs=(
            P(("dp", "tensor"), None),
            P(("dp", "tensor"), None),
            P(("dp", "tensor"), None),
            P("dp", "tensor"),
            P("tensor", "dp"),
            P(),
            P(),
        ),
        out_specs=(P(("dp", "tensor"), None), P(("dp", "tensor"), None), P("dp", "tensor")),
        check_vma=False,
    )
```

profile of v0, /device:TPU:0, one launch (start us, length us, event | category | flops | bytes accessed | tf_op | source)
XLA Modules:
  0.0 433.2 jit_solution(13483230134785074585)
XLA Ops:
  7.2 0.0 all-gather.4.cloned.1.call-start
  7.2 0.7 all-gather.4.cloned.1.call-update
  7.9 0.0 all-gather.6.cloned.1.call-start
  7.9 0.7 all-gather.6.cloned.1.call-update
  8.6 0.0 all-gather.8.cloned.1.call-start
  8.7 0.8 select_reduce_fusion
  9.5 0.6 dynamic-slice.2
  10.8 17.4 %all_gather.18 = bf16[128,3072]{1,0:T(8,128)(2,1)S(1)} all-gather(bf16[16,3072]{1,0:T(8,128)(2,1)} %param.9), channel_id=1, replica_groups=mesh['dp'=4,'tensor'=8] {'tensor'}, dimensions={0}, use_global_device_ids=true | all-gather | bytes 884736 | tf_op jit(solution)/shard_map/all_gather | solution.py:74
  28.2 15.9 %all_gather.21 = bf16[128,3072]{1,0:T(8,128)(2,1)S(1)} all-gather(bf16[16,3072]{1,0:T(8,128)(2,1)} %param.10), channel_id=1, replica_groups=mesh['dp'=4,'tensor'=8] {'tensor'}, dimensions={0}, use_global_device_ids=true | all-gather | bytes 884736 | tf_op jit(solution)/shard_map/all_gather | solution.py:75
  44.1 16.5 %all_gather.22 = bf16[128,3072]{1,0:T(8,128)(2,1)S(1)} all-gather(bf16[16,3072]{1,0:T(8,128)(2,1)} %param.11), channel_id=1, replica_groups=mesh['dp'=4,'tensor'=8] {'tensor'}, dimensions={0}, use_global_device_ids=true | all-gather | bytes 884736 | tf_op jit(solution)/shard_map/all_gather | solution.py:76
  60.6 48.3 %all-gather.4.cloned.1.call-done = bf16[3072,1536]{1,0:T(8,128)(2,1)} async-done(((bf16[768,1536]{1,0:T(8,128)(2,1)}), bf16[3072,1536]{1,0:T(8,128)(2,1)}) %all-gather.4.cloned.1.call-update) | async-done | bytes 9437200 | tf_op jit(solution)/shard_map/all_gather | solution.py:70
  108.9 98.2 %all-gather.6.cloned.1.call-done = bf16[1536,3072]{1,0:T(8,128)(2,1)} async-done(((bf16[1536,768]{1,0:T(8,128)(2,1)}), bf16[1536,3072]{1,0:T(8,128)(2,1)}) %all-gather.6.cloned.1.call-update) | async-done | bytes 9437200 | tf_op jit(solution)/shard_map/all_gather | solution.py:71
  207.1 0.1 broadcast.29
  207.2 1.0 broadcast.29.clone
  208.2 0.8 broadcast_in_dim.51
  209.0 113.1 %while.15 = (s32[]{:T(128)}, bf16[128,3072]{1,0:T(8,128)(2,1)S(1)}, bf16[128,3072]{1,0:T(8,128)(2,1)}, bf16[128,1536]{1,0:T(8,128)(2,1)}, s32[]{:T(128)}, /*inde...) while((s32[]{:T(128)}, bf16[128,3072]{1,0:T(8,128)(2,1)S(1)}, ...), condition=%wide.region_2.3_spmd, body=%wide.region_1.2_spmd.sunk | while | flops 1512701952 | bytes 49057512 | solution.py:60
  209.0 5.3 %fusion.58 = f32[32,1536]{1,0:T(8,128)S(1)} fusion(bf16[3072,1536]{1,0:T(8,128)(2,1)} %get-tuple-element.221, bf16[128,3072]{1,0:T(8,128)(2,1)S(1)} %get-tuple-element.220, s32[]{:T(128)S(6)} %select_n.64), kind=kOutput, calls=%fused_computation.22.clone.1 | convolution fusion | flops 301989888 | bytes 9830404 | tf_op jit(solution)/shard_map/while/body/dot_general | solution.py:35
  214.3 10.4 %fusion.60 = bf16[128,3072]{1,0:T(8,128)(2,1)} fusion(bf16[128,3072]{1,0:T(8,128)(2,1)} %get-tuple-element.201, s32[]{:T(128)S(6)} %select_n.64, bf16[1536,3072]{1,0:T(8,128)(2,1)} %get-tuple-element.222, bf16[3072,1536]{1,0:T(8,128)(2,1)} %get-tuple-element.221, bf16[128,3072]{1,0:T(8,128)(2,1)S(1)} %get-tuple-element.223, ...), kind=kOutput, calls=%fused_computation.5.clone.1 | convolution fusion | flops 605110272 | bytes 19465728 | tf_op jit(solution)/shard_map/while/body/dot_general | solution.py:44
  224.7 5.4 %fusion.59 = bf16[128,3072]{1,0:T(8,128)(2,1)S(1)} fusion(bf16[128,3072]{1,0:T(8,128)(2,1)S(1)} %get-tuple-element.200, s32[]{:T(128)S(6)} %select_n.64, bf16[1536,3072]{1,0:T(8,128)(2,1)} %get-tuple-element.222, pred[32]{0:T(512)(128)(4,1)S(1)} %add_compare_fusion.2, f32[32,1536]{1,0:T(8,128)S(1)} %fusion.58), kind=kOutput, calls=%fused_computation.3.clone.1 | convolution fusion | flops 302628864 | bytes 9830916 | tf_op jit(solution)/shard_map/while/body/dot_general | solution.py:41
  230.0 7.2 %fusion.61 = bf16[128,1536]{1,0:T(8,128)(2,1)} fusion(bf16[128,1536]{1,0:T(8,128)(2,1)} %get-tuple-element.202, s32[]{:T(128)S(6)} %select_n.64, bf16[1536,3072]{1,0:T(8,128)(2,1)} %get-tuple-element.222, bf16[128,3072]{1,0:T(8,128)(2,1)S(1)} %get-tuple-element.224, pred[32]{0:T(512)(128)(4,1)S(1)} %add_compare_fusion.2, f32[32,1536]{1,0:T(8,128)S(1)} %fusion.58), kind=kOutput, calls=%fused_computation.11.clone.1 | convolution fusion | flops 302972928 | bytes 9930240 | tf_op jit(solution)/shard_map/while/body/dot_general | solution.py:46
  237.2 5.3 %fusion.58 = f32[32,1536]{1,0:T(8,128)S(1)} fusion(bf16[3072,1536]{1,0:T(8,128)(2,1)} %get-tuple-element.221, bf16[128,3072]{1,0:T(8,128)(2,1)S(1)} %get-tuple-element.220, s32[]{:T(128)S(6)} %select_n.64), kind=kOutput, calls=%fused_computation.22.clone.1 | convolution fusion | flops 301989888 | bytes 9830404 | tf_op jit(solution)/shard_map/while/body/dot_general | solution.py:35
  242.6 10.4 %fusion.60 = bf16[128,3072]{1,0:T(8,128)(2,1)} fusion(bf16[128,3072]{1,0:T(8,128)(2,1)} %get-tuple-element.201, s32[]{:T(128)S(6)} %select_n.64, bf16[1536,3072]{1,0:T(8,128)(2,1)} %get-tuple-element.222, bf16[3072,1536]{1,0:T(8,128)(2,1)} %get-tuple-element.221, bf16[128,3072]{1,0:T(8,128)(2,1)S(1)} %get-tuple-element.223, ...), kind=kOutput, calls=%fused_computation.5.clone.1 | convolution fusion | flops 605110272 | bytes 19465728 | tf_op jit(solution)/shard_map/while/body/dot_general | solution.py:44
  252.9 5.4 %fusion.59 = bf16[128,3072]{1,0:T(8,128)(2,1)S(1)} fusion(bf16[128,3072]{1,0:T(8,128)(2,1)S(1)} %get-tuple-element.200, s32[]{:T(128)S(6)} %select_n.64, bf16[1536,3072]{1,0:T(8,128)(2,1)} %get-tuple-element.222, pred[32]{0:T(512)(128)(4,1)S(1)} %add_compare_fusion.2, f32[32,1536]{1,0:T(8,128)S(1)} %fusion.58), kind=kOutput, calls=%fused_computation.3.clone.1 | convolution fusion | flops 302628864 | bytes 9830916 | tf_op jit(solution)/shard_map/while/body/dot_general | solution.py:41
  258.3 7.2 %fusion.61 = bf16[128,1536]{1,0:T(8,128)(2,1)} fusion(bf16[128,1536]{1,0:T(8,128)(2,1)} %get-tuple-element.202, s32[]{:T(128)S(6)} %select_n.64, bf16[1536,3072]{1,0:T(8,128)(2,1)} %get-tuple-element.222, bf16[128,3072]{1,0:T(8,128)(2,1)S(1)} %get-tuple-element.224, pred[32]{0:T(512)(128)(4,1)S(1)} %add_compare_fusion.2, f32[32,1536]{1,0:T(8,128)S(1)} %fusion.58), kind=kOutput, calls=%fused_computation.11.clone.1 | convolution fusion | flops 302972928 | bytes 9930240 | tf_op jit(solution)/shard_map/while/body/dot_general | solution.py:46
  265.5 5.3 %fusion.58 = f32[32,1536]{1,0:T(8,128)S(1)} fusion(bf16[3072,1536]{1,0:T(8,128)(2,1)} %get-tuple-element.221, bf16[128,3072]{1,0:T(8,128)(2,1)S(1)} %get-tuple-element.220, s32[]{:T(128)S(6)} %select_n.64), kind=kOutput, calls=%fused_computation.22.clone.1 | convolution fusion | flops 301989888 | bytes 9830404 | tf_op jit(solution)/shard_map/while/body/dot_general | solution.py:35
  270.9 10.4 %fusion.60 = bf16[128,3072]{1,0:T(8,128)(2,1)} fusion(bf16[128,3072]{1,0:T(8,128)(2,1)} %get-tuple-element.201, s32[]{:T(128)S(6)} %select_n.64, bf16[1536,3072]{1,0:T(8,128)(2,1)} %get-tuple-element.222, bf16[3072,1536]{1,0:T(8,128)(2,1)} %get-tuple-element.221, bf16[128,3072]{1,0:T(8,128)(2,1)S(1)} %get-tuple-element.223, ...), kind=kOutput, calls=%fused_computation.5.clone.1 | convolution fusion | flops 605110272 | bytes 19465728 | tf_op jit(solution)/shard_map/while/body/dot_general | solution.py:44
  281.2 5.4 %fusion.59 = bf16[128,3072]{1,0:T(8,128)(2,1)S(1)} fusion(bf16[128,3072]{1,0:T(8,128)(2,1)S(1)} %get-tuple-element.200, s32[]{:T(128)S(6)} %select_n.64, bf16[1536,3072]{1,0:T(8,128)(2,1)} %get-tuple-element.222, pred[32]{0:T(512)(128)(4,1)S(1)} %add_compare_fusion.2, f32[32,1536]{1,0:T(8,128)S(1)} %fusion.58), kind=kOutput, calls=%fused_computation.3.clone.1 | convolution fusion | flops 302628864 | bytes 9830916 | tf_op jit(solution)/shard_map/while/body/dot_general | solution.py:41
  286.6 7.2 %fusion.61 = bf16[128,1536]{1,0:T(8,128)(2,1)} fusion(bf16[128,1536]{1,0:T(8,128)(2,1)} %get-tuple-element.202, s32[]{:T(128)S(6)} %select_n.64, bf16[1536,3072]{1,0:T(8,128)(2,1)} %get-tuple-element.222, bf16[128,3072]{1,0:T(8,128)(2,1)S(1)} %get-tuple-element.224, pred[32]{0:T(512)(128)(4,1)S(1)} %add_compare_fusion.2, f32[32,1536]{1,0:T(8,128)S(1)} %fusion.58), kind=kOutput, calls=%fused_computation.11.clone.1 | convolution fusion | flops 302972928 | bytes 9930240 | tf_op jit(solution)/shard_map/while/body/dot_general | solution.py:46
  293.8 5.3 %fusion.58 = f32[32,1536]{1,0:T(8,128)S(1)} fusion(bf16[3072,1536]{1,0:T(8,128)(2,1)} %get-tuple-element.221, bf16[128,3072]{1,0:T(8,128)(2,1)S(1)} %get-tuple-element.220, s32[]{:T(128)S(6)} %select_n.64), kind=kOutput, calls=%fused_computation.22.clone.1 | convolution fusion | flops 301989888 | bytes 9830404 | tf_op jit(solution)/shard_map/while/body/dot_general | solution.py:35
  299.2 10.4 %fusion.60 = bf16[128,3072]{1,0:T(8,128)(2,1)} fusion(bf16[128,3072]{1,0:T(8,128)(2,1)} %get-tuple-element.201, s32[]{:T(128)S(6)} %select_n.64, bf16[1536,3072]{1,0:T(8,128)(2,1)} %get-tuple-element.222, bf16[3072,1536]{1,0:T(8,128)(2,1)} %get-tuple-element.221, bf16[128,3072]{1,0:T(8,128)(2,1)S(1)} %get-tuple-element.223, ...), kind=kOutput, calls=%fused_computation.5.clone.1 | convolution fusion | flops 605110272 | bytes 19465728 | tf_op jit(solution)/shard_map/while/body/dot_general | solution.py:44
  309.5 5.4 %fusion.59 = bf16[128,3072]{1,0:T(8,128)(2,1)S(1)} fusion(bf16[128,3072]{1,0:T(8,128)(2,1)S(1)} %get-tuple-element.200, s32[]{:T(128)S(6)} %select_n.64, bf16[1536,3072]{1,0:T(8,128)(2,1)} %get-tuple-element.222, pred[32]{0:T(512)(128)(4,1)S(1)} %add_compare_fusion.2, f32[32,1536]{1,0:T(8,128)S(1)} %fusion.58), kind=kOutput, calls=%fused_computation.3.clone.1 | convolution fusion | flops 302628864 | bytes 9830916 | tf_op jit(solution)/shard_map/while/body/dot_general | solution.py:41
  314.9 7.2 %fusion.61 = bf16[128,1536]{1,0:T(8,128)(2,1)} fusion(bf16[128,1536]{1,0:T(8,128)(2,1)} %get-tuple-element.202, s32[]{:T(128)S(6)} %select_n.64, bf16[1536,3072]{1,0:T(8,128)(2,1)} %get-tuple-element.222, bf16[128,3072]{1,0:T(8,128)(2,1)S(1)} %get-tuple-element.224, pred[32]{0:T(512)(128)(4,1)S(1)} %add_compare_fusion.2, f32[32,1536]{1,0:T(8,128)S(1)} %fusion.58), kind=kOutput, calls=%fused_computation.11.clone.1 | convolution fusion | flops 302972928 | bytes 9930240 | tf_op jit(solution)/shard_map/while/body/dot_general | solution.py:46
  322.1 0.0 copy-start.1
  322.1 0.0 all-gather.8.cloned.1.call-update
  322.1 0.0 reduce-scatter.3.cloned.1.call-start
  322.2 0.9 copy-done.1
  323.0 0.0 reduce-scatter.3.cloned.1.call-update
  323.1 0.4 copy.18
  323.4 1.2 copy.19
  324.6 3.5 all-to-all-start
  328.1 0.2 reduce-scatter.5.cloned.1.call-start
  328.3 0.4 reduce-scatter.5.cloned.1.call-update
  328.7 14.6 %all-to-all-done = bf16[128,4,768]{2,0,1:T(8,128)(2,1)S(1)} async-done(((bf16[128,4,768]{2,0,1:T(8,128)(2,1)}), bf16[128,4,768]{2,0,1:T(8,128)(2,1)S(1)}, u32[]{:S(2)}, u32[]{:S(2)}) %all-to-all-start) | async-done | bytes 786464 | tf_op jit(solution)/shard_map/all_to_all | solution.py:87
  343.3 0.0 copy-start
  343.3 16.4 %all-gather.8.cloned.1.call-done = bf16[512,1536]{1,0:T(8,128)(2,1)} async-done(((bf16[128,1536]{1,0:T(8,128)(2,1)}), bf16[512,1536]{1,0:T(8,128)(2,1)}) %all-gather.8.cloned.1.call-update) | async-done | bytes 1572880 | tf_op jit(solution)/shard_map/all_gather | solution.py:90
  359.7 0.0 copy-done
  359.7 4.2 convert_bitcast_fusion
  364.0 3.5 convert_reduce_fusion
  367.5 6.1 %copy.21 = f32[768,1536]{1,0:T(8,128)} copy(f32[768,1536]{0,1:T(8,128)} %convert_reduce_fusion) | data formatting | bytes 9437184
  373.6 20.4 %reduce-scatter.3.cloned.1.call-done = bf16[16,3072]{1,0:T(8,128)(2,1)} async-done(((bf16[128,3072]{1,0:T(8,128)(2,1)}), bf16[16,3072]{1,0:T(8,128)(2,1)}) %reduce-scatter.3.cloned.1.call-update) | async-done | bytes 98320 | tf_op jit(solution)/shard_map/reduce_scatter | solution.py:100
  394.0 32.7 %reduce-scatter.5.cloned.1.call-done = bf16[16,3072]{1,0:T(8,128)(2,1)} async-done(((bf16[128,3072]{1,0:T(8,128)(2,1)}), bf16[16,3072]{1,0:T(8,128)(2,1)}) %reduce-scatter.5.cloned.1.call-update) | async-done | bytes 98320 | tf_op jit(solution)/shard_map/reduce_scatter | solution.py:106
  (4 shorter events, 0.0 us)
Async XLA Ops:
  7.2 101.7 %all-gather.4.cloned.1.call-start = ((), (), s32[]{:S(2)}) async-start(), calls=%async_computation.3 | async-start | bytes 11796480 | tf_op jit(solution)/shard_map/all_gather | solution.py:70
  7.9 199.2 %all-gather.6.cloned.1.call-start = ((), (), s32[]{:S(2)}) async-start(), calls=%async_computation.4 | async-start | bytes 11796480 | tf_op jit(solution)/shard_map/all_gather | solution.py:71
  8.6 351.1 %all-gather.8.cloned.1.call-start = ((), (), s32[]{:S(2)}) async-start(), calls=%async_computation.7 | async-start | bytes 1966080 | tf_op jit(solution)/shard_map/all_gather | solution.py:90
  322.1 0.9 copy-start.1
  322.1 71.9 %reduce-scatter.3.cloned.1.call-start = ((), (), s32[]{:S(2)}) async-start(), calls=%async_computation.5 | async-start | bytes 884736 | tf_op jit(solution)/shard_map/reduce_scatter | solution.py:100
  324.6 18.7 %all-to-all-start = ((bf16[128,4,768]{2,0,1:T(8,128)(2,1)}), bf16[128,4,768]{2,0,1:T(8,128)(2,1)S(1)}, u32[]{:S(2)}, u32[]{:S(2)}) async-start(bf16[128,4,768]{2,0,1:T(8,128)(2,1)} %copy.19), calls=%async_computation.2 | async-start | bytes 1572864 | tf_op jit(solution)/shard_map/all_to_all | solution.py:87
  328.1 98.6 %reduce-scatter.5.cloned.1.call-start = ((), (), s32[]{:S(2)}) async-start(), calls=%async_computation.6 | async-start | bytes 884736 | tf_op jit(solution)/shard_map/reduce_scatter | solution.py:106
  343.3 16.4 %copy-start = (bf16[128,4,768]{2,0,1:T(8,128)(2,1)}, bf16[128,4,768]{2,0,1:T(8,128)(2,1)S(1)}, u32[]{:S(2)}) copy-start(bf16[128,4,768]{2,0,1:T(8,128)(2,1)S(1)} %all-to-all-done) | copy-start | bytes 2359300
Sparse Core Ops, SparseCore 0:
  9.8 99.0 all-gather.3
  110.8 96.3 all-gather.5
  322.3 37.4 all-gather.7
  362.5 31.5 reduce-scatter.2
  396.8 29.8 reduce-scatter.4
where the time goes:
time: 433 us
  waiting for transfers between devices  232 us (54%)
  matrix products  117 us (27%)
  blocking collectives  49.9 us (12%)
  between operations  14.5 us (3%)
  local copies, waits for them, and re-layouts  10.9 us (3%)
  other arithmetic  4.33 us (1%)
    all_gather x1, waiting for transfers between devices, local(): lax.all_gather(w_out, 'dp', axis=1, tiled=True)  98.2 us
    all_gather x1, waiting for transfers between devices, local(): lax.all_gather(w_in, 'dp', axis=0, tiled=True)  48.3 us
    dot_general x4, matrix products, one_block(): jnp.dot(dact_half, whole_out, preferred_element_type=jnp.float32)  41.4 us
    reduce_scatter x1, waiting for transfers between devices, local(): lax.psum_scatter(tan_part.astype(jnp.float32).astype(jnp.bfloat16), 'tens...  32.7 us
    dot_general x4, matrix products, one_block(): lax.dot_general(cot_block, whole_out, (((1,), (1,)), ((), ())), preferred...  28.9 us
    dot_general x4, matrix products, one_block(): jnp.dot(act_half, whole_out, preferred_element_type=jnp.float32)  21.5 us
    dot_general x4, matrix products, one_block(): pre_act = jnp.dot(tok_block, whole_in, preferred_element_type=jnp.float32)  21.2 us
    reduce_scatter x1, waiting for transfers between devices, local(): lax.psum_scatter(out_part.astype(jnp.float32).astype(jnp.bfloat16), 'tens...  20.4 us
  transfers between devices with their start and end apart: 6, of which 6 were waited for; matrix products, arithmetic and copies ran while one was open for 4% of the time, Pallas kernels for 0%

commit v1 on v0

v1 whole, which is shorter than its diff:
```python
import math

import jax
import jax.numpy as jnp
from jax import lax
from jax.sharding import PartitionSpec as P

tanh_coef = math.sqrt(2.0 / math.pi)
cubic_coef = 0.044715


def gelu_pair(pre_act):
    inner_arg = tanh_coef * (pre_act + cubic_coef * pre_act * pre_act * pre_act)
    tanh_val = jnp.tanh(inner_arg)
    act_val = 0.5 * pre_act * (1.0 + tanh_val)
    slope_val = 0.5 * (1.0 + tanh_val) + 0.5 * pre_act * (1.0 - tanh_val * tanh_val) * tanh_coef * (
        1.0 + 3.0 * cubic_coef * pre_act * pre_act
    )
    return (act_val, slope_val)


def shift(value, dp_count, step):
    if step % dp_count == 0:
        return value
    return lax.ppermute(value, "dp", [(i, (i + step) % dp_count) for i in range(dp_count)])


def dot(a, b):
    return jnp.dot(a, b, preferred_element_type=jnp.float32)


def local(tokens, tangent_in, cotangent, w_in, w_out, clip_len, clip_dev):
    dp_count = lax.axis_size("dp")
    me = lax.axis_index("dp")
    live_rows = jnp.sum(jnp.where(clip_dev == me, clip_len, 0))
    own_rows, model_cols = tokens.shape
    own_cols = model_cols // dp_count
    steps = range(dp_count)

    rows = jnp.stack([tokens, tangent_in, cotangent]).reshape(3, own_rows, dp_count, own_cols)
    pieces = [
        shift(
            lax.dynamic_index_in_dim(rows, (me + s) % dp_count, 2, keepdims=False), dp_count, s
        )
        for s in steps
    ]
    whole = lax.all_gather(jnp.stack(pieces), "tensor", axis=2, tiled=True)
    group_rows = whole.shape[2]

    f32_own = None
    arrived = []
    for s in list(steps)[1:] + [0]:
        part = [dot(whole[s, 0], w_in), dot(whole[s, 1], w_in)]
        part.append(
            lax.dot_general(
                whole[s, 2], w_out, (((1,), (1,)), ((), ())), preferred_element_type=jnp.float32
            )
        )
        if s == 0:
            f32_own = part
        else:
            arrived.append(shift(jnp.stack([p.astype(jnp.bfloat16) for p in part]), dp_count, -s))
    sums = list(f32_own)
    for piece in arrived:
        sums = [total + piece[k].astype(jnp.float32) for k, total in enumerate(sums)]
    pre_act, pre_tan, back_grad = sums
    keep_row = (jnp.arange(group_rows, dtype=jnp.int32) < live_rows)[:, None]
    act_val, slope_val = gelu_pair(pre_act)
    hidden = jnp.stack(
        [
            jnp.where(keep_row, val, 0.0).astype(jnp.bfloat16)
            for val in (act_val, slope_val * pre_tan, slope_val * back_grad)
        ]
    )

    gathered = [shift(hidden, dp_count, s) for s in steps]
    outs = []
    for s in steps:
        outs.append(
            jnp.stack([dot(gathered[s][k], w_out).astype(jnp.bfloat16) for k in range(2)])
        )
    summed = lax.psum_scatter(jnp.stack(outs), "tensor", scatter_dimension=2, tiled=True)
    cols = jnp.stack([shift(summed[s], dp_count, -s) for s in steps])
    cols = jnp.roll(cols, me, axis=0)
    out, tan = [
        cols[:, k].transpose(1, 0, 2).reshape(own_rows, model_cols) for k in range(2)
    ]
    grad_w_in = lax.dot_general(
        jnp.concatenate([whole[s, 0] for s in steps]),
        jnp.concatenate([gathered[s][2] for s in steps]),
        (((0,), (0,)), ((), ())),
        preferred_element_type=jnp.float32,
    )
    return (out, tan, grad_w_in)


def solution(mesh):
    return jax.shard_map(
        local,
        mesh=mesh,
        in_specs=(
            P(("dp", "tensor"), None),
            P(("dp", "tensor"), None),
            P(("dp", "tensor"), None),
            P("dp", "tensor"),
            P("tensor", "dp"),
            P(),
            P(),
        ),
        out_specs=(P(("dp", "tensor"), None), P(("dp", "tensor"), None), P("dp", "tensor")),
        check_vma=False,
    )
```

time: 433 us -> 229 us (0.53)
  matrix products: 117 us -> 19.3 us
  waiting for transfers between devices: 232 us -> 163 us
  blocking collectives: 49.9 us -> 0 us
  starting transfers between devices: 3.87 us -> 15.7 us
    all_gather x3 -> x1, waiting for transfers between devices: 163 us -> 32.9 us  [local(): whole = lax.all_gather(jnp.stack(pieces), 'tensor', axis=2, tiled=True)]
    ppermute x0 -> x12, waiting for transfers between devices: none -> 103 us  [shift(): lax.ppermute(value, 'dp', [(i, (i + step) % dp_count) for i in range(dp_c...]
    dot_general x17 -> x21, matrix products: 117 us -> 19.3 us  [the longest x16 10.4 us: dot(): return jnp.dot(a, b, preferred_element_type=jnp.float32)]
    all_gather x3 -> x0, blocking collectives: 49.9 us -> none  [the longest x1 17.4 us: local(): lax.all_gather(tokens, 'tensor', axis=0, tiled=True)]
    reduce_scatter x2 -> x1, waiting for transfers between devices: 53.1 us -> 27.2 us  [local(): lax.psum_scatter(jnp.stack(outs), 'tensor', scatter_dimension=2, tiled=True)]
    ppermute x0 -> x12, starting transfers between devices: none -> 15.6 us  [shift(): lax.ppermute(value, 'dp', [(i, (i + step) % dp_count) for i in range(dp_c...]
    all_to_all x1 -> x0, waiting for transfers between devices: 14.6 us -> none  [local(): lax.all_to_all(split_rows, 'dp', split_axis=1, concat_axis=0, tiled=True)]
    unnamed x5 -> x29, local copies, waits for them, and re-layouts: 6.96 us -> 1.11 us
  transfers between devices with their start and end apart: 6 -> 14, of which waited for: 6 -> 11; matrix products, arithmetic and copies ran while one was open for 4% -> 8% of each run, Pallas kernels for 0% -> 0%
where the time goes in v1:
time: 229 us
  waiting for transfers between devices  163 us (71%)
  matrix products  19.3 us (8%)
  starting transfers between devices  15.7 us (7%)
  between operations  14.5 us (6%)
  local copies, waits for them, and re-layouts  11.9 us (5%)
  other arithmetic  4.06 us (2%)
    ppermute x12, waiting for transfers between devices, shift(): lax.ppermute(value, 'dp', [(i, (i + step) % dp_count) for i in range(dp_c...  103 us
    all_gather x1, waiting for transfers between devices, local(): whole = lax.all_gather(jnp.stack(pieces), 'tensor', axis=2, tiled=True)  32.9 us
    reduce_scatter x1, waiting for transfers between devices, local(): lax.psum_scatter(jnp.stack(outs), 'tensor', scatter_dimension=2, tiled=True)  27.2 us
    ppermute x12, starting transfers between devices, shift(): lax.ppermute(value, 'dp', [(i, (i + step) % dp_count) for i in range(dp_c...  15.6 us
    dot_general x16, matrix products, dot(): return jnp.dot(a, b, preferred_element_type=jnp.float32)  10.4 us
    dot_general x1, matrix products, local(): lax.dot_general(jnp.concatenate([whole[s, 0] for s in steps]), jnp.concat...  5.07 us
  transfers between devices with their start and end apart: 14, of which 11 were waited for; matrix products, arithmetic and copies ran while one was open for 8% of the time, Pallas kernels for 0%

profile of v1, /device:TPU:0, one launch (start us, length us, event | category | flops | bytes accessed | tf_op | source)
XLA Modules:
  0.0 228.9 jit_solution(3162742398630093695)
XLA Ops:
  7.3 1.1 stack.136
  8.4 0.9 stack.137
  9.3 0.9 stack.138
  10.4 0.7 constant_dynamic-slice_fusion.3
  11.1 3.0 %collective-permute-start = (bf16[3,16,768]{2,1,0:T(8,128)(2,1)S(1)}, bf16[3,16,768]{2,1,0:T(8,128)(2,1)S(1)}, u32[]{:S(2)}, u32[]{:S(2)}) collective-permute-start(bf16[3,16,768]{2,1,0:T(8,128)(2,1)S(1)} %bitcast.231), channel_id=1, source_target_pairs={{0,8},{8,16},{16,24},{24,0},{1,9},{9,17},{17,25},{25,1},{2,10},{10... | collective-permute-start | bytes 221192 | tf_op jit(solution)/shard_map/ppermute | solution.py:25
  14.1 1.6 collective-permute-start.1
  15.7 1.5 collective-permute-start.2
  17.2 0.2 collective-permute-done
  17.5 1.5 collective-permute-done.1
  18.9 1.2 collective-permute-done.2
  20.1 0.8 pad_maximum_fusion.5
  21.0 32.9 %all-gather.2.cloned.1.call-done = bf16[4,3,128,768]{3,2,1,0:T(8,128)(2,1)} async-done(((bf16[4,3,16,768]{3,2,1,0:T(8,128)(2,1)}), bf16[4,3,128,768]{3,2,1,0:T(8,128)(2,1)}) %all-gather.2.cloned.1.call-update) | async-done | bytes 2359312 | tf_op jit(solution)/shard_map/all_gather | solution.py:47
  53.8 1.6 fusion.1
  55.4 1.4 fusion
  56.8 0.9 fusion.2
  57.7 0.1 pad_maximum_fusion.1
  57.9 2.4 %collective-permute-start.3 = (bf16[3,128,1536]{2,1,0:T(8,128)(2,1)S(1)}, bf16[3,128,1536]{2,1,0:T(8,128)(2,1)S(1)}, u32[]{:S(2)}, u32[]{:S(2)}) collective-permute-start(bf16[3,128,1536]{2,1,0:T(8,128)(2,1)S(1)} %pad_maximum_fusion.1), channel_id=1, source_target_pairs={{0,24},{8,0},{16,8},{24,16},{1,25},{9,1},{17,9},{25,17},{2,26},{10... | collective-permute-start | bytes 3538952 | tf_op jit(solution)/shard_map/ppermute | solution.py:25
  60.3 0.9 fusion.5
  61.2 0.5 fusion.4
  61.7 0.5 fusion.3
  62.2 0.1 pad_maximum_fusion.2
  62.3 0.6 collective-permute-start.4
  62.9 0.9 fusion.8
  63.8 0.5 fusion.7
  64.3 0.5 fusion.6
  64.8 0.1 pad_maximum_fusion.3
  65.0 0.6 collective-permute-start.5
  65.6 0.6 fusion.45
  66.2 0.6 iota_compare_fusion
  66.9 19.8 %collective-permute-done.3 = bf16[3,128,1536]{2,1,0:T(8,128)(2,1)S(1)} collective-permute-done((bf16[3,128,1536]{2,1,0:T(8,128)(2,1)S(1)}, bf16[3,128,1536]{2,1,0:T(8,128)(2,1)S(1)}, u32[]{:S(2)}, u32[]{:S(2)}) %collective-permute-start.3) | collective-permute-done | bytes 1179680 | tf_op jit(solution)/shard_map/ppermute | solution.py:25
  86.7 28.8 %collective-permute-done.4 = bf16[3,128,1536]{2,1,0:T(8,128)(2,1)S(1)} collective-permute-done((bf16[3,128,1536]{2,1,0:T(8,128)(2,1)S(1)}, bf16[3,128,1536]{2,1,0:T(8,128)(2,1)S(1)}, u32[]{:S(2)}, u32[]{:S(2)}) %collective-permute-start.4) | collective-permute-done | bytes 1179680 | tf_op jit(solution)/shard_map/ppermute | solution.py:25
  115.5 0.7 select_convert_fusion
  116.2 1.0 fusion.42
  117.2 1.2 fusion.39
  118.4 0.1 pad_maximum_fusion.4
  118.5 0.1 collective-permute-start.8
  118.6 0.6 collective-permute-start.7
  119.2 1.9 collective-permute-start.6
  121.2 0.5 fusion.17
  121.7 0.5 fusion.18
  122.2 25.3 %collective-permute-done.8 = bf16[3,128,1536]{2,1,0:T(8,128)(2,1)S(1)} collective-permute-done((bf16[3,128,1536]{2,1,0:T(8,128)(2,1)S(1)}, bf16[3,128,1536]{2,1,0:T(8,128)(2,1)S(1)}, u32[]{:S(2)}, u32[]{:S(2)}) %collective-permute-start.8) | collective-permute-done | bytes 1179680 | tf_op jit(solution)/shard_map/ppermute | solution.py:25
  147.5 0.5 fusion.24
  148.0 0.5 fusion.23
  148.5 22.4 %collective-permute-done.7 = bf16[3,128,1536]{2,1,0:T(8,128)(2,1)S(1)} collective-permute-done((bf16[3,128,1536]{2,1,0:T(8,128)(2,1)S(1)}, bf16[3,128,1536]{2,1,0:T(8,128)(2,1)S(1)}, u32[]{:S(2)}, u32[]{:S(2)}) %collective-permute-start.7) | collective-permute-done | bytes 1179680 | tf_op jit(solution)/shard_map/ppermute | solution.py:25
  170.9 0.5 fusion.22
  171.4 0.5 fusion.21
  171.9 0.1 copy-done.3
  172.0 0.5 fusion.20
  172.5 0.5 fusion.19
  173.1 1.3 pad_maximum_fusion
  174.4 2.1 slice_bitcast_fusion.47
  176.6 0.8 slice_bitcast_fusion
  177.3 1.0 slice_bitcast_fusion.1
  178.4 1.0 slice_bitcast_fusion.2
  179.4 27.2 %reduce-scatter.2.cloned.1.call-done = bf16[4,2,16,768]{3,2,1,0:T(8,128)(2,1)} async-done(((bf16[4,2,128,768]{3,2,1,0:T(8,128)(2,1)}), bf16[4,2,16,768]{3,2,1,0:T(8,128)(2,1)}) %reduce-scatter.2.cloned.1.call-update) | async-done | bytes 196624 | tf_op jit(solution)/shard_map/reduce_scatter | solution.py:82
  206.6 0.9 slice_bitcast_fusion.48
  207.5 2.3 %collective-permute-start.9 = (bf16[2,16,768]{2,1,0:T(8,128)(2,1)S(1)}, bf16[2,16,768]{2,1,0:T(8,128)(2,1)S(1)}, u32[]{:S(2)}, u32[]{:S(2)}) collective-permute-start(bf16[2,16,768]{2,1,0:T(8,128)(2,1)S(1)} %get-tuple-element.16), channel_id=1, source_target_pairs={{0,24},{8,0},{16,8},{24,16},{1,25},{9,1},{17,9},{25,17},{2,26},{10... | collective-permute-start | bytes 147464 | tf_op jit(solution)/shard_map/ppermute | solution.py:25
  209.8 5.1 %fusion.9 = f32[768,1536]{1,0:T(8,128)} fusion(bf16[128,1536]{1,0:T(8,128)(2,1)} %slice_bitcast_fusion, bf16[128,1536]{1,0:T(8,128)(2,1)S(1)} %slice_bitcast_fusion.1, bf16[128,1536]{1,0:T(8,128)(2,1)S(1)} %slice_bitcast_fusion.2, bf16[128,1536]{1,0:T(8,128)(2,1)} %copy-done.5, bf16[128,768]{1,0:T(8,128)(2,1)} %get-tuple-element.4, ...), kind=kOutput, calls=%fused_computation.19 | convolution fusion | flops 1217396736 | bytes 7077888 | tf_op jit(solution)/shard_map/dot_general | solution.py:88
  214.9 1.0 collective-permute-start.10
  215.8 3.1 %collective-permute-done.10 = bf16[2,16,768]{2,1,0:T(8,128)(2,1)S(1)} collective-permute-done((bf16[2,16,768]{2,1,0:T(8,128)(2,1)S(1)}, bf16[2,16,768]{2,1,0:T(8,128)(2,1)S(1)}, u32[]{:S(2)}, u32[]{:S(2)}) %collective-permute-start.10) | collective-permute-done | bytes 49184 | tf_op jit(solution)/shard_map/ppermute | solution.py:25
  219.0 0.9 collective-permute-done.11
  219.9 0.8 slice_dynamic-update-slice_fusion.1
  220.7 0.6 copy.19
  221.4 0.6 copy.18
  (41 shorter events, 0.6 us)
Async XLA Ops:
  7.2 46.7 %copy-start = (bf16[768,1536]{1,0:T(8,128)(2,1)S(1)}, bf16[768,1536]{1,0:T(8,128)(2,1)}, u32[]{:S(2)}) copy-start(bf16[768,1536]{1,0:T(8,128)(2,1)} %param.10) | copy-start | bytes 7077892
  7.2 46.7 %all-gather.2.cloned.1.call-start = ((), (), s32[]{:S(2)}) async-start(), calls=%async_computation.1 | async-start | bytes 2654208 | tf_op jit(solution)/shard_map/all_gather | solution.py:47
  11.1 6.3 %collective-permute-start = (bf16[3,16,768]{2,1,0:T(8,128)(2,1)S(1)}, bf16[3,16,768]{2,1,0:T(8,128)(2,1)S(1)}, u32[]{:S(2)}, u32[]{:S(2)}) collective-permute-start(bf16[3,16,768]{2,1,0:T(8,128)(2,1)S(1)} %bitcast.231), channel_id=1, source_target_pairs={{0,8},{8,16},{16,24},{24,0},{1,9},{9,17},{17,25},{25,1},{2,10},{10... | collective-permute-start | bytes 221192 | tf_op jit(solution)/shard_map/ppermute | solution.py:25
  14.1 4.8 %collective-permute-start.1 = (bf16[3,16,768]{2,1,0:T(8,128)(2,1)S(1)}, bf16[3,16,768]{2,1,0:T(8,128)(2,1)S(1)}, u32[]{:S(2)}, u32[]{:S(2)}) collective-permute-start(bf16[3,16,768]{2,1,0:T(8,128)(2,1)S(1)} %bitcast.232), channel_id=1, source_target_pairs={{0,16},{8,24},{16,0},{24,8},{1,17},{9,25},{17,1},{25,9},{2,18},{10... | collective-permute-start | bytes 221192 | tf_op jit(solution)/shard_map/ppermute | solution.py:25
  15.7 4.4 %collective-permute-start.2 = (bf16[3,16,768]{2,1,0:T(8,128)(2,1)S(1)}, bf16[3,16,768]{2,1,0:T(8,128)(2,1)S(1)}, u32[]{:S(2)}, u32[]{:S(2)}) collective-permute-start(bf16[3,16,768]{2,1,0:T(8,128)(2,1)S(1)} %bitcast.233), channel_id=1, source_target_pairs={{0,24},{8,0},{16,8},{24,16},{1,25},{9,1},{17,9},{25,17},{2,26},{10... | collective-permute-start | bytes 221192 | tf_op jit(solution)/shard_map/ppermute | solution.py:25
  20.9 185.7 %reduce-scatter.2.cloned.1.call-start = ((), (), s32[]{:S(2)}) async-start(), calls=%async_computation.2 | async-start | bytes 1769472 | tf_op jit(solution)/shard_map/reduce_scatter | solution.py:82
  53.8 3.0 %copy-start.1 = (bf16[1536,768]{1,0:T(8,128)(2,1)S(1)}, bf16[1536,768]{1,0:T(8,128)(2,1)}, u32[]{:S(2)}) copy-start(bf16[1536,768]{1,0:T(8,128)(2,1)} %param.11) | copy-start | bytes 7077892
  53.8 3.0 %copy-start.2 = (bf16[4,3,128,768]{3,2,1,0:T(8,128)(2,1)S(1)}, bf16[4,3,128,768]{3,2,1,0:T(8,128)(2,1)}, u32[]{:S(2)}) copy-start(bf16[4,3,128,768]{3,2,1,0:T(8,128)(2,1)} %all-gather.2.cloned.1.call-done) | copy-start | bytes 7077892
  57.9 28.9 %collective-permute-start.3 = (bf16[3,128,1536]{2,1,0:T(8,128)(2,1)S(1)}, bf16[3,128,1536]{2,1,0:T(8,128)(2,1)S(1)}, u32[]{:S(2)}, u32[]{:S(2)}) collective-permute-start(bf16[3,128,1536]{2,1,0:T(8,128)(2,1)S(1)} %pad_maximum_fusion.1), channel_id=1, source_target_pairs={{0,24},{8,0},{16,8},{24,16},{1,25},{9,1},{17,9},{25,17},{2,26},{10... | collective-permute-start | bytes 3538952 | tf_op jit(solution)/shard_map/ppermute | solution.py:25
  62.3 53.2 %collective-permute-start.4 = (bf16[3,128,1536]{2,1,0:T(8,128)(2,1)S(1)}, bf16[3,128,1536]{2,1,0:T(8,128)(2,1)S(1)}, u32[]{:S(2)}, u32[]{:S(2)}) collective-permute-start(bf16[3,128,1536]{2,1,0:T(8,128)(2,1)S(1)} %pad_maximum_fusion.2), channel_id=1, source_target_pairs={{0,16},{8,24},{16,0},{24,8},{1,17},{9,25},{17,1},{25,9},{2,18},{10... | collective-permute-start | bytes 3538952 | tf_op jit(solution)/shard_map/ppermute | solution.py:25
  64.3 1.3 copy-start.6
  64.3 1.3 copy-start.7
  65.0 50.5 %collective-permute-start.5 = (bf16[3,128,1536]{2,1,0:T(8,128)(2,1)S(1)}, bf16[3,128,1536]{2,1,0:T(8,128)(2,1)S(1)}, u32[]{:S(2)}, u32[]{:S(2)}) collective-permute-start(bf16[3,128,1536]{2,1,0:T(8,128)(2,1)S(1)} %pad_maximum_fusion.3), channel_id=1, source_target_pairs={{0,8},{8,16},{16,24},{24,0},{1,9},{9,17},{17,25},{25,1},{2,10},{10... | collective-permute-start | bytes 3538952 | tf_op jit(solution)/shard_map/ppermute | solution.py:25
  118.4 3.3 %copy-start.5 = (bf16[128,1536]{1,0:T(8,128)(2,1)}, bf16[128,1536]{1,0:T(8,128)(2,1)S(1)}, u32[]{:S(2)}) copy-start(bf16[128,1536]{1,0:T(8,128)(2,1)S(1)} %fusion.39) | copy-start | bytes 1179652
  118.5 29.0 %collective-permute-start.8 = (bf16[3,128,1536]{2,1,0:T(8,128)(2,1)S(1)}, bf16[3,128,1536]{2,1,0:T(8,128)(2,1)S(1)}, u32[]{:S(2)}, u32[]{:S(2)}) collective-permute-start(bf16[3,128,1536]{2,1,0:T(8,128)(2,1)S(1)} %pad_maximum_fusion.4), channel_id=1, source_target_pairs={{0,24},{8,0},{16,8},{24,16},{1,25},{9,1},{17,9},{25,17},{2,26},{10... | collective-permute-start | bytes 3538952 | tf_op jit(solution)/shard_map/ppermute | solution.py:25
  118.6 52.3 %collective-permute-start.7 = (bf16[3,128,1536]{2,1,0:T(8,128)(2,1)S(1)}, bf16[3,128,1536]{2,1,0:T(8,128)(2,1)S(1)}, u32[]{:S(2)}, u32[]{:S(2)}) collective-permute-start(bf16[3,128,1536]{2,1,0:T(8,128)(2,1)S(1)} %pad_maximum_fusion.4), channel_id=1, source_target_pairs={{0,16},{8,24},{16,0},{24,8},{1,17},{9,25},{17,1},{25,9},{2,18},{10... | collective-permute-start | bytes 3538952 | tf_op jit(solution)/shard_map/ppermute | solution.py:25
  119.2 52.8 %collective-permute-start.6 = (bf16[3,128,1536]{2,1,0:T(8,128)(2,1)S(1)}, bf16[3,128,1536]{2,1,0:T(8,128)(2,1)S(1)}, u32[]{:S(2)}, u32[]{:S(2)}) collective-permute-start(bf16[3,128,1536]{2,1,0:T(8,128)(2,1)S(1)} %pad_maximum_fusion.4), channel_id=1, source_target_pairs={{0,8},{8,16},{16,24},{24,0},{1,9},{9,17},{17,25},{25,1},{2,10},{10... | collective-permute-start | bytes 3538952 | tf_op jit(solution)/shard_map/ppermute | solution.py:25
  170.9 1.0 copy-start.3
  172.0 1.0 copy-start.4
  207.5 8.4 %collective-permute-start.9 = (bf16[2,16,768]{2,1,0:T(8,128)(2,1)S(1)}, bf16[2,16,768]{2,1,0:T(8,128)(2,1)S(1)}, u32[]{:S(2)}, u32[]{:S(2)}) collective-permute-start(bf16[2,16,768]{2,1,0:T(8,128)(2,1)S(1)} %get-tuple-element.16), channel_id=1, source_target_pairs={{0,24},{8,0},{16,8},{24,16},{1,25},{9,1},{17,9},{25,17},{2,26},{10... | collective-permute-start | bytes 147464 | tf_op jit(solution)/shard_map/ppermute | solution.py:25
  214.9 5.0 %collective-permute-start.11 = (bf16[2,16,768]{2,1,0:T(8,128)(2,1)S(1)}, bf16[2,16,768]{2,1,0:T(8,128)(2,1)S(1)}, u32[]{:S(2)}, u32[]{:S(2)}) collective-permute-start(bf16[2,16,768]{2,1,0:T(8,128)(2,1)S(1)} %get-tuple-element.13), channel_id=1, source_target_pairs={{0,8},{8,16},{16,24},{24,0},{1,9},{9,17},{17,25},{25,1},{2,10},{10... | collective-permute-start | bytes 147464 | tf_op jit(solution)/shard_map/ppermute | solution.py:25
  214.9 4.1 %collective-permute-start.10 = (bf16[2,16,768]{2,1,0:T(8,128)(2,1)S(1)}, bf16[2,16,768]{2,1,0:T(8,128)(2,1)S(1)}, u32[]{:S(2)}, u32[]{:S(2)}) collective-permute-start(bf16[2,16,768]{2,1,0:T(8,128)(2,1)S(1)} %get-tuple-element.15), channel_id=1, source_target_pairs={{0,16},{8,24},{16,0},{24,8},{1,17},{9,25},{17,1},{25,9},{2,18},{10... | collective-permute-start | bytes 147464 | tf_op jit(solution)/shard_map/ppermute | solution.py:25
Sparse Core Ops, SparseCore 0:
  21.0 32.7 all-gather.1
  174.6 31.9 reduce-scatter.1

commit v2 on v1

v2 whole, which is shorter than its diff:
```python
import math

import jax
import jax.numpy as jnp
from jax import lax
from jax.sharding import PartitionSpec as P

tanh_coef = math.sqrt(2.0 / math.pi)
cubic_coef = 0.044715


def gelu_pair(pre_act):
    inner_arg = tanh_coef * (pre_act + cubic_coef * pre_act * pre_act * pre_act)
    tanh_val = jnp.tanh(inner_arg)
    act_val = 0.5 * pre_act * (1.0 + tanh_val)
    slope_val = 0.5 * (1.0 + tanh_val) + 0.5 * pre_act * (1.0 - tanh_val * tanh_val) * tanh_coef * (
        1.0 + 3.0 * cubic_coef * pre_act * pre_act
    )
    return (act_val, slope_val)


def dot(a, b):
    return jnp.dot(a, b, preferred_element_type=jnp.float32)


def dp_grid(dp_count):
    lo = int(math.sqrt(dp_count))
    while dp_count % lo:
        lo -= 1
    return dp_count // lo, lo


def shift(value, grid, step):
    hi, lo = grid
    if step[0] % hi == 0 and step[1] % lo == 0:
        return value
    pairs = [
        (a * lo + b, (a + step[0]) % hi * lo + (b + step[1]) % lo)
        for a in range(hi)
        for b in range(lo)
    ]
    return lax.ppermute(value, "dp", pairs)


def axis_step(axis, size):
    return (size, 0) if axis == 0 else (0, size)


def half(value):
    return value.astype(jnp.bfloat16)


def sum_to_owner(part, grid, first):
    second = 1 - first
    n1, n2 = grid[first], grid[second]

    def slot(i, j):
        return (i, j) if first == 0 else (j, i)

    arrived = [
        shift(
            half(jnp.stack([part(slot(i, j)) for j in range(n2)])), grid, axis_step(first, -i)
        )
        for i in range(1, n1)
    ]
    sums = []
    for j in list(range(1, n2)) + [0]:
        total = part(slot(0, j))
        for piece in arrived:
            total = total + piece[j].astype(jnp.float32)
        sums.append(total if j == 0 else shift(half(total), grid, axis_step(second, -j)))
    total = sums[-1]
    for piece in sums[:-1]:
        total = total + piece.astype(jnp.float32)
    return total


def gather_groups(value, grid, first):
    second = 1 - first
    n1, n2 = grid[first], grid[second]
    held = jnp.stack([shift(value, grid, axis_step(first, i)) for i in range(n1)])
    found = {}
    for j in range(n2):
        there = shift(held, grid, axis_step(second, j))
        for i in range(n1):
            found[(i, j) if first == 0 else (j, i)] = there[i]
    return found


def local(tokens, tangent_in, cotangent, w_in, w_out, clip_len, clip_dev):
    dp_count = lax.axis_size("dp")
    grid = dp_grid(dp_count)
    me = lax.axis_index("dp")
    me_hi, me_lo = me // grid[1], me % grid[1]
    live_rows = jnp.sum(jnp.where(clip_dev == me, clip_len, 0))
    own_rows, model_cols = tokens.shape
    own_cols = model_cols // dp_count
    slots = [(i, j) for i in range(grid[0]) for j in range(grid[1])]
    place = {s: k for k, s in enumerate(slots)}

    def own_channels(rows):
        rows = rows.reshape(own_rows, dp_count, own_cols)
        pieces = []
        for i, j in slots:
            target = (me_hi + i) % grid[0] * grid[1] + (me_lo + j) % grid[1]
            piece = lax.dynamic_index_in_dim(rows, target, 1, keepdims=False)
            pieces.append(shift(piece, grid, (i, j)))
        return lax.all_gather(jnp.stack(pieces), "tensor", axis=1, tiled=True)

    tok_cols, tan_cols, cot_cols = [own_channels(v) for v in (tokens, tangent_in, cotangent)]
    group_rows = tok_cols.shape[1]
    cut = group_rows // 2
    halves = [(0, slice(0, cut)), (1, slice(cut, group_rows))]

    def up(cols):
        return [
            sum_to_owner(lambda s, r=rows: dot(cols[place[s], r], w_in), grid, first)
            for first, rows in halves
        ]

    def back(cols):
        return [
            sum_to_owner(
                lambda s, r=rows: lax.dot_general(
                    cols[place[s], r],
                    w_out,
                    (((1,), (1,)), ((), ())),
                    preferred_element_type=jnp.float32,
                ),
                grid,
                first,
            )
            for first, rows in halves
        ]

    row_at = jnp.arange(group_rows, dtype=jnp.int32)
    keep = [(row_at[rows] < live_rows)[:, None] for _, rows in halves]

    def everywhere(values):
        values = [half(jnp.where(k, v, 0.0)) for k, v in zip(keep, values)]
        found = [gather_groups(v, grid, 1 - first) for v, (first, _) in zip(values, halves)]
        return jnp.stack([jnp.concatenate([f[s] for f in found]) for s in slots])

    def down(hidden):
        flat = hidden.reshape(dp_count * group_rows, -1)
        terms = half(dot(flat, w_out)).reshape(dp_count, group_rows, own_cols)
        summed = lax.psum_scatter(terms, "tensor", scatter_dimension=1, tiled=True)
        cols = jnp.stack(
            [shift(summed[place[(i, j)]], grid, (-i, -j)) for i, j in slots]
        ).reshape(*grid, own_rows, own_cols)
        cols = jnp.roll(jnp.roll(cols, me_hi, axis=0), me_lo, axis=1)
        return cols.transpose(2, 0, 1, 3).reshape(own_rows, model_cols)

    pre_act = up(tok_cols)
    pairs = [gelu_pair(p) for p in pre_act]
    act_all = everywhere([a for a, _ in pairs])
    pre_tan = up(tan_cols)
    dact_all = everywhere([s * t for (_, s), t in zip(pairs, pre_tan)])
    back_grad = back(cot_cols)
    grad_all = everywhere([s * g for (_, s), g in zip(pairs, back_grad)])
    out = down(act_all)
    tan = down(dact_all)
    grad_w_in = lax.dot_general(
        tok_cols.reshape(dp_count * group_rows, own_cols),
        grad_all.reshape(dp_count * group_rows, -1),
        (((0,), (0,)), ((), ())),
        preferred_element_type=jnp.float32,
    )
    return (out, tan, grad_w_in)


def solution(mesh):
    return jax.shard_map(
        local,
        mesh=mesh,
        in_specs=(
            P(("dp", "tensor"), None),
            P(("dp", "tensor"), None),
            P(("dp", "tensor"), None),
            P("dp", "tensor"),
            P("tensor", "dp"),
            P(),
            P(),
        ),
        out_specs=(P(("dp", "tensor"), None), P(("dp", "tensor"), None), P("dp", "tensor")),
        check_vma=False,
    )
```

time: 229 us -> 231 us (level)
  waiting for transfers between devices: 163 us -> 74.1 us
  blocking collectives: 0 us -> 47.7 us
  starting transfers between devices: 15.7 us -> 48.2 us
  other arithmetic: 4.06 us -> 8.93 us
  matrix products: 19.3 us -> 24 us
    ppermute x12 -> x39, waiting for transfers between devices: 103 us -> 31.3 us  [shift(): return lax.ppermute(value, 'dp', pairs)]
    all_gather x0 -> x3, blocking collectives: none -> 47.7 us  [own_channels(): return lax.all_gather(jnp.stack(pieces), 'tensor', axis=1, tiled=True)]
    all_gather x1 -> x0, waiting for transfers between devices: 32.9 us -> none  [local(): whole = lax.all_gather(jnp.stack(pieces), 'tensor', axis=2, tiled=True)]
    ppermute x12 -> x39, starting transfers between devices: 15.6 us -> 47.9 us  [shift(): return lax.ppermute(value, 'dp', pairs)]
    reduce_scatter x1 -> x2, waiting for transfers between devices: 27.2 us -> 42.8 us  [down(): summed = lax.psum_scatter(terms, 'tensor', scatter_dimension=1, tiled=True)]
    dot_general x16 -> x18, matrix products: 10.4 us -> 13.6 us  [dot(): return jnp.dot(a, b, preferred_element_type=jnp.float32)]
    reshape x2 -> x7, local copies, waits for them, and re-layouts: 1.29 us -> 4.48 us  [the longest x3 2.96 us: own_channels(): rows = rows.reshape(own_rows, dp_count, own_cols)]
    another operation x4 -> x0, local copies, waits for them, and re-layouts: 3.02 us -> none  [local(): jnp.stack([tokens, tangent_in, cotangent])]
  transfers between devices with their start and end apart: 14 -> 41, of which waited for: 11 -> 16; matrix products, arithmetic and copies ran while one was open for 8% -> 16% of each run, Pallas kernels for 0% -> 0%
where the time goes in v2:
time: 231 us; the launch traced here: 230 us
  waiting for transfers between devices  74.1 us (32%)
  starting transfers between devices  48.2 us (21%)
  blocking collectives  47.7 us (21%)
  matrix products  24 us (10%)
  between operations  14.8 us (6%)
  local copies, waits for them, and re-layouts  12.5 us (5%)
  other arithmetic  8.93 us (4%)
    ppermute x39, starting transfers between devices, shift(): return lax.ppermute(value, 'dp', pairs)  47.9 us
    all_gather x3, blocking collectives, own_channels(): return lax.all_gather(jnp.stack(pieces), 'tensor', axis=1, tiled=True)  47.7 us
    reduce_scatter x2, waiting for transfers between devices, down(): summed = lax.psum_scatter(terms, 'tensor', scatter_dimension=1, tiled=True)  42.8 us
    ppermute x39, waiting for transfers between devices, shift(): return lax.ppermute(value, 'dp', pairs)  31.3 us
    dot_general x18, matrix products, dot(): return jnp.dot(a, b, preferred_element_type=jnp.float32)  13.6 us
    dot_general x8, matrix products, back(): lax.dot_general(cols[place[s], r], w_out, (((1,), (1,)), ((), ())), prefe...  6.77 us
  transfers between devices with their start and end apart: 41, of which 16 were waited for; matrix products, arithmetic and copies ran while one was open for 16% of the time, Pallas kernels for 0%

profile of v2, /device:TPU:0, one launch (start us, length us, event | category | flops | bytes accessed | tf_op | source)
XLA Modules:
  0.0 230.2 jit_solution(15923125212245087493)
XLA Ops:
  7.3 1.1 reshape.80
  8.7 3.0 %collective-permute-start.28 = (bf16[16,768]{1,0:T(8,128)(2,1)S(1)}, bf16[16,768]{1,0:T(8,128)(2,1)S(1)}, u32[]{:S(2)}, u32[]{:S(2)}) collective-permute-start(bf16[16,768]{1,0:T(8,128)(2,1)S(1)} %bitcast.396), channel_id=1, source_target_pairs={{0,8},{8,0},{16,24},{24,16},{1,9},{9,1},{17,25},{25,17},{2,10},{10... | collective-permute-start | bytes 73736 | tf_op jit(solution)/shard_map/ppermute | solution.py:42
  11.7 1.5 collective-permute-start.29
  13.2 0.9 reshape.70
  14.5 1.9 collective-permute-start
  16.4 1.5 collective-permute-start.1
  17.9 1.3 fusion.71
  20.6 0.9 reshape.75
  22.6 2.8 %collective-permute-start.16 = (bf16[16,768]{1,0:T(8,128)(2,1)S(1)}, bf16[16,768]{1,0:T(8,128)(2,1)S(1)}, u32[]{:S(2)}, u32[]{:S(2)}) collective-permute-start(bf16[16,768]{1,0:T(8,128)(2,1)S(1)} %bitcast.402), channel_id=1, source_target_pairs={{0,24},{8,16},{16,8},{24,0},{1,25},{9,17},{17,9},{25,1},{2,26},{10... | collective-permute-start | bytes 73736 | tf_op jit(solution)/shard_map/ppermute | solution.py:42
  25.5 16.4 %all_gather.9 = bf16[4,128,768]{2,1,0:T(8,128)(2,1)S(1)} all-gather(bf16[4,16,768]{2,1,0:T(8,128)(2,1)S(1)} %pad_maximum_fusion.14), channel_id=1, replica_groups=mesh['dp'=4,'tensor'=8] {'tensor'}, dimensions={1}, use_global_device_ids=true | all-gather | bytes 884736 | tf_op jit(solution)/shard_map/all_gather | solution.py:108
  44.6 15.3 %all_gather.10 = bf16[4,128,768]{2,1,0:T(8,128)(2,1)S(1)} all-gather(bf16[4,16,768]{2,1,0:T(8,128)(2,1)S(1)} %pad_maximum_fusion.16), channel_id=1, replica_groups=mesh['dp'=4,'tensor'=8] {'tensor'}, dimensions={1}, use_global_device_ids=true | all-gather | bytes 884736 | tf_op jit(solution)/shard_map/all_gather | solution.py:108
  62.1 16.0 %all_gather.11 = bf16[4,128,768]{2,1,0:T(8,128)(2,1)S(1)} all-gather(bf16[4,16,768]{2,1,0:T(8,128)(2,1)S(1)} %pad_maximum_fusion.18), channel_id=1, replica_groups=mesh['dp'=4,'tensor'=8] {'tensor'}, dimensions={1}, use_global_device_ids=true | all-gather | bytes 884736 | tf_op jit(solution)/shard_map/all_gather | solution.py:108
  78.1 0.8 fusion.11
  78.9 0.8 fusion.9
  79.7 0.8 fusion.8
  80.6 1.6 collective-permute-start.3
  82.3 1.6 collective-permute-start.5
  85.1 1.6 collective-permute-start.31
  86.7 0.8 fusion.10
  87.6 5.1 %collective-permute-done.3 = bf16[2,64,1536]{2,1,0:T(8,128)(2,1)S(1)} collective-permute-done((bf16[2,64,1536]{2,1,0:T(8,128)(2,1)S(1)}, bf16[2,64,1536]{2,1,0:T(8,128)(2,1)S(1)}, u32[]{:S(2)}, u32[]{:S(2)}) %collective-permute-start.3) | collective-permute-done | bytes 393248 | tf_op jit(solution)/shard_map/ppermute | solution.py:42
  92.6 1.5 collective-permute-start.33
  94.7 1.1 collective-permute-start.4
  96.3 4.7 %collective-permute-done.17 = bf16[2,64,1536]{2,1,0:T(8,128)(2,1)S(1)} collective-permute-done((bf16[2,64,1536]{2,1,0:T(8,128)(2,1)S(1)}, bf16[2,64,1536]{2,1,0:T(8,128)(2,1)S(1)}, u32[]{:S(2)}, u32[]{:S(2)}) %collective-permute-start.17) | collective-permute-done | bytes 393248 | tf_op jit(solution)/shard_map/ppermute | solution.py:42
  101.1 1.5 collective-permute-start.6
  103.1 1.6 collective-permute-start.18
  105.2 4.3 %collective-permute-done.31 = bf16[2,64,1536]{2,1,0:T(8,128)(2,1)S(1)} collective-permute-done((bf16[2,64,1536]{2,1,0:T(8,128)(2,1)S(1)}, bf16[2,64,1536]{2,1,0:T(8,128)(2,1)S(1)}, u32[]{:S(2)}, u32[]{:S(2)}) %collective-permute-start.31) | collective-permute-done | bytes 393248 | tf_op jit(solution)/shard_map/ppermute | solution.py:42
  109.5 1.5 collective-permute-start.20
  111.0 0.8 fusion.34
  111.8 1.6 collective-permute-start.32
  113.4 0.8 fusion.29
  114.2 1.0 collective-permute-start.34
  115.8 1.2 collective-permute-start.8
  117.6 2.0 collective-permute-done.18
  119.6 1.5 collective-permute-start.7
  124.3 0.9 fusion.38
  126.0 1.5 collective-permute-start.35
  127.5 0.9 fusion.33
  128.4 1.6 collective-permute-start.36
  130.7 1.5 collective-permute-done.21
  132.7 0.8 pad_maximum_fusion.9
  133.5 1.5 collective-permute-start.24
  135.0 0.8 pad_maximum_fusion.8
  136.4 1.5 collective-permute-start.23
  137.9 0.8 pad_maximum_fusion.13
  139.2 0.8 pad_maximum_fusion.12
  140.0 4.8 %collective-permute-done.9 = bf16[2,64,1536]{2,1,0:T(8,128)(2,1)S(1)} collective-permute-done((bf16[2,64,1536]{2,1,0:T(8,128)(2,1)S(1)}, bf16[2,64,1536]{2,1,0:T(8,128)(2,1)S(1)}, u32[]{:S(2)}, u32[]{:S(2)}) %collective-permute-start.9) | collective-permute-done | bytes 393248 | tf_op jit(solution)/shard_map/ppermute | solution.py:42
  144.9 1.5 collective-permute-start.37
  146.8 2.3 %convolution_convert_fusion.13 = bf16[512,768]{1,0:T(8,128)(2,1)} fusion(bf16[512,1536]{1,0:T(8,128)(2,1)S(1)} %bitcast.362, bf16[1536,768]{1,0:T(8,128)(2,1)S(1)} %copy-done.1), kind=kOutput, calls=%fused_computation.35 | convolution fusion | flops 1208352768 | bytes 4718592 | tf_op jit(solution)/shard_map/dot_general | solution.py:23
  149.4 3.4 %collective-permute-done.24 = bf16[2,64,1536]{2,1,0:T(8,128)(2,1)} collective-permute-done((bf16[2,64,1536]{2,1,0:T(8,128)(2,1)}, bf16[2,64,1536]{2,1,0:T(8,128)(2,1)}, u32[]{:S(2)}, u32[]{:S(2)}) %collective-permute-start.24) | collective-permute-done | bytes 393248 | tf_op jit(solution)/shard_map/ppermute | solution.py:42
  152.8 1.0 slice_bitcast_fusion.10
  153.9 1.0 slice_bitcast_fusion.11
  155.3 1.4 copy-done.2
  156.6 2.3 convolution_convert_fusion.12
  159.6 1.1 slice_bitcast_fusion.2
  160.9 1.1 slice_bitcast_fusion.3
  162.1 3.6 %convolution_bitcast_fusion = f32[768,1536]{1,0:T(8,128)} fusion(bf16[4,128,768]{2,1,0:T(8,128)(2,1)S(1)} %all_gather.9, bf16[1,128,1536]{2,1,0:T(8,128)(2,1)S(1)} %maximum_bitcast_fusion.11, bf16[1,128,1536]{2,1,0:T(8,128)(2,1)S(1)} %maximum_bitcast_fusion.10, bf16[1,128,1536]{2,1,0:T(8,128)(2,1)S(1)} %maximum_bitcast_fusion.9, ...), kind=kOutput, calls=%fused_computation | convolution fusion | flops 1210318848 | bytes 7077888 | tf_op jit(solution)/shard_map/dot_general | solution.py:163
  165.7 14.9 %reduce-scatter.3.cloned.1.call-done = bf16[4,16,768]{2,1,0:T(8,128)(2,1)} async-done(((bf16[4,128,768]{2,1,0:T(8,128)(2,1)}), bf16[4,16,768]{2,1,0:T(8,128)(2,1)}) %reduce-scatter.3.cloned.1.call-update) | async-done | bytes 98320 | tf_op jit(solution)/shard_map/reduce_scatter | solution.py:147
  180.7 0.8 fusion.74
  181.5 2.5 %collective-permute-start.13 = (bf16[16,768]{1,0:T(8,128)(2,1)S(1)}, bf16[16,768]{1,0:T(8,128)(2,1)S(1)}, u32[]{:S(2)}, u32[]{:S(2)}) collective-permute-start(bf16[16,768]{1,0:T(8,128)(2,1)S(1)} %get-tuple-element.30), channel_id=1, source_target_pairs={{0,24},{8,16},{16,8},{24,0},{1,25},{9,17},{17,9},{25,1},{2,26},{10... | collective-permute-start | bytes 73736 | tf_op jit(solution)/shard_map/ppermute | solution.py:42
  185.0 27.8 %reduce-scatter.5.cloned.1.call-done = bf16[4,16,768]{2,1,0:T(8,128)(2,1)} async-done(((bf16[4,128,768]{2,1,0:T(8,128)(2,1)}), bf16[4,16,768]{2,1,0:T(8,128)(2,1)}) %reduce-scatter.5.cloned.1.call-update) | async-done | bytes 98320 | tf_op jit(solution)/shard_map/reduce_scatter | solution.py:147
  212.8 0.8 fusion.73
  213.6 2.5 %collective-permute-start.27 = (bf16[16,768]{1,0:T(8,128)(2,1)S(1)}, bf16[16,768]{1,0:T(8,128)(2,1)S(1)}, u32[]{:S(2)}, u32[]{:S(2)}) collective-permute-start(bf16[16,768]{1,0:T(8,128)(2,1)S(1)} %get-tuple-element.22), channel_id=1, source_target_pairs={{0,24},{8,16},{16,8},{24,0},{1,25},{9,17},{17,9},{25,1},{2,26},{10... | collective-permute-start | bytes 73736 | tf_op jit(solution)/shard_map/ppermute | solution.py:42
  217.3 1.1 collective-permute-done.27
  218.4 1.5 collective-permute-done.26
  (143 shorter events, 26.4 us)
Async XLA Ops:
  7.2 34.7 %copy-start = (bf16[768,1536]{1,0:T(8,128)(2,1)S(1)}, bf16[768,1536]{1,0:T(8,128)(2,1)}, u32[]{:S(2)}) copy-start(bf16[768,1536]{1,0:T(8,128)(2,1)} %param.14) | copy-start | bytes 7077892
  7.2 173.5 %reduce-scatter.3.cloned.1.call-start = ((), (), s32[]{:S(2)}) async-start(), calls=%async_computation.2 | async-start | bytes 884736 | tf_op jit(solution)/shard_map/reduce_scatter | solution.py:147
  8.7 53.4 %collective-permute-start.28 = (bf16[16,768]{1,0:T(8,128)(2,1)S(1)}, bf16[16,768]{1,0:T(8,128)(2,1)S(1)}, u32[]{:S(2)}, u32[]{:S(2)}) collective-permute-start(bf16[16,768]{1,0:T(8,128)(2,1)S(1)} %bitcast.396), channel_id=1, source_target_pairs={{0,8},{8,0},{16,24},{24,16},{1,9},{9,1},{17,25},{25,17},{2,10},{10... | collective-permute-start | bytes 73736 | tf_op jit(solution)/shard_map/ppermute | solution.py:42
  11.7 50.4 %collective-permute-start.29 = (bf16[16,768]{1,0:T(8,128)(2,1)S(1)}, bf16[16,768]{1,0:T(8,128)(2,1)S(1)}, u32[]{:S(2)}, u32[]{:S(2)}) collective-permute-start(bf16[16,768]{1,0:T(8,128)(2,1)S(1)} %bitcast.397), channel_id=1, source_target_pairs={{0,16},{8,24},{16,0},{24,8},{1,17},{9,25},{17,1},{25,9},{2,18},{10... | collective-permute-start | bytes 73736 | tf_op jit(solution)/shard_map/ppermute | solution.py:42
  14.4 7.5 %collective-permute-start.2 = (bf16[16,768]{1,0:T(8,128)(2,1)S(1)}, bf16[16,768]{1,0:T(8,128)(2,1)S(1)}, u32[]{:S(2)}, u32[]{:S(2)}) collective-permute-start(bf16[16,768]{1,0:T(8,128)(2,1)S(1)} %bitcast.401), channel_id=1, source_target_pairs={{0,24},{8,16},{16,8},{24,0},{1,25},{9,17},{17,9},{25,1},{2,26},{10... | collective-permute-start | bytes 73736 | tf_op jit(solution)/shard_map/ppermute | solution.py:42
  14.5 8.1 %collective-permute-start = (bf16[16,768]{1,0:T(8,128)(2,1)S(1)}, bf16[16,768]{1,0:T(8,128)(2,1)S(1)}, u32[]{:S(2)}, u32[]{:S(2)}) collective-permute-start(bf16[16,768]{1,0:T(8,128)(2,1)S(1)} %bitcast.400), channel_id=1, source_target_pairs={{0,8},{8,0},{16,24},{24,16},{1,9},{9,1},{17,25},{25,17},{2,10},{10... | collective-permute-start | bytes 73736 | tf_op jit(solution)/shard_map/ppermute | solution.py:42
  16.4 6.2 %collective-permute-start.1 = (bf16[16,768]{1,0:T(8,128)(2,1)S(1)}, bf16[16,768]{1,0:T(8,128)(2,1)S(1)}, u32[]{:S(2)}, u32[]{:S(2)}) collective-permute-start(bf16[16,768]{1,0:T(8,128)(2,1)S(1)} %bitcast.399), channel_id=1, source_target_pairs={{0,16},{8,24},{16,0},{24,8},{1,17},{9,25},{17,1},{25,9},{2,18},{10... | collective-permute-start | bytes 73736 | tf_op jit(solution)/shard_map/ppermute | solution.py:42
  21.9 22.1 %collective-permute-start.14 = (bf16[16,768]{1,0:T(8,128)(2,1)S(1)}, bf16[16,768]{1,0:T(8,128)(2,1)S(1)}, u32[]{:S(2)}, u32[]{:S(2)}) collective-permute-start(bf16[16,768]{1,0:T(8,128)(2,1)S(1)} %bitcast.404), channel_id=1, source_target_pairs={{0,8},{8,0},{16,24},{24,16},{1,9},{9,1},{17,25},{25,17},{2,10},{10... | collective-permute-start | bytes 73736 | tf_op jit(solution)/shard_map/ppermute | solution.py:42
  22.5 22.0 %collective-permute-start.15 = (bf16[16,768]{1,0:T(8,128)(2,1)S(1)}, bf16[16,768]{1,0:T(8,128)(2,1)S(1)}, u32[]{:S(2)}, u32[]{:S(2)}) collective-permute-start(bf16[16,768]{1,0:T(8,128)(2,1)S(1)} %bitcast.403), channel_id=1, source_target_pairs={{0,16},{8,24},{16,0},{24,8},{1,17},{9,25},{17,1},{25,9},{2,18},{10... | collective-permute-start | bytes 73736 | tf_op jit(solution)/shard_map/ppermute | solution.py:42
  22.6 21.9 %collective-permute-start.16 = (bf16[16,768]{1,0:T(8,128)(2,1)S(1)}, bf16[16,768]{1,0:T(8,128)(2,1)S(1)}, u32[]{:S(2)}, u32[]{:S(2)}) collective-permute-start(bf16[16,768]{1,0:T(8,128)(2,1)S(1)} %bitcast.402), channel_id=1, source_target_pairs={{0,24},{8,16},{16,8},{24,0},{1,25},{9,17},{17,9},{25,1},{2,26},{10... | collective-permute-start | bytes 73736 | tf_op jit(solution)/shard_map/ppermute | solution.py:42
  44.0 18.0 %collective-permute-start.30 = (bf16[16,768]{1,0:T(8,128)(2,1)S(1)}, bf16[16,768]{1,0:T(8,128)(2,1)S(1)}, u32[]{:S(2)}, u32[]{:S(2)}) collective-permute-start(bf16[16,768]{1,0:T(8,128)(2,1)S(1)} %bitcast.398), channel_id=1, source_target_pairs={{0,24},{8,16},{16,8},{24,0},{1,25},{9,17},{17,9},{25,1},{2,26},{10... | collective-permute-start | bytes 73736 | tf_op jit(solution)/shard_map/ppermute | solution.py:42
  61.5 16.6 %copy-start.1 = (bf16[1536,768]{1,0:T(8,128)(2,1)S(1)}, bf16[1536,768]{1,0:T(8,128)(2,1)}, u32[]{:S(2)}) copy-start(bf16[1536,768]{1,0:T(8,128)(2,1)} %param.15) | copy-start | bytes 7077892
  80.6 12.0 %collective-permute-start.3 = (bf16[2,64,1536]{2,1,0:T(8,128)(2,1)S(1)}, bf16[2,64,1536]{2,1,0:T(8,128)(2,1)S(1)}, u32[]{:S(2)}, u32[]{:S(2)}) collective-permute-start(bf16[2,64,1536]{2,1,0:T(8,128)(2,1)S(1)} %pad_maximum_fusion.2), channel_id=1, source_target_pairs={{0,16},{8,24},{16,0},{24,8},{1,17},{9,25},{17,1},{25,9},{2,18},{10... | collective-permute-start | bytes 1179656 | tf_op jit(solution)/shard_map/ppermute | solution.py:42
  82.3 12.4 %collective-permute-start.5 = (bf16[2,64,1536]{2,1,0:T(8,128)(2,1)S(1)}, bf16[2,64,1536]{2,1,0:T(8,128)(2,1)S(1)}, u32[]{:S(2)}, u32[]{:S(2)}) collective-permute-start(bf16[2,64,1536]{2,1,0:T(8,128)(2,1)S(1)} %pad_maximum_fusion.3), channel_id=1, source_target_pairs={{0,8},{8,0},{16,24},{24,16},{1,9},{9,1},{17,25},{25,17},{2,10},{10... | collective-permute-start | bytes 1179656 | tf_op jit(solution)/shard_map/ppermute | solution.py:42
  83.9 17.2 %collective-permute-start.17 = (bf16[2,64,1536]{2,1,0:T(8,128)(2,1)S(1)}, bf16[2,64,1536]{2,1,0:T(8,128)(2,1)S(1)}, u32[]{:S(2)}, u32[]{:S(2)}) collective-permute-start(bf16[2,64,1536]{2,1,0:T(8,128)(2,1)S(1)} %pad_maximum_fusion.6), channel_id=1, source_target_pairs={{0,16},{8,24},{16,0},{24,8},{1,17},{9,25},{17,1},{25,9},{2,18},{10... | collective-permute-start | bytes 1179656 | tf_op jit(solution)/shard_map/ppermute | solution.py:42
  84.5 18.6 %collective-permute-start.19 = (bf16[2,64,1536]{2,1,0:T(8,128)(2,1)S(1)}, bf16[2,64,1536]{2,1,0:T(8,128)(2,1)S(1)}, u32[]{:S(2)}, u32[]{:S(2)}) collective-permute-start(bf16[2,64,1536]{2,1,0:T(8,128)(2,1)S(1)} %pad_maximum_fusion.7), channel_id=1, source_target_pairs={{0,8},{8,0},{16,24},{24,16},{1,9},{9,1},{17,25},{25,17},{2,10},{10... | collective-permute-start | bytes 1179656 | tf_op jit(solution)/shard_map/ppermute | solution.py:42
  85.1 24.4 %collective-permute-start.31 = (bf16[2,64,1536]{2,1,0:T(8,128)(2,1)S(1)}, bf16[2,64,1536]{2,1,0:T(8,128)(2,1)S(1)}, u32[]{:S(2)}, u32[]{:S(2)}) collective-permute-start(bf16[2,64,1536]{2,1,0:T(8,128)(2,1)S(1)} %pad_maximum_fusion.10), channel_id=1, source_target_pairs={{0,16},{8,24},{16,0},{24,8},{1,17},{9,25},{17,1},{25,9},{2,18},{10... | collective-permute-start | bytes 1179656 | tf_op jit(solution)/shard_map/ppermute | solution.py:42
  92.6 19.2 %collective-permute-start.33 = (bf16[2,64,1536]{2,1,0:T(8,128)(2,1)S(1)}, bf16[2,64,1536]{2,1,0:T(8,128)(2,1)S(1)}, u32[]{:S(2)}, u32[]{:S(2)}) collective-permute-start(bf16[2,64,1536]{2,1,0:T(8,128)(2,1)S(1)} %pad_maximum_fusion.11), channel_id=1, source_target_pairs={{0,8},{8,0},{16,24},{24,16},{1,9},{9,1},{17,25},{25,17},{2,10},{10... | collective-permute-start | bytes 1179656 | tf_op jit(solution)/shard_map/ppermute | solution.py:42
  94.7 21.2 %collective-permute-start.4 = (bf16[64,1536]{1,0:T(8,128)(2,1)S(1)}, bf16[64,1536]{1,0:T(8,128)(2,1)S(1)}, u32[]{:S(2)}, u32[]{:S(2)}) collective-permute-start(bf16[64,1536]{1,0:T(8,128)(2,1)S(1)} %fusion.51), channel_id=1, source_target_pairs={{0,8},{8,0},{16,24},{24,16},{1,9},{9,1},{17,25},{25,17},{2,10},{10... | collective-permute-start | bytes 589832 | tf_op jit(solution)/shard_map/ppermute | solution.py:42
  101.1 13.2 %collective-permute-start.6 = (bf16[64,1536]{1,0:T(8,128)(2,1)S(1)}, bf16[64,1536]{1,0:T(8,128)(2,1)S(1)}, u32[]{:S(2)}, u32[]{:S(2)}) collective-permute-start(bf16[64,1536]{1,0:T(8,128)(2,1)S(1)} %fusion.49), channel_id=1, source_target_pairs={{0,16},{8,24},{16,0},{24,8},{1,17},{9,25},{17,1},{25,9},{2,18},{10... | collective-permute-start | bytes 589832 | tf_op jit(solution)/shard_map/ppermute | solution.py:42
  103.1 16.5 %collective-permute-start.18 = (bf16[64,1536]{1,0:T(8,128)(2,1)S(1)}, bf16[64,1536]{1,0:T(8,128)(2,1)S(1)}, u32[]{:S(2)}, u32[]{:S(2)}) collective-permute-start(bf16[64,1536]{1,0:T(8,128)(2,1)S(1)} %fusion.44), channel_id=1, source_target_pairs={{0,8},{8,0},{16,24},{24,16},{1,9},{9,1},{17,25},{25,17},{2,10},{10... | collective-permute-start | bytes 589832 | tf_op jit(solution)/shard_map/ppermute | solution.py:42
  109.5 12.3 %collective-permute-start.20 = (bf16[64,1536]{1,0:T(8,128)(2,1)S(1)}, bf16[64,1536]{1,0:T(8,128)(2,1)S(1)}, u32[]{:S(2)}, u32[]{:S(2)}) collective-permute-start(bf16[64,1536]{1,0:T(8,128)(2,1)S(1)} %fusion.39), channel_id=1, source_target_pairs={{0,16},{8,24},{16,0},{24,8},{1,17},{9,25},{17,1},{25,9},{2,18},{10... | collective-permute-start | bytes 589832 | tf_op jit(solution)/shard_map/ppermute | solution.py:42
  111.8 11.9 %collective-permute-start.32 = (bf16[64,1536]{1,0:T(8,128)(2,1)S(1)}, bf16[64,1536]{1,0:T(8,128)(2,1)S(1)}, u32[]{:S(2)}, u32[]{:S(2)}) collective-permute-start(bf16[64,1536]{1,0:T(8,128)(2,1)S(1)} %fusion.34), channel_id=1, source_target_pairs={{0,8},{8,0},{16,24},{24,16},{1,9},{9,1},{17,25},{25,17},{2,10},{10... | collective-permute-start | bytes 589832 | tf_op jit(solution)/shard_map/ppermute | solution.py:42
  114.2 11.7 %collective-permute-start.34 = (bf16[64,1536]{1,0:T(8,128)(2,1)S(1)}, bf16[64,1536]{1,0:T(8,128)(2,1)S(1)}, u32[]{:S(2)}, u32[]{:S(2)}) collective-permute-start(bf16[64,1536]{1,0:T(8,128)(2,1)S(1)} %fusion.29), channel_id=1, source_target_pairs={{0,16},{8,24},{16,0},{24,8},{1,17},{9,25},{17,1},{25,9},{2,18},{10... | collective-permute-start | bytes 589832 | tf_op jit(solution)/shard_map/ppermute | solution.py:42
  115.8 12.6 %collective-permute-start.8 = (bf16[64,1536]{1,0:T(8,128)(2,1)S(1)}, bf16[64,1536]{1,0:T(8,128)(2,1)S(1)}, u32[]{:S(2)}, u32[]{:S(2)}) collective-permute-start(bf16[64,1536]{1,0:T(8,128)(2,1)S(1)} %get-tuple-element.37), channel_id=1, source_target_pairs={{0,16},{8,24},{16,0},{24,8},{1,17},{9,25},{17,1},{25,9},{2,18},{10... | collective-permute-start | bytes 589832 | tf_op jit(solution)/shard_map/ppermute | solution.py:42
  119.6 10.5 %collective-permute-start.7 = (bf16[64,1536]{1,0:T(8,128)(2,1)S(1)}, bf16[64,1536]{1,0:T(8,128)(2,1)S(1)}, u32[]{:S(2)}, u32[]{:S(2)}) collective-permute-start(bf16[64,1536]{1,0:T(8,128)(2,1)S(1)} %get-tuple-element.39), channel_id=1, source_target_pairs={{0,8},{8,0},{16,24},{24,16},{1,9},{9,1},{17,25},{25,17},{2,10},{10... | collective-permute-start | bytes 589832 | tf_op jit(solution)/shard_map/ppermute | solution.py:42
  121.8 10.4 %collective-permute-start.21 = (bf16[64,1536]{1,0:T(8,128)(2,1)S(1)}, bf16[64,1536]{1,0:T(8,128)(2,1)S(1)}, u32[]{:S(2)}, u32[]{:S(2)}) collective-permute-start(bf16[64,1536]{1,0:T(8,128)(2,1)S(1)} %fusion.48), channel_id=1, source_target_pairs={{0,8},{8,0},{16,24},{24,16},{1,9},{9,1},{17,25},{25,17},{2,10},{10... | collective-permute-start | bytes 589832 | tf_op jit(solution)/shard_map/ppermute | solution.py:42
  123.8 9.7 %collective-permute-start.22 = (bf16[64,1536]{1,0:T(8,128)(2,1)S(1)}, bf16[64,1536]{1,0:T(8,128)(2,1)S(1)}, u32[]{:S(2)}, u32[]{:S(2)}) collective-permute-start(bf16[64,1536]{1,0:T(8,128)(2,1)S(1)} %fusion.43), channel_id=1, source_target_pairs={{0,16},{8,24},{16,0},{24,8},{1,17},{9,25},{17,1},{25,9},{2,18},{10... | collective-permute-start | bytes 589832 | tf_op jit(solution)/shard_map/ppermute | solution.py:42
  126.0 10.5 %collective-permute-start.35 = (bf16[64,1536]{1,0:T(8,128)(2,1)S(1)}, bf16[64,1536]{1,0:T(8,128)(2,1)S(1)}, u32[]{:S(2)}, u32[]{:S(2)}) collective-permute-start(bf16[64,1536]{1,0:T(8,128)(2,1)S(1)} %fusion.38), channel_id=1, source_target_pairs={{0,8},{8,0},{16,24},{24,16},{1,9},{9,1},{17,25},{25,17},{2,10},{10... | collective-permute-start | bytes 589832 | tf_op jit(solution)/shard_map/ppermute | solution.py:42
  128.4 10.3 %collective-permute-start.36 = (bf16[64,1536]{1,0:T(8,128)(2,1)S(1)}, bf16[64,1536]{1,0:T(8,128)(2,1)S(1)}, u32[]{:S(2)}, u32[]{:S(2)}) collective-permute-start(bf16[64,1536]{1,0:T(8,128)(2,1)S(1)} %fusion.33), channel_id=1, source_target_pairs={{0,16},{8,24},{16,0},{24,8},{1,17},{9,25},{17,1},{25,9},{2,18},{10... | collective-permute-start | bytes 589832 | tf_op jit(solution)/shard_map/ppermute | solution.py:42
  130.1 14.8 %collective-permute-start.9 = (bf16[2,64,1536]{2,1,0:T(8,128)(2,1)S(1)}, bf16[2,64,1536]{2,1,0:T(8,128)(2,1)S(1)}, u32[]{:S(2)}, u32[]{:S(2)}) collective-permute-start(bf16[2,64,1536]{2,1,0:T(8,128)(2,1)S(1)} %pad_maximum_fusion.4), channel_id=1, source_target_pairs={{0,8},{8,0},{16,24},{24,16},{1,9},{9,1},{17,25},{25,17},{2,10},{10... | collective-permute-start | bytes 1179656 | tf_op jit(solution)/shard_map/ppermute | solution.py:42
  132.2 14.2 %copy-start.6 = (bf16[64,1536]{1,0:T(8,128)(2,1)}, bf16[64,1536]{1,0:T(8,128)(2,1)S(1)}, u32[]{:S(2)}) copy-start(bf16[64,1536]{1,0:T(8,128)(2,1)S(1)} %collective-permute-done.21) | copy-start | bytes 589828
  132.2 14.2 %collective-permute-start.10 = (bf16[2,64,1536]{2,1,0:T(8,128)(2,1)S(1)}, bf16[2,64,1536]{2,1,0:T(8,128)(2,1)S(1)}, u32[]{:S(2)}, u32[]{:S(2)}) collective-permute-start(bf16[2,64,1536]{2,1,0:T(8,128)(2,1)S(1)} %pad_maximum_fusion.5), channel_id=1, source_target_pairs={{0,16},{8,24},{16,0},{24,8},{1,17},{9,25},{17,1},{25,9},{2,18},{10... | collective-permute-start | bytes 1179656 | tf_op jit(solution)/shard_map/ppermute | solution.py:42
  133.5 12.9 %copy-start.10 = (bf16[64,1536]{1,0:T(8,128)(2,1)}, bf16[64,1536]{1,0:T(8,128)(2,1)S(1)}, u32[]{:S(2)}) copy-start(bf16[64,1536]{1,0:T(8,128)(2,1)S(1)} %collective-permute-done.22) | copy-start | bytes 589828
  133.5 19.3 %collective-permute-start.24 = (bf16[2,64,1536]{2,1,0:T(8,128)(2,1)}, bf16[2,64,1536]{2,1,0:T(8,128)(2,1)}, u32[]{:S(2)}, u32[]{:S(2)}) collective-permute-start(bf16[2,64,1536]{2,1,0:T(8,128)(2,1)} %pad_maximum_fusion.9), channel_id=1, source_target_pairs={{0,16},{8,24},{16,0},{24,8},{1,17},{9,25},{17,1},{25,9},{2,18},{10... | collective-permute-start | bytes 1179656 | tf_op jit(solution)/shard_map/ppermute | solution.py:42
  136.4 10.1 %copy-start.4 = (bf16[64,1536]{1,0:T(8,128)(2,1)}, bf16[64,1536]{1,0:T(8,128)(2,1)S(1)}, u32[]{:S(2)}) copy-start(bf16[64,1536]{1,0:T(8,128)(2,1)S(1)} %collective-permute-done.35) | copy-start | bytes 589828
  136.4 17.4 %collective-permute-start.23 = (bf16[2,64,1536]{2,1,0:T(8,128)(2,1)}, bf16[2,64,1536]{2,1,0:T(8,128)(2,1)}, u32[]{:S(2)}, u32[]{:S(2)}) collective-permute-start(bf16[2,64,1536]{2,1,0:T(8,128)(2,1)} %pad_maximum_fusion.8), channel_id=1, source_target_pairs={{0,8},{8,0},{16,24},{24,16},{1,9},{9,1},{17,25},{25,17},{2,10},{10... | collective-permute-start | bytes 1179656 | tf_op jit(solution)/shard_map/ppermute | solution.py:42
  138.7 7.8 %copy-start.8 = (bf16[64,1536]{1,0:T(8,128)(2,1)}, bf16[64,1536]{1,0:T(8,128)(2,1)S(1)}, u32[]{:S(2)}) copy-start(bf16[64,1536]{1,0:T(8,128)(2,1)S(1)} %collective-permute-done.36) | copy-start | bytes 589828
  138.7 20.9 %collective-permute-start.38 = (bf16[2,64,1536]{2,1,0:T(8,128)(2,1)}, bf16[2,64,1536]{2,1,0:T(8,128)(2,1)}, u32[]{:S(2)}, u32[]{:S(2)}) collective-permute-start(bf16[2,64,1536]{2,1,0:T(8,128)(2,1)} %pad_maximum_fusion.13), channel_id=1, source_target_pairs={{0,16},{8,24},{16,0},{24,8},{1,17},{9,25},{17,1},{25,9},{2,18},{10... | collective-permute-start | bytes 1179656 | tf_op jit(solution)/shard_map/ppermute | solution.py:42
  144.9 16.1 %collective-permute-start.37 = (bf16[2,64,1536]{2,1,0:T(8,128)(2,1)}, bf16[2,64,1536]{2,1,0:T(8,128)(2,1)}, u32[]{:S(2)}, u32[]{:S(2)}) collective-permute-start(bf16[2,64,1536]{2,1,0:T(8,128)(2,1)} %pad_maximum_fusion.12), channel_id=1, source_target_pairs={{0,8},{8,0},{16,24},{24,16},{1,9},{9,1},{17,25},{25,17},{2,10},{10... | collective-permute-start | bytes 1179656 | tf_op jit(solution)/shard_map/ppermute | solution.py:42
  149.1 63.7 %reduce-scatter.5.cloned.1.call-start = ((), (), s32[]{:S(2)}) async-start(), calls=%async_computation.3 | async-start | bytes 884736 | tf_op jit(solution)/shard_map/reduce_scatter | solution.py:147
  149.4 5.6 %copy-start.11 = (bf16[64,1536]{1,0:T(8,128)(2,1)S(1)}, bf16[64,1536]{1,0:T(8,128)(2,1)}, u32[]{:S(2)}) copy-start(bf16[64,1536]{1,0:T(8,128)(2,1)} %copy-done.10) | copy-start | bytes 589828
  149.4 5.6 %copy-start.7 = (bf16[64,1536]{1,0:T(8,128)(2,1)S(1)}, bf16[64,1536]{1,0:T(8,128)(2,1)}, u32[]{:S(2)}) copy-start(bf16[64,1536]{1,0:T(8,128)(2,1)} %copy-done.6) | copy-start | bytes 589828
  149.4 5.7 %copy-start.3 = (bf16[1,128,1536]{2,1,0:T(8,128)(2,1)S(1)}, bf16[1,128,1536]{2,1,0:T(8,128)(2,1)}, u32[]{:S(2)}) copy-start(bf16[1,128,1536]{2,1,0:T(8,128)(2,1)} %maximum_bitcast_fusion.4) | copy-start | bytes 1179652
  155.0 1.7 copy-start.2
  158.9 3.1 %copy-start.9 = (bf16[64,1536]{1,0:T(8,128)(2,1)S(1)}, bf16[64,1536]{1,0:T(8,128)(2,1)}, u32[]{:S(2)}) copy-start(bf16[64,1536]{1,0:T(8,128)(2,1)} %copy-done.8) | copy-start | bytes 589828
  158.9 3.1 %copy-start.5 = (bf16[64,1536]{1,0:T(8,128)(2,1)S(1)}, bf16[64,1536]{1,0:T(8,128)(2,1)}, u32[]{:S(2)}) copy-start(bf16[64,1536]{1,0:T(8,128)(2,1)} %copy-done.4) | copy-start | bytes 589828
  181.5 35.3 %collective-permute-start.13 = (bf16[16,768]{1,0:T(8,128)(2,1)S(1)}, bf16[16,768]{1,0:T(8,128)(2,1)S(1)}, u32[]{:S(2)}, u32[]{:S(2)}) collective-permute-start(bf16[16,768]{1,0:T(8,128)(2,1)S(1)} %get-tuple-element.30), channel_id=1, source_target_pairs={{0,24},{8,16},{16,8},{24,0},{1,25},{9,17},{17,9},{25,1},{2,26},{10... | collective-permute-start | bytes 73736 | tf_op jit(solution)/shard_map/ppermute | solution.py:42
  184.0 33.2 %collective-permute-start.12 = (bf16[16,768]{1,0:T(8,128)(2,1)S(1)}, bf16[16,768]{1,0:T(8,128)(2,1)S(1)}, u32[]{:S(2)}, u32[]{:S(2)}) collective-permute-start(bf16[16,768]{1,0:T(8,128)(2,1)S(1)} %get-tuple-element.31), channel_id=1, source_target_pairs={{0,16},{8,24},{16,0},{24,8},{1,17},{9,25},{17,1},{25,9},{2,18},{10... | collective-permute-start | bytes 73736 | tf_op jit(solution)/shard_map/ppermute | solution.py:42
  184.6 32.6 %collective-permute-start.11 = (bf16[16,768]{1,0:T(8,128)(2,1)S(1)}, bf16[16,768]{1,0:T(8,128)(2,1)S(1)}, u32[]{:S(2)}, u32[]{:S(2)}) collective-permute-start(bf16[16,768]{1,0:T(8,128)(2,1)S(1)} %get-tuple-element.32), channel_id=1, source_target_pairs={{0,8},{8,0},{16,24},{24,16},{1,9},{9,1},{17,25},{25,17},{2,10},{10... | collective-permute-start | bytes 73736 | tf_op jit(solution)/shard_map/ppermute | solution.py:42
  213.6 4.8 %collective-permute-start.27 = (bf16[16,768]{1,0:T(8,128)(2,1)S(1)}, bf16[16,768]{1,0:T(8,128)(2,1)S(1)}, u32[]{:S(2)}, u32[]{:S(2)}) collective-permute-start(bf16[16,768]{1,0:T(8,128)(2,1)S(1)} %get-tuple-element.22), channel_id=1, source_target_pairs={{0,24},{8,16},{16,8},{24,0},{1,25},{9,17},{17,9},{25,1},{2,26},{10... | collective-permute-start | bytes 73736 | tf_op jit(solution)/shard_map/ppermute | solution.py:42
  216.1 3.8 %collective-permute-start.26 = (bf16[16,768]{1,0:T(8,128)(2,1)S(1)}, bf16[16,768]{1,0:T(8,128)(2,1)S(1)}, u32[]{:S(2)}, u32[]{:S(2)}) collective-permute-start(bf16[16,768]{1,0:T(8,128)(2,1)S(1)} %get-tuple-element.23), channel_id=1, source_target_pairs={{0,16},{8,24},{16,0},{24,8},{1,17},{9,25},{17,1},{25,9},{2,18},{10... | collective-permute-start | bytes 73736 | tf_op jit(solution)/shard_map/ppermute | solution.py:42
  216.8 3.8 %collective-permute-start.25 = (bf16[16,768]{1,0:T(8,128)(2,1)S(1)}, bf16[16,768]{1,0:T(8,128)(2,1)S(1)}, u32[]{:S(2)}, u32[]{:S(2)}) collective-permute-start(bf16[16,768]{1,0:T(8,128)(2,1)S(1)} %get-tuple-element.24), channel_id=1, source_target_pairs={{0,8},{8,0},{16,24},{24,16},{1,9},{9,1},{17,25},{25,17},{2,10},{10... | collective-permute-start | bytes 73736 | tf_op jit(solution)/shard_map/ppermute | solution.py:42
Sparse Core Ops, SparseCore 0:
  149.2 31.3 reduce-scatter.2
  183.0 29.7 reduce-scatter.4

commit v3 on v2

--- a/solution.py
+++ b/solution.py
@@ -30,7 +30,7 @@
     return dp_count // lo, lo
 
 
-def shift(value, grid, step):
+def shift(value, grid, step, axis="dp"):
     hi, lo = grid
     if step[0] % hi == 0 and step[1] % lo == 0:
         return value
@@ -39,7 +39,7 @@
         for a in range(hi)
         for b in range(lo)
     ]
-    return lax.ppermute(value, "dp", pairs)
+    return lax.ppermute(value, axis, pairs)
 
 
 def axis_step(axis, size):
@@ -98,16 +98,28 @@
     slots = [(i, j) for i in range(grid[0]) for j in range(grid[1])]
     place = {s: k for k, s in enumerate(slots)}
 
-    def own_channels(rows):
-        rows = rows.reshape(own_rows, dp_count, own_cols)
+    tensor_count = lax.axis_size("tensor")
+    cores = 2 - tensor_count % 2
+    pod = (tensor_count // cores, cores)
+    at = lax.axis_index("tensor")
+    at_hi, at_lo = at // cores, at % cores
+
+    def own_channels(arrays):
+        count = len(arrays)
         pieces = []
         for i, j in slots:
             target = (me_hi + i) % grid[0] * grid[1] + (me_lo + j) % grid[1]
-            piece = lax.dynamic_index_in_dim(rows, target, 1, keepdims=False)
+            piece = jnp.stack(
+                [lax.dynamic_slice_in_dim(v, target * own_cols, own_cols, 1) for v in arrays]
+            )
             pieces.append(shift(piece, grid, (i, j)))
-        return lax.all_gather(jnp.stack(pieces), "tensor", axis=1, tiled=True)
-
-    tok_cols, tan_cols, cot_cols = [own_channels(v) for v in (tokens, tangent_in, cotangent)]
+        block = jnp.stack(pieces, axis=1)
+        held = jnp.stack([shift(block, pod, (i, 0), "tensor") for i in range(pod[0])], axis=2)
+        both = jnp.stack([shift(held, pod, (0, k), "tensor") for k in range(pod[1])], axis=3)
+        return both.reshape(count, dp_count, tensor_count * own_rows, own_cols)
+
+    (tok_cols,) = own_channels([tokens])
+    tan_cols, cot_cols = own_channels([tangent_in, cotangent])
     group_rows = tok_cols.shape[1]
     cut = group_rows // 2
     halves = [(0, slice(0, cut)), (1, slice(cut, group_rows))]
@@ -133,7 +145,12 @@
             for first, rows in halves
         ]
 
-    row_at = jnp.arange(group_rows, dtype=jnp.int32)
+    back_hi = (at_hi - jnp.arange(pod[0], dtype=jnp.int32)) % pod[0]
+    back_lo = (at_lo - jnp.arange(pod[1], dtype=jnp.int32)) % pod[1]
+    row_at = (
+        (back_hi[:, None] * cores + back_lo[None, :])[:, :, None] * own_rows
+        + jnp.arange(own_rows, dtype=jnp.int32)
+    ).reshape(group_rows)
     keep = [(row_at[rows] < live_rows)[:, None] for _, rows in halves]
 
     def everywhere(values):
@@ -143,8 +160,14 @@
 
     def down(hidden):
         flat = hidden.reshape(dp_count * group_rows, -1)
-        terms = half(dot(flat, w_out)).reshape(dp_count, group_rows, own_cols)
-        summed = lax.psum_scatter(terms, "tensor", scatter_dimension=1, tiled=True)
+        terms = dot(flat, w_out).reshape(dp_count, *pod, own_rows, own_cols)
+        near = terms[:, :, 0]
+        for k in range(1, pod[1]):
+            near = near + shift(half(terms[:, :, k]), pod, (0, -k), "tensor").astype(jnp.float32)
+        total = near[:, 0]
+        for i in range(1, pod[0]):
+            total = total + shift(half(near[:, i]), pod, (-i, 0), "tensor").astype(jnp.float32)
+        summed = half(total)
         cols = jnp.stack(
             [shift(summed[place[(i, j)]], grid, (-i, -j)) for i, j in slots]
         ).reshape(*grid, own_rows, own_cols)

time: 231 us -> 179 us (0.77)
  blocking collectives: 47.7 us -> 0 us
  starting transfers between devices: 48.2 us -> 64.7 us
  between operations: 14.8 us -> 1.37 us
  local copies, waits for them, and re-layouts: 12.5 us -> 5.17 us
    all_gather x3 -> x0, blocking collectives: 47.7 us -> none  [own_channels(): return lax.all_gather(jnp.stack(pieces), 'tensor', axis=1, tiled=True)]
    reduce_scatter x2 -> x0, waiting for transfers between devices: 42.8 us -> none  [down(): summed = lax.psum_scatter(terms, 'tensor', scatter_dimension=1, tiled=True)]
    ppermute x39 -> x52, waiting for transfers between devices: 31.3 us -> 73.7 us  [shift(): return lax.ppermute(value, axis, pairs)]
    ppermute x39 -> x52, starting transfers between devices: 47.9 us -> 64.7 us  [shift(): return lax.ppermute(value, axis, pairs)]
    squeeze x6, local copies, waits for them, and re-layouts: 4.26 us -> 0.16 us  [gather_groups(): found[(i, j) if first == 0 else (j, i)] = there[i]]
    reshape x5 -> x0, local copies, waits for them, and re-layouts: 3.11 us -> none  [the longest x3 2.96 us: own_channels(): rows = rows.reshape(own_rows, dp_count, own_cols)]
    another operation x6, other arithmetic: 3.22 us -> 0.23 us  [gather_groups(): jnp.stack([shift(value, grid, axis_step(first, i)) for i in range(n1)])]
    another operation x3 -> x12, other arithmetic: 0.05 us -> 3.04 us  [the longest x3 1.42 us: own_channels(): jnp.stack([shift(held, pod, (0, k), 'tensor') for k in range(pod[1])], ax...]
  transfers between devices with their start and end apart: 41 -> 52, of which waited for: 16 -> 19; matrix products, arithmetic and copies ran while one was open for 16% -> 20% of each run, Pallas kernels for 0% -> 0%
where the time goes in v3:
time: 179 us
  waiting for transfers between devices  73.7 us (41%)
  starting transfers between devices  64.7 us (36%)
  matrix products  26.1 us (15%)
  other arithmetic  7.97 us (4%)
  local copies, waits for them, and re-layouts  5.17 us (3%)
    ppermute x52, waiting for transfers between devices, shift(): return lax.ppermute(value, axis, pairs)  73.7 us
    ppermute x52, starting transfers between devices, shift(): return lax.ppermute(value, axis, pairs)  64.7 us
    dot_general x18, matrix products, dot(): return jnp.dot(a, b, preferred_element_type=jnp.float32)  14.8 us
    dot_general x8, matrix products, back(): lax.dot_general(cols[place[s], r], w_out, (((1,), (1,)), ((), ())), prefe...  7.71 us
    dot_general x1, matrix products, local(): lax.dot_general(tok_cols.reshape(dp_count * group_rows, own_cols), grad_a...  3.6 us
  transfers between devices with their start and end apart: 52, of which 19 were waited for; matrix products, arithmetic and copies ran while one was open for 20% of the time, Pallas kernels for 0%

profile of v3, /device:TPU:0, one launch (start us, length us, event | category | flops | bytes accessed | tf_op | source)
XLA Modules:
  0.0 179.0 jit_solution(3970453074398301184)
XLA Ops:
  0.7 0.9 dynamic-slice_bitcast_fusion.6
  2.5 4.0 %collective-permute-start.24 = (bf16[2,16,768]{2,1,0:T(8,128)(2,1)S(1)}, bf16[2,16,768]{2,1,0:T(8,128)(2,1)S(1)}, u32[]{:S(2)}, u32[]{:S(2)}) collective-permute-start(bf16[2,16,768]{2,1,0:T(8,128)(2,1)S(1)} %pad_maximum_fusion.31), channel_id=1, source_target_pairs={{0,24},{8,16},{16,8},{24,0},{1,25},{9,17},{17,9},{25,1},{2,26},{10... | collective-permute-start | bytes 147464 | tf_op jit(solution)/shard_map/ppermute | solution.py:42
  7.8 1.5 collective-permute-start.2
  9.4 1.9 %collective-permute-start = (bf16[1,16,768]{2,1,0:T(8,128)(2,1)S(1)}, bf16[1,16,768]{2,1,0:T(8,128)(2,1)S(1)}, u32[]{:S(2)}, u32[]{:S(2)}) collective-permute-start(bf16[1,16,768]{2,1,0:T(8,128)(2,1)S(1)} %get-tuple-element.54), channel_id=1, source_target_pairs={{0,8},{8,0},{16,24},{24,16},{1,9},{9,1},{17,25},{25,17},{2,10},{10... | collective-permute-start | bytes 73736 | tf_op jit(solution)/shard_map/ppermute | solution.py:42
  11.4 1.2 collective-permute-done.2
  13.3 4.0 %collective-permute-start.5 = (bf16[1,4,16,768]{3,2,1,0:T(8,128)(2,1)S(1)}, bf16[1,4,16,768]{3,2,1,0:T(8,128)(2,1)S(1)}, u32[]{:S(2)}, u32[]{:S(2)}) collective-permute-start(bf16[1,4,16,768]{3,2,1,0:T(8,128)(2,1)S(1)} %get-tuple-element.52), channel_id=1, source_target_pairs={{0,6},{1,7},{2,0},{3,1},{4,2},{5,3},{6,4},{7,5},{8,14},{9,15},{10,... | collective-permute-start | bytes 294920 | tf_op jit(solution)/shard_map/ppermute | solution.py:42
  17.3 1.0 collective-permute-start.3
  18.4 1.3 fusion.96
  19.7 1.5 collective-permute-start.22
  21.2 3.3 %collective-permute-done.4 = bf16[1,4,16,768]{3,2,1,0:T(8,128)(2,1)S(1)} collective-permute-done((bf16[1,4,16,768]{3,2,1,0:T(8,128)(2,1)S(1)}, bf16[1,4,16,768]{3,2,1,0:T(8,128)(2,1)S(1)}, u32[]{:S(2)}, u32[]{:S(2)}) %collective-permute-start.4) | collective-permute-done | bytes 98336 | tf_op jit(solution)/shard_map/ppermute | solution.py:42
  24.7 3.4 %collective-permute-start.27 = (bf16[2,4,16,768]{3,2,1,0:T(8,128)(2,1)S(1)}, bf16[2,4,16,768]{3,2,1,0:T(8,128)(2,1)S(1)}, u32[]{:S(2)}, u32[]{:S(2)}) collective-permute-start(bf16[2,4,16,768]{3,2,1,0:T(8,128)(2,1)S(1)} %get-tuple-element.34), channel_id=1, source_target_pairs={{0,6},{1,7},{2,0},{3,1},{4,2},{5,3},{6,4},{7,5},{8,14},{9,15},{10,... | collective-permute-start | bytes 589832 | tf_op jit(solution)/shard_map/ppermute | solution.py:42
  28.8 4.8 %collective-permute-done.27 = bf16[2,4,16,768]{3,2,1,0:T(8,128)(2,1)S(1)} collective-permute-done((bf16[2,4,16,768]{3,2,1,0:T(8,128)(2,1)S(1)}, bf16[2,4,16,768]{3,2,1,0:T(8,128)(2,1)S(1)}, u32[]{:S(2)}, u32[]{:S(2)}) %collective-permute-start.27) | collective-permute-done | bytes 196640 | tf_op jit(solution)/shard_map/ppermute | solution.py:42
  33.6 11.0 %collective-permute-done.26 = bf16[2,4,16,768]{3,2,1,0:T(8,128)(2,1)S(1)} collective-permute-done((bf16[2,4,16,768]{3,2,1,0:T(8,128)(2,1)S(1)}, bf16[2,4,16,768]{3,2,1,0:T(8,128)(2,1)S(1)}, u32[]{:S(2)}, u32[]{:S(2)}) %collective-permute-start.26) | collective-permute-done | bytes 196640 | tf_op jit(solution)/shard_map/ppermute | solution.py:42
  44.7 1.3 pad_maximum_fusion.3
  49.0 1.7 collective-permute-start.9
  51.4 1.5 collective-permute-start.7
  53.8 7.0 %collective-permute-done.9 = bf16[2,64,1536]{2,1,0:T(8,128)(2,1)} collective-permute-done((bf16[2,64,1536]{2,1,0:T(8,128)(2,1)}, bf16[2,64,1536]{2,1,0:T(8,128)(2,1)}, u32[]{:S(2)}, u32[]{:S(2)}) %collective-permute-start.9) | collective-permute-done | bytes 393248 | tf_op jit(solution)/shard_map/ppermute | solution.py:42
  60.8 1.5 fusion.65
  62.3 1.6 collective-permute-start.10
  64.5 1.7 collective-permute-start.8
  66.2 1.3 pad_maximum_fusion.1
  70.2 0.8 fusion.15
  71.0 0.8 fusion.14
  71.9 0.8 fusion.13
  72.7 0.8 fusion.12
  74.7 1.7 collective-permute-start.46
  76.4 1.6 collective-permute-start.44
  78.0 1.5 select_convert_fusion
  80.8 15.9 %collective-permute-done.12 = bf16[64,1536]{1,0:T(8,128)(2,1)S(1)} collective-permute-done((bf16[64,1536]{1,0:T(8,128)(2,1)S(1)}, bf16[64,1536]{1,0:T(8,128)(2,1)S(1)}, u32[]{:S(2)}, u32[]{:S(2)}) %collective-permute-start.12) | collective-permute-done | bytes 196640 | tf_op jit(solution)/shard_map/ppermute | solution.py:42
  96.7 1.6 collective-permute-start.11
  98.4 4.5 %collective-permute-done.11 = bf16[64,1536]{1,0:T(8,128)(2,1)S(1)} collective-permute-done((bf16[64,1536]{1,0:T(8,128)(2,1)S(1)}, bf16[64,1536]{1,0:T(8,128)(2,1)S(1)}, u32[]{:S(2)}, u32[]{:S(2)}) %collective-permute-start.11) | collective-permute-done | bytes 196640 | tf_op jit(solution)/shard_map/ppermute | solution.py:42
  102.9 1.6 collective-permute-start.13
  105.7 1.6 collective-permute-start.32
  108.3 0.8 fusion.45
  109.7 0.8 fusion.50
  110.5 9.8 %collective-permute-done.32 = bf16[64,1536]{1,0:T(8,128)(2,1)S(1)} collective-permute-done((bf16[64,1536]{1,0:T(8,128)(2,1)S(1)}, bf16[64,1536]{1,0:T(8,128)(2,1)S(1)}, u32[]{:S(2)}, u32[]{:S(2)}) %collective-permute-start.32) | collective-permute-done | bytes 196640 | tf_op jit(solution)/shard_map/ppermute | solution.py:42
  120.3 1.6 fusion.59
  123.0 1.3 collective-permute-done.47
  124.3 0.8 collective-permute-start.33
  125.1 1.8 %fusion.49 = bf16[64,1536]{1,0:T(8,128)(2,1)S(1)} fusion(bf16[64,1536]{1,0:T(8,128)(2,1)S(1)} %collective-permute-done.47, bf16[2,64,1536]{2,1,0:T(8,128)(2,1)S(1)} %collective-permute-done.46, pred[64]{0:T(512)(128)(4,1)S(1)} %lt.138, bf16[1536,768]{1,0:T(8,128)(2,1)S(1)} %copy-done.1, bf16[4,128,768]{2,1,0:T(8,128)(2,1)S(1)} %bitcast.452, ...), kind=kOutput, calls=%fused_computation.102 | convolution fusion | flops 153747456 | bytes 3834368 | tf_op jit(solution)/shard_map/dot_general | solution.py:136
  127.0 1.8 collective-permute-start.49
  128.7 0.9 fusion.54
  130.0 1.6 fusion.2
  131.8 2.1 %collective-permute-start.35 = (bf16[2,64,1536]{2,1,0:T(8,128)(2,1)S(1)}, bf16[2,64,1536]{2,1,0:T(8,128)(2,1)S(1)}, u32[]{:S(2)}, u32[]{:S(2)}) collective-permute-start(bf16[2,64,1536]{2,1,0:T(8,128)(2,1)S(1)} %pad_maximum_fusion.16), channel_id=1, source_target_pairs={{0,8},{8,0},{16,24},{24,16},{1,9},{9,1},{17,25},{25,17},{2,10},{10... | collective-permute-start | bytes 1179656 | tf_op jit(solution)/shard_map/ppermute | solution.py:42
  134.7 2.0 %collective-permute-start.17 = (bf16[4,16,768]{2,1,0:T(8,128)(2,1)S(1)}, bf16[4,16,768]{2,1,0:T(8,128)(2,1)S(1)}, u32[]{:S(2)}, u32[]{:S(2)}) collective-permute-start(bf16[4,16,768]{2,1,0:T(8,128)(2,1)S(1)} %get-tuple-element.26), channel_id=1, source_target_pairs={{0,4},{1,5},{2,6},{3,7},{4,0},{5,1},{6,2},{7,3},{8,12},{9,13},{10,... | collective-permute-start | bytes 294920 | tf_op jit(solution)/shard_map/ppermute | solution.py:42
  136.7 2.8 %collective-permute-start.16 = (bf16[4,16,768]{2,1,0:T(8,128)(2,1)S(1)}, bf16[4,16,768]{2,1,0:T(8,128)(2,1)S(1)}, u32[]{:S(2)}, u32[]{:S(2)}) collective-permute-start(bf16[4,16,768]{2,1,0:T(8,128)(2,1)S(1)} %get-tuple-element.24), channel_id=1, source_target_pairs={{0,6},{1,7},{2,0},{3,1},{4,2},{5,3},{6,4},{7,5},{8,14},{9,15},{10,... | collective-permute-start | bytes 294920 | tf_op jit(solution)/shard_map/ppermute | solution.py:42
  139.6 2.0 %collective-permute-done.18 = bf16[4,16,768]{2,1,0:T(8,128)(2,1)S(1)} collective-permute-done((bf16[4,16,768]{2,1,0:T(8,128)(2,1)S(1)}, bf16[4,16,768]{2,1,0:T(8,128)(2,1)S(1)}, u32[]{:S(2)}, u32[]{:S(2)}) %collective-permute-start.18) | collective-permute-done | bytes 98336 | tf_op jit(solution)/shard_map/ppermute | solution.py:42
  141.6 1.0 collective-permute-start.36
  142.7 2.5 %collective-permute-done.17 = bf16[4,16,768]{2,1,0:T(8,128)(2,1)S(1)} collective-permute-done((bf16[4,16,768]{2,1,0:T(8,128)(2,1)S(1)}, bf16[4,16,768]{2,1,0:T(8,128)(2,1)S(1)}, u32[]{:S(2)}, u32[]{:S(2)}) %collective-permute-start.17) | collective-permute-done | bytes 98336 | tf_op jit(solution)/shard_map/ppermute | solution.py:42
  145.2 1.3 collective-permute-start.21
  146.5 1.7 collective-permute-start.20
  148.8 1.3 collective-permute-done.21
  150.1 1.5 collective-permute-start.50
  152.3 1.0 collective-permute-start.51
  153.5 1.4 fusion
  155.1 3.9 %collective-permute-done.50 = bf16[2,64,1536]{2,1,0:T(8,128)(2,1)S(1)} collective-permute-done((bf16[2,64,1536]{2,1,0:T(8,128)(2,1)S(1)}, bf16[2,64,1536]{2,1,0:T(8,128)(2,1)S(1)}, u32[]{:S(2)}, u32[]{:S(2)}) %collective-permute-start.50) | collective-permute-done | bytes 393248 | tf_op jit(solution)/shard_map/ppermute | solution.py:42
  159.0 1.7 collective-permute-done.51
  161.0 1.9 %collective-permute-start.40 = (bf16[4,16,768]{2,1,0:T(8,128)(2,1)S(1)}, bf16[4,16,768]{2,1,0:T(8,128)(2,1)S(1)}, u32[]{:S(2)}, u32[]{:S(2)}) collective-permute-start(bf16[4,16,768]{2,1,0:T(8,128)(2,1)S(1)} %get-tuple-element.18), channel_id=1, source_target_pairs={{0,2},{1,3},{2,4},{3,5},{4,6},{5,7},{6,0},{7,1},{8,10},{9,11},{10,... | collective-permute-start | bytes 294920 | tf_op jit(solution)/shard_map/ppermute | solution.py:42
  162.9 2.1 %collective-permute-start.39 = (bf16[4,16,768]{2,1,0:T(8,128)(2,1)S(1)}, bf16[4,16,768]{2,1,0:T(8,128)(2,1)S(1)}, u32[]{:S(2)}, u32[]{:S(2)}) collective-permute-start(bf16[4,16,768]{2,1,0:T(8,128)(2,1)S(1)} %get-tuple-element.19), channel_id=1, source_target_pairs={{0,4},{1,5},{2,6},{3,7},{4,0},{5,1},{6,2},{7,3},{8,12},{9,13},{10,... | collective-permute-start | bytes 294920 | tf_op jit(solution)/shard_map/ppermute | solution.py:42
  165.0 2.8 %collective-permute-start.38 = (bf16[4,16,768]{2,1,0:T(8,128)(2,1)S(1)}, bf16[4,16,768]{2,1,0:T(8,128)(2,1)S(1)}, u32[]{:S(2)}, u32[]{:S(2)}) collective-permute-start(bf16[4,16,768]{2,1,0:T(8,128)(2,1)S(1)} %get-tuple-element.17), channel_id=1, source_target_pairs={{0,6},{1,7},{2,0},{3,1},{4,2},{5,3},{6,4},{7,5},{8,14},{9,15},{10,... | collective-permute-start | bytes 294920 | tf_op jit(solution)/shard_map/ppermute | solution.py:42
  168.9 1.2 collective-permute-done.38
  170.1 1.2 collective-permute-start.43
  171.3 1.7 collective-permute-start.42
  173.7 3.6 %fusion.111 = f32[768,1536]{1,0:T(8,128)} fusion(bf16[512,768]{1,0:T(8,128)(2,1)S(1)} %bitcast.444, bf16[512,1536]{1,0:T(8,128)(2,1)S(1)} %bitcast.445), kind=kOutput, calls=%fused_computation.275 | convolution fusion | flops 1207959552 | bytes 7077888 | tf_op jit(solution)/shard_map/dot_general | solution.py:186
  (144 shorter events, 24.8 us)
Async XLA Ops:
  0.6 45.4 %copy-start = (bf16[768,1536]{1,0:T(8,128)(2,1)S(1)}, bf16[768,1536]{1,0:T(8,128)(2,1)}, u32[]{:S(2)}) copy-start(bf16[768,1536]{1,0:T(8,128)(2,1)} %param.14) | copy-start | bytes 7077892
  2.5 22.1 %collective-permute-start.24 = (bf16[2,16,768]{2,1,0:T(8,128)(2,1)S(1)}, bf16[2,16,768]{2,1,0:T(8,128)(2,1)S(1)}, u32[]{:S(2)}, u32[]{:S(2)}) collective-permute-start(bf16[2,16,768]{2,1,0:T(8,128)(2,1)S(1)} %pad_maximum_fusion.31), channel_id=1, source_target_pairs={{0,24},{8,16},{16,8},{24,0},{1,25},{9,17},{17,9},{25,1},{2,26},{10... | collective-permute-start | bytes 147464 | tf_op jit(solution)/shard_map/ppermute | solution.py:42
  6.5 18.1 %collective-permute-start.23 = (bf16[2,16,768]{2,1,0:T(8,128)(2,1)S(1)}, bf16[2,16,768]{2,1,0:T(8,128)(2,1)S(1)}, u32[]{:S(2)}, u32[]{:S(2)}) collective-permute-start(bf16[2,16,768]{2,1,0:T(8,128)(2,1)S(1)} %pad_maximum_fusion.30), channel_id=1, source_target_pairs={{0,16},{8,24},{16,0},{24,8},{1,17},{9,25},{17,1},{25,9},{2,18},{10... | collective-permute-start | bytes 147464 | tf_op jit(solution)/shard_map/ppermute | solution.py:42
  7.8 4.8 %collective-permute-start.2 = (bf16[1,16,768]{2,1,0:T(8,128)(2,1)S(1)}, bf16[1,16,768]{2,1,0:T(8,128)(2,1)S(1)}, u32[]{:S(2)}, u32[]{:S(2)}) collective-permute-start(bf16[1,16,768]{2,1,0:T(8,128)(2,1)S(1)} %get-tuple-element.55), channel_id=1, source_target_pairs={{0,24},{8,16},{16,8},{24,0},{1,25},{9,17},{17,9},{25,1},{2,26},{10... | collective-permute-start | bytes 73736 | tf_op jit(solution)/shard_map/ppermute | solution.py:42
  9.3 3.8 %collective-permute-start.1 = (bf16[1,16,768]{2,1,0:T(8,128)(2,1)S(1)}, bf16[1,16,768]{2,1,0:T(8,128)(2,1)S(1)}, u32[]{:S(2)}, u32[]{:S(2)}) collective-permute-start(bf16[1,16,768]{2,1,0:T(8,128)(2,1)S(1)} %get-tuple-element.56), channel_id=1, source_target_pairs={{0,16},{8,24},{16,0},{24,8},{1,17},{9,25},{17,1},{25,9},{2,18},{10... | collective-permute-start | bytes 73736 | tf_op jit(solution)/shard_map/ppermute | solution.py:42
  9.4 3.8 %collective-permute-start = (bf16[1,16,768]{2,1,0:T(8,128)(2,1)S(1)}, bf16[1,16,768]{2,1,0:T(8,128)(2,1)S(1)}, u32[]{:S(2)}, u32[]{:S(2)}) collective-permute-start(bf16[1,16,768]{2,1,0:T(8,128)(2,1)S(1)} %get-tuple-element.54), channel_id=1, source_target_pairs={{0,8},{8,0},{16,24},{24,16},{1,9},{9,1},{17,25},{25,17},{2,10},{10... | collective-permute-start | bytes 73736 | tf_op jit(solution)/shard_map/ppermute | solution.py:42
  13.3 6.4 %collective-permute-start.5 = (bf16[1,4,16,768]{3,2,1,0:T(8,128)(2,1)S(1)}, bf16[1,4,16,768]{3,2,1,0:T(8,128)(2,1)S(1)}, u32[]{:S(2)}, u32[]{:S(2)}) collective-permute-start(bf16[1,4,16,768]{3,2,1,0:T(8,128)(2,1)S(1)} %get-tuple-element.52), channel_id=1, source_target_pairs={{0,6},{1,7},{2,0},{3,1},{4,2},{5,3},{6,4},{7,5},{8,14},{9,15},{10,... | collective-permute-start | bytes 294920 | tf_op jit(solution)/shard_map/ppermute | solution.py:42
  17.3 7.1 %collective-permute-start.4 = (bf16[1,4,16,768]{3,2,1,0:T(8,128)(2,1)S(1)}, bf16[1,4,16,768]{3,2,1,0:T(8,128)(2,1)S(1)}, u32[]{:S(2)}, u32[]{:S(2)}) collective-permute-start(bf16[1,4,16,768]{3,2,1,0:T(8,128)(2,1)S(1)} %get-tuple-element.52), channel_id=1, source_target_pairs={{0,4},{1,5},{2,6},{3,7},{4,0},{5,1},{6,2},{7,3},{8,12},{9,13},{10,... | collective-permute-start | bytes 294920 | tf_op jit(solution)/shard_map/ppermute | solution.py:42
  17.3 7.1 %collective-permute-start.3 = (bf16[1,4,16,768]{3,2,1,0:T(8,128)(2,1)S(1)}, bf16[1,4,16,768]{3,2,1,0:T(8,128)(2,1)S(1)}, u32[]{:S(2)}, u32[]{:S(2)}) collective-permute-start(bf16[1,4,16,768]{3,2,1,0:T(8,128)(2,1)S(1)} %get-tuple-element.52), channel_id=1, source_target_pairs={{0,2},{1,3},{2,4},{3,5},{4,6},{5,7},{6,0},{7,1},{8,10},{9,11},{10,... | collective-permute-start | bytes 294920 | tf_op jit(solution)/shard_map/ppermute | solution.py:42
  19.7 4.9 %collective-permute-start.22 = (bf16[2,16,768]{2,1,0:T(8,128)(2,1)S(1)}, bf16[2,16,768]{2,1,0:T(8,128)(2,1)S(1)}, u32[]{:S(2)}, u32[]{:S(2)}) collective-permute-start(bf16[2,16,768]{2,1,0:T(8,128)(2,1)S(1)} %pad_maximum_fusion.29), channel_id=1, source_target_pairs={{0,8},{8,0},{16,24},{24,16},{1,9},{9,1},{17,25},{25,17},{2,10},{10... | collective-permute-start | bytes 147464 | tf_op jit(solution)/shard_map/ppermute | solution.py:42
  24.5 21.5 %collective-permute-start.6 = (bf16[1,4,4,16,768]{4,3,2,1,0:T(8,128)(2,1)S(1)}, bf16[1,4,4,16,768]{4,3,2,1,0:T(8,128)(2,1)S(1)}, u32[]{:S(2)}, u32[]{:S(2)}) collective-permute-start(bf16[1,4,4,16,768]{4,3,2,1,0:T(8,128)(2,1)S(1)} %get-tuple-element.32), channel_id=1, source_target_pairs={{0,1},{1,0},{2,3},{3,2},{4,5},{5,4},{6,7},{7,6},{8,9},{9,8},{10,11... | collective-permute-start | bytes 1179656 | tf_op jit(solution)/shard_map/ppermute | solution.py:42
  24.7 9.0 %collective-permute-start.27 = (bf16[2,4,16,768]{3,2,1,0:T(8,128)(2,1)S(1)}, bf16[2,4,16,768]{3,2,1,0:T(8,128)(2,1)S(1)}, u32[]{:S(2)}, u32[]{:S(2)}) collective-permute-start(bf16[2,4,16,768]{3,2,1,0:T(8,128)(2,1)S(1)} %get-tuple-element.34), channel_id=1, source_target_pairs={{0,6},{1,7},{2,0},{3,1},{4,2},{5,3},{6,4},{7,5},{8,14},{9,15},{10,... | collective-permute-start | bytes 589832 | tf_op jit(solution)/shard_map/ppermute | solution.py:42
  28.1 16.6 %collective-permute-start.26 = (bf16[2,4,16,768]{3,2,1,0:T(8,128)(2,1)S(1)}, bf16[2,4,16,768]{3,2,1,0:T(8,128)(2,1)S(1)}, u32[]{:S(2)}, u32[]{:S(2)}) collective-permute-start(bf16[2,4,16,768]{3,2,1,0:T(8,128)(2,1)S(1)} %get-tuple-element.34), channel_id=1, source_target_pairs={{0,4},{1,5},{2,6},{3,7},{4,0},{5,1},{6,2},{7,3},{8,12},{9,13},{10,... | collective-permute-start | bytes 589832 | tf_op jit(solution)/shard_map/ppermute | solution.py:42
  28.5 16.1 %collective-permute-start.25 = (bf16[2,4,16,768]{3,2,1,0:T(8,128)(2,1)S(1)}, bf16[2,4,16,768]{3,2,1,0:T(8,128)(2,1)S(1)}, u32[]{:S(2)}, u32[]{:S(2)}) collective-permute-start(bf16[2,4,16,768]{3,2,1,0:T(8,128)(2,1)S(1)} %get-tuple-element.34), channel_id=1, source_target_pairs={{0,2},{1,3},{2,4},{3,5},{4,6},{5,7},{6,0},{7,1},{8,10},{9,11},{10,... | collective-permute-start | bytes 589832 | tf_op jit(solution)/shard_map/ppermute | solution.py:42
  46.0 20.2 %collective-permute-start.28 = (bf16[2,4,4,16,768]{4,3,2,1,0:T(8,128)(2,1)}, bf16[2,4,4,16,768]{4,3,2,1,0:T(8,128)(2,1)}, u32[]{:S(2)}, u32[]{:S(2)}) collective-permute-start(bf16[2,4,4,16,768]{4,3,2,1,0:T(8,128)(2,1)} %get-tuple-element.11), channel_id=1, source_target_pairs={{0,1},{1,0},{2,3},{3,2},{4,5},{5,4},{6,7},{7,6},{8,9},{9,8},{10,11... | collective-permute-start | bytes 2359304 | tf_op jit(solution)/shard_map/ppermute | solution.py:42
  49.0 11.8 %collective-permute-start.9 = (bf16[2,64,1536]{2,1,0:T(8,128)(2,1)}, bf16[2,64,1536]{2,1,0:T(8,128)(2,1)}, u32[]{:S(2)}, u32[]{:S(2)}) collective-permute-start(bf16[2,64,1536]{2,1,0:T(8,128)(2,1)} %pad_maximum_fusion.6), channel_id=1, source_target_pairs={{0,8},{8,0},{16,24},{24,16},{1,9},{9,1},{17,25},{25,17},{2,10},{10... | collective-permute-start | bytes 1179656 | tf_op jit(solution)/shard_map/ppermute | solution.py:42
  51.4 12.5 %collective-permute-start.7 = (bf16[2,64,1536]{2,1,0:T(8,128)(2,1)}, bf16[2,64,1536]{2,1,0:T(8,128)(2,1)S(1)}, u32[]{:S(2)}, u32[]{:S(2)}) collective-permute-start(bf16[2,64,1536]{2,1,0:T(8,128)(2,1)} %pad_maximum_fusion.5), channel_id=1, source_target_pairs={{0,16},{8,24},{16,0},{24,8},{1,17},{9,25},{17,1},{25,9},{2,18},{10... | collective-permute-start | bytes 1179656 | tf_op jit(solution)/shard_map/ppermute | solution.py:42
  53.8 12.4 %copy-start.2 = (bf16[2,4,4,1,16,768]{5,4,3,2,1,0:T(8,128)(2,1)S(1)}, bf16[2,4,4,1,16,768]{5,4,3,2,1,0:T(8,128)(2,1)}, u32[]{:S(2)}) copy-start(bf16[2,4,4,1,16,768]{5,4,3,2,1,0:T(8,128)(2,1)} %get-tuple-element.12) | copy-start | bytes 2359300
  62.3 14.1 %collective-permute-start.10 = (bf16[64,1536]{1,0:T(8,128)(2,1)S(1)}, bf16[64,1536]{1,0:T(8,128)(2,1)S(1)}, u32[]{:S(2)}, u32[]{:S(2)}) collective-permute-start(bf16[64,1536]{1,0:T(8,128)(2,1)S(1)} %fusion.65), channel_id=1, source_target_pairs={{0,16},{8,24},{16,0},{24,8},{1,17},{9,25},{17,1},{25,9},{2,18},{10... | collective-permute-start | bytes 589832 | tf_op jit(solution)/shard_map/ppermute | solution.py:42
  64.5 15.1 %collective-permute-start.8 = (bf16[64,1536]{1,0:T(8,128)(2,1)S(1)}, bf16[64,1536]{1,0:T(8,128)(2,1)S(1)}, u32[]{:S(2)}, u32[]{:S(2)}) collective-permute-start(bf16[64,1536]{1,0:T(8,128)(2,1)S(1)} %fusion.67), channel_id=1, source_target_pairs={{0,8},{8,0},{16,24},{24,16},{1,9},{9,1},{17,25},{25,17},{2,10},{10... | collective-permute-start | bytes 589832 | tf_op jit(solution)/shard_map/ppermute | solution.py:42
  68.5 1.7 copy-start.1
  73.6 31.0 %collective-permute-start.31 = (bf16[2,64,1536]{2,1,0:T(8,128)(2,1)S(1)}, bf16[2,64,1536]{2,1,0:T(8,128)(2,1)S(1)}, u32[]{:S(2)}, u32[]{:S(2)}) collective-permute-start(bf16[2,64,1536]{2,1,0:T(8,128)(2,1)S(1)} %pad_maximum_fusion.14), channel_id=1, source_target_pairs={{0,8},{8,0},{16,24},{24,16},{1,9},{9,1},{17,25},{25,17},{2,10},{10... | collective-permute-start | bytes 1179656 | tf_op jit(solution)/shard_map/ppermute | solution.py:42
  74.1 31.6 %collective-permute-start.29 = (bf16[2,64,1536]{2,1,0:T(8,128)(2,1)S(1)}, bf16[2,64,1536]{2,1,0:T(8,128)(2,1)S(1)}, u32[]{:S(2)}, u32[]{:S(2)}) collective-permute-start(bf16[2,64,1536]{2,1,0:T(8,128)(2,1)S(1)} %pad_maximum_fusion.13), channel_id=1, source_target_pairs={{0,16},{8,24},{16,0},{24,8},{1,17},{9,25},{17,1},{25,9},{2,18},{10... | collective-permute-start | bytes 1179656 | tf_op jit(solution)/shard_map/ppermute | solution.py:42
  74.7 33.1 %collective-permute-start.46 = (bf16[2,64,1536]{2,1,0:T(8,128)(2,1)S(1)}, bf16[2,64,1536]{2,1,0:T(8,128)(2,1)S(1)}, u32[]{:S(2)}, u32[]{:S(2)}) collective-permute-start(bf16[2,64,1536]{2,1,0:T(8,128)(2,1)S(1)} %pad_maximum_fusion.22), channel_id=1, source_target_pairs={{0,8},{8,0},{16,24},{24,16},{1,9},{9,1},{17,25},{25,17},{2,10},{10... | collective-permute-start | bytes 1179656 | tf_op jit(solution)/shard_map/ppermute | solution.py:42
  76.4 32.7 %collective-permute-start.44 = (bf16[2,64,1536]{2,1,0:T(8,128)(2,1)S(1)}, bf16[2,64,1536]{2,1,0:T(8,128)(2,1)S(1)}, u32[]{:S(2)}, u32[]{:S(2)}) collective-permute-start(bf16[2,64,1536]{2,1,0:T(8,128)(2,1)S(1)} %pad_maximum_fusion.21), channel_id=1, source_target_pairs={{0,16},{8,24},{16,0},{24,8},{1,17},{9,25},{17,1},{25,9},{2,18},{10... | collective-permute-start | bytes 1179656 | tf_op jit(solution)/shard_map/ppermute | solution.py:42
  79.6 17.1 %collective-permute-start.12 = (bf16[64,1536]{1,0:T(8,128)(2,1)S(1)}, bf16[64,1536]{1,0:T(8,128)(2,1)S(1)}, u32[]{:S(2)}, u32[]{:S(2)}) collective-permute-start(bf16[64,1536]{1,0:T(8,128)(2,1)S(1)} %get-tuple-element.59), channel_id=1, source_target_pairs={{0,16},{8,24},{16,0},{24,8},{1,17},{9,25},{17,1},{25,9},{2,18},{10... | collective-permute-start | bytes 589832 | tf_op jit(solution)/shard_map/ppermute | solution.py:42
  96.7 6.2 %collective-permute-start.11 = (bf16[64,1536]{1,0:T(8,128)(2,1)S(1)}, bf16[64,1536]{1,0:T(8,128)(2,1)S(1)}, u32[]{:S(2)}, u32[]{:S(2)}) collective-permute-start(bf16[64,1536]{1,0:T(8,128)(2,1)S(1)} %get-tuple-element.61), channel_id=1, source_target_pairs={{0,8},{8,0},{16,24},{24,16},{1,9},{9,1},{17,25},{25,17},{2,10},{10... | collective-permute-start | bytes 589832 | tf_op jit(solution)/shard_map/ppermute | solution.py:42
  102.9 26.8 %collective-permute-start.13 = (bf16[2,64,1536]{2,1,0:T(8,128)(2,1)S(1)}, bf16[2,64,1536]{2,1,0:T(8,128)(2,1)S(1)}, u32[]{:S(2)}, u32[]{:S(2)}) collective-permute-start(bf16[2,64,1536]{2,1,0:T(8,128)(2,1)S(1)} %pad_maximum_fusion.8), channel_id=1, source_target_pairs={{0,8},{8,0},{16,24},{24,16},{1,9},{9,1},{17,25},{25,17},{2,10},{10... | collective-permute-start | bytes 1179656 | tf_op jit(solution)/shard_map/ppermute | solution.py:42
  104.6 25.3 %collective-permute-start.14 = (bf16[2,64,1536]{2,1,0:T(8,128)(2,1)S(1)}, bf16[2,64,1536]{2,1,0:T(8,128)(2,1)S(1)}, u32[]{:S(2)}, u32[]{:S(2)}) collective-permute-start(bf16[2,64,1536]{2,1,0:T(8,128)(2,1)S(1)} %pad_maximum_fusion.10), channel_id=1, source_target_pairs={{0,16},{8,24},{16,0},{24,8},{1,17},{9,25},{17,1},{25,9},{2,18},{10... | collective-permute-start | bytes 1179656 | tf_op jit(solution)/shard_map/ppermute | solution.py:42
  105.7 14.6 %collective-permute-start.32 = (bf16[64,1536]{1,0:T(8,128)(2,1)S(1)}, bf16[64,1536]{1,0:T(8,128)(2,1)S(1)}, u32[]{:S(2)}, u32[]{:S(2)}) collective-permute-start(bf16[64,1536]{1,0:T(8,128)(2,1)S(1)} %fusion.55), channel_id=1, source_target_pairs={{0,16},{8,24},{16,0},{24,8},{1,17},{9,25},{17,1},{25,9},{2,18},{10... | collective-permute-start | bytes 589832 | tf_op jit(solution)/shard_map/ppermute | solution.py:42
  107.8 14.1 %collective-permute-start.30 = (bf16[64,1536]{1,0:T(8,128)(2,1)S(1)}, bf16[64,1536]{1,0:T(8,128)(2,1)S(1)}, u32[]{:S(2)}, u32[]{:S(2)}) collective-permute-start(bf16[64,1536]{1,0:T(8,128)(2,1)S(1)} %fusion.60), channel_id=1, source_target_pairs={{0,8},{8,0},{16,24},{24,16},{1,9},{9,1},{17,25},{25,17},{2,10},{10... | collective-permute-start | bytes 589832 | tf_op jit(solution)/shard_map/ppermute | solution.py:42
  109.1 15.2 %collective-permute-start.47 = (bf16[64,1536]{1,0:T(8,128)(2,1)S(1)}, bf16[64,1536]{1,0:T(8,128)(2,1)S(1)}, u32[]{:S(2)}, u32[]{:S(2)}) collective-permute-start(bf16[64,1536]{1,0:T(8,128)(2,1)S(1)} %fusion.45), channel_id=1, source_target_pairs={{0,16},{8,24},{16,0},{24,8},{1,17},{9,25},{17,1},{25,9},{2,18},{10... | collective-permute-start | bytes 589832 | tf_op jit(solution)/shard_map/ppermute | solution.py:42
  120.3 6.7 %collective-permute-start.45 = (bf16[64,1536]{1,0:T(8,128)(2,1)S(1)}, bf16[64,1536]{1,0:T(8,128)(2,1)S(1)}, u32[]{:S(2)}, u32[]{:S(2)}) collective-permute-start(bf16[64,1536]{1,0:T(8,128)(2,1)S(1)} %fusion.50), channel_id=1, source_target_pairs={{0,8},{8,0},{16,24},{24,16},{1,9},{9,1},{17,25},{25,17},{2,10},{10... | collective-permute-start | bytes 589832 | tf_op jit(solution)/shard_map/ppermute | solution.py:42
  121.9 9.8 %collective-permute-start.34 = (bf16[64,1536]{1,0:T(8,128)(2,1)S(1)}, bf16[64,1536]{1,0:T(8,128)(2,1)S(1)}, u32[]{:S(2)}, u32[]{:S(2)}) collective-permute-start(bf16[64,1536]{1,0:T(8,128)(2,1)S(1)} %fusion.59), channel_id=1, source_target_pairs={{0,16},{8,24},{16,0},{24,8},{1,17},{9,25},{17,1},{25,9},{2,18},{10... | collective-permute-start | bytes 589832 | tf_op jit(solution)/shard_map/ppermute | solution.py:42
  124.3 9.5 %collective-permute-start.33 = (bf16[64,1536]{1,0:T(8,128)(2,1)S(1)}, bf16[64,1536]{1,0:T(8,128)(2,1)S(1)}, u32[]{:S(2)}, u32[]{:S(2)}) collective-permute-start(bf16[64,1536]{1,0:T(8,128)(2,1)S(1)} %fusion.64), channel_id=1, source_target_pairs={{0,8},{8,0},{16,24},{24,16},{1,9},{9,1},{17,25},{25,17},{2,10},{10... | collective-permute-start | bytes 589832 | tf_op jit(solution)/shard_map/ppermute | solution.py:42
  127.0 9.7 %collective-permute-start.49 = (bf16[64,1536]{1,0:T(8,128)(2,1)S(1)}, bf16[64,1536]{1,0:T(8,128)(2,1)S(1)}, u32[]{:S(2)}, u32[]{:S(2)}) collective-permute-start(bf16[64,1536]{1,0:T(8,128)(2,1)S(1)} %fusion.49), channel_id=1, source_target_pairs={{0,16},{8,24},{16,0},{24,8},{1,17},{9,25},{17,1},{25,9},{2,18},{10... | collective-permute-start | bytes 589832 | tf_op jit(solution)/shard_map/ppermute | solution.py:42
  129.7 18.5 %collective-permute-start.48 = (bf16[64,1536]{1,0:T(8,128)(2,1)S(1)}, bf16[64,1536]{1,0:T(8,128)(2,1)S(1)}, u32[]{:S(2)}, u32[]{:S(2)}) collective-permute-start(bf16[64,1536]{1,0:T(8,128)(2,1)S(1)} %fusion.54), channel_id=1, source_target_pairs={{0,8},{8,0},{16,24},{24,16},{1,9},{9,1},{17,25},{25,17},{2,10},{10... | collective-permute-start | bytes 589832 | tf_op jit(solution)/shard_map/ppermute | solution.py:42
  131.6 2.3 %collective-permute-start.15 = (bf16[4,4,16,768]{3,2,1,0:T(8,128)(2,1)S(1)}, bf16[4,4,16,768]{3,2,1,0:T(8,128)(2,1)S(1)}, u32[]{:S(2)}, u32[]{:S(2)}) collective-permute-start(bf16[4,4,16,768]{3,2,1,0:T(8,128)(2,1)S(1)} %fusion.43), channel_id=1, source_target_pairs={{0,1},{1,0},{2,3},{3,2},{4,5},{5,4},{6,7},{7,6},{8,9},{9,8},{10,11... | collective-permute-start | bytes 1179656 | tf_op jit(solution)/shard_map/ppermute | solution.py:42
  131.8 21.6 %collective-permute-start.35 = (bf16[2,64,1536]{2,1,0:T(8,128)(2,1)S(1)}, bf16[2,64,1536]{2,1,0:T(8,128)(2,1)S(1)}, u32[]{:S(2)}, u32[]{:S(2)}) collective-permute-start(bf16[2,64,1536]{2,1,0:T(8,128)(2,1)S(1)} %pad_maximum_fusion.16), channel_id=1, source_target_pairs={{0,8},{8,0},{16,24},{24,16},{1,9},{9,1},{17,25},{25,17},{2,10},{10... | collective-permute-start | bytes 1179656 | tf_op jit(solution)/shard_map/ppermute | solution.py:42
  134.0 7.6 %collective-permute-start.18 = (bf16[4,16,768]{2,1,0:T(8,128)(2,1)S(1)}, bf16[4,16,768]{2,1,0:T(8,128)(2,1)S(1)}, u32[]{:S(2)}, u32[]{:S(2)}) collective-permute-start(bf16[4,16,768]{2,1,0:T(8,128)(2,1)S(1)} %get-tuple-element.25), channel_id=1, source_target_pairs={{0,2},{1,3},{2,4},{3,5},{4,6},{5,7},{6,0},{7,1},{8,10},{9,11},{10,... | collective-permute-start | bytes 294920 | tf_op jit(solution)/shard_map/ppermute | solution.py:42
  134.7 10.4 %collective-permute-start.17 = (bf16[4,16,768]{2,1,0:T(8,128)(2,1)S(1)}, bf16[4,16,768]{2,1,0:T(8,128)(2,1)S(1)}, u32[]{:S(2)}, u32[]{:S(2)}) collective-permute-start(bf16[4,16,768]{2,1,0:T(8,128)(2,1)S(1)} %get-tuple-element.26), channel_id=1, source_target_pairs={{0,4},{1,5},{2,6},{3,7},{4,0},{5,1},{6,2},{7,3},{8,12},{9,13},{10,... | collective-permute-start | bytes 294920 | tf_op jit(solution)/shard_map/ppermute | solution.py:42
  136.7 8.4 %collective-permute-start.16 = (bf16[4,16,768]{2,1,0:T(8,128)(2,1)S(1)}, bf16[4,16,768]{2,1,0:T(8,128)(2,1)S(1)}, u32[]{:S(2)}, u32[]{:S(2)}) collective-permute-start(bf16[4,16,768]{2,1,0:T(8,128)(2,1)S(1)} %get-tuple-element.24), channel_id=1, source_target_pairs={{0,6},{1,7},{2,0},{3,1},{4,2},{5,3},{6,4},{7,5},{8,14},{9,15},{10,... | collective-permute-start | bytes 294920 | tf_op jit(solution)/shard_map/ppermute | solution.py:42
  141.6 11.8 %collective-permute-start.36 = (bf16[2,64,1536]{2,1,0:T(8,128)(2,1)S(1)}, bf16[2,64,1536]{2,1,0:T(8,128)(2,1)S(1)}, u32[]{:S(2)}, u32[]{:S(2)}) collective-permute-start(bf16[2,64,1536]{2,1,0:T(8,128)(2,1)S(1)} %pad_maximum_fusion.18), channel_id=1, source_target_pairs={{0,16},{8,24},{16,0},{24,8},{1,17},{9,25},{17,1},{25,9},{2,18},{10... | collective-permute-start | bytes 1179656 | tf_op jit(solution)/shard_map/ppermute | solution.py:42
  145.2 4.9 %collective-permute-start.21 = (bf16[16,768]{1,0:T(8,128)(2,1)S(1)}, bf16[16,768]{1,0:T(8,128)(2,1)S(1)}, u32[]{:S(2)}, u32[]{:S(2)}) collective-permute-start(bf16[16,768]{1,0:T(8,128)(2,1)S(1)} %get-tuple-element.48), channel_id=1, source_target_pairs={{0,24},{8,16},{16,8},{24,0},{1,25},{9,17},{17,9},{25,1},{2,26},{10... | collective-permute-start | bytes 73736 | tf_op jit(solution)/shard_map/ppermute | solution.py:42
  146.5 5.8 %collective-permute-start.20 = (bf16[16,768]{1,0:T(8,128)(2,1)S(1)}, bf16[16,768]{1,0:T(8,128)(2,1)S(1)}, u32[]{:S(2)}, u32[]{:S(2)}) collective-permute-start(bf16[16,768]{1,0:T(8,128)(2,1)S(1)} %get-tuple-element.49), channel_id=1, source_target_pairs={{0,16},{8,24},{16,0},{24,8},{1,17},{9,25},{17,1},{25,9},{2,18},{10... | collective-permute-start | bytes 73736 | tf_op jit(solution)/shard_map/ppermute | solution.py:42
  148.2 5.1 %collective-permute-start.19 = (bf16[16,768]{1,0:T(8,128)(2,1)S(1)}, bf16[16,768]{1,0:T(8,128)(2,1)S(1)}, u32[]{:S(2)}, u32[]{:S(2)}) collective-permute-start(bf16[16,768]{1,0:T(8,128)(2,1)S(1)} %get-tuple-element.50), channel_id=1, source_target_pairs={{0,8},{8,0},{16,24},{24,16},{1,9},{9,1},{17,25},{25,17},{2,10},{10... | collective-permute-start | bytes 73736 | tf_op jit(solution)/shard_map/ppermute | solution.py:42
  150.1 8.9 %collective-permute-start.50 = (bf16[2,64,1536]{2,1,0:T(8,128)(2,1)S(1)}, bf16[2,64,1536]{2,1,0:T(8,128)(2,1)S(1)}, u32[]{:S(2)}, u32[]{:S(2)}) collective-permute-start(bf16[2,64,1536]{2,1,0:T(8,128)(2,1)S(1)} %pad_maximum_fusion.23), channel_id=1, source_target_pairs={{0,8},{8,0},{16,24},{24,16},{1,9},{9,1},{17,25},{25,17},{2,10},{10... | collective-permute-start | bytes 1179656 | tf_op jit(solution)/shard_map/ppermute | solution.py:42
  152.3 8.4 %collective-permute-start.51 = (bf16[2,64,1536]{2,1,0:T(8,128)(2,1)S(1)}, bf16[2,64,1536]{2,1,0:T(8,128)(2,1)S(1)}, u32[]{:S(2)}, u32[]{:S(2)}) collective-permute-start(bf16[2,64,1536]{2,1,0:T(8,128)(2,1)S(1)} %pad_maximum_fusion.24), channel_id=1, source_target_pairs={{0,16},{8,24},{16,0},{24,8},{1,17},{9,25},{17,1},{25,9},{2,18},{10... | collective-permute-start | bytes 1179656 | tf_op jit(solution)/shard_map/ppermute | solution.py:42
  155.0 5.9 %collective-permute-start.37 = (bf16[4,4,16,768]{3,2,1,0:T(8,128)(2,1)S(1)}, bf16[4,4,16,768]{3,2,1,0:T(8,128)(2,1)S(1)}, u32[]{:S(2)}, u32[]{:S(2)}) collective-permute-start(bf16[4,4,16,768]{3,2,1,0:T(8,128)(2,1)S(1)} %fusion.44), channel_id=1, source_target_pairs={{0,1},{1,0},{2,3},{3,2},{4,5},{5,4},{6,7},{7,6},{8,9},{9,8},{10,11... | collective-permute-start | bytes 1179656 | tf_op jit(solution)/shard_map/ppermute | solution.py:42
  161.0 7.0 %collective-permute-start.40 = (bf16[4,16,768]{2,1,0:T(8,128)(2,1)S(1)}, bf16[4,16,768]{2,1,0:T(8,128)(2,1)S(1)}, u32[]{:S(2)}, u32[]{:S(2)}) collective-permute-start(bf16[4,16,768]{2,1,0:T(8,128)(2,1)S(1)} %get-tuple-element.18), channel_id=1, source_target_pairs={{0,2},{1,3},{2,4},{3,5},{4,6},{5,7},{6,0},{7,1},{8,10},{9,11},{10,... | collective-permute-start | bytes 294920 | tf_op jit(solution)/shard_map/ppermute | solution.py:42
  162.9 5.9 %collective-permute-start.39 = (bf16[4,16,768]{2,1,0:T(8,128)(2,1)S(1)}, bf16[4,16,768]{2,1,0:T(8,128)(2,1)S(1)}, u32[]{:S(2)}, u32[]{:S(2)}) collective-permute-start(bf16[4,16,768]{2,1,0:T(8,128)(2,1)S(1)} %get-tuple-element.19), channel_id=1, source_target_pairs={{0,4},{1,5},{2,6},{3,7},{4,0},{5,1},{6,2},{7,3},{8,12},{9,13},{10,... | collective-permute-start | bytes 294920 | tf_op jit(solution)/shard_map/ppermute | solution.py:42
  165.0 5.1 %collective-permute-start.38 = (bf16[4,16,768]{2,1,0:T(8,128)(2,1)S(1)}, bf16[4,16,768]{2,1,0:T(8,128)(2,1)S(1)}, u32[]{:S(2)}, u32[]{:S(2)}) collective-permute-start(bf16[4,16,768]{2,1,0:T(8,128)(2,1)S(1)} %get-tuple-element.17), channel_id=1, source_target_pairs={{0,6},{1,7},{2,0},{3,1},{4,2},{5,3},{6,4},{7,5},{8,14},{9,15},{10,... | collective-permute-start | bytes 294920 | tf_op jit(solution)/shard_map/ppermute | solution.py:42
  170.1 7.2 %collective-permute-start.43 = (bf16[16,768]{1,0:T(8,128)(2,1)S(1)}, bf16[16,768]{1,0:T(8,128)(2,1)S(1)}, u32[]{:S(2)}, u32[]{:S(2)}) collective-permute-start(bf16[16,768]{1,0:T(8,128)(2,1)S(1)} %get-tuple-element.36), channel_id=1, source_target_pairs={{0,24},{8,16},{16,8},{24,0},{1,25},{9,17},{17,9},{25,1},{2,26},{10... | collective-permute-start | bytes 73736 | tf_op jit(solution)/shard_map/ppermute | solution.py:42
  171.3 6.0 %collective-permute-start.42 = (bf16[16,768]{1,0:T(8,128)(2,1)S(1)}, bf16[16,768]{1,0:T(8,128)(2,1)S(1)}, u32[]{:S(2)}, u32[]{:S(2)}) collective-permute-start(bf16[16,768]{1,0:T(8,128)(2,1)S(1)} %get-tuple-element.37), channel_id=1, source_target_pairs={{0,16},{8,24},{16,0},{24,8},{1,17},{9,25},{17,1},{25,9},{2,18},{10... | collective-permute-start | bytes 73736 | tf_op jit(solution)/shard_map/ppermute | solution.py:42
  173.1 4.2 %collective-permute-start.41 = (bf16[16,768]{1,0:T(8,128)(2,1)S(1)}, bf16[16,768]{1,0:T(8,128)(2,1)S(1)}, u32[]{:S(2)}, u32[]{:S(2)}) collective-permute-start(bf16[16,768]{1,0:T(8,128)(2,1)S(1)} %get-tuple-element.38), channel_id=1, source_target_pairs={{0,8},{8,0},{16,24},{24,16},{1,9},{9,1},{17,25},{25,17},{2,10},{10... | collective-permute-start | bytes 73736 | tf_op jit(solution)/shard_map/ppermute | solution.py:42

commit v4 on v3

--- a/solution.py
+++ b/solution.py
@@ -104,41 +104,42 @@
     at = lax.axis_index("tensor")
     at_hi, at_lo = at // cores, at % cores
 
-    def own_channels(arrays):
-        count = len(arrays)
-        pieces = []
-        for i, j in slots:
-            target = (me_hi + i) % grid[0] * grid[1] + (me_lo + j) % grid[1]
-            piece = jnp.stack(
-                [lax.dynamic_slice_in_dim(v, target * own_cols, own_cols, 1) for v in arrays]
-            )
-            pieces.append(shift(piece, grid, (i, j)))
-        block = jnp.stack(pieces, axis=1)
+    pieces = []
+    for i, j in slots:
+        target = (me_hi + i) % grid[0] * grid[1] + (me_lo + j) % grid[1]
+        piece = jnp.stack(
+            [
+                lax.dynamic_slice_in_dim(v, target * own_cols, own_cols, 1)
+                for v in (tokens, tangent_in, cotangent)
+            ]
+        )
+        pieces.append(shift(piece, grid, (i, j)))
+
+    def own_channels(block):
         held = jnp.stack([shift(block, pod, (i, 0), "tensor") for i in range(pod[0])], axis=2)
         both = jnp.stack([shift(held, pod, (0, k), "tensor") for k in range(pod[1])], axis=3)
-        return both.reshape(count, dp_count, tensor_count * own_rows, own_cols)
-
-    (tok_cols,) = own_channels([tokens])
-    tan_cols, cot_cols = own_channels([tangent_in, cotangent])
+        return both.reshape(-1, dp_count, tensor_count * own_rows, own_cols)
+
+    (tok_cols,) = own_channels(jnp.stack([p[:1] for p in pieces], axis=1))
+    later = jnp.stack([p[1:] for p in pieces], axis=1)
+    later, _ = lax.optimization_barrier((later, tok_cols))
+    tan_cols, cot_cols = own_channels(later)
     group_rows = tok_cols.shape[1]
     cut = group_rows // 2
     halves = [(0, slice(0, cut)), (1, slice(cut, group_rows))]
 
-    def up(cols):
-        return [
-            sum_to_owner(lambda s, r=rows: dot(cols[place[s], r], w_in), grid, first)
-            for first, rows in halves
-        ]
-
-    def back(cols):
+    def up(rows):
+        return dot(rows, w_in)
+
+    def back(rows):
+        return lax.dot_general(
+            rows, w_out, (((1,), (1,)), ((), ())), preferred_element_type=jnp.float32
+        )
+
+    def sums(terms):
         return [
             sum_to_owner(
-                lambda s, r=rows: lax.dot_general(
-                    cols[place[s], r],
-                    w_out,
-                    (((1,), (1,)), ((), ())),
-                    preferred_element_type=jnp.float32,
-                ),
+                lambda s, r=rows: jnp.stack([f(cols[place[s], r]) for f, cols in terms]),
                 grid,
                 first,
             )
@@ -167,22 +168,20 @@
         total = near[:, 0]
         for i in range(1, pod[0]):
             total = total + shift(half(near[:, i]), pod, (-i, 0), "tensor").astype(jnp.float32)
-        summed = half(total)
-        cols = jnp.stack(
-            [shift(summed[place[(i, j)]], grid, (-i, -j)) for i, j in slots]
-        ).reshape(*grid, own_rows, own_cols)
-        cols = jnp.roll(jnp.roll(cols, me_hi, axis=0), me_lo, axis=1)
-        return cols.transpose(2, 0, 1, 3).reshape(own_rows, model_cols)
-
-    pre_act = up(tok_cols)
+        return half(total)
+
+    pre_act = [p[0] for p in sums([(up, tok_cols)])]
     pairs = [gelu_pair(p) for p in pre_act]
     act_all = everywhere([a for a, _ in pairs])
-    pre_tan = up(tan_cols)
-    dact_all = everywhere([s * t for (_, s), t in zip(pairs, pre_tan)])
-    back_grad = back(cot_cols)
-    grad_all = everywhere([s * g for (_, s), g in zip(pairs, back_grad)])
-    out = down(act_all)
-    tan = down(dact_all)
+    both = sums([(up, tan_cols), (back, cot_cols)])
+    dact_all = everywhere([s * v[0] for (_, s), v in zip(pairs, both)])
+    grad_all = everywhere([s * v[1] for (_, s), v in zip(pairs, both)])
+    summed = jnp.stack([down(act_all), down(dact_all)], axis=1)
+    cols = jnp.stack(
+        [shift(summed[place[(i, j)]], grid, (-i, -j)) for i, j in slots]
+    ).reshape(*grid, 2, own_rows, own_cols)
+    cols = jnp.roll(jnp.roll(cols, me_hi, axis=0), me_lo, axis=1)
+    out, tan = cols.transpose(2, 3, 0, 1, 4).reshape(2, own_rows, model_cols)
     grad_w_in = lax.dot_general(
         tok_cols.reshape(dp_count * group_rows, own_cols),
         grad_all.reshape(dp_count * group_rows, -1),

time: 179 us -> 172 us (0.961)
  starting transfers between devices: 64.7 us -> 47.3 us
  waiting for transfers between devices: 73.7 us -> 83.8 us
    ppermute x52 -> x42, starting transfers between devices: 64.7 us -> 47.3 us  [shift(): return lax.ppermute(value, axis, pairs)]
    ppermute x52 -> x42, waiting for transfers between devices: 73.7 us -> 83.8 us  [shift(): return lax.ppermute(value, axis, pairs)]
  transfers between devices with their start and end apart: 52 -> 42, of which waited for: 19 -> 23; matrix products, arithmetic and copies ran while one was open for 20% -> 20% of each run, Pallas kernels for 0% -> 0%
where the time goes in v4:
time: 172 us; the launch traced here: 171 us
  waiting for transfers between devices  83.8 us (49%)
  starting transfers between devices  47.3 us (28%)
  matrix products  25.7 us (15%)
  other arithmetic  8.73 us (5%)
  local copies, waits for them, and re-layouts  4.45 us (3%)
    ppermute x42, waiting for transfers between devices, shift(): return lax.ppermute(value, axis, pairs)  83.8 us
    ppermute x42, starting transfers between devices, shift(): return lax.ppermute(value, axis, pairs)  47.3 us
    dot_general x18, matrix products, dot(): return jnp.dot(a, b, preferred_element_type=jnp.float32)  15.5 us
    dot_general x8, matrix products, back(): lax.dot_general(rows, w_out, (((1,), (1,)), ((), ())), preferred_element_...  6.63 us
    dot_general x1, matrix products, local(): lax.dot_general(tok_cols.reshape(dp_count * group_rows, own_cols), grad_a...  3.6 us
  transfers between devices with their start and end apart: 42, of which 23 were waited for; matrix products, arithmetic and copies ran while one was open for 20% of the time, Pallas kernels for 0%

profile of v4, /device:TPU:0, one launch (start us, length us, event | category | flops | bytes accessed | tf_op | source)
XLA Modules:
  0.0 171.4 jit_solution(8857571062582419393)
XLA Ops:
  0.7 0.9 dynamic-slice_bitcast_fusion.11
  1.7 0.9 dynamic-slice_bitcast_fusion
  2.6 4.0 %collective-permute-start.2 = (bf16[3,16,768]{2,1,0:T(8,128)(2,1)S(1)}, bf16[3,16,768]{2,1,0:T(8,128)(2,1)S(1)}, u32[]{:S(2)}, u32[]{:S(2)}) collective-permute-start(bf16[3,16,768]{2,1,0:T(8,128)(2,1)S(1)} %pad_maximum_fusion.29), channel_id=1, source_target_pairs={{0,24},{8,16},{16,8},{24,0},{1,25},{9,17},{17,9},{25,1},{2,26},{10... | collective-permute-start | bytes 221192 | tf_op jit(solution)/shard_map/ppermute | solution.py:42
  7.5 1.3 fusion.94
  8.9 2.1 %collective-permute-done.1 = bf16[3,16,768]{2,1,0:T(8,128)(2,1)S(1)} collective-permute-done((bf16[3,16,768]{2,1,0:T(8,128)(2,1)S(1)}, bf16[3,16,768]{2,1,0:T(8,128)(2,1)S(1)}, u32[]{:S(2)}, u32[]{:S(2)}) %collective-permute-start.1) | collective-permute-done | bytes 73760 | tf_op jit(solution)/shard_map/ppermute | solution.py:42
  11.6 3.7 %collective-permute-start.5 = (bf16[1,4,16,768]{3,2,1,0:T(8,128)(2,1)S(1)}, bf16[1,4,16,768]{3,2,1,0:T(8,128)(2,1)S(1)}, u32[]{:S(2)}, u32[]{:S(2)}) collective-permute-start(bf16[1,4,16,768]{3,2,1,0:T(8,128)(2,1)S(1)} %get-tuple-element.52), channel_id=1, source_target_pairs={{0,6},{1,7},{2,0},{3,1},{4,2},{5,3},{6,4},{7,5},{8,14},{9,15},{10,... | collective-permute-start | bytes 294920 | tf_op jit(solution)/shard_map/ppermute | solution.py:42
  15.3 1.0 collective-permute-start.3
  16.3 2.1 %collective-permute-done.5 = bf16[1,4,16,768]{3,2,1,0:T(8,128)(2,1)S(1)} collective-permute-done((bf16[1,4,16,768]{3,2,1,0:T(8,128)(2,1)S(1)}, bf16[1,4,16,768]{3,2,1,0:T(8,128)(2,1)S(1)}, u32[]{:S(2)}, u32[]{:S(2)}) %collective-permute-start.5) | collective-permute-done | bytes 98336 | tf_op jit(solution)/shard_map/ppermute | solution.py:42
  18.4 5.1 %collective-permute-done.4 = bf16[1,4,16,768]{3,2,1,0:T(8,128)(2,1)S(1)} collective-permute-done((bf16[1,4,16,768]{3,2,1,0:T(8,128)(2,1)S(1)}, bf16[1,4,16,768]{3,2,1,0:T(8,128)(2,1)S(1)}, u32[]{:S(2)}, u32[]{:S(2)}) %collective-permute-start.4) | collective-permute-done | bytes 98336 | tf_op jit(solution)/shard_map/ppermute | solution.py:42
  23.7 1.6 collective-permute-done.6
  25.4 1.5 collective-permute-start.21
  27.3 1.9 %collective-permute-start.19 = (bf16[2,4,16,768]{3,2,0,1:T(8,128)(2,1)S(1)}, bf16[2,4,16,768]{3,2,0,1:T(8,128)(2,1)S(1)}, u32[]{:S(2)}, u32[]{:S(2)}) collective-permute-start(bf16[2,4,16,768]{3,2,0,1:T(8,128)(2,1)S(1)} %pad_maximum_fusion.24), channel_id=1, source_target_pairs={{0,2},{1,3},{2,4},{3,5},{4,6},{5,7},{6,0},{7,1},{8,10},{9,11},{10,... | collective-permute-start | bytes 589832 | tf_op jit(solution)/shard_map/ppermute | solution.py:42
  30.9 1.4 collective-permute-start.9
  32.9 12.2 %collective-permute-done.20 = bf16[2,4,16,768]{3,2,0,1:T(8,128)(2,1)S(1)} collective-permute-done((bf16[2,4,16,768]{3,2,0,1:T(8,128)(2,1)S(1)}, bf16[2,4,16,768]{3,2,0,1:T(8,128)(2,1)S(1)}, u32[]{:S(2)}, u32[]{:S(2)}) %collective-permute-start.20) | collective-permute-done | bytes 196640 | tf_op jit(solution)/shard_map/ppermute | solution.py:42
  45.0 1.3 fusion.100
  46.3 0.8 pad_maximum_fusion.8
  47.1 1.4 collective-permute-start.7
  49.3 1.5 fusion.68
  50.9 0.7 collective-permute-start.10
  51.6 7.8 %collective-permute-done.7 = bf16[2,1,64,1536]{3,2,1,0:T(8,128)(2,1)} collective-permute-done((bf16[2,1,64,1536]{3,2,1,0:T(8,128)(2,1)}, bf16[2,1,64,1536]{3,2,1,0:T(8,128)(2,1)}, u32[]{:S(2)}, u32[]{:S(2)}) %collective-permute-start.7) | collective-permute-done | bytes 393248 | tf_op jit(solution)/shard_map/ppermute | solution.py:42
  59.3 1.5 fusion.67
  60.8 1.4 collective-permute-start.8
  62.2 1.4 fusion.24
  64.1 0.8 convolution_bitcast_fusion.2
  65.0 0.8 convolution_bitcast_fusion
  66.9 0.8 fusion.15
  68.3 0.8 fusion.13
  69.7 0.8 fusion.11
  71.1 0.8 fusion.9
  72.6 0.7 collective-permute-start.25
  73.5 0.8 convolution_bitcast_fusion.6
  74.3 1.5 collective-permute-start.23
  76.3 0.8 convolution_bitcast_fusion.4
  77.7 13.5 %collective-permute-done.25 = bf16[2,2,64,1536]{3,2,1,0:T(8,128)(2,1)S(1)} collective-permute-done((bf16[2,2,64,1536]{3,2,1,0:T(8,128)(2,1)S(1)}, bf16[2,2,64,1536]{3,2,1,0:T(8,128)(2,1)S(1)}, u32[]{:S(2)}, u32[]{:S(2)}) %collective-permute-start.25) | collective-permute-done | bytes 786464 | tf_op jit(solution)/shard_map/ppermute | solution.py:42
  91.3 0.7 collective-permute-start.26
  92.0 1.2 collective-permute-done.23
  93.2 2.2 %collective-permute-start.24 = (bf16[2,64,1536]{2,1,0:T(8,128)(2,1)S(1)}, bf16[2,64,1536]{2,1,0:T(8,128)(2,1)S(1)}, u32[]{:S(2)}, u32[]{:S(2)}) collective-permute-start(bf16[2,64,1536]{2,1,0:T(8,128)(2,1)S(1)} %fusion.28), channel_id=1, source_target_pairs={{0,8},{8,0},{16,24},{24,16},{1,9},{9,1},{17,25},{25,17},{2,10},{10... | collective-permute-start | bytes 1179656 | tf_op jit(solution)/shard_map/ppermute | solution.py:42
  95.4 5.7 %collective-permute-done.26 = bf16[2,64,1536]{2,1,0:T(8,128)(2,1)S(1)} collective-permute-done((bf16[2,64,1536]{2,1,0:T(8,128)(2,1)S(1)}, bf16[2,64,1536]{2,1,0:T(8,128)(2,1)S(1)}, u32[]{:S(2)}, u32[]{:S(2)}) %collective-permute-start.26) | collective-permute-done | bytes 393248 | tf_op jit(solution)/shard_map/ppermute | solution.py:42
  101.2 1.7 fusion.60
  102.8 1.5 collective-permute-start.12
  104.4 1.7 fusion.62
  106.8 1.5 collective-permute-start.28
  109.6 1.5 collective-permute-start.39
  111.9 2.1 %collective-permute-done.11 = bf16[64,1536]{1,0:T(8,128)(2,1)S(1)} collective-permute-done((bf16[64,1536]{1,0:T(8,128)(2,1)S(1)}, bf16[64,1536]{1,0:T(8,128)(2,1)S(1)}, u32[]{:S(2)}, u32[]{:S(2)}) %collective-permute-start.11) | collective-permute-done | bytes 196640 | tf_op jit(solution)/shard_map/ppermute | solution.py:42
  114.7 1.4 collective-permute-start.14
  116.2 2.0 %collective-permute-done.27 = bf16[64,1536]{1,0:T(8,128)(2,1)S(1)} collective-permute-done((bf16[64,1536]{1,0:T(8,128)(2,1)S(1)}, bf16[64,1536]{1,0:T(8,128)(2,1)S(1)}, u32[]{:S(2)}, u32[]{:S(2)}) %collective-permute-start.27) | collective-permute-done | bytes 196640 | tf_op jit(solution)/shard_map/ppermute | solution.py:42
  118.9 1.4 collective-permute-start.30
  120.4 2.0 %collective-permute-done.38 = bf16[64,1536]{1,0:T(8,128)(2,1)S(1)} collective-permute-done((bf16[64,1536]{1,0:T(8,128)(2,1)S(1)}, bf16[64,1536]{1,0:T(8,128)(2,1)S(1)}, u32[]{:S(2)}, u32[]{:S(2)}) %collective-permute-start.38) | collective-permute-done | bytes 196640 | tf_op jit(solution)/shard_map/ppermute | solution.py:42
  123.1 7.8 %collective-permute-done.13 = bf16[2,64,1536]{2,1,0:T(8,128)(2,1)S(1)} collective-permute-done((bf16[2,64,1536]{2,1,0:T(8,128)(2,1)S(1)}, bf16[2,64,1536]{2,1,0:T(8,128)(2,1)S(1)}, u32[]{:S(2)}, u32[]{:S(2)}) %collective-permute-start.13) | collective-permute-done | bytes 393248 | tf_op jit(solution)/shard_map/ppermute | solution.py:42
  131.8 1.4 fusion
  133.4 5.9 %collective-permute-done.29 = bf16[2,64,1536]{2,1,0:T(8,128)(2,1)S(1)} collective-permute-done((bf16[2,64,1536]{2,1,0:T(8,128)(2,1)S(1)}, bf16[2,64,1536]{2,1,0:T(8,128)(2,1)S(1)}, u32[]{:S(2)}, u32[]{:S(2)}) %collective-permute-start.29) | collective-permute-done | bytes 393248 | tf_op jit(solution)/shard_map/ppermute | solution.py:42
  139.5 1.4 fusion.2
  141.0 4.0 %collective-permute-done.40 = bf16[2,64,1536]{2,1,0:T(8,128)(2,1)S(1)} collective-permute-done((bf16[2,64,1536]{2,1,0:T(8,128)(2,1)S(1)}, bf16[2,64,1536]{2,1,0:T(8,128)(2,1)S(1)}, u32[]{:S(2)}, u32[]{:S(2)}) %collective-permute-start.40) | collective-permute-done | bytes 393248 | tf_op jit(solution)/shard_map/ppermute | solution.py:42
  146.0 2.0 %collective-permute-start.17 = (bf16[4,16,768]{2,1,0:T(8,128)(2,1)S(1)}, bf16[4,16,768]{2,1,0:T(8,128)(2,1)S(1)}, u32[]{:S(2)}, u32[]{:S(2)}) collective-permute-start(bf16[4,16,768]{2,1,0:T(8,128)(2,1)S(1)} %get-tuple-element.31), channel_id=1, source_target_pairs={{0,4},{1,5},{2,6},{3,7},{4,0},{5,1},{6,2},{7,3},{8,12},{9,13},{10,... | collective-permute-start | bytes 294920 | tf_op jit(solution)/shard_map/ppermute | solution.py:42
  148.0 2.8 %collective-permute-start.16 = (bf16[4,16,768]{2,1,0:T(8,128)(2,1)S(1)}, bf16[4,16,768]{2,1,0:T(8,128)(2,1)S(1)}, u32[]{:S(2)}, u32[]{:S(2)}) collective-permute-start(bf16[4,16,768]{2,1,0:T(8,128)(2,1)S(1)} %get-tuple-element.29), channel_id=1, source_target_pairs={{0,6},{1,7},{2,0},{3,1},{4,2},{5,3},{6,4},{7,5},{8,14},{9,15},{10,... | collective-permute-start | bytes 294920 | tf_op jit(solution)/shard_map/ppermute | solution.py:42
  152.2 2.7 %collective-permute-start.32 = (bf16[4,16,768]{2,1,0:T(8,128)(2,1)S(1)}, bf16[4,16,768]{2,1,0:T(8,128)(2,1)S(1)}, u32[]{:S(2)}, u32[]{:S(2)}) collective-permute-start(bf16[4,16,768]{2,1,0:T(8,128)(2,1)S(1)} %get-tuple-element.36), channel_id=1, source_target_pairs={{0,6},{1,7},{2,0},{3,1},{4,2},{5,3},{6,4},{7,5},{8,14},{9,15},{10,... | collective-permute-start | bytes 294920 | tf_op jit(solution)/shard_map/ppermute | solution.py:42
  154.9 2.3 %collective-permute-done.17 = bf16[4,16,768]{2,1,0:T(8,128)(2,1)S(1)} collective-permute-done((bf16[4,16,768]{2,1,0:T(8,128)(2,1)S(1)}, bf16[4,16,768]{2,1,0:T(8,128)(2,1)S(1)}, u32[]{:S(2)}, u32[]{:S(2)}) %collective-permute-start.17) | collective-permute-done | bytes 98336 | tf_op jit(solution)/shard_map/ppermute | solution.py:42
  157.2 1.2 collective-permute-done.34
  158.5 3.9 %collective-permute-done.33 = bf16[4,16,768]{2,1,0:T(8,128)(2,1)S(1)} collective-permute-done((bf16[4,16,768]{2,1,0:T(8,128)(2,1)S(1)}, bf16[4,16,768]{2,1,0:T(8,128)(2,1)S(1)}, u32[]{:S(2)}, u32[]{:S(2)}) %collective-permute-start.33) | collective-permute-done | bytes 98336 | tf_op jit(solution)/shard_map/ppermute | solution.py:42
  162.5 1.4 collective-permute-start.37
  164.0 2.0 %collective-permute-start.35 = (bf16[2,16,768]{2,1,0:T(8,128)(2,1)S(1)}, bf16[2,16,768]{2,1,0:T(8,128)(2,1)S(1)}, u32[]{:S(2)}, u32[]{:S(2)}) collective-permute-start(bf16[2,16,768]{2,1,0:T(8,128)(2,1)S(1)} %get-tuple-element.48), channel_id=1, source_target_pairs={{0,8},{8,0},{16,24},{24,16},{1,9},{9,1},{17,25},{25,17},{2,10},{10... | collective-permute-start | bytes 147464 | tf_op jit(solution)/shard_map/ppermute | solution.py:42
  166.0 3.6 %fusion.106 = f32[768,1536]{1,0:T(8,128)} fusion(bf16[512,768]{1,0:T(8,128)(2,1)S(1)} %bitcast.474, bf16[512,1536]{1,0:T(8,128)(2,1)S(1)} %bitcast.465), kind=kOutput, calls=%fused_computation.291 | convolution fusion | flops 1207959552 | bytes 7077888 | tf_op jit(solution)/shard_map/dot_general | solution.py:185
  170.0 0.7 unstack.29
  170.7 0.7 unstack.31
  (137 shorter events, 20.0 us)
Async XLA Ops:
  0.6 28.6 %copy-start = (bf16[768,1536]{1,0:T(8,128)(2,1)S(1)}, bf16[768,1536]{1,0:T(8,128)(2,1)}, u32[]{:S(2)}) copy-start(bf16[768,1536]{1,0:T(8,128)(2,1)} %param.10) | copy-start | bytes 7077892
  2.6 6.3 %collective-permute-start.2 = (bf16[3,16,768]{2,1,0:T(8,128)(2,1)S(1)}, bf16[3,16,768]{2,1,0:T(8,128)(2,1)S(1)}, u32[]{:S(2)}, u32[]{:S(2)}) collective-permute-start(bf16[3,16,768]{2,1,0:T(8,128)(2,1)S(1)} %pad_maximum_fusion.29), channel_id=1, source_target_pairs={{0,24},{8,16},{16,8},{24,0},{1,25},{9,17},{17,9},{25,1},{2,26},{10... | collective-permute-start | bytes 221192 | tf_op jit(solution)/shard_map/ppermute | solution.py:42
  6.6 4.4 %collective-permute-start.1 = (bf16[3,16,768]{2,1,0:T(8,128)(2,1)S(1)}, bf16[3,16,768]{2,1,0:T(8,128)(2,1)S(1)}, u32[]{:S(2)}, u32[]{:S(2)}) collective-permute-start(bf16[3,16,768]{2,1,0:T(8,128)(2,1)S(1)} %pad_maximum_fusion.28), channel_id=1, source_target_pairs={{0,16},{8,24},{16,0},{24,8},{1,17},{9,25},{17,1},{25,9},{2,18},{10... | collective-permute-start | bytes 221192 | tf_op jit(solution)/shard_map/ppermute | solution.py:42
  7.2 4.4 %collective-permute-start = (bf16[3,16,768]{2,1,0:T(8,128)(2,1)S(1)}, bf16[3,16,768]{2,1,0:T(8,128)(2,1)S(1)}, u32[]{:S(2)}, u32[]{:S(2)}) collective-permute-start(bf16[3,16,768]{2,1,0:T(8,128)(2,1)S(1)} %pad_maximum_fusion.27), channel_id=1, source_target_pairs={{0,8},{8,0},{16,24},{24,16},{1,9},{9,1},{17,25},{25,17},{2,10},{10... | collective-permute-start | bytes 221192 | tf_op jit(solution)/shard_map/ppermute | solution.py:42
  11.6 6.8 %collective-permute-start.5 = (bf16[1,4,16,768]{3,2,1,0:T(8,128)(2,1)S(1)}, bf16[1,4,16,768]{3,2,1,0:T(8,128)(2,1)S(1)}, u32[]{:S(2)}, u32[]{:S(2)}) collective-permute-start(bf16[1,4,16,768]{3,2,1,0:T(8,128)(2,1)S(1)} %get-tuple-element.52), channel_id=1, source_target_pairs={{0,6},{1,7},{2,0},{3,1},{4,2},{5,3},{6,4},{7,5},{8,14},{9,15},{10,... | collective-permute-start | bytes 294920 | tf_op jit(solution)/shard_map/ppermute | solution.py:42
  15.3 8.2 %collective-permute-start.4 = (bf16[1,4,16,768]{3,2,1,0:T(8,128)(2,1)S(1)}, bf16[1,4,16,768]{3,2,1,0:T(8,128)(2,1)S(1)}, u32[]{:S(2)}, u32[]{:S(2)}) collective-permute-start(bf16[1,4,16,768]{3,2,1,0:T(8,128)(2,1)S(1)} %get-tuple-element.52), channel_id=1, source_target_pairs={{0,4},{1,5},{2,6},{3,7},{4,0},{5,1},{6,2},{7,3},{8,12},{9,13},{10,... | collective-permute-start | bytes 294920 | tf_op jit(solution)/shard_map/ppermute | solution.py:42
  15.3 8.2 %collective-permute-start.3 = (bf16[1,4,16,768]{3,2,1,0:T(8,128)(2,1)S(1)}, bf16[1,4,16,768]{3,2,1,0:T(8,128)(2,1)S(1)}, u32[]{:S(2)}, u32[]{:S(2)}) collective-permute-start(bf16[1,4,16,768]{3,2,1,0:T(8,128)(2,1)S(1)} %get-tuple-element.52), channel_id=1, source_target_pairs={{0,2},{1,3},{2,4},{3,5},{4,6},{5,7},{6,0},{7,1},{8,10},{9,11},{10,... | collective-permute-start | bytes 294920 | tf_op jit(solution)/shard_map/ppermute | solution.py:42
  23.5 1.8 %collective-permute-start.6 = (bf16[1,4,4,16,768]{4,3,2,1,0:T(8,128)(2,1)S(1)}, bf16[1,4,4,16,768]{4,3,2,1,0:T(8,128)(2,1)S(1)}, u32[]{:S(2)}, u32[]{:S(2)}) collective-permute-start(bf16[1,4,4,16,768]{4,3,2,1,0:T(8,128)(2,1)S(1)} %get-tuple-element.44), channel_id=1, source_target_pairs={{0,1},{1,0},{2,3},{3,2},{4,5},{5,4},{6,7},{7,6},{8,9},{9,8},{10,11... | collective-permute-start | bytes 1179656 | tf_op jit(solution)/shard_map/ppermute | solution.py:42
  25.4 7.5 %collective-permute-start.21 = (bf16[2,4,16,768]{3,2,0,1:T(8,128)(2,1)S(1)}, bf16[2,4,16,768]{3,2,0,1:T(8,128)(2,1)S(1)}, u32[]{:S(2)}, u32[]{:S(2)}) collective-permute-start(bf16[2,4,16,768]{3,2,0,1:T(8,128)(2,1)S(1)} %pad_maximum_fusion.24), channel_id=1, source_target_pairs={{0,6},{1,7},{2,0},{3,1},{4,2},{5,3},{6,4},{7,5},{8,14},{9,15},{10,... | collective-permute-start | bytes 589832 | tf_op jit(solution)/shard_map/ppermute | solution.py:42
  26.9 18.2 %collective-permute-start.20 = (bf16[2,4,16,768]{3,2,0,1:T(8,128)(2,1)S(1)}, bf16[2,4,16,768]{3,2,0,1:T(8,128)(2,1)S(1)}, u32[]{:S(2)}, u32[]{:S(2)}) collective-permute-start(bf16[2,4,16,768]{3,2,0,1:T(8,128)(2,1)S(1)} %pad_maximum_fusion.24), channel_id=1, source_target_pairs={{0,4},{1,5},{2,6},{3,7},{4,0},{5,1},{6,2},{7,3},{8,12},{9,13},{10,... | collective-permute-start | bytes 589832 | tf_op jit(solution)/shard_map/ppermute | solution.py:42
  27.3 17.8 %collective-permute-start.19 = (bf16[2,4,16,768]{3,2,0,1:T(8,128)(2,1)S(1)}, bf16[2,4,16,768]{3,2,0,1:T(8,128)(2,1)S(1)}, u32[]{:S(2)}, u32[]{:S(2)}) collective-permute-start(bf16[2,4,16,768]{3,2,0,1:T(8,128)(2,1)S(1)} %pad_maximum_fusion.24), channel_id=1, source_target_pairs={{0,2},{1,3},{2,4},{3,5},{4,6},{5,7},{6,0},{7,1},{8,10},{9,11},{10,... | collective-permute-start | bytes 589832 | tf_op jit(solution)/shard_map/ppermute | solution.py:42
  30.9 18.5 %collective-permute-start.9 = (bf16[2,1,64,1536]{3,2,1,0:T(8,128)(2,1)S(1)}, bf16[2,1,64,1536]{3,2,1,0:T(8,128)(2,1)}, u32[]{:S(2)}, u32[]{:S(2)}) collective-permute-start(bf16[2,1,64,1536]{3,2,1,0:T(8,128)(2,1)S(1)} %pad_maximum_fusion.9), channel_id=1, source_target_pairs={{0,8},{8,0},{16,24},{24,16},{1,9},{9,1},{17,25},{25,17},{2,10},{10... | collective-permute-start | bytes 1179656 | tf_op jit(solution)/shard_map/ppermute | solution.py:42
  46.3 15.9 %collective-permute-start.22 = (bf16[2,4,4,16,768]{4,3,0,1,2:T(8,128)(2,1)}, bf16[2,4,4,16,768]{4,3,0,1,2:T(8,128)(2,1)}, u32[]{:S(2)}, u32[]{:S(2)}) collective-permute-start(bf16[2,4,4,16,768]{4,3,0,1,2:T(8,128)(2,1)} %get-tuple-element.20), channel_id=1, source_target_pairs={{0,1},{1,0},{2,3},{3,2},{4,5},{5,4},{6,7},{7,6},{8,9},{9,8},{10,11... | collective-permute-start | bytes 2359304 | tf_op jit(solution)/shard_map/ppermute | solution.py:42
  47.1 12.2 %collective-permute-start.7 = (bf16[2,1,64,1536]{3,2,1,0:T(8,128)(2,1)}, bf16[2,1,64,1536]{3,2,1,0:T(8,128)(2,1)}, u32[]{:S(2)}, u32[]{:S(2)}) collective-permute-start(bf16[2,1,64,1536]{3,2,1,0:T(8,128)(2,1)} %pad_maximum_fusion.8), channel_id=1, source_target_pairs={{0,16},{8,24},{16,0},{24,8},{1,17},{9,25},{17,1},{25,9},{2,18},{10... | collective-permute-start | bytes 1179656 | tf_op jit(solution)/shard_map/ppermute | solution.py:42
  49.3 12.9 %copy-start.2 = (bf16[2,4,4,1,16,768]{5,4,0,1,2,3:T(8,128)(2,1)S(1)}, bf16[2,4,4,1,16,768]{5,4,0,1,2,3:T(8,128)(2,1)}, u32[]{:S(2)}) copy-start(bf16[2,4,4,1,16,768]{5,4,0,1,2,3:T(8,128)(2,1)} %get-tuple-element.19) | copy-start | bytes 2359300
  50.9 50.3 %collective-permute-start.10 = (bf16[1,64,1536]{2,1,0:T(8,128)(2,1)S(1)}, bf16[1,64,1536]{2,1,0:T(8,128)(2,1)S(1)}, u32[]{:S(2)}, u32[]{:S(2)}) collective-permute-start(bf16[1,64,1536]{2,1,0:T(8,128)(2,1)S(1)} %fusion.68), channel_id=1, source_target_pairs={{0,16},{8,24},{16,0},{24,8},{1,17},{9,25},{17,1},{25,9},{2,18},{10... | collective-permute-start | bytes 589832 | tf_op jit(solution)/shard_map/ppermute | solution.py:42
  60.8 43.6 %collective-permute-start.8 = (bf16[1,64,1536]{2,1,0:T(8,128)(2,1)S(1)}, bf16[1,64,1536]{2,1,0:T(8,128)(2,1)S(1)}, u32[]{:S(2)}, u32[]{:S(2)}) collective-permute-start(bf16[1,64,1536]{2,1,0:T(8,128)(2,1)S(1)} %fusion.67), channel_id=1, source_target_pairs={{0,8},{8,0},{16,24},{24,16},{1,9},{9,1},{17,25},{25,17},{2,10},{10... | collective-permute-start | bytes 589832 | tf_op jit(solution)/shard_map/ppermute | solution.py:42
  62.2 1.9 %copy-start.1 = (bf16[1536,768]{1,0:T(8,128)(2,1)S(1)}, bf16[1536,768]{1,0:T(8,128)(2,1)}, u32[]{:S(2)}) copy-start(bf16[1536,768]{1,0:T(8,128)(2,1)} %param.11) | copy-start | bytes 7077892
  72.6 18.6 %collective-permute-start.25 = (bf16[2,2,64,1536]{3,2,1,0:T(8,128)(2,1)S(1)}, bf16[2,2,64,1536]{3,2,1,0:T(8,128)(2,1)S(1)}, u32[]{:S(2)}, u32[]{:S(2)}) collective-permute-start(bf16[2,2,64,1536]{3,2,1,0:T(8,128)(2,1)S(1)} %pad_maximum_fusion.6), channel_id=1, source_target_pairs={{0,8},{8,0},{16,24},{24,16},{1,9},{9,1},{17,25},{25,17},{2,10},{10... | collective-permute-start | bytes 2359304 | tf_op jit(solution)/shard_map/ppermute | solution.py:42
  74.3 18.8 %collective-permute-start.23 = (bf16[2,2,64,1536]{3,2,1,0:T(8,128)(2,1)S(1)}, bf16[2,2,64,1536]{3,2,1,0:T(8,128)(2,1)S(1)}, u32[]{:S(2)}, u32[]{:S(2)}) collective-permute-start(bf16[2,2,64,1536]{3,2,1,0:T(8,128)(2,1)S(1)} %pad_maximum_fusion.5), channel_id=1, source_target_pairs={{0,16},{8,24},{16,0},{24,8},{1,17},{9,25},{17,1},{25,9},{2,18},{10... | collective-permute-start | bytes 2359304 | tf_op jit(solution)/shard_map/ppermute | solution.py:42
  91.3 9.8 %collective-permute-start.26 = (bf16[2,64,1536]{2,1,0:T(8,128)(2,1)S(1)}, bf16[2,64,1536]{2,1,0:T(8,128)(2,1)S(1)}, u32[]{:S(2)}, u32[]{:S(2)}) collective-permute-start(bf16[2,64,1536]{2,1,0:T(8,128)(2,1)S(1)} %fusion.30), channel_id=1, source_target_pairs={{0,16},{8,24},{16,0},{24,8},{1,17},{9,25},{17,1},{25,9},{2,18},{10... | collective-permute-start | bytes 1179656 | tf_op jit(solution)/shard_map/ppermute | solution.py:42
  93.2 11.1 %collective-permute-start.24 = (bf16[2,64,1536]{2,1,0:T(8,128)(2,1)S(1)}, bf16[2,64,1536]{2,1,0:T(8,128)(2,1)S(1)}, u32[]{:S(2)}, u32[]{:S(2)}) collective-permute-start(bf16[2,64,1536]{2,1,0:T(8,128)(2,1)S(1)} %fusion.28), channel_id=1, source_target_pairs={{0,8},{8,0},{16,24},{24,16},{1,9},{9,1},{17,25},{25,17},{2,10},{10... | collective-permute-start | bytes 1179656 | tf_op jit(solution)/shard_map/ppermute | solution.py:42
  102.8 8.3 %collective-permute-start.12 = (bf16[64,1536]{1,0:T(8,128)(2,1)S(1)}, bf16[64,1536]{1,0:T(8,128)(2,1)S(1)}, u32[]{:S(2)}, u32[]{:S(2)}) collective-permute-start(bf16[64,1536]{1,0:T(8,128)(2,1)S(1)} %get-tuple-element.24), channel_id=1, source_target_pairs={{0,16},{8,24},{16,0},{24,8},{1,17},{9,25},{17,1},{25,9},{2,18},{10... | collective-permute-start | bytes 589832 | tf_op jit(solution)/shard_map/ppermute | solution.py:42
  106.1 7.9 %collective-permute-start.11 = (bf16[64,1536]{1,0:T(8,128)(2,1)S(1)}, bf16[64,1536]{1,0:T(8,128)(2,1)S(1)}, u32[]{:S(2)}, u32[]{:S(2)}) collective-permute-start(bf16[64,1536]{1,0:T(8,128)(2,1)S(1)} %get-tuple-element.22), channel_id=1, source_target_pairs={{0,8},{8,0},{16,24},{24,16},{1,9},{9,1},{17,25},{25,17},{2,10},{10... | collective-permute-start | bytes 589832 | tf_op jit(solution)/shard_map/ppermute | solution.py:42
  106.8 7.9 %collective-permute-start.28 = (bf16[64,1536]{1,0:T(8,128)(2,1)S(1)}, bf16[64,1536]{1,0:T(8,128)(2,1)S(1)}, u32[]{:S(2)}, u32[]{:S(2)}) collective-permute-start(bf16[64,1536]{1,0:T(8,128)(2,1)S(1)} %get-tuple-element.18), channel_id=1, source_target_pairs={{0,16},{8,24},{16,0},{24,8},{1,17},{9,25},{17,1},{25,9},{2,18},{10... | collective-permute-start | bytes 589832 | tf_op jit(solution)/shard_map/ppermute | solution.py:42
  108.3 10.0 %collective-permute-start.27 = (bf16[64,1536]{1,0:T(8,128)(2,1)S(1)}, bf16[64,1536]{1,0:T(8,128)(2,1)S(1)}, u32[]{:S(2)}, u32[]{:S(2)}) collective-permute-start(bf16[64,1536]{1,0:T(8,128)(2,1)S(1)} %get-tuple-element.14), channel_id=1, source_target_pairs={{0,8},{8,0},{16,24},{24,16},{1,9},{9,1},{17,25},{25,17},{2,10},{10... | collective-permute-start | bytes 589832 | tf_op jit(solution)/shard_map/ppermute | solution.py:42
  109.6 9.3 %collective-permute-start.39 = (bf16[64,1536]{1,0:T(8,128)(2,1)S(1)}, bf16[64,1536]{1,0:T(8,128)(2,1)S(1)}, u32[]{:S(2)}, u32[]{:S(2)}) collective-permute-start(bf16[64,1536]{1,0:T(8,128)(2,1)S(1)} %get-tuple-element.17), channel_id=1, source_target_pairs={{0,16},{8,24},{16,0},{24,8},{1,17},{9,25},{17,1},{25,9},{2,18},{10... | collective-permute-start | bytes 589832 | tf_op jit(solution)/shard_map/ppermute | solution.py:42
  111.2 11.3 %collective-permute-start.38 = (bf16[64,1536]{1,0:T(8,128)(2,1)S(1)}, bf16[64,1536]{1,0:T(8,128)(2,1)S(1)}, u32[]{:S(2)}, u32[]{:S(2)}) collective-permute-start(bf16[64,1536]{1,0:T(8,128)(2,1)S(1)} %get-tuple-element.13), channel_id=1, source_target_pairs={{0,8},{8,0},{16,24},{24,16},{1,9},{9,1},{17,25},{25,17},{2,10},{10... | collective-permute-start | bytes 589832 | tf_op jit(solution)/shard_map/ppermute | solution.py:42
  114.0 16.9 %collective-permute-start.13 = (bf16[2,64,1536]{2,1,0:T(8,128)(2,1)S(1)}, bf16[2,64,1536]{2,1,0:T(8,128)(2,1)S(1)}, u32[]{:S(2)}, u32[]{:S(2)}) collective-permute-start(bf16[2,64,1536]{2,1,0:T(8,128)(2,1)S(1)} %pad_maximum_fusion.11), channel_id=1, source_target_pairs={{0,8},{8,0},{16,24},{24,16},{1,9},{9,1},{17,25},{25,17},{2,10},{10... | collective-permute-start | bytes 1179656 | tf_op jit(solution)/shard_map/ppermute | solution.py:42
  114.7 16.8 %collective-permute-start.14 = (bf16[2,64,1536]{2,1,0:T(8,128)(2,1)S(1)}, bf16[2,64,1536]{2,1,0:T(8,128)(2,1)S(1)}, u32[]{:S(2)}, u32[]{:S(2)}) collective-permute-start(bf16[2,64,1536]{2,1,0:T(8,128)(2,1)S(1)} %pad_maximum_fusion.13), channel_id=1, source_target_pairs={{0,16},{8,24},{16,0},{24,8},{1,17},{9,25},{17,1},{25,9},{2,18},{10... | collective-permute-start | bytes 1179656 | tf_op jit(solution)/shard_map/ppermute | solution.py:42
  118.2 21.1 %collective-permute-start.29 = (bf16[2,64,1536]{2,1,0:T(8,128)(2,1)S(1)}, bf16[2,64,1536]{2,1,0:T(8,128)(2,1)S(1)}, u32[]{:S(2)}, u32[]{:S(2)}) collective-permute-start(bf16[2,64,1536]{2,1,0:T(8,128)(2,1)S(1)} %pad_maximum_fusion.17), channel_id=1, source_target_pairs={{0,8},{8,0},{16,24},{24,16},{1,9},{9,1},{17,25},{25,17},{2,10},{10... | collective-permute-start | bytes 1179656 | tf_op jit(solution)/shard_map/ppermute | solution.py:42
  118.9 20.4 %collective-permute-start.30 = (bf16[2,64,1536]{2,1,0:T(8,128)(2,1)S(1)}, bf16[2,64,1536]{2,1,0:T(8,128)(2,1)S(1)}, u32[]{:S(2)}, u32[]{:S(2)}) collective-permute-start(bf16[2,64,1536]{2,1,0:T(8,128)(2,1)S(1)} %pad_maximum_fusion.19), channel_id=1, source_target_pairs={{0,16},{8,24},{16,0},{24,8},{1,17},{9,25},{17,1},{25,9},{2,18},{10... | collective-permute-start | bytes 1179656 | tf_op jit(solution)/shard_map/ppermute | solution.py:42
  122.4 22.5 %collective-permute-start.40 = (bf16[2,64,1536]{2,1,0:T(8,128)(2,1)S(1)}, bf16[2,64,1536]{2,1,0:T(8,128)(2,1)S(1)}, u32[]{:S(2)}, u32[]{:S(2)}) collective-permute-start(bf16[2,64,1536]{2,1,0:T(8,128)(2,1)S(1)} %pad_maximum_fusion.22), channel_id=1, source_target_pairs={{0,8},{8,0},{16,24},{24,16},{1,9},{9,1},{17,25},{25,17},{2,10},{10... | collective-permute-start | bytes 1179656 | tf_op jit(solution)/shard_map/ppermute | solution.py:42
  130.9 14.1 %collective-permute-start.41 = (bf16[2,64,1536]{2,1,0:T(8,128)(2,1)S(1)}, bf16[2,64,1536]{2,1,0:T(8,128)(2,1)S(1)}, u32[]{:S(2)}, u32[]{:S(2)}) collective-permute-start(bf16[2,64,1536]{2,1,0:T(8,128)(2,1)S(1)} %pad_maximum_fusion.23), channel_id=1, source_target_pairs={{0,16},{8,24},{16,0},{24,8},{1,17},{9,25},{17,1},{25,9},{2,18},{10... | collective-permute-start | bytes 1179656 | tf_op jit(solution)/shard_map/ppermute | solution.py:42
  133.3 12.1 %collective-permute-start.15 = (bf16[4,4,16,768]{3,2,1,0:T(8,128)(2,1)S(1)}, bf16[4,4,16,768]{3,2,1,0:T(8,128)(2,1)S(1)}, u32[]{:S(2)}, u32[]{:S(2)}) collective-permute-start(bf16[4,4,16,768]{3,2,1,0:T(8,128)(2,1)S(1)} %fusion.51), channel_id=1, source_target_pairs={{0,1},{1,0},{2,3},{3,2},{4,5},{5,4},{6,7},{7,6},{8,9},{9,8},{10,11... | collective-permute-start | bytes 1179656 | tf_op jit(solution)/shard_map/ppermute | solution.py:42
  140.9 9.9 %collective-permute-start.31 = (bf16[4,4,16,768]{3,2,0,1:T(8,128)(2,1)S(1)}, bf16[4,4,16,768]{3,2,0,1:T(8,128)(2,1)S(1)}, u32[]{:S(2)}, u32[]{:S(2)}) collective-permute-start(bf16[4,4,16,768]{3,2,0,1:T(8,128)(2,1)S(1)} %fusion.52), channel_id=1, source_target_pairs={{0,1},{1,0},{2,3},{3,2},{4,5},{5,4},{6,7},{7,6},{8,9},{9,8},{10,11... | collective-permute-start | bytes 1179656 | tf_op jit(solution)/shard_map/ppermute | solution.py:42
  145.5 6.7 %collective-permute-start.18 = (bf16[4,16,768]{2,1,0:T(8,128)(2,1)S(1)}, bf16[4,16,768]{2,1,0:T(8,128)(2,1)S(1)}, u32[]{:S(2)}, u32[]{:S(2)}) collective-permute-start(bf16[4,16,768]{2,1,0:T(8,128)(2,1)S(1)} %get-tuple-element.30), channel_id=1, source_target_pairs={{0,2},{1,3},{2,4},{3,5},{4,6},{5,7},{6,0},{7,1},{8,10},{9,11},{10,... | collective-permute-start | bytes 294920 | tf_op jit(solution)/shard_map/ppermute | solution.py:42
  146.0 11.2 %collective-permute-start.17 = (bf16[4,16,768]{2,1,0:T(8,128)(2,1)S(1)}, bf16[4,16,768]{2,1,0:T(8,128)(2,1)S(1)}, u32[]{:S(2)}, u32[]{:S(2)}) collective-permute-start(bf16[4,16,768]{2,1,0:T(8,128)(2,1)S(1)} %get-tuple-element.31), channel_id=1, source_target_pairs={{0,4},{1,5},{2,6},{3,7},{4,0},{5,1},{6,2},{7,3},{8,12},{9,13},{10,... | collective-permute-start | bytes 294920 | tf_op jit(solution)/shard_map/ppermute | solution.py:42
  148.0 9.2 %collective-permute-start.16 = (bf16[4,16,768]{2,1,0:T(8,128)(2,1)S(1)}, bf16[4,16,768]{2,1,0:T(8,128)(2,1)S(1)}, u32[]{:S(2)}, u32[]{:S(2)}) collective-permute-start(bf16[4,16,768]{2,1,0:T(8,128)(2,1)S(1)} %get-tuple-element.29), channel_id=1, source_target_pairs={{0,6},{1,7},{2,0},{3,1},{4,2},{5,3},{6,4},{7,5},{8,14},{9,15},{10,... | collective-permute-start | bytes 294920 | tf_op jit(solution)/shard_map/ppermute | solution.py:42
  151.0 7.5 %collective-permute-start.34 = (bf16[4,16,768]{2,1,0:T(8,128)(2,1)S(1)}, bf16[4,16,768]{2,1,0:T(8,128)(2,1)S(1)}, u32[]{:S(2)}, u32[]{:S(2)}) collective-permute-start(bf16[4,16,768]{2,1,0:T(8,128)(2,1)S(1)} %get-tuple-element.37), channel_id=1, source_target_pairs={{0,2},{1,3},{2,4},{3,5},{4,6},{5,7},{6,0},{7,1},{8,10},{9,11},{10,... | collective-permute-start | bytes 294920 | tf_op jit(solution)/shard_map/ppermute | solution.py:42
  151.1 11.3 %collective-permute-start.33 = (bf16[4,16,768]{2,1,0:T(8,128)(2,1)S(1)}, bf16[4,16,768]{2,1,0:T(8,128)(2,1)S(1)}, u32[]{:S(2)}, u32[]{:S(2)}) collective-permute-start(bf16[4,16,768]{2,1,0:T(8,128)(2,1)S(1)} %get-tuple-element.38), channel_id=1, source_target_pairs={{0,4},{1,5},{2,6},{3,7},{4,0},{5,1},{6,2},{7,3},{8,12},{9,13},{10,... | collective-permute-start | bytes 294920 | tf_op jit(solution)/shard_map/ppermute | solution.py:42
  152.2 10.2 %collective-permute-start.32 = (bf16[4,16,768]{2,1,0:T(8,128)(2,1)S(1)}, bf16[4,16,768]{2,1,0:T(8,128)(2,1)S(1)}, u32[]{:S(2)}, u32[]{:S(2)}) collective-permute-start(bf16[4,16,768]{2,1,0:T(8,128)(2,1)S(1)} %get-tuple-element.36), channel_id=1, source_target_pairs={{0,6},{1,7},{2,0},{3,1},{4,2},{5,3},{6,4},{7,5},{8,14},{9,15},{10,... | collective-permute-start | bytes 294920 | tf_op jit(solution)/shard_map/ppermute | solution.py:42
  162.5 7.2 %collective-permute-start.37 = (bf16[2,16,768]{2,1,0:T(8,128)(2,1)S(1)}, bf16[2,16,768]{2,1,0:T(8,128)(2,1)S(1)}, u32[]{:S(2)}, u32[]{:S(2)}) collective-permute-start(bf16[2,16,768]{2,1,0:T(8,128)(2,1)S(1)} %get-tuple-element.49), channel_id=1, source_target_pairs={{0,24},{8,16},{16,8},{24,0},{1,25},{9,17},{17,9},{25,1},{2,26},{10... | collective-permute-start | bytes 147464 | tf_op jit(solution)/shard_map/ppermute | solution.py:42
  163.8 5.8 %collective-permute-start.36 = (bf16[2,16,768]{2,1,0:T(8,128)(2,1)S(1)}, bf16[2,16,768]{2,1,0:T(8,128)(2,1)S(1)}, u32[]{:S(2)}, u32[]{:S(2)}) collective-permute-start(bf16[2,16,768]{2,1,0:T(8,128)(2,1)S(1)} %get-tuple-element.50), channel_id=1, source_target_pairs={{0,16},{8,24},{16,0},{24,8},{1,17},{9,25},{17,1},{25,9},{2,18},{10... | collective-permute-start | bytes 147464 | tf_op jit(solution)/shard_map/ppermute | solution.py:42
  164.0 5.7 %collective-permute-start.35 = (bf16[2,16,768]{2,1,0:T(8,128)(2,1)S(1)}, bf16[2,16,768]{2,1,0:T(8,128)(2,1)S(1)}, u32[]{:S(2)}, u32[]{:S(2)}) collective-permute-start(bf16[2,16,768]{2,1,0:T(8,128)(2,1)S(1)} %get-tuple-element.48), channel_id=1, source_target_pairs={{0,8},{8,0},{16,24},{24,16},{1,9},{9,1},{17,25},{25,17},{2,10},{10... | collective-permute-start | bytes 147464 | tf_op jit(solution)/shard_map/ppermute | solution.py:42

commit v5 on v4

--- a/solution.py
+++ b/solution.py
@@ -40,6 +40,10 @@
         for b in range(lo)
     ]
     return lax.ppermute(value, axis, pairs)
+
+
+def after(value, *others):
+    return lax.optimization_barrier((value, others))[0]
 
 
 def axis_step(axis, size):
@@ -75,14 +79,16 @@
     return total
 
 
-def gather_groups(value, grid, first):
+def gather_first(value, grid, first):
+    return jnp.stack([shift(value, grid, axis_step(first, i)) for i in range(grid[first])])
+
+
+def gather_second(held, grid, first):
     second = 1 - first
-    n1, n2 = grid[first], grid[second]
-    held = jnp.stack([shift(value, grid, axis_step(first, i)) for i in range(n1)])
     found = {}
-    for j in range(n2):
+    for j in range(grid[second]):
         there = shift(held, grid, axis_step(second, j))
-        for i in range(n1):
+        for i in range(grid[first]):
             found[(i, j) if first == 0 else (j, i)] = there[i]
     return found
 
@@ -115,15 +121,15 @@
         )
         pieces.append(shift(piece, grid, (i, j)))
 
-    def own_channels(block):
-        held = jnp.stack([shift(block, pod, (i, 0), "tensor") for i in range(pod[0])], axis=2)
+    def from_chips(block):
+        return jnp.stack([shift(block, pod, (i, 0), "tensor") for i in range(pod[0])], axis=2)
+
+    def from_cores(held):
         both = jnp.stack([shift(held, pod, (0, k), "tensor") for k in range(pod[1])], axis=3)
         return both.reshape(-1, dp_count, tensor_count * own_rows, own_cols)
 
-    (tok_cols,) = own_channels(jnp.stack([p[:1] for p in pieces], axis=1))
-    later = jnp.stack([p[1:] for p in pieces], axis=1)
-    later, _ = lax.optimization_barrier((later, tok_cols))
-    tan_cols, cot_cols = own_channels(later)
+    (tok_cols,) = from_cores(from_chips(jnp.stack([p[:1] for p in pieces], axis=1)))
+    later = from_chips(after(jnp.stack([p[1:] for p in pieces], axis=1), tok_cols))
     group_rows = tok_cols.shape[1]
     cut = group_rows // 2
     halves = [(0, slice(0, cut)), (1, slice(cut, group_rows))]
@@ -154,17 +160,23 @@
     ).reshape(group_rows)
     keep = [(row_at[rows] < live_rows)[:, None] for _, rows in halves]
 
-    def everywhere(values):
+    def spread(values):
         values = [half(jnp.where(k, v, 0.0)) for k, v in zip(keep, values)]
-        found = [gather_groups(v, grid, 1 - first) for v, (first, _) in zip(values, halves)]
+        return [gather_first(v, grid, 1 - first) for v, (first, _) in zip(values, halves)]
+
+    def everywhere(held):
+        found = [gather_second(v, grid, 1 - first) for v, (first, _) in zip(held, halves)]
         return jnp.stack([jnp.concatenate([f[s] for f in found]) for s in slots])
 
-    def down(hidden):
+    def down_cores(hidden):
         flat = hidden.reshape(dp_count * group_rows, -1)
         terms = dot(flat, w_out).reshape(dp_count, *pod, own_rows, own_cols)
         near = terms[:, :, 0]
         for k in range(1, pod[1]):
             near = near + shift(half(terms[:, :, k]), pod, (0, -k), "tensor").astype(jnp.float32)
+        return near
+
+    def down_chips(near):
         total = near[:, 0]
         for i in range(1, pod[0]):
             total = total + shift(half(near[:, i]), pod, (-i, 0), "tensor").astype(jnp.float32)
@@ -172,11 +184,18 @@
 
     pre_act = [p[0] for p in sums([(up, tok_cols)])]
     pairs = [gelu_pair(p) for p in pre_act]
-    act_all = everywhere([a for a, _ in pairs])
+    act_held = spread([a for a, _ in pairs])
+    later = from_cores(after(later, pre_act))
+    tan_cols, cot_cols = after(later, act_held)
+    act_all = everywhere(act_held)
     both = sums([(up, tan_cols), (back, cot_cols)])
-    dact_all = everywhere([s * v[0] for (_, s), v in zip(pairs, both)])
-    grad_all = everywhere([s * v[1] for (_, s), v in zip(pairs, both)])
-    summed = jnp.stack([down(act_all), down(dact_all)], axis=1)
+    out_near = down_cores(act_all)
+    both = after(both, out_near)
+    dact_held = spread([s * v[0] for (_, s), v in zip(pairs, both)])
+    dact_all = everywhere(dact_held)
+    back_grad = after([v[1] for v in both], dact_held)
+    grad_all = everywhere(spread([s * v for (_, s), v in zip(pairs, back_grad)]))
+    summed = jnp.stack([down_chips(out_near), down_chips(down_cores(dact_all))], axis=1)
     cols = jnp.stack(
         [shift(summed[place[(i, j)]], grid, (-i, -j)) for i, j in slots]
     ).reshape(*grid, 2, own_rows, own_cols)

time: 172 us -> 160 us (0.930)
  waiting for transfers between devices: 83.8 us -> 70 us
    ppermute x42, waiting for transfers between devices: 83.8 us -> 70 us  [shift(): return lax.ppermute(value, axis, pairs)]
  transfers between devices with their start and end apart: 42 -> 42, of which waited for: 23 -> 24; matrix products, arithmetic and copies ran while one was open for 20% -> 20% of each run, Pallas kernels for 0% -> 0%
where the time goes in v5:
time: 160 us
  waiting for transfers between devices  70 us (44%)
  starting transfers between devices  48.1 us (30%)
  matrix products  25.4 us (16%)
  other arithmetic  9.15 us (6%)
  local copies, waits for them, and re-layouts  5.73 us (4%)
    ppermute x42, waiting for transfers between devices, shift(): return lax.ppermute(value, axis, pairs)  70 us
    ppermute x42, starting transfers between devices, shift(): return lax.ppermute(value, axis, pairs)  48.1 us
    dot_general x18, matrix products, dot(): return jnp.dot(a, b, preferred_element_type=jnp.float32)  15.2 us
    dot_general x8, matrix products, back(): lax.dot_general(rows, w_out, (((1,), (1,)), ((), ())), preferred_element_...  6.66 us
    dot_general x1, matrix products, local(): lax.dot_general(tok_cols.reshape(dp_count * group_rows, own_cols), grad_a...  3.6 us
  transfers between devices with their start and end apart: 42, of which 24 were waited for; matrix products, arithmetic and copies ran while one was open for 20% of the time, Pallas kernels for 0%

profile of v5, /device:TPU:0, one launch (start us, length us, event | category | flops | bytes accessed | tf_op | source)
XLA Modules:
  0.0 159.7 jit_solution(2926240859706641977)
XLA Ops:
  0.7 0.9 dynamic-slice_bitcast_fusion.11
  1.7 0.9 dynamic-slice_bitcast_fusion
  2.6 4.0 %collective-permute-start.2 = (bf16[3,16,768]{2,1,0:T(8,128)(2,1)S(1)}, bf16[3,16,768]{2,1,0:T(8,128)(2,1)S(1)}, u32[]{:S(2)}, u32[]{:S(2)}) collective-permute-start(bf16[3,16,768]{2,1,0:T(8,128)(2,1)S(1)} %pad_maximum_fusion.29), channel_id=1, source_target_pairs={{0,24},{8,16},{16,8},{24,0},{1,25},{9,17},{17,9},{25,1},{2,26},{10... | collective-permute-start | bytes 221192 | tf_op jit(solution)/shard_map/ppermute | solution.py:42
  7.5 1.3 fusion.95
  8.9 2.1 %collective-permute-done.1 = bf16[3,16,768]{2,1,0:T(8,128)(2,1)S(1)} collective-permute-done((bf16[3,16,768]{2,1,0:T(8,128)(2,1)S(1)}, bf16[3,16,768]{2,1,0:T(8,128)(2,1)S(1)}, u32[]{:S(2)}, u32[]{:S(2)}) %collective-permute-start.1) | collective-permute-done | bytes 73760 | tf_op jit(solution)/shard_map/ppermute | solution.py:42
  11.6 3.7 %collective-permute-start.5 = (bf16[1,4,16,768]{3,2,1,0:T(8,128)(2,1)S(1)}, bf16[1,4,16,768]{3,2,1,0:T(8,128)(2,1)S(1)}, u32[]{:S(2)}, u32[]{:S(2)}) collective-permute-start(bf16[1,4,16,768]{3,2,1,0:T(8,128)(2,1)S(1)} %get-tuple-element.54), channel_id=1, source_target_pairs={{0,6},{1,7},{2,0},{3,1},{4,2},{5,3},{6,4},{7,5},{8,14},{9,15},{10,... | collective-permute-start | bytes 294920 | tf_op jit(solution)/shard_map/ppermute | solution.py:42
  15.3 1.0 collective-permute-start.3
  16.3 2.1 %collective-permute-done.5 = bf16[1,4,16,768]{3,2,1,0:T(8,128)(2,1)S(1)} collective-permute-done((bf16[1,4,16,768]{3,2,1,0:T(8,128)(2,1)S(1)}, bf16[1,4,16,768]{3,2,1,0:T(8,128)(2,1)S(1)}, u32[]{:S(2)}, u32[]{:S(2)}) %collective-permute-start.5) | collective-permute-done | bytes 98336 | tf_op jit(solution)/shard_map/ppermute | solution.py:42
  18.4 5.1 %collective-permute-done.4 = bf16[1,4,16,768]{3,2,1,0:T(8,128)(2,1)S(1)} collective-permute-done((bf16[1,4,16,768]{3,2,1,0:T(8,128)(2,1)S(1)}, bf16[1,4,16,768]{3,2,1,0:T(8,128)(2,1)S(1)}, u32[]{:S(2)}, u32[]{:S(2)}) %collective-permute-start.4) | collective-permute-done | bytes 98336 | tf_op jit(solution)/shard_map/ppermute | solution.py:42
  23.7 1.6 %collective-permute-done.6 = bf16[1,4,4,16,768]{4,3,2,1,0:T(8,128)(2,1)S(1)} collective-permute-done((bf16[1,4,4,16,768]{4,3,2,1,0:T(8,128)(2,1)S(1)}, bf16[1,4,4,16,768]{4,3,2,1,0:T(8,128)(2,1)S(1)}, u32[]{:S(2)}, u32[]{:S(2)}) %collective-permute-start.6) | collective-permute-done | bytes 393248 | tf_op jit(solution)/shard_map/ppermute | solution.py:42
  27.5 1.5 collective-permute-start.21
  29.4 1.9 %collective-permute-start.19 = (bf16[2,4,16,768]{3,2,0,1:T(8,128)(2,1)S(1)}, bf16[2,4,16,768]{3,2,0,1:T(8,128)(2,1)}, u32[]{:S(2)}, u32[]{:S(2)}) collective-permute-start(bf16[2,4,16,768]{3,2,0,1:T(8,128)(2,1)S(1)} %pad_maximum_fusion.24), channel_id=1, source_target_pairs={{0,2},{1,3},{2,4},{3,5},{4,6},{5,7},{6,0},{7,1},{8,10},{9,11},{10,... | collective-permute-start | bytes 589832 | tf_op jit(solution)/shard_map/ppermute | solution.py:42
  32.1 1.4 collective-permute-start.9
  35.8 11.5 %collective-permute-done.20 = bf16[2,4,16,768]{3,2,0,1:T(8,128)(2,1)} collective-permute-done((bf16[2,4,16,768]{3,2,0,1:T(8,128)(2,1)S(1)}, bf16[2,4,16,768]{3,2,0,1:T(8,128)(2,1)}, u32[]{:S(2)}, u32[]{:S(2)}) %collective-permute-start.20) | collective-permute-done | bytes 196640 | tf_op jit(solution)/shard_map/ppermute | solution.py:42
  47.3 1.1 pad_maximum_fusion.4
  48.5 1.5 fusion.69
  50.0 1.5 collective-permute-start.10
  51.4 1.5 fusion.68
  53.6 3.8 %collective-permute-done.10 = bf16[1,64,1536]{2,1,0:T(8,128)(2,1)S(1)} collective-permute-done((bf16[1,64,1536]{2,1,0:T(8,128)(2,1)S(1)}, bf16[1,64,1536]{2,1,0:T(8,128)(2,1)S(1)}, u32[]{:S(2)}, u32[]{:S(2)}) %collective-permute-start.10) | collective-permute-done | bytes 196640 | tf_op jit(solution)/shard_map/ppermute | solution.py:42
  57.3 1.5 select_convert_fusion.4
  58.9 1.5 collective-permute-start.12
  60.5 1.5 select_convert_fusion.5
  62.9 2.6 %collective-permute-done.12 = bf16[64,1536]{1,0:T(8,128)(2,1)S(1)} collective-permute-done((bf16[64,1536]{1,0:T(8,128)(2,1)S(1)}, bf16[64,1536]{1,0:T(8,128)(2,1)S(1)}, u32[]{:S(2)}, u32[]{:S(2)}) %collective-permute-start.12) | collective-permute-done | bytes 196640 | tf_op jit(solution)/shard_map/ppermute | solution.py:42
  65.5 1.4 collective-permute-start.13
  66.9 2.7 %collective-permute-done.11 = bf16[64,1536]{1,0:T(8,128)(2,1)S(1)} collective-permute-done((bf16[64,1536]{1,0:T(8,128)(2,1)S(1)}, bf16[64,1536]{1,0:T(8,128)(2,1)S(1)}, u32[]{:S(2)}, u32[]{:S(2)}) %collective-permute-start.11) | collective-permute-done | bytes 196640 | tf_op jit(solution)/shard_map/ppermute | solution.py:42
  70.3 1.5 copy-done.1
  71.8 0.8 convolution_bitcast_fusion.6
  72.6 0.8 convolution_bitcast_fusion.4
  73.5 0.8 fusion.11
  75.4 0.8 fusion.9
  76.8 0.8 fusion.15
  78.1 0.8 fusion.13
  79.7 2.1 %collective-permute-start.23 = (bf16[2,2,64,1536]{3,2,1,0:T(8,128)(2,1)S(1)}, bf16[2,2,64,1536]{3,2,1,0:T(8,128)(2,1)S(1)}, u32[]{:S(2)}, u32[]{:S(2)}) collective-permute-start(bf16[2,2,64,1536]{3,2,1,0:T(8,128)(2,1)S(1)} %pad_maximum_fusion.5), channel_id=1, source_target_pairs={{0,16},{8,24},{16,0},{24,8},{1,17},{9,25},{17,1},{25,9},{2,18},{10... | collective-permute-start | bytes 2359304 | tf_op jit(solution)/shard_map/ppermute | solution.py:42
  82.5 0.8 convolution_bitcast_fusion.2
  83.5 1.4 fusion
  85.6 0.8 convolution_bitcast_fusion
  87.3 2.1 %collective-permute-start.17 = (bf16[4,16,768]{2,1,0:T(8,128)(2,1)S(1)}, bf16[4,16,768]{2,1,0:T(8,128)(2,1)S(1)}, u32[]{:S(2)}, u32[]{:S(2)}) collective-permute-start(bf16[4,16,768]{2,1,0:T(8,128)(2,1)S(1)} %get-tuple-element.33), channel_id=1, source_target_pairs={{0,4},{1,5},{2,6},{3,7},{4,0},{5,1},{6,2},{7,3},{8,12},{9,13},{10,... | collective-permute-start | bytes 294920 | tf_op jit(solution)/shard_map/ppermute | solution.py:42
  89.4 2.8 %collective-permute-start.16 = (bf16[4,16,768]{2,1,0:T(8,128)(2,1)S(1)}, bf16[4,16,768]{2,1,0:T(8,128)(2,1)S(1)}, u32[]{:S(2)}, u32[]{:S(2)}) collective-permute-start(bf16[4,16,768]{2,1,0:T(8,128)(2,1)S(1)} %get-tuple-element.31), channel_id=1, source_target_pairs={{0,6},{1,7},{2,0},{3,1},{4,2},{5,3},{6,4},{7,5},{8,14},{9,15},{10,... | collective-permute-start | bytes 294920 | tf_op jit(solution)/shard_map/ppermute | solution.py:42
  92.8 1.7 %collective-permute-done.18 = bf16[4,16,768]{2,1,0:T(8,128)(2,1)S(1)} collective-permute-done((bf16[4,16,768]{2,1,0:T(8,128)(2,1)S(1)}, bf16[4,16,768]{2,1,0:T(8,128)(2,1)S(1)}, u32[]{:S(2)}, u32[]{:S(2)}) %collective-permute-start.18) | collective-permute-done | bytes 98336 | tf_op jit(solution)/shard_map/ppermute | solution.py:42
  94.5 3.4 %collective-permute-done.17 = bf16[4,16,768]{2,1,0:T(8,128)(2,1)S(1)} collective-permute-done((bf16[4,16,768]{2,1,0:T(8,128)(2,1)S(1)}, bf16[4,16,768]{2,1,0:T(8,128)(2,1)S(1)}, u32[]{:S(2)}, u32[]{:S(2)}) %collective-permute-start.17) | collective-permute-done | bytes 98336 | tf_op jit(solution)/shard_map/ppermute | solution.py:42
  98.1 2.1 %collective-permute-start.24 = (bf16[2,64,1536]{2,1,0:T(8,128)(2,1)S(1)}, bf16[2,64,1536]{2,1,0:T(8,128)(2,1)S(1)}, u32[]{:S(2)}, u32[]{:S(2)}) collective-permute-start(bf16[2,64,1536]{2,1,0:T(8,128)(2,1)S(1)} %fusion.27), channel_id=1, source_target_pairs={{0,8},{8,0},{16,24},{24,16},{1,9},{9,1},{17,25},{25,17},{2,10},{10... | collective-permute-start | bytes 1179656 | tf_op jit(solution)/shard_map/ppermute | solution.py:42
  100.4 7.4 %collective-permute-done.24 = bf16[2,64,1536]{2,1,0:T(8,128)(2,1)S(1)} collective-permute-done((bf16[2,64,1536]{2,1,0:T(8,128)(2,1)S(1)}, bf16[2,64,1536]{2,1,0:T(8,128)(2,1)S(1)}, u32[]{:S(2)}, u32[]{:S(2)}) %collective-permute-start.24) | collective-permute-done | bytes 393248 | tf_op jit(solution)/shard_map/ppermute | solution.py:42
  107.9 1.5 collective-permute-done.26
  111.0 1.7 %collective-permute-start.27 = (bf16[64,1536]{1,0:T(8,128)(2,1)S(1)}, bf16[64,1536]{1,0:T(8,128)(2,1)S(1)}, u32[]{:S(2)}, u32[]{:S(2)}) collective-permute-start(bf16[64,1536]{1,0:T(8,128)(2,1)S(1)} %fusion.67), channel_id=1, source_target_pairs={{0,8},{8,0},{16,24},{24,16},{1,9},{9,1},{17,25},{25,17},{2,10},{10... | collective-permute-start | bytes 589832 | tf_op jit(solution)/shard_map/ppermute | solution.py:42
  112.7 4.6 %collective-permute-done.28 = bf16[64,1536]{1,0:T(8,128)(2,1)S(1)} collective-permute-done((bf16[64,1536]{1,0:T(8,128)(2,1)S(1)}, bf16[64,1536]{1,0:T(8,128)(2,1)S(1)}, u32[]{:S(2)}, u32[]{:S(2)}) %collective-permute-start.28) | collective-permute-done | bytes 196640 | tf_op jit(solution)/shard_map/ppermute | solution.py:42
  117.4 1.0 collective-permute-done.27
  118.4 2.1 %collective-permute-start.30 = (bf16[2,64,1536]{2,1,0:T(8,128)(2,1)S(1)}, bf16[2,64,1536]{2,1,0:T(8,128)(2,1)S(1)}, u32[]{:S(2)}, u32[]{:S(2)}) collective-permute-start(bf16[2,64,1536]{2,1,0:T(8,128)(2,1)S(1)} %pad_maximum_fusion.19), channel_id=1, source_target_pairs={{0,16},{8,24},{16,0},{24,8},{1,17},{9,25},{17,1},{25,9},{2,18},{10... | collective-permute-start | bytes 1179656 | tf_op jit(solution)/shard_map/ppermute | solution.py:42
  121.2 2.0 %collective-permute-start.38 = (bf16[64,1536]{1,0:T(8,128)(2,1)S(1)}, bf16[64,1536]{1,0:T(8,128)(2,1)S(1)}, u32[]{:S(2)}, u32[]{:S(2)}) collective-permute-start(bf16[64,1536]{1,0:T(8,128)(2,1)S(1)} %select_convert_fusion.1), channel_id=1, source_target_pairs={{0,8},{8,0},{16,24},{24,16},{1,9},{9,1},{17,25},{25,17},{2,10},{10... | collective-permute-start | bytes 589832 | tf_op jit(solution)/shard_map/ppermute | solution.py:42
  123.3 6.7 %collective-permute-done.39 = bf16[64,1536]{1,0:T(8,128)(2,1)S(1)} collective-permute-done((bf16[64,1536]{1,0:T(8,128)(2,1)S(1)}, bf16[64,1536]{1,0:T(8,128)(2,1)S(1)}, u32[]{:S(2)}, u32[]{:S(2)}) %collective-permute-start.39) | collective-permute-done | bytes 196640 | tf_op jit(solution)/shard_map/ppermute | solution.py:42
  130.0 1.1 collective-permute-start.40
  131.0 1.5 collective-permute-done.38
  132.5 1.2 collective-permute-start.41
  133.9 1.4 fusion.2
  135.4 2.4 %collective-permute-done.40 = bf16[2,64,1536]{2,1,0:T(8,128)(2,1)S(1)} collective-permute-done((bf16[2,64,1536]{2,1,0:T(8,128)(2,1)S(1)}, bf16[2,64,1536]{2,1,0:T(8,128)(2,1)S(1)}, u32[]{:S(2)}, u32[]{:S(2)}) %collective-permute-start.40) | collective-permute-done | bytes 393248 | tf_op jit(solution)/shard_map/ppermute | solution.py:42
  137.8 2.5 %collective-permute-done.41 = bf16[2,64,1536]{2,1,0:T(8,128)(2,1)S(1)} collective-permute-done((bf16[2,64,1536]{2,1,0:T(8,128)(2,1)S(1)}, bf16[2,64,1536]{2,1,0:T(8,128)(2,1)S(1)}, u32[]{:S(2)}, u32[]{:S(2)}) %collective-permute-start.41) | collective-permute-done | bytes 393248 | tf_op jit(solution)/shard_map/ppermute | solution.py:42
  140.7 2.6 %collective-permute-start.34 = (bf16[4,16,768]{2,1,0:T(8,128)(2,1)S(1)}, bf16[4,16,768]{2,1,0:T(8,128)(2,1)S(1)}, u32[]{:S(2)}, u32[]{:S(2)}) collective-permute-start(bf16[4,16,768]{2,1,0:T(8,128)(2,1)S(1)} %get-tuple-element.35), channel_id=1, source_target_pairs={{0,2},{1,3},{2,4},{3,5},{4,6},{5,7},{6,0},{7,1},{8,10},{9,11},{10,... | collective-permute-start | bytes 294920 | tf_op jit(solution)/shard_map/ppermute | solution.py:42
  143.3 2.1 %collective-permute-start.33 = (bf16[4,16,768]{2,1,0:T(8,128)(2,1)S(1)}, bf16[4,16,768]{2,1,0:T(8,128)(2,1)S(1)}, u32[]{:S(2)}, u32[]{:S(2)}) collective-permute-start(bf16[4,16,768]{2,1,0:T(8,128)(2,1)S(1)} %get-tuple-element.36), channel_id=1, source_target_pairs={{0,4},{1,5},{2,6},{3,7},{4,0},{5,1},{6,2},{7,3},{8,12},{9,13},{10,... | collective-permute-start | bytes 294920 | tf_op jit(solution)/shard_map/ppermute | solution.py:42
  145.9 1.6 %collective-permute-done.34 = bf16[4,16,768]{2,1,0:T(8,128)(2,1)S(1)} collective-permute-done((bf16[4,16,768]{2,1,0:T(8,128)(2,1)S(1)}, bf16[4,16,768]{2,1,0:T(8,128)(2,1)S(1)}, u32[]{:S(2)}, u32[]{:S(2)}) %collective-permute-start.34) | collective-permute-done | bytes 98336 | tf_op jit(solution)/shard_map/ppermute | solution.py:42
  147.5 2.2 %collective-permute-done.33 = bf16[4,16,768]{2,1,0:T(8,128)(2,1)S(1)} collective-permute-done((bf16[4,16,768]{2,1,0:T(8,128)(2,1)S(1)}, bf16[4,16,768]{2,1,0:T(8,128)(2,1)S(1)}, u32[]{:S(2)}, u32[]{:S(2)}) %collective-permute-start.33) | collective-permute-done | bytes 98336 | tf_op jit(solution)/shard_map/ppermute | solution.py:42
  149.7 1.0 collective-permute-done.32
  150.8 1.5 collective-permute-start.37
  152.3 1.1 collective-permute-start.36
  153.5 0.9 collective-permute-start.35
  154.3 3.6 %fusion.106 = f32[768,1536]{1,0:T(8,128)} fusion(bf16[512,768]{1,0:T(8,128)(2,1)S(1)} %bitcast.451, bf16[512,1536]{1,0:T(8,128)(2,1)S(1)} %bitcast.452), kind=kOutput, calls=%fused_computation.287 | convolution fusion | flops 1207959552 | bytes 7077888 | tf_op jit(solution)/shard_map/dot_general | solution.py:204
  (141 shorter events, 21.4 us)
Async XLA Ops:
  0.6 24.8 %copy-start = (bf16[768,1536]{1,0:T(8,128)(2,1)S(1)}, bf16[768,1536]{1,0:T(8,128)(2,1)}, u32[]{:S(2)}) copy-start(bf16[768,1536]{1,0:T(8,128)(2,1)} %param.10) | copy-start | bytes 7077892
  2.6 6.3 %collective-permute-start.2 = (bf16[3,16,768]{2,1,0:T(8,128)(2,1)S(1)}, bf16[3,16,768]{2,1,0:T(8,128)(2,1)S(1)}, u32[]{:S(2)}, u32[]{:S(2)}) collective-permute-start(bf16[3,16,768]{2,1,0:T(8,128)(2,1)S(1)} %pad_maximum_fusion.29), channel_id=1, source_target_pairs={{0,24},{8,16},{16,8},{24,0},{1,25},{9,17},{17,9},{25,1},{2,26},{10... | collective-permute-start | bytes 221192 | tf_op jit(solution)/shard_map/ppermute | solution.py:42
  6.6 4.4 %collective-permute-start.1 = (bf16[3,16,768]{2,1,0:T(8,128)(2,1)S(1)}, bf16[3,16,768]{2,1,0:T(8,128)(2,1)S(1)}, u32[]{:S(2)}, u32[]{:S(2)}) collective-permute-start(bf16[3,16,768]{2,1,0:T(8,128)(2,1)S(1)} %pad_maximum_fusion.28), channel_id=1, source_target_pairs={{0,16},{8,24},{16,0},{24,8},{1,17},{9,25},{17,1},{25,9},{2,18},{10... | collective-permute-start | bytes 221192 | tf_op jit(solution)/shard_map/ppermute | solution.py:42
  7.2 4.4 %collective-permute-start = (bf16[3,16,768]{2,1,0:T(8,128)(2,1)S(1)}, bf16[3,16,768]{2,1,0:T(8,128)(2,1)S(1)}, u32[]{:S(2)}, u32[]{:S(2)}) collective-permute-start(bf16[3,16,768]{2,1,0:T(8,128)(2,1)S(1)} %pad_maximum_fusion.27), channel_id=1, source_target_pairs={{0,8},{8,0},{16,24},{24,16},{1,9},{9,1},{17,25},{25,17},{2,10},{10... | collective-permute-start | bytes 221192 | tf_op jit(solution)/shard_map/ppermute | solution.py:42
  11.6 6.8 %collective-permute-start.5 = (bf16[1,4,16,768]{3,2,1,0:T(8,128)(2,1)S(1)}, bf16[1,4,16,768]{3,2,1,0:T(8,128)(2,1)S(1)}, u32[]{:S(2)}, u32[]{:S(2)}) collective-permute-start(bf16[1,4,16,768]{3,2,1,0:T(8,128)(2,1)S(1)} %get-tuple-element.54), channel_id=1, source_target_pairs={{0,6},{1,7},{2,0},{3,1},{4,2},{5,3},{6,4},{7,5},{8,14},{9,15},{10,... | collective-permute-start | bytes 294920 | tf_op jit(solution)/shard_map/ppermute | solution.py:42
  15.3 8.2 %collective-permute-start.4 = (bf16[1,4,16,768]{3,2,1,0:T(8,128)(2,1)S(1)}, bf16[1,4,16,768]{3,2,1,0:T(8,128)(2,1)S(1)}, u32[]{:S(2)}, u32[]{:S(2)}) collective-permute-start(bf16[1,4,16,768]{3,2,1,0:T(8,128)(2,1)S(1)} %get-tuple-element.54), channel_id=1, source_target_pairs={{0,4},{1,5},{2,6},{3,7},{4,0},{5,1},{6,2},{7,3},{8,12},{9,13},{10,... | collective-permute-start | bytes 294920 | tf_op jit(solution)/shard_map/ppermute | solution.py:42
  15.3 8.2 %collective-permute-start.3 = (bf16[1,4,16,768]{3,2,1,0:T(8,128)(2,1)S(1)}, bf16[1,4,16,768]{3,2,1,0:T(8,128)(2,1)S(1)}, u32[]{:S(2)}, u32[]{:S(2)}) collective-permute-start(bf16[1,4,16,768]{3,2,1,0:T(8,128)(2,1)S(1)} %get-tuple-element.54), channel_id=1, source_target_pairs={{0,2},{1,3},{2,4},{3,5},{4,6},{5,7},{6,0},{7,1},{8,10},{9,11},{10,... | collective-permute-start | bytes 294920 | tf_op jit(solution)/shard_map/ppermute | solution.py:42
  23.5 1.8 %collective-permute-start.6 = (bf16[1,4,4,16,768]{4,3,2,1,0:T(8,128)(2,1)S(1)}, bf16[1,4,4,16,768]{4,3,2,1,0:T(8,128)(2,1)S(1)}, u32[]{:S(2)}, u32[]{:S(2)}) collective-permute-start(bf16[1,4,4,16,768]{4,3,2,1,0:T(8,128)(2,1)S(1)} %get-tuple-element.46), channel_id=1, source_target_pairs={{0,1},{1,0},{2,3},{3,2},{4,5},{5,4},{6,7},{7,6},{8,9},{9,8},{10,11... | collective-permute-start | bytes 1179656 | tf_op jit(solution)/shard_map/ppermute | solution.py:42
  27.5 8.2 %collective-permute-start.21 = (bf16[2,4,16,768]{3,2,0,1:T(8,128)(2,1)S(1)}, bf16[2,4,16,768]{3,2,0,1:T(8,128)(2,1)S(1)}, u32[]{:S(2)}, u32[]{:S(2)}) collective-permute-start(bf16[2,4,16,768]{3,2,0,1:T(8,128)(2,1)S(1)} %pad_maximum_fusion.24), channel_id=1, source_target_pairs={{0,6},{1,7},{2,0},{3,1},{4,2},{5,3},{6,4},{7,5},{8,14},{9,15},{10,... | collective-permute-start | bytes 589832 | tf_op jit(solution)/shard_map/ppermute | solution.py:42
  29.0 18.3 %collective-permute-start.20 = (bf16[2,4,16,768]{3,2,0,1:T(8,128)(2,1)S(1)}, bf16[2,4,16,768]{3,2,0,1:T(8,128)(2,1)}, u32[]{:S(2)}, u32[]{:S(2)}) collective-permute-start(bf16[2,4,16,768]{3,2,0,1:T(8,128)(2,1)S(1)} %pad_maximum_fusion.24), channel_id=1, source_target_pairs={{0,4},{1,5},{2,6},{3,7},{4,0},{5,1},{6,2},{7,3},{8,12},{9,13},{10,... | collective-permute-start | bytes 589832 | tf_op jit(solution)/shard_map/ppermute | solution.py:42
  29.4 17.9 %collective-permute-start.19 = (bf16[2,4,16,768]{3,2,0,1:T(8,128)(2,1)S(1)}, bf16[2,4,16,768]{3,2,0,1:T(8,128)(2,1)}, u32[]{:S(2)}, u32[]{:S(2)}) collective-permute-start(bf16[2,4,16,768]{3,2,0,1:T(8,128)(2,1)S(1)} %pad_maximum_fusion.24), channel_id=1, source_target_pairs={{0,2},{1,3},{2,4},{3,5},{4,6},{5,7},{6,0},{7,1},{8,10},{9,11},{10,... | collective-permute-start | bytes 589832 | tf_op jit(solution)/shard_map/ppermute | solution.py:42
  32.1 16.3 %collective-permute-start.9 = (bf16[2,1,64,1536]{3,2,1,0:T(8,128)(2,1)}, bf16[2,1,64,1536]{3,2,1,0:T(8,128)(2,1)}, u32[]{:S(2)}, u32[]{:S(2)}) collective-permute-start(bf16[2,1,64,1536]{3,2,1,0:T(8,128)(2,1)} %pad_maximum_fusion.9), channel_id=1, source_target_pairs={{0,8},{8,0},{16,24},{24,16},{1,9},{9,1},{17,25},{25,17},{2,10},{10... | collective-permute-start | bytes 1179656 | tf_op jit(solution)/shard_map/ppermute | solution.py:42
  34.3 17.1 %collective-permute-start.7 = (bf16[2,1,64,1536]{3,2,1,0:T(8,128)(2,1)}, bf16[2,1,64,1536]{3,2,1,0:T(8,128)(2,1)}, u32[]{:S(2)}, u32[]{:S(2)}) collective-permute-start(bf16[2,1,64,1536]{3,2,1,0:T(8,128)(2,1)} %pad_maximum_fusion.8), channel_id=1, source_target_pairs={{0,16},{8,24},{16,0},{24,8},{1,17},{9,25},{17,1},{25,9},{2,18},{10... | collective-permute-start | bytes 1179656 | tf_op jit(solution)/shard_map/ppermute | solution.py:42
  48.4 21.3 %collective-permute-start.22 = (bf16[2,4,4,16,768]{4,3,0,1,2:T(8,128)(2,1)S(1)}, bf16[2,4,4,16,768]{4,3,0,1,2:T(8,128)(2,1)S(1)}, u32[]{:S(2)}, u32[]{:S(2)}) collective-permute-start(bf16[2,4,4,16,768]{4,3,0,1,2:T(8,128)(2,1)S(1)} %pad_maximum_fusion.4), channel_id=1, source_target_pairs={{0,1},{1,0},{2,3},{3,2},{4,5},{5,4},{6,7},{7,6},{8,9},{9,8},{10,11... | collective-permute-start | bytes 2359304 | tf_op jit(solution)/shard_map/ppermute | solution.py:42
  50.0 7.4 %collective-permute-start.10 = (bf16[1,64,1536]{2,1,0:T(8,128)(2,1)S(1)}, bf16[1,64,1536]{2,1,0:T(8,128)(2,1)S(1)}, u32[]{:S(2)}, u32[]{:S(2)}) collective-permute-start(bf16[1,64,1536]{2,1,0:T(8,128)(2,1)S(1)} %fusion.69), channel_id=1, source_target_pairs={{0,16},{8,24},{16,0},{24,8},{1,17},{9,25},{17,1},{25,9},{2,18},{10... | collective-permute-start | bytes 589832 | tf_op jit(solution)/shard_map/ppermute | solution.py:42
  52.9 7.6 %collective-permute-start.8 = (bf16[1,64,1536]{2,1,0:T(8,128)(2,1)S(1)}, bf16[1,64,1536]{2,1,0:T(8,128)(2,1)S(1)}, u32[]{:S(2)}, u32[]{:S(2)}) collective-permute-start(bf16[1,64,1536]{2,1,0:T(8,128)(2,1)S(1)} %fusion.68), channel_id=1, source_target_pairs={{0,8},{8,0},{16,24},{24,16},{1,9},{9,1},{17,25},{25,17},{2,10},{10... | collective-permute-start | bytes 589832 | tf_op jit(solution)/shard_map/ppermute | solution.py:42
  58.9 6.6 %collective-permute-start.12 = (bf16[64,1536]{1,0:T(8,128)(2,1)S(1)}, bf16[64,1536]{1,0:T(8,128)(2,1)S(1)}, u32[]{:S(2)}, u32[]{:S(2)}) collective-permute-start(bf16[64,1536]{1,0:T(8,128)(2,1)S(1)} %get-tuple-element.69), channel_id=1, source_target_pairs={{0,16},{8,24},{16,0},{24,8},{1,17},{9,25},{17,1},{25,9},{2,18},{10... | collective-permute-start | bytes 589832 | tf_op jit(solution)/shard_map/ppermute | solution.py:42
  62.0 7.6 %collective-permute-start.11 = (bf16[64,1536]{1,0:T(8,128)(2,1)S(1)}, bf16[64,1536]{1,0:T(8,128)(2,1)S(1)}, u32[]{:S(2)}, u32[]{:S(2)}) collective-permute-start(bf16[64,1536]{1,0:T(8,128)(2,1)S(1)} %get-tuple-element.71), channel_id=1, source_target_pairs={{0,8},{8,0},{16,24},{24,16},{1,9},{9,1},{17,25},{25,17},{2,10},{10... | collective-permute-start | bytes 589832 | tf_op jit(solution)/shard_map/ppermute | solution.py:42
  65.5 17.9 %collective-permute-start.13 = (bf16[2,64,1536]{2,1,0:T(8,128)(2,1)S(1)}, bf16[2,64,1536]{2,1,0:T(8,128)(2,1)S(1)}, u32[]{:S(2)}, u32[]{:S(2)}) collective-permute-start(bf16[2,64,1536]{2,1,0:T(8,128)(2,1)S(1)} %pad_maximum_fusion.11), channel_id=1, source_target_pairs={{0,8},{8,0},{16,24},{24,16},{1,9},{9,1},{17,25},{25,17},{2,10},{10... | collective-permute-start | bytes 1179656 | tf_op jit(solution)/shard_map/ppermute | solution.py:42
  69.7 13.7 %collective-permute-start.14 = (bf16[2,64,1536]{2,1,0:T(8,128)(2,1)S(1)}, bf16[2,64,1536]{2,1,0:T(8,128)(2,1)S(1)}, u32[]{:S(2)}, u32[]{:S(2)}) collective-permute-start(bf16[2,64,1536]{2,1,0:T(8,128)(2,1)S(1)} %pad_maximum_fusion.13), channel_id=1, source_target_pairs={{0,16},{8,24},{16,0},{24,8},{1,17},{9,25},{17,1},{25,9},{2,18},{10... | collective-permute-start | bytes 1179656 | tf_op jit(solution)/shard_map/ppermute | solution.py:42
  70.1 1.7 %copy-start.1 = (bf16[1536,768]{1,0:T(8,128)(2,1)S(1)}, bf16[1536,768]{1,0:T(8,128)(2,1)}, u32[]{:S(2)}) copy-start(bf16[1536,768]{1,0:T(8,128)(2,1)} %param.11) | copy-start | bytes 7077892
  79.7 18.4 %collective-permute-start.23 = (bf16[2,2,64,1536]{3,2,1,0:T(8,128)(2,1)S(1)}, bf16[2,2,64,1536]{3,2,1,0:T(8,128)(2,1)S(1)}, u32[]{:S(2)}, u32[]{:S(2)}) collective-permute-start(bf16[2,2,64,1536]{3,2,1,0:T(8,128)(2,1)S(1)} %pad_maximum_fusion.5), channel_id=1, source_target_pairs={{0,16},{8,24},{16,0},{24,8},{1,17},{9,25},{17,1},{25,9},{2,18},{10... | collective-permute-start | bytes 2359304 | tf_op jit(solution)/shard_map/ppermute | solution.py:42
  81.9 18.3 %collective-permute-start.25 = (bf16[2,2,64,1536]{3,2,1,0:T(8,128)(2,1)S(1)}, bf16[2,2,64,1536]{3,2,1,0:T(8,128)(2,1)S(1)}, u32[]{:S(2)}, u32[]{:S(2)}) collective-permute-start(bf16[2,2,64,1536]{3,2,1,0:T(8,128)(2,1)S(1)} %pad_maximum_fusion.6), channel_id=1, source_target_pairs={{0,8},{8,0},{16,24},{24,16},{1,9},{9,1},{17,25},{25,17},{2,10},{10... | collective-permute-start | bytes 2359304 | tf_op jit(solution)/shard_map/ppermute | solution.py:42
  85.0 1.8 %collective-permute-start.15 = (bf16[4,4,16,768]{3,2,1,0:T(8,128)(2,1)S(1)}, bf16[4,4,16,768]{3,2,1,0:T(8,128)(2,1)S(1)}, u32[]{:S(2)}, u32[]{:S(2)}) collective-permute-start(bf16[4,4,16,768]{3,2,1,0:T(8,128)(2,1)S(1)} %fusion.56), channel_id=1, source_target_pairs={{0,1},{1,0},{2,3},{3,2},{4,5},{5,4},{6,7},{7,6},{8,9},{9,8},{10,11... | collective-permute-start | bytes 1179656 | tf_op jit(solution)/shard_map/ppermute | solution.py:42
  86.9 7.6 %collective-permute-start.18 = (bf16[4,16,768]{2,1,0:T(8,128)(2,1)S(1)}, bf16[4,16,768]{2,1,0:T(8,128)(2,1)S(1)}, u32[]{:S(2)}, u32[]{:S(2)}) collective-permute-start(bf16[4,16,768]{2,1,0:T(8,128)(2,1)S(1)} %get-tuple-element.32), channel_id=1, source_target_pairs={{0,2},{1,3},{2,4},{3,5},{4,6},{5,7},{6,0},{7,1},{8,10},{9,11},{10,... | collective-permute-start | bytes 294920 | tf_op jit(solution)/shard_map/ppermute | solution.py:42
  87.3 10.6 %collective-permute-start.17 = (bf16[4,16,768]{2,1,0:T(8,128)(2,1)S(1)}, bf16[4,16,768]{2,1,0:T(8,128)(2,1)S(1)}, u32[]{:S(2)}, u32[]{:S(2)}) collective-permute-start(bf16[4,16,768]{2,1,0:T(8,128)(2,1)S(1)} %get-tuple-element.33), channel_id=1, source_target_pairs={{0,4},{1,5},{2,6},{3,7},{4,0},{5,1},{6,2},{7,3},{8,12},{9,13},{10,... | collective-permute-start | bytes 294920 | tf_op jit(solution)/shard_map/ppermute | solution.py:42
  89.4 8.5 %collective-permute-start.16 = (bf16[4,16,768]{2,1,0:T(8,128)(2,1)S(1)}, bf16[4,16,768]{2,1,0:T(8,128)(2,1)S(1)}, u32[]{:S(2)}, u32[]{:S(2)}) collective-permute-start(bf16[4,16,768]{2,1,0:T(8,128)(2,1)S(1)} %get-tuple-element.31), channel_id=1, source_target_pairs={{0,6},{1,7},{2,0},{3,1},{4,2},{5,3},{6,4},{7,5},{8,14},{9,15},{10,... | collective-permute-start | bytes 294920 | tf_op jit(solution)/shard_map/ppermute | solution.py:42
  98.1 9.6 %collective-permute-start.24 = (bf16[2,64,1536]{2,1,0:T(8,128)(2,1)S(1)}, bf16[2,64,1536]{2,1,0:T(8,128)(2,1)S(1)}, u32[]{:S(2)}, u32[]{:S(2)}) collective-permute-start(bf16[2,64,1536]{2,1,0:T(8,128)(2,1)S(1)} %fusion.27), channel_id=1, source_target_pairs={{0,8},{8,0},{16,24},{24,16},{1,9},{9,1},{17,25},{25,17},{2,10},{10... | collective-permute-start | bytes 1179656 | tf_op jit(solution)/shard_map/ppermute | solution.py:42
  100.3 9.1 %collective-permute-start.26 = (bf16[2,64,1536]{2,1,0:T(8,128)(2,1)S(1)}, bf16[2,64,1536]{2,1,0:T(8,128)(2,1)S(1)}, u32[]{:S(2)}, u32[]{:S(2)}) collective-permute-start(bf16[2,64,1536]{2,1,0:T(8,128)(2,1)S(1)} %fusion.29), channel_id=1, source_target_pairs={{0,16},{8,24},{16,0},{24,8},{1,17},{9,25},{17,1},{25,9},{2,18},{10... | collective-permute-start | bytes 1179656 | tf_op jit(solution)/shard_map/ppermute | solution.py:42
  110.6 6.7 %collective-permute-start.28 = (bf16[64,1536]{1,0:T(8,128)(2,1)S(1)}, bf16[64,1536]{1,0:T(8,128)(2,1)S(1)}, u32[]{:S(2)}, u32[]{:S(2)}) collective-permute-start(bf16[64,1536]{1,0:T(8,128)(2,1)S(1)} %fusion.65), channel_id=1, source_target_pairs={{0,16},{8,24},{16,0},{24,8},{1,17},{9,25},{17,1},{25,9},{2,18},{10... | collective-permute-start | bytes 589832 | tf_op jit(solution)/shard_map/ppermute | solution.py:42
  111.0 7.4 %collective-permute-start.27 = (bf16[64,1536]{1,0:T(8,128)(2,1)S(1)}, bf16[64,1536]{1,0:T(8,128)(2,1)S(1)}, u32[]{:S(2)}, u32[]{:S(2)}) collective-permute-start(bf16[64,1536]{1,0:T(8,128)(2,1)S(1)} %fusion.67), channel_id=1, source_target_pairs={{0,8},{8,0},{16,24},{24,16},{1,9},{9,1},{17,25},{25,17},{2,10},{10... | collective-permute-start | bytes 589832 | tf_op jit(solution)/shard_map/ppermute | solution.py:42
  117.3 16.4 %collective-permute-start.29 = (bf16[2,64,1536]{2,1,0:T(8,128)(2,1)S(1)}, bf16[2,64,1536]{2,1,0:T(8,128)(2,1)S(1)}, u32[]{:S(2)}, u32[]{:S(2)}) collective-permute-start(bf16[2,64,1536]{2,1,0:T(8,128)(2,1)S(1)} %pad_maximum_fusion.17), channel_id=1, source_target_pairs={{0,8},{8,0},{16,24},{24,16},{1,9},{9,1},{17,25},{25,17},{2,10},{10... | collective-permute-start | bytes 1179656 | tf_op jit(solution)/shard_map/ppermute | solution.py:42
  118.4 15.4 %collective-permute-start.30 = (bf16[2,64,1536]{2,1,0:T(8,128)(2,1)S(1)}, bf16[2,64,1536]{2,1,0:T(8,128)(2,1)S(1)}, u32[]{:S(2)}, u32[]{:S(2)}) collective-permute-start(bf16[2,64,1536]{2,1,0:T(8,128)(2,1)S(1)} %pad_maximum_fusion.19), channel_id=1, source_target_pairs={{0,16},{8,24},{16,0},{24,8},{1,17},{9,25},{17,1},{25,9},{2,18},{10... | collective-permute-start | bytes 1179656 | tf_op jit(solution)/shard_map/ppermute | solution.py:42
  120.8 9.1 %collective-permute-start.39 = (bf16[64,1536]{1,0:T(8,128)(2,1)S(1)}, bf16[64,1536]{1,0:T(8,128)(2,1)S(1)}, u32[]{:S(2)}, u32[]{:S(2)}) collective-permute-start(bf16[64,1536]{1,0:T(8,128)(2,1)S(1)} %select_convert_fusion), channel_id=1, source_target_pairs={{0,16},{8,24},{16,0},{24,8},{1,17},{9,25},{17,1},{25,9},{2,18},{10... | collective-permute-start | bytes 589832 | tf_op jit(solution)/shard_map/ppermute | solution.py:42
  121.2 11.3 %collective-permute-start.38 = (bf16[64,1536]{1,0:T(8,128)(2,1)S(1)}, bf16[64,1536]{1,0:T(8,128)(2,1)S(1)}, u32[]{:S(2)}, u32[]{:S(2)}) collective-permute-start(bf16[64,1536]{1,0:T(8,128)(2,1)S(1)} %select_convert_fusion.1), channel_id=1, source_target_pairs={{0,8},{8,0},{16,24},{24,16},{1,9},{9,1},{17,25},{25,17},{2,10},{10... | collective-permute-start | bytes 589832 | tf_op jit(solution)/shard_map/ppermute | solution.py:42
  130.0 7.8 %collective-permute-start.40 = (bf16[2,64,1536]{2,1,0:T(8,128)(2,1)S(1)}, bf16[2,64,1536]{2,1,0:T(8,128)(2,1)S(1)}, u32[]{:S(2)}, u32[]{:S(2)}) collective-permute-start(bf16[2,64,1536]{2,1,0:T(8,128)(2,1)S(1)} %pad_maximum_fusion.22), channel_id=1, source_target_pairs={{0,8},{8,0},{16,24},{24,16},{1,9},{9,1},{17,25},{25,17},{2,10},{10... | collective-permute-start | bytes 1179656 | tf_op jit(solution)/shard_map/ppermute | solution.py:42
  132.5 7.8 %collective-permute-start.41 = (bf16[2,64,1536]{2,1,0:T(8,128)(2,1)S(1)}, bf16[2,64,1536]{2,1,0:T(8,128)(2,1)S(1)}, u32[]{:S(2)}, u32[]{:S(2)}) collective-permute-start(bf16[2,64,1536]{2,1,0:T(8,128)(2,1)S(1)} %pad_maximum_fusion.23), channel_id=1, source_target_pairs={{0,16},{8,24},{16,0},{24,8},{1,17},{9,25},{17,1},{25,9},{2,18},{10... | collective-permute-start | bytes 1179656 | tf_op jit(solution)/shard_map/ppermute | solution.py:42
  135.4 5.2 %collective-permute-start.31 = (bf16[4,4,16,768]{3,2,0,1:T(8,128)(2,1)S(1)}, bf16[4,4,16,768]{3,2,0,1:T(8,128)(2,1)S(1)}, u32[]{:S(2)}, u32[]{:S(2)}) collective-permute-start(bf16[4,4,16,768]{3,2,0,1:T(8,128)(2,1)S(1)} %fusion.57), channel_id=1, source_target_pairs={{0,1},{1,0},{2,3},{3,2},{4,5},{5,4},{6,7},{7,6},{8,9},{9,8},{10,11... | collective-permute-start | bytes 1179656 | tf_op jit(solution)/shard_map/ppermute | solution.py:42
  140.7 6.8 %collective-permute-start.34 = (bf16[4,16,768]{2,1,0:T(8,128)(2,1)S(1)}, bf16[4,16,768]{2,1,0:T(8,128)(2,1)S(1)}, u32[]{:S(2)}, u32[]{:S(2)}) collective-permute-start(bf16[4,16,768]{2,1,0:T(8,128)(2,1)S(1)} %get-tuple-element.35), channel_id=1, source_target_pairs={{0,2},{1,3},{2,4},{3,5},{4,6},{5,7},{6,0},{7,1},{8,10},{9,11},{10,... | collective-permute-start | bytes 294920 | tf_op jit(solution)/shard_map/ppermute | solution.py:42
  143.3 6.4 %collective-permute-start.33 = (bf16[4,16,768]{2,1,0:T(8,128)(2,1)S(1)}, bf16[4,16,768]{2,1,0:T(8,128)(2,1)S(1)}, u32[]{:S(2)}, u32[]{:S(2)}) collective-permute-start(bf16[4,16,768]{2,1,0:T(8,128)(2,1)S(1)} %get-tuple-element.36), channel_id=1, source_target_pairs={{0,4},{1,5},{2,6},{3,7},{4,0},{5,1},{6,2},{7,3},{8,12},{9,13},{10,... | collective-permute-start | bytes 294920 | tf_op jit(solution)/shard_map/ppermute | solution.py:42
  145.4 5.3 %collective-permute-start.32 = (bf16[4,16,768]{2,1,0:T(8,128)(2,1)S(1)}, bf16[4,16,768]{2,1,0:T(8,128)(2,1)S(1)}, u32[]{:S(2)}, u32[]{:S(2)}) collective-permute-start(bf16[4,16,768]{2,1,0:T(8,128)(2,1)S(1)} %get-tuple-element.34), channel_id=1, source_target_pairs={{0,6},{1,7},{2,0},{3,1},{4,2},{5,3},{6,4},{7,5},{8,14},{9,15},{10,... | collective-permute-start | bytes 294920 | tf_op jit(solution)/shard_map/ppermute | solution.py:42
  150.8 7.2 %collective-permute-start.37 = (bf16[2,16,768]{2,1,0:T(8,128)(2,1)S(1)}, bf16[2,16,768]{2,1,0:T(8,128)(2,1)S(1)}, u32[]{:S(2)}, u32[]{:S(2)}) collective-permute-start(bf16[2,16,768]{2,1,0:T(8,128)(2,1)S(1)} %get-tuple-element.51), channel_id=1, source_target_pairs={{0,24},{8,16},{16,8},{24,0},{1,25},{9,17},{17,9},{25,1},{2,26},{10... | collective-permute-start | bytes 147464 | tf_op jit(solution)/shard_map/ppermute | solution.py:42
  152.3 5.6 %collective-permute-start.36 = (bf16[2,16,768]{2,1,0:T(8,128)(2,1)S(1)}, bf16[2,16,768]{2,1,0:T(8,128)(2,1)S(1)}, u32[]{:S(2)}, u32[]{:S(2)}) collective-permute-start(bf16[2,16,768]{2,1,0:T(8,128)(2,1)S(1)} %get-tuple-element.52), channel_id=1, source_target_pairs={{0,16},{8,24},{16,0},{24,8},{1,17},{9,25},{17,1},{25,9},{2,18},{10... | collective-permute-start | bytes 147464 | tf_op jit(solution)/shard_map/ppermute | solution.py:42
  153.5 4.5 %collective-permute-start.35 = (bf16[2,16,768]{2,1,0:T(8,128)(2,1)S(1)}, bf16[2,16,768]{2,1,0:T(8,128)(2,1)S(1)}, u32[]{:S(2)}, u32[]{:S(2)}) collective-permute-start(bf16[2,16,768]{2,1,0:T(8,128)(2,1)S(1)} %get-tuple-element.50), channel_id=1, source_target_pairs={{0,8},{8,0},{16,24},{24,16},{1,9},{9,1},{17,25},{25,17},{2,10},{10... | collective-permute-start | bytes 147464 | tf_op jit(solution)/shard_map/ppermute | solution.py:42

commit v6 on v5

--- a/solution.py
+++ b/solution.py
@@ -183,9 +183,10 @@
         return half(total)
 
     pre_act = [p[0] for p in sums([(up, tok_cols)])]
+    pre_act, later = lax.optimization_barrier((pre_act, later))
     pairs = [gelu_pair(p) for p in pre_act]
     act_held = spread([a for a, _ in pairs])
-    later = from_cores(after(later, pre_act))
+    later = from_cores(later)
     tan_cols, cot_cols = after(later, act_held)
     act_all = everywhere(act_held)
     both = sums([(up, tan_cols), (back, cot_cols)])
@@ -193,7 +194,7 @@
     both = after(both, out_near)
     dact_held = spread([s * v[0] for (_, s), v in zip(pairs, both)])
     dact_all = everywhere(dact_held)
-    back_grad = after([v[1] for v in both], dact_held)
+    dact_all, back_grad = lax.optimization_barrier((dact_all, [v[1] for v in both]))
     grad_all = everywhere(spread([s * v for (_, s), v in zip(pairs, back_grad)]))
     summed = jnp.stack([down_chips(out_near), down_chips(down_cores(dact_all))], axis=1)
     cols = jnp.stack(

time: 160 us -> 174 us (1.087)
  local copies, waits for them, and re-layouts: 5.73 us -> 10.9 us
  starting transfers between devices: 48.1 us -> 52.6 us
  waiting for transfers between devices: 70 us -> 72.7 us
    another operation x5, local copies, waits for them, and re-layouts: 1.54 us -> 6.12 us  [local(): out, tan = cols.transpose(2, 3, 0, 1, 4).reshape(2, own_rows, model_cols)]
    ppermute x42, starting transfers between devices: 48.1 us -> 52.6 us  [shift(): return lax.ppermute(value, axis, pairs)]
    ppermute x42, waiting for transfers between devices: 70 us -> 72.7 us  [shift(): return lax.ppermute(value, axis, pairs)]
    squeeze x6, local copies, waits for them, and re-layouts: 0.16 us -> 2.25 us  [gather_second(): found[(i, j) if first == 0 else (j, i)] = there[i]]
    another operation x6 -> x8, other arithmetic: 0.23 us -> 2.09 us  [gather_first(): jnp.stack([shift(value, grid, axis_step(first, i)) for i in range(grid[fi...]
  transfers between devices with their start and end apart: 42 -> 42, of which waited for: 24 -> 24; matrix products, arithmetic and copies ran while one was open for 20% -> 19% of each run, Pallas kernels for 0% -> 0%
where the time goes in v6:
time: 174 us
  waiting for transfers between devices  72.7 us (42%)
  starting transfers between devices  52.6 us (30%)
  matrix products  25.3 us (15%)
  local copies, waits for them, and re-layouts  10.9 us (6%)
  other arithmetic  10.6 us (6%)
    ppermute x42, waiting for transfers between devices, shift(): return lax.ppermute(value, axis, pairs)  72.7 us
    ppermute x42, starting transfers between devices, shift(): return lax.ppermute(value, axis, pairs)  52.6 us
    dot_general x18, matrix products, dot(): return jnp.dot(a, b, preferred_element_type=jnp.float32)  15.1 us
    dot_general x8, matrix products, back(): lax.dot_general(rows, w_out, (((1,), (1,)), ((), ())), preferred_element_...  6.66 us
    another operation x5, local copies, waits for them, and re-layouts, local(): out, tan = cols.transpose(2, 3, 0, 1, 4).reshape(2, own_rows, model_cols)  6.12 us
    dot_general x1, matrix products, local(): lax.dot_general(tok_cols.reshape(dp_count * group_rows, own_cols), grad_a...  3.6 us
  transfers between devices with their start and end apart: 42, of which 24 were waited for; matrix products, arithmetic and copies ran while one was open for 19% of the time, Pallas kernels for 0%

profile of v6, /device:TPU:0, one launch (start us, length us, event | category | flops | bytes accessed | tf_op | source)
XLA Modules:
  0.0 173.5 jit_solution(14927285694771107641)
XLA Ops:
  0.7 0.9 dynamic-slice_bitcast_fusion.11
  1.7 0.9 dynamic-slice_bitcast_fusion
  2.6 4.0 %collective-permute-start.2 = (bf16[3,16,768]{2,1,0:T(8,128)(2,1)S(1)}, bf16[3,16,768]{2,1,0:T(8,128)(2,1)S(1)}, u32[]{:S(2)}, u32[]{:S(2)}) collective-permute-start(bf16[3,16,768]{2,1,0:T(8,128)(2,1)S(1)} %pad_maximum_fusion.25), channel_id=1, source_target_pairs={{0,24},{8,16},{16,8},{24,0},{1,25},{9,17},{17,9},{25,1},{2,26},{10... | collective-permute-start | bytes 221192 | tf_op jit(solution)/shard_map/ppermute | solution.py:42
  7.5 1.3 fusion.81
  8.9 2.1 %collective-permute-done.1 = bf16[3,16,768]{2,1,0:T(8,128)(2,1)S(1)} collective-permute-done((bf16[3,16,768]{2,1,0:T(8,128)(2,1)S(1)}, bf16[3,16,768]{2,1,0:T(8,128)(2,1)S(1)}, u32[]{:S(2)}, u32[]{:S(2)}) %collective-permute-start.1) | collective-permute-done | bytes 73760 | tf_op jit(solution)/shard_map/ppermute | solution.py:42
  11.6 3.7 %collective-permute-start.5 = (bf16[1,4,16,768]{3,2,1,0:T(8,128)(2,1)S(1)}, bf16[1,4,16,768]{3,2,1,0:T(8,128)(2,1)S(1)}, u32[]{:S(2)}, u32[]{:S(2)}) collective-permute-start(bf16[1,4,16,768]{3,2,1,0:T(8,128)(2,1)S(1)} %get-tuple-element.64), channel_id=1, source_target_pairs={{0,6},{1,7},{2,0},{3,1},{4,2},{5,3},{6,4},{7,5},{8,14},{9,15},{10,... | collective-permute-start | bytes 294920 | tf_op jit(solution)/shard_map/ppermute | solution.py:42
  15.3 1.0 collective-permute-start.3
  16.3 2.1 %collective-permute-done.5 = bf16[1,4,16,768]{3,2,1,0:T(8,128)(2,1)S(1)} collective-permute-done((bf16[1,4,16,768]{3,2,1,0:T(8,128)(2,1)S(1)}, bf16[1,4,16,768]{3,2,1,0:T(8,128)(2,1)S(1)}, u32[]{:S(2)}, u32[]{:S(2)}) %collective-permute-start.5) | collective-permute-done | bytes 98336 | tf_op jit(solution)/shard_map/ppermute | solution.py:42
  18.4 5.1 %collective-permute-done.4 = bf16[1,4,16,768]{3,2,1,0:T(8,128)(2,1)S(1)} collective-permute-done((bf16[1,4,16,768]{3,2,1,0:T(8,128)(2,1)S(1)}, bf16[1,4,16,768]{3,2,1,0:T(8,128)(2,1)S(1)}, u32[]{:S(2)}, u32[]{:S(2)}) %collective-permute-start.4) | collective-permute-done | bytes 98336 | tf_op jit(solution)/shard_map/ppermute | solution.py:42
  23.7 1.6 collective-permute-done.6
  27.5 1.5 collective-permute-start.13
  29.4 1.9 %collective-permute-start.11 = (bf16[2,4,16,768]{3,2,0,1:T(8,128)(2,1)S(1)}, bf16[2,4,16,768]{3,2,0,1:T(8,128)(2,1)}, u32[]{:S(2)}, u32[]{:S(2)}) collective-permute-start(bf16[2,4,16,768]{3,2,0,1:T(8,128)(2,1)S(1)} %pad_maximum_fusion.20), channel_id=1, source_target_pairs={{0,2},{1,3},{2,4},{3,5},{4,6},{5,7},{6,0},{7,1},{8,10},{9,11},{10,... | collective-permute-start | bytes 589832 | tf_op jit(solution)/shard_map/ppermute | solution.py:42
  32.2 1.4 collective-permute-start.7
  35.8 11.5 %collective-permute-done.12 = bf16[2,4,16,768]{3,2,0,1:T(8,128)(2,1)} collective-permute-done((bf16[2,4,16,768]{3,2,0,1:T(8,128)(2,1)S(1)}, bf16[2,4,16,768]{3,2,0,1:T(8,128)(2,1)}, u32[]{:S(2)}, u32[]{:S(2)}) %collective-permute-start.12) | collective-permute-done | bytes 196640 | tf_op jit(solution)/shard_map/ppermute | solution.py:42
  47.3 1.1 pad_maximum_fusion.4
  48.4 1.5 fusion.54
  49.9 1.4 collective-permute-start.8
  51.3 1.5 fusion.55
  53.5 2.9 %collective-permute-done.8 = bf16[1,64,1536]{2,1,0:T(8,128)(2,1)S(1)} collective-permute-done((bf16[1,64,1536]{2,1,0:T(8,128)(2,1)S(1)}, bf16[1,64,1536]{2,1,0:T(8,128)(2,1)S(1)}, u32[]{:S(2)}, u32[]{:S(2)}) %collective-permute-start.8) | collective-permute-done | bytes 196640 | tf_op jit(solution)/shard_map/ppermute | solution.py:42
  56.4 1.5 fusion.49
  57.8 1.2 collective-permute-done.10
  59.0 1.5 fusion.45
  61.8 1.5 collective-permute-start.14
  63.3 3.2 %collective-permute-done.15 = bf16[64,1536]{1,0:T(8,128)(2,1)S(1)} collective-permute-done((bf16[64,1536]{1,0:T(8,128)(2,1)S(1)}, bf16[64,1536]{1,0:T(8,128)(2,1)S(1)}, u32[]{:S(2)}, u32[]{:S(2)}) %collective-permute-start.15) | collective-permute-done | bytes 196640 | tf_op jit(solution)/shard_map/ppermute | solution.py:42
  67.3 1.2 collective-permute-done.14
  68.5 2.3 %collective-permute-start.17 = (bf16[2,64,1536]{2,1,0:T(8,128)(2,1)S(1)}, bf16[2,64,1536]{2,1,0:T(8,128)(2,1)S(1)}, u32[]{:S(2)}, u32[]{:S(2)}) collective-permute-start(bf16[2,64,1536]{2,1,0:T(8,128)(2,1)S(1)} %pad_maximum_fusion.13), channel_id=1, source_target_pairs={{0,16},{8,24},{16,0},{24,8},{1,17},{9,25},{17,1},{25,9},{2,18},{10... | collective-permute-start | bytes 1179656 | tf_op jit(solution)/shard_map/ppermute | solution.py:42
  70.8 5.1 %collective-permute-done.16 = bf16[2,64,1536]{2,1,0:T(8,128)(2,1)S(1)} collective-permute-done((bf16[2,64,1536]{2,1,0:T(8,128)(2,1)S(1)}, bf16[2,64,1536]{2,1,0:T(8,128)(2,1)S(1)}, u32[]{:S(2)}, u32[]{:S(2)}) %collective-permute-start.16) | collective-permute-done | bytes 393248 | tf_op jit(solution)/shard_map/ppermute | solution.py:42
  76.7 1.4 fusion
  79.5 0.8 convolution_bitcast_fusion.4
  81.5 0.8 fusion.11
  82.8 0.8 fusion.9
  85.0 0.8 fusion.15
  86.4 0.8 fusion.13
  88.0 2.1 %collective-permute-start.23 = (bf16[2,2,64,1536]{3,2,1,0:T(8,128)(2,1)S(1)}, bf16[2,2,64,1536]{3,2,1,0:T(8,128)(2,1)S(1)}, u32[]{:S(2)}, u32[]{:S(2)}) collective-permute-start(bf16[2,2,64,1536]{3,2,1,0:T(8,128)(2,1)S(1)} %pad_maximum_fusion.5), channel_id=1, source_target_pairs={{0,16},{8,24},{16,0},{24,8},{1,17},{9,25},{17,1},{25,9},{2,18},{10... | collective-permute-start | bytes 2359304 | tf_op jit(solution)/shard_map/ppermute | solution.py:42
  90.9 0.8 convolution_bitcast_fusion
  92.4 2.1 %collective-permute-start.20 = (bf16[4,16,768]{2,1,0:T(8,128)(2,1)S(1)}, bf16[4,16,768]{2,1,0:T(8,128)(2,1)S(1)}, u32[]{:S(2)}, u32[]{:S(2)}) collective-permute-start(bf16[4,16,768]{2,1,0:T(8,128)(2,1)S(1)} %get-tuple-element.35), channel_id=1, source_target_pairs={{0,4},{1,5},{2,6},{3,7},{4,0},{5,1},{6,2},{7,3},{8,12},{9,13},{10,... | collective-permute-start | bytes 294920 | tf_op jit(solution)/shard_map/ppermute | solution.py:42
  94.5 2.8 %collective-permute-start.19 = (bf16[4,16,768]{2,1,0:T(8,128)(2,1)S(1)}, bf16[4,16,768]{2,1,0:T(8,128)(2,1)S(1)}, u32[]{:S(2)}, u32[]{:S(2)}) collective-permute-start(bf16[4,16,768]{2,1,0:T(8,128)(2,1)S(1)} %get-tuple-element.33), channel_id=1, source_target_pairs={{0,6},{1,7},{2,0},{3,1},{4,2},{5,3},{6,4},{7,5},{8,14},{9,15},{10,... | collective-permute-start | bytes 294920 | tf_op jit(solution)/shard_map/ppermute | solution.py:42
  97.9 1.6 collective-permute-done.21
  99.5 3.5 %collective-permute-done.20 = bf16[4,16,768]{2,1,0:T(8,128)(2,1)S(1)} collective-permute-done((bf16[4,16,768]{2,1,0:T(8,128)(2,1)S(1)}, bf16[4,16,768]{2,1,0:T(8,128)(2,1)S(1)}, u32[]{:S(2)}, u32[]{:S(2)}) %collective-permute-start.20) | collective-permute-done | bytes 98336 | tf_op jit(solution)/shard_map/ppermute | solution.py:42
  103.0 5.2 %collective-permute-done.23 = bf16[2,2,64,1536]{3,2,1,0:T(8,128)(2,1)S(1)} collective-permute-done((bf16[2,2,64,1536]{3,2,1,0:T(8,128)(2,1)S(1)}, bf16[2,2,64,1536]{3,2,1,0:T(8,128)(2,1)S(1)}, u32[]{:S(2)}, u32[]{:S(2)}) %collective-permute-start.23) | collective-permute-done | bytes 786464 | tf_op jit(solution)/shard_map/ppermute | solution.py:42
  108.3 1.8 %collective-permute-start.24 = (bf16[2,64,1536]{2,1,0:T(8,128)(2,1)S(1)}, bf16[2,64,1536]{2,1,0:T(8,128)(2,1)S(1)}, u32[]{:S(2)}, u32[]{:S(2)}) collective-permute-start(bf16[2,64,1536]{2,1,0:T(8,128)(2,1)S(1)} %fusion.27), channel_id=1, source_target_pairs={{0,8},{8,0},{16,24},{24,16},{1,9},{9,1},{17,25},{25,17},{2,10},{10... | collective-permute-start | bytes 1179656 | tf_op jit(solution)/shard_map/ppermute | solution.py:42
  110.6 8.7 %collective-permute-done.24 = bf16[2,64,1536]{2,1,0:T(8,128)(2,1)S(1)} collective-permute-done((bf16[2,64,1536]{2,1,0:T(8,128)(2,1)S(1)}, bf16[2,64,1536]{2,1,0:T(8,128)(2,1)S(1)}, u32[]{:S(2)}, u32[]{:S(2)}) %collective-permute-start.24) | collective-permute-done | bytes 393248 | tf_op jit(solution)/shard_map/ppermute | solution.py:42
  119.4 1.3 collective-permute-done.26
  122.0 1.6 collective-permute-start.27
  123.6 3.6 %collective-permute-done.28 = bf16[64,1536]{1,0:T(8,128)(2,1)S(1)} collective-permute-done((bf16[64,1536]{1,0:T(8,128)(2,1)S(1)}, bf16[64,1536]{1,0:T(8,128)(2,1)S(1)}, u32[]{:S(2)}, u32[]{:S(2)}) %collective-permute-start.28) | collective-permute-done | bytes 196640 | tf_op jit(solution)/shard_map/ppermute | solution.py:42
  128.3 2.5 %collective-permute-start.30 = (bf16[2,64,1536]{2,1,0:T(8,128)(2,1)S(1)}, bf16[2,64,1536]{2,1,0:T(8,128)(2,1)S(1)}, u32[]{:S(2)}, u32[]{:S(2)}) collective-permute-start(bf16[2,64,1536]{2,1,0:T(8,128)(2,1)S(1)} %pad_maximum_fusion.17), channel_id=1, source_target_pairs={{0,16},{8,24},{16,0},{24,8},{1,17},{9,25},{17,1},{25,9},{2,18},{10... | collective-permute-start | bytes 1179656 | tf_op jit(solution)/shard_map/ppermute | solution.py:42
  130.8 5.4 %collective-permute-done.29 = bf16[2,64,1536]{2,1,0:T(8,128)(2,1)S(1)} collective-permute-done((bf16[2,64,1536]{2,1,0:T(8,128)(2,1)S(1)}, bf16[2,64,1536]{2,1,0:T(8,128)(2,1)S(1)}, u32[]{:S(2)}, u32[]{:S(2)}) %collective-permute-start.29) | collective-permute-done | bytes 393248 | tf_op jit(solution)/shard_map/ppermute | solution.py:42
  136.9 1.4 fusion.2
  138.7 2.1 %collective-permute-start.39 = (bf16[64,1536]{1,0:T(8,128)(2,1)S(1)}, bf16[64,1536]{1,0:T(8,128)(2,1)S(1)}, u32[]{:S(2)}, u32[]{:S(2)}) collective-permute-start(bf16[64,1536]{1,0:T(8,128)(2,1)S(1)} %select_convert_fusion), channel_id=1, source_target_pairs={{0,16},{8,24},{16,0},{24,8},{1,17},{9,25},{17,1},{25,9},{2,18},{10... | collective-permute-start | bytes 589832 | tf_op jit(solution)/shard_map/ppermute | solution.py:42
  141.9 2.1 %collective-permute-start.33 = (bf16[4,16,768]{2,1,0:T(8,128)(2,1)S(1)}, bf16[4,16,768]{2,1,0:T(8,128)(2,1)S(1)}, u32[]{:S(2)}, u32[]{:S(2)}) collective-permute-start(bf16[4,16,768]{2,1,0:T(8,128)(2,1)S(1)} %get-tuple-element.38), channel_id=1, source_target_pairs={{0,4},{1,5},{2,6},{3,7},{4,0},{5,1},{6,2},{7,3},{8,12},{9,13},{10,... | collective-permute-start | bytes 294920 | tf_op jit(solution)/shard_map/ppermute | solution.py:42
  144.0 2.8 %collective-permute-start.32 = (bf16[4,16,768]{2,1,0:T(8,128)(2,1)S(1)}, bf16[4,16,768]{2,1,0:T(8,128)(2,1)S(1)}, u32[]{:S(2)}, u32[]{:S(2)}) collective-permute-start(bf16[4,16,768]{2,1,0:T(8,128)(2,1)S(1)} %get-tuple-element.36), channel_id=1, source_target_pairs={{0,6},{1,7},{2,0},{3,1},{4,2},{5,3},{6,4},{7,5},{8,14},{9,15},{10,... | collective-permute-start | bytes 294920 | tf_op jit(solution)/shard_map/ppermute | solution.py:42
  147.6 2.0 %collective-permute-start.40 = (bf16[2,64,1536]{2,1,0:T(8,128)(2,1)}, bf16[2,64,1536]{2,1,0:T(8,128)(2,1)}, u32[]{:S(2)}, u32[]{:S(2)}) collective-permute-start(bf16[2,64,1536]{2,1,0:T(8,128)(2,1)} %pad_maximum_fusion.18), channel_id=1, source_target_pairs={{0,8},{8,0},{16,24},{24,16},{1,9},{9,1},{17,25},{25,17},{2,10},{10... | collective-permute-start | bytes 1179656 | tf_op jit(solution)/shard_map/ppermute | solution.py:42
  149.6 2.8 %collective-permute-done.33 = bf16[4,16,768]{2,1,0:T(8,128)(2,1)S(1)} collective-permute-done((bf16[4,16,768]{2,1,0:T(8,128)(2,1)S(1)}, bf16[4,16,768]{2,1,0:T(8,128)(2,1)S(1)}, u32[]{:S(2)}, u32[]{:S(2)}) %collective-permute-start.33) | collective-permute-done | bytes 98336 | tf_op jit(solution)/shard_map/ppermute | solution.py:42
  152.5 1.5 collective-permute-start.37
  154.0 1.8 %collective-permute-start.36 = (bf16[2,16,768]{2,1,0:T(8,128)(2,1)S(1)}, bf16[2,16,768]{2,1,0:T(8,128)(2,1)S(1)}, u32[]{:S(2)}, u32[]{:S(2)}) collective-permute-start(bf16[2,16,768]{2,1,0:T(8,128)(2,1)S(1)} %get-tuple-element.54), channel_id=1, source_target_pairs={{0,16},{8,24},{16,0},{24,8},{1,17},{9,25},{17,1},{25,9},{2,18},{10... | collective-permute-start | bytes 147464 | tf_op jit(solution)/shard_map/ppermute | solution.py:42
  156.1 0.8 pad_maximum_fusion.19
  156.9 1.7 %collective-permute-start.41 = (bf16[2,64,1536]{2,1,0:T(8,128)(2,1)}, bf16[2,64,1536]{2,1,0:T(8,128)(2,1)}, u32[]{:S(2)}, u32[]{:S(2)}) collective-permute-start(bf16[2,64,1536]{2,1,0:T(8,128)(2,1)} %pad_maximum_fusion.19), channel_id=1, source_target_pairs={{0,16},{8,24},{16,0},{24,8},{1,17},{9,25},{17,1},{25,9},{2,18},{10... | collective-permute-start | bytes 1179656 | tf_op jit(solution)/shard_map/ppermute | solution.py:42
  158.6 2.4 %collective-permute-done.37 = bf16[2,16,768]{2,1,0:T(8,128)(2,1)S(1)} collective-permute-done((bf16[2,16,768]{2,1,0:T(8,128)(2,1)S(1)}, bf16[2,16,768]{2,1,0:T(8,128)(2,1)S(1)}, u32[]{:S(2)}, u32[]{:S(2)}) %collective-permute-start.37) | collective-permute-done | bytes 49184 | tf_op jit(solution)/shard_map/ppermute | solution.py:42
  162.6 1.6 unstack.29
  164.2 1.6 copy.36
  165.8 1.6 unstack.31
  167.4 1.1 slice_bitcast_fusion.13
  168.5 1.0 slice_bitcast_fusion.12
  169.9 3.6 %fusion.92 = f32[768,1536]{1,0:T(8,128)} fusion(bf16[512,768]{1,0:T(8,128)(2,1)S(1)} %bitcast.452, bf16[512,1536]{1,0:T(8,128)(2,1)S(1)} %bitcast.453), kind=kOutput, calls=%fused_computation.267 | convolution fusion | flops 1207959552 | bytes 7077888 | tf_op jit(solution)/shard_map/dot_general | solution.py:205
  (152 shorter events, 26.7 us)
Async XLA Ops:
  0.6 24.8 %copy-start = (bf16[768,1536]{1,0:T(8,128)(2,1)S(1)}, bf16[768,1536]{1,0:T(8,128)(2,1)}, u32[]{:S(2)}) copy-start(bf16[768,1536]{1,0:T(8,128)(2,1)} %param.10) | copy-start | bytes 7077892
  2.6 6.3 %collective-permute-start.2 = (bf16[3,16,768]{2,1,0:T(8,128)(2,1)S(1)}, bf16[3,16,768]{2,1,0:T(8,128)(2,1)S(1)}, u32[]{:S(2)}, u32[]{:S(2)}) collective-permute-start(bf16[3,16,768]{2,1,0:T(8,128)(2,1)S(1)} %pad_maximum_fusion.25), channel_id=1, source_target_pairs={{0,24},{8,16},{16,8},{24,0},{1,25},{9,17},{17,9},{25,1},{2,26},{10... | collective-permute-start | bytes 221192 | tf_op jit(solution)/shard_map/ppermute | solution.py:42
  6.6 4.4 %collective-permute-start.1 = (bf16[3,16,768]{2,1,0:T(8,128)(2,1)S(1)}, bf16[3,16,768]{2,1,0:T(8,128)(2,1)S(1)}, u32[]{:S(2)}, u32[]{:S(2)}) collective-permute-start(bf16[3,16,768]{2,1,0:T(8,128)(2,1)S(1)} %pad_maximum_fusion.24), channel_id=1, source_target_pairs={{0,16},{8,24},{16,0},{24,8},{1,17},{9,25},{17,1},{25,9},{2,18},{10... | collective-permute-start | bytes 221192 | tf_op jit(solution)/shard_map/ppermute | solution.py:42
  7.2 4.4 %collective-permute-start = (bf16[3,16,768]{2,1,0:T(8,128)(2,1)S(1)}, bf16[3,16,768]{2,1,0:T(8,128)(2,1)S(1)}, u32[]{:S(2)}, u32[]{:S(2)}) collective-permute-start(bf16[3,16,768]{2,1,0:T(8,128)(2,1)S(1)} %pad_maximum_fusion.23), channel_id=1, source_target_pairs={{0,8},{8,0},{16,24},{24,16},{1,9},{9,1},{17,25},{25,17},{2,10},{10... | collective-permute-start | bytes 221192 | tf_op jit(solution)/shard_map/ppermute | solution.py:42
  11.6 6.8 %collective-permute-start.5 = (bf16[1,4,16,768]{3,2,1,0:T(8,128)(2,1)S(1)}, bf16[1,4,16,768]{3,2,1,0:T(8,128)(2,1)S(1)}, u32[]{:S(2)}, u32[]{:S(2)}) collective-permute-start(bf16[1,4,16,768]{3,2,1,0:T(8,128)(2,1)S(1)} %get-tuple-element.64), channel_id=1, source_target_pairs={{0,6},{1,7},{2,0},{3,1},{4,2},{5,3},{6,4},{7,5},{8,14},{9,15},{10,... | collective-permute-start | bytes 294920 | tf_op jit(solution)/shard_map/ppermute | solution.py:42
  15.3 8.2 %collective-permute-start.4 = (bf16[1,4,16,768]{3,2,1,0:T(8,128)(2,1)S(1)}, bf16[1,4,16,768]{3,2,1,0:T(8,128)(2,1)S(1)}, u32[]{:S(2)}, u32[]{:S(2)}) collective-permute-start(bf16[1,4,16,768]{3,2,1,0:T(8,128)(2,1)S(1)} %get-tuple-element.64), channel_id=1, source_target_pairs={{0,4},{1,5},{2,6},{3,7},{4,0},{5,1},{6,2},{7,3},{8,12},{9,13},{10,... | collective-permute-start | bytes 294920 | tf_op jit(solution)/shard_map/ppermute | solution.py:42
  15.3 8.2 %collective-permute-start.3 = (bf16[1,4,16,768]{3,2,1,0:T(8,128)(2,1)S(1)}, bf16[1,4,16,768]{3,2,1,0:T(8,128)(2,1)S(1)}, u32[]{:S(2)}, u32[]{:S(2)}) collective-permute-start(bf16[1,4,16,768]{3,2,1,0:T(8,128)(2,1)S(1)} %get-tuple-element.64), channel_id=1, source_target_pairs={{0,2},{1,3},{2,4},{3,5},{4,6},{5,7},{6,0},{7,1},{8,10},{9,11},{10,... | collective-permute-start | bytes 294920 | tf_op jit(solution)/shard_map/ppermute | solution.py:42
  23.5 1.8 %collective-permute-start.6 = (bf16[1,4,4,16,768]{4,3,2,1,0:T(8,128)(2,1)S(1)}, bf16[1,4,4,16,768]{4,3,2,1,0:T(8,128)(2,1)S(1)}, u32[]{:S(2)}, u32[]{:S(2)}) collective-permute-start(bf16[1,4,4,16,768]{4,3,2,1,0:T(8,128)(2,1)S(1)} %get-tuple-element.48), channel_id=1, source_target_pairs={{0,1},{1,0},{2,3},{3,2},{4,5},{5,4},{6,7},{7,6},{8,9},{9,8},{10,11... | collective-permute-start | bytes 1179656 | tf_op jit(solution)/shard_map/ppermute | solution.py:42
  27.5 8.2 %collective-permute-start.13 = (bf16[2,4,16,768]{3,2,0,1:T(8,128)(2,1)S(1)}, bf16[2,4,16,768]{3,2,0,1:T(8,128)(2,1)S(1)}, u32[]{:S(2)}, u32[]{:S(2)}) collective-permute-start(bf16[2,4,16,768]{3,2,0,1:T(8,128)(2,1)S(1)} %pad_maximum_fusion.20), channel_id=1, source_target_pairs={{0,6},{1,7},{2,0},{3,1},{4,2},{5,3},{6,4},{7,5},{8,14},{9,15},{10,... | collective-permute-start | bytes 589832 | tf_op jit(solution)/shard_map/ppermute | solution.py:42
  29.0 18.3 %collective-permute-start.12 = (bf16[2,4,16,768]{3,2,0,1:T(8,128)(2,1)S(1)}, bf16[2,4,16,768]{3,2,0,1:T(8,128)(2,1)}, u32[]{:S(2)}, u32[]{:S(2)}) collective-permute-start(bf16[2,4,16,768]{3,2,0,1:T(8,128)(2,1)S(1)} %pad_maximum_fusion.20), channel_id=1, source_target_pairs={{0,4},{1,5},{2,6},{3,7},{4,0},{5,1},{6,2},{7,3},{8,12},{9,13},{10,... | collective-permute-start | bytes 589832 | tf_op jit(solution)/shard_map/ppermute | solution.py:42
  29.4 17.9 %collective-permute-start.11 = (bf16[2,4,16,768]{3,2,0,1:T(8,128)(2,1)S(1)}, bf16[2,4,16,768]{3,2,0,1:T(8,128)(2,1)}, u32[]{:S(2)}, u32[]{:S(2)}) collective-permute-start(bf16[2,4,16,768]{3,2,0,1:T(8,128)(2,1)S(1)} %pad_maximum_fusion.20), channel_id=1, source_target_pairs={{0,2},{1,3},{2,4},{3,5},{4,6},{5,7},{6,0},{7,1},{8,10},{9,11},{10,... | collective-permute-start | bytes 589832 | tf_op jit(solution)/shard_map/ppermute | solution.py:42
  32.2 16.3 %collective-permute-start.7 = (bf16[2,1,64,1536]{3,2,1,0:T(8,128)(2,1)}, bf16[2,1,64,1536]{3,2,1,0:T(8,128)(2,1)}, u32[]{:S(2)}, u32[]{:S(2)}) collective-permute-start(bf16[2,1,64,1536]{3,2,1,0:T(8,128)(2,1)} %pad_maximum_fusion.8), channel_id=1, source_target_pairs={{0,16},{8,24},{16,0},{24,8},{1,17},{9,25},{17,1},{25,9},{2,18},{10... | collective-permute-start | bytes 1179656 | tf_op jit(solution)/shard_map/ppermute | solution.py:42
  34.4 17.0 %collective-permute-start.9 = (bf16[2,1,64,1536]{3,2,1,0:T(8,128)(2,1)}, bf16[2,1,64,1536]{3,2,1,0:T(8,128)(2,1)}, u32[]{:S(2)}, u32[]{:S(2)}) collective-permute-start(bf16[2,1,64,1536]{3,2,1,0:T(8,128)(2,1)} %pad_maximum_fusion.9), channel_id=1, source_target_pairs={{0,8},{8,0},{16,24},{24,16},{1,9},{9,1},{17,25},{25,17},{2,10},{10... | collective-permute-start | bytes 1179656 | tf_op jit(solution)/shard_map/ppermute | solution.py:42
  49.9 6.5 %collective-permute-start.8 = (bf16[1,64,1536]{2,1,0:T(8,128)(2,1)S(1)}, bf16[1,64,1536]{2,1,0:T(8,128)(2,1)S(1)}, u32[]{:S(2)}, u32[]{:S(2)}) collective-permute-start(bf16[1,64,1536]{2,1,0:T(8,128)(2,1)S(1)} %fusion.54), channel_id=1, source_target_pairs={{0,8},{8,0},{16,24},{24,16},{1,9},{9,1},{17,25},{25,17},{2,10},{10... | collective-permute-start | bytes 589832 | tf_op jit(solution)/shard_map/ppermute | solution.py:42
  52.8 6.2 %collective-permute-start.10 = (bf16[1,64,1536]{2,1,0:T(8,128)(2,1)S(1)}, bf16[1,64,1536]{2,1,0:T(8,128)(2,1)S(1)}, u32[]{:S(2)}, u32[]{:S(2)}) collective-permute-start(bf16[1,64,1536]{2,1,0:T(8,128)(2,1)S(1)} %fusion.55), channel_id=1, source_target_pairs={{0,16},{8,24},{16,0},{24,8},{1,17},{9,25},{17,1},{25,9},{2,18},{10... | collective-permute-start | bytes 589832 | tf_op jit(solution)/shard_map/ppermute | solution.py:42
  60.8 5.7 %collective-permute-start.15 = (bf16[64,1536]{1,0:T(8,128)(2,1)S(1)}, bf16[64,1536]{1,0:T(8,128)(2,1)S(1)}, u32[]{:S(2)}, u32[]{:S(2)}) collective-permute-start(bf16[64,1536]{1,0:T(8,128)(2,1)S(1)} %select_convert_fusion.2), channel_id=1, source_target_pairs={{0,16},{8,24},{16,0},{24,8},{1,17},{9,25},{17,1},{25,9},{2,18},{10... | collective-permute-start | bytes 589832 | tf_op jit(solution)/shard_map/ppermute | solution.py:42
  61.8 6.7 %collective-permute-start.14 = (bf16[64,1536]{1,0:T(8,128)(2,1)S(1)}, bf16[64,1536]{1,0:T(8,128)(2,1)S(1)}, u32[]{:S(2)}, u32[]{:S(2)}) collective-permute-start(bf16[64,1536]{1,0:T(8,128)(2,1)S(1)} %select_convert_fusion.3), channel_id=1, source_target_pairs={{0,8},{8,0},{16,24},{24,16},{1,9},{9,1},{17,25},{25,17},{2,10},{10... | collective-permute-start | bytes 589832 | tf_op jit(solution)/shard_map/ppermute | solution.py:42
  63.3 15.0 %collective-permute-start.22 = (bf16[2,4,4,16,768]{4,3,0,1,2:T(8,128)(2,1)S(1)}, bf16[2,4,4,16,768]{4,3,0,1,2:T(8,128)(2,1)S(1)}, u32[]{:S(2)}, u32[]{:S(2)}) collective-permute-start(bf16[2,4,4,16,768]{4,3,0,1,2:T(8,128)(2,1)S(1)} %pad_maximum_fusion.4), channel_id=1, source_target_pairs={{0,1},{1,0},{2,3},{3,2},{4,5},{5,4},{6,7},{7,6},{8,9},{9,8},{10,11... | collective-permute-start | bytes 2359304 | tf_op jit(solution)/shard_map/ppermute | solution.py:42
  66.6 9.4 %collective-permute-start.16 = (bf16[2,64,1536]{2,1,0:T(8,128)(2,1)S(1)}, bf16[2,64,1536]{2,1,0:T(8,128)(2,1)S(1)}, u32[]{:S(2)}, u32[]{:S(2)}) collective-permute-start(bf16[2,64,1536]{2,1,0:T(8,128)(2,1)S(1)} %pad_maximum_fusion.11), channel_id=1, source_target_pairs={{0,8},{8,0},{16,24},{24,16},{1,9},{9,1},{17,25},{25,17},{2,10},{10... | collective-permute-start | bytes 1179656 | tf_op jit(solution)/shard_map/ppermute | solution.py:42
  68.5 8.2 %copy-start.1 = (bf16[1536,768]{1,0:T(8,128)(2,1)S(1)}, bf16[1536,768]{1,0:T(8,128)(2,1)}, u32[]{:S(2)}) copy-start(bf16[1536,768]{1,0:T(8,128)(2,1)} %param.11) | copy-start | bytes 7077892
  68.5 8.0 %collective-permute-start.17 = (bf16[2,64,1536]{2,1,0:T(8,128)(2,1)S(1)}, bf16[2,64,1536]{2,1,0:T(8,128)(2,1)S(1)}, u32[]{:S(2)}, u32[]{:S(2)}) collective-permute-start(bf16[2,64,1536]{2,1,0:T(8,128)(2,1)S(1)} %pad_maximum_fusion.13), channel_id=1, source_target_pairs={{0,16},{8,24},{16,0},{24,8},{1,17},{9,25},{17,1},{25,9},{2,18},{10... | collective-permute-start | bytes 1179656 | tf_op jit(solution)/shard_map/ppermute | solution.py:42
  78.2 13.6 %collective-permute-start.18 = (bf16[4,4,16,768]{3,2,1,0:T(8,128)(2,1)S(1)}, bf16[4,4,16,768]{3,2,1,0:T(8,128)(2,1)S(1)}, u32[]{:S(2)}, u32[]{:S(2)}) collective-permute-start(bf16[4,4,16,768]{3,2,1,0:T(8,128)(2,1)S(1)} %fusion.40), channel_id=1, source_target_pairs={{0,1},{1,0},{2,3},{3,2},{4,5},{5,4},{6,7},{7,6},{8,9},{9,8},{10,11... | collective-permute-start | bytes 1179656 | tf_op jit(solution)/shard_map/ppermute | solution.py:42
  88.0 20.3 %collective-permute-start.23 = (bf16[2,2,64,1536]{3,2,1,0:T(8,128)(2,1)S(1)}, bf16[2,2,64,1536]{3,2,1,0:T(8,128)(2,1)S(1)}, u32[]{:S(2)}, u32[]{:S(2)}) collective-permute-start(bf16[2,2,64,1536]{3,2,1,0:T(8,128)(2,1)S(1)} %pad_maximum_fusion.5), channel_id=1, source_target_pairs={{0,16},{8,24},{16,0},{24,8},{1,17},{9,25},{17,1},{25,9},{2,18},{10... | collective-permute-start | bytes 2359304 | tf_op jit(solution)/shard_map/ppermute | solution.py:42
  90.2 19.9 %collective-permute-start.25 = (bf16[2,2,64,1536]{3,2,1,0:T(8,128)(2,1)S(1)}, bf16[2,2,64,1536]{3,2,1,0:T(8,128)(2,1)S(1)}, u32[]{:S(2)}, u32[]{:S(2)}) collective-permute-start(bf16[2,2,64,1536]{3,2,1,0:T(8,128)(2,1)S(1)} %pad_maximum_fusion.6), channel_id=1, source_target_pairs={{0,8},{8,0},{16,24},{24,16},{1,9},{9,1},{17,25},{25,17},{2,10},{10... | collective-permute-start | bytes 2359304 | tf_op jit(solution)/shard_map/ppermute | solution.py:42
  91.9 7.6 %collective-permute-start.21 = (bf16[4,16,768]{2,1,0:T(8,128)(2,1)S(1)}, bf16[4,16,768]{2,1,0:T(8,128)(2,1)S(1)}, u32[]{:S(2)}, u32[]{:S(2)}) collective-permute-start(bf16[4,16,768]{2,1,0:T(8,128)(2,1)S(1)} %get-tuple-element.34), channel_id=1, source_target_pairs={{0,2},{1,3},{2,4},{3,5},{4,6},{5,7},{6,0},{7,1},{8,10},{9,11},{10,... | collective-permute-start | bytes 294920 | tf_op jit(solution)/shard_map/ppermute | solution.py:42
  92.4 10.6 %collective-permute-start.20 = (bf16[4,16,768]{2,1,0:T(8,128)(2,1)S(1)}, bf16[4,16,768]{2,1,0:T(8,128)(2,1)S(1)}, u32[]{:S(2)}, u32[]{:S(2)}) collective-permute-start(bf16[4,16,768]{2,1,0:T(8,128)(2,1)S(1)} %get-tuple-element.35), channel_id=1, source_target_pairs={{0,4},{1,5},{2,6},{3,7},{4,0},{5,1},{6,2},{7,3},{8,12},{9,13},{10,... | collective-permute-start | bytes 294920 | tf_op jit(solution)/shard_map/ppermute | solution.py:42
  94.5 8.5 %collective-permute-start.19 = (bf16[4,16,768]{2,1,0:T(8,128)(2,1)S(1)}, bf16[4,16,768]{2,1,0:T(8,128)(2,1)S(1)}, u32[]{:S(2)}, u32[]{:S(2)}) collective-permute-start(bf16[4,16,768]{2,1,0:T(8,128)(2,1)S(1)} %get-tuple-element.33), channel_id=1, source_target_pairs={{0,6},{1,7},{2,0},{3,1},{4,2},{5,3},{6,4},{7,5},{8,14},{9,15},{10,... | collective-permute-start | bytes 294920 | tf_op jit(solution)/shard_map/ppermute | solution.py:42
  108.3 11.0 %collective-permute-start.24 = (bf16[2,64,1536]{2,1,0:T(8,128)(2,1)S(1)}, bf16[2,64,1536]{2,1,0:T(8,128)(2,1)S(1)}, u32[]{:S(2)}, u32[]{:S(2)}) collective-permute-start(bf16[2,64,1536]{2,1,0:T(8,128)(2,1)S(1)} %fusion.27), channel_id=1, source_target_pairs={{0,8},{8,0},{16,24},{24,16},{1,9},{9,1},{17,25},{25,17},{2,10},{10... | collective-permute-start | bytes 1179656 | tf_op jit(solution)/shard_map/ppermute | solution.py:42
  110.2 10.5 %collective-permute-start.26 = (bf16[2,64,1536]{2,1,0:T(8,128)(2,1)S(1)}, bf16[2,64,1536]{2,1,0:T(8,128)(2,1)S(1)}, u32[]{:S(2)}, u32[]{:S(2)}) collective-permute-start(bf16[2,64,1536]{2,1,0:T(8,128)(2,1)S(1)} %fusion.29), channel_id=1, source_target_pairs={{0,16},{8,24},{16,0},{24,8},{1,17},{9,25},{17,1},{25,9},{2,18},{10... | collective-permute-start | bytes 1179656 | tf_op jit(solution)/shard_map/ppermute | solution.py:42
  121.4 5.7 %collective-permute-start.28 = (bf16[64,1536]{1,0:T(8,128)(2,1)S(1)}, bf16[64,1536]{1,0:T(8,128)(2,1)S(1)}, u32[]{:S(2)}, u32[]{:S(2)}) collective-permute-start(bf16[64,1536]{1,0:T(8,128)(2,1)S(1)} %fusion.51), channel_id=1, source_target_pairs={{0,16},{8,24},{16,0},{24,8},{1,17},{9,25},{17,1},{25,9},{2,18},{10... | collective-permute-start | bytes 589832 | tf_op jit(solution)/shard_map/ppermute | solution.py:42
  122.0 6.2 %collective-permute-start.27 = (bf16[64,1536]{1,0:T(8,128)(2,1)S(1)}, bf16[64,1536]{1,0:T(8,128)(2,1)S(1)}, u32[]{:S(2)}, u32[]{:S(2)}) collective-permute-start(bf16[64,1536]{1,0:T(8,128)(2,1)S(1)} %fusion.53), channel_id=1, source_target_pairs={{0,8},{8,0},{16,24},{24,16},{1,9},{9,1},{17,25},{25,17},{2,10},{10... | collective-permute-start | bytes 589832 | tf_op jit(solution)/shard_map/ppermute | solution.py:42
  127.2 9.0 %collective-permute-start.29 = (bf16[2,64,1536]{2,1,0:T(8,128)(2,1)S(1)}, bf16[2,64,1536]{2,1,0:T(8,128)(2,1)S(1)}, u32[]{:S(2)}, u32[]{:S(2)}) collective-permute-start(bf16[2,64,1536]{2,1,0:T(8,128)(2,1)S(1)} %pad_maximum_fusion.16), channel_id=1, source_target_pairs={{0,8},{8,0},{16,24},{24,16},{1,9},{9,1},{17,25},{25,17},{2,10},{10... | collective-permute-start | bytes 1179656 | tf_op jit(solution)/shard_map/ppermute | solution.py:42
  128.3 8.3 %collective-permute-start.30 = (bf16[2,64,1536]{2,1,0:T(8,128)(2,1)S(1)}, bf16[2,64,1536]{2,1,0:T(8,128)(2,1)S(1)}, u32[]{:S(2)}, u32[]{:S(2)}) collective-permute-start(bf16[2,64,1536]{2,1,0:T(8,128)(2,1)S(1)} %pad_maximum_fusion.17), channel_id=1, source_target_pairs={{0,16},{8,24},{16,0},{24,8},{1,17},{9,25},{17,1},{25,9},{2,18},{10... | collective-permute-start | bytes 1179656 | tf_op jit(solution)/shard_map/ppermute | solution.py:42
  138.3 2.8 %collective-permute-start.31 = (bf16[4,4,16,768]{3,2,0,1:T(8,128)(2,1)S(1)}, bf16[4,4,16,768]{3,2,0,1:T(8,128)(2,1)S(1)}, u32[]{:S(2)}, u32[]{:S(2)}) collective-permute-start(bf16[4,4,16,768]{3,2,0,1:T(8,128)(2,1)S(1)} %fusion.41), channel_id=1, source_target_pairs={{0,1},{1,0},{2,3},{3,2},{4,5},{5,4},{6,7},{7,6},{8,9},{9,8},{10,11... | collective-permute-start | bytes 1179656 | tf_op jit(solution)/shard_map/ppermute | solution.py:42
  138.7 8.1 %collective-permute-start.39 = (bf16[64,1536]{1,0:T(8,128)(2,1)S(1)}, bf16[64,1536]{1,0:T(8,128)(2,1)S(1)}, u32[]{:S(2)}, u32[]{:S(2)}) collective-permute-start(bf16[64,1536]{1,0:T(8,128)(2,1)S(1)} %select_convert_fusion), channel_id=1, source_target_pairs={{0,16},{8,24},{16,0},{24,8},{1,17},{9,25},{17,1},{25,9},{2,18},{10... | collective-permute-start | bytes 589832 | tf_op jit(solution)/shard_map/ppermute | solution.py:42
  141.1 15.0 %collective-permute-start.38 = (bf16[64,1536]{1,0:T(8,128)(2,1)S(1)}, bf16[64,1536]{1,0:T(8,128)(2,1)S(1)}, u32[]{:S(2)}, u32[]{:S(2)}) collective-permute-start(bf16[64,1536]{1,0:T(8,128)(2,1)S(1)} %select_convert_fusion.1), channel_id=1, source_target_pairs={{0,8},{8,0},{16,24},{24,16},{1,9},{9,1},{17,25},{25,17},{2,10},{10... | collective-permute-start | bytes 589832 | tf_op jit(solution)/shard_map/ppermute | solution.py:42
  141.3 8.3 %collective-permute-start.34 = (bf16[4,16,768]{2,1,0:T(8,128)(2,1)S(1)}, bf16[4,16,768]{2,1,0:T(8,128)(2,1)S(1)}, u32[]{:S(2)}, u32[]{:S(2)}) collective-permute-start(bf16[4,16,768]{2,1,0:T(8,128)(2,1)S(1)} %get-tuple-element.37), channel_id=1, source_target_pairs={{0,2},{1,3},{2,4},{3,5},{4,6},{5,7},{6,0},{7,1},{8,10},{9,11},{10,... | collective-permute-start | bytes 294920 | tf_op jit(solution)/shard_map/ppermute | solution.py:42
  141.9 10.5 %collective-permute-start.33 = (bf16[4,16,768]{2,1,0:T(8,128)(2,1)S(1)}, bf16[4,16,768]{2,1,0:T(8,128)(2,1)S(1)}, u32[]{:S(2)}, u32[]{:S(2)}) collective-permute-start(bf16[4,16,768]{2,1,0:T(8,128)(2,1)S(1)} %get-tuple-element.38), channel_id=1, source_target_pairs={{0,4},{1,5},{2,6},{3,7},{4,0},{5,1},{6,2},{7,3},{8,12},{9,13},{10,... | collective-permute-start | bytes 294920 | tf_op jit(solution)/shard_map/ppermute | solution.py:42
  144.0 8.4 %collective-permute-start.32 = (bf16[4,16,768]{2,1,0:T(8,128)(2,1)S(1)}, bf16[4,16,768]{2,1,0:T(8,128)(2,1)S(1)}, u32[]{:S(2)}, u32[]{:S(2)}) collective-permute-start(bf16[4,16,768]{2,1,0:T(8,128)(2,1)S(1)} %get-tuple-element.36), channel_id=1, source_target_pairs={{0,6},{1,7},{2,0},{3,1},{4,2},{5,3},{6,4},{7,5},{8,14},{9,15},{10,... | collective-permute-start | bytes 294920 | tf_op jit(solution)/shard_map/ppermute | solution.py:42
  146.8 15.1 %copy-start.2 = (bf16[64,1536]{1,0:T(8,128)(2,1)}, bf16[64,1536]{1,0:T(8,128)(2,1)S(1)}, u32[]{:S(2)}) copy-start(bf16[64,1536]{1,0:T(8,128)(2,1)S(1)} %collective-permute-done.39) | copy-start | bytes 589828
  147.6 19.8 %collective-permute-start.40 = (bf16[2,64,1536]{2,1,0:T(8,128)(2,1)}, bf16[2,64,1536]{2,1,0:T(8,128)(2,1)}, u32[]{:S(2)}, u32[]{:S(2)}) collective-permute-start(bf16[2,64,1536]{2,1,0:T(8,128)(2,1)} %pad_maximum_fusion.18), channel_id=1, source_target_pairs={{0,8},{8,0},{16,24},{24,16},{1,9},{9,1},{17,25},{25,17},{2,10},{10... | collective-permute-start | bytes 1179656 | tf_op jit(solution)/shard_map/ppermute | solution.py:42
  152.5 8.5 %collective-permute-start.37 = (bf16[2,16,768]{2,1,0:T(8,128)(2,1)S(1)}, bf16[2,16,768]{2,1,0:T(8,128)(2,1)S(1)}, u32[]{:S(2)}, u32[]{:S(2)}) collective-permute-start(bf16[2,16,768]{2,1,0:T(8,128)(2,1)S(1)} %get-tuple-element.53), channel_id=1, source_target_pairs={{0,24},{8,16},{16,8},{24,0},{1,25},{9,17},{17,9},{25,1},{2,26},{10... | collective-permute-start | bytes 147464 | tf_op jit(solution)/shard_map/ppermute | solution.py:42
  154.0 7.0 %collective-permute-start.36 = (bf16[2,16,768]{2,1,0:T(8,128)(2,1)S(1)}, bf16[2,16,768]{2,1,0:T(8,128)(2,1)S(1)}, u32[]{:S(2)}, u32[]{:S(2)}) collective-permute-start(bf16[2,16,768]{2,1,0:T(8,128)(2,1)S(1)} %get-tuple-element.54), channel_id=1, source_target_pairs={{0,16},{8,24},{16,0},{24,8},{1,17},{9,25},{17,1},{25,9},{2,18},{10... | collective-permute-start | bytes 147464 | tf_op jit(solution)/shard_map/ppermute | solution.py:42
  155.8 5.3 %collective-permute-start.35 = (bf16[2,16,768]{2,1,0:T(8,128)(2,1)S(1)}, bf16[2,16,768]{2,1,0:T(8,128)(2,1)S(1)}, u32[]{:S(2)}, u32[]{:S(2)}) collective-permute-start(bf16[2,16,768]{2,1,0:T(8,128)(2,1)S(1)} %get-tuple-element.52), channel_id=1, source_target_pairs={{0,8},{8,0},{16,24},{24,16},{1,9},{9,1},{17,25},{25,17},{2,10},{10... | collective-permute-start | bytes 147464 | tf_op jit(solution)/shard_map/ppermute | solution.py:42
  156.1 5.9 %copy-start.4 = (bf16[64,1536]{1,0:T(8,128)(2,1)}, bf16[64,1536]{1,0:T(8,128)(2,1)S(1)}, u32[]{:S(2)}) copy-start(bf16[64,1536]{1,0:T(8,128)(2,1)S(1)} %collective-permute-done.38) | copy-start | bytes 589828
  156.9 11.6 %collective-permute-start.41 = (bf16[2,64,1536]{2,1,0:T(8,128)(2,1)}, bf16[2,64,1536]{2,1,0:T(8,128)(2,1)}, u32[]{:S(2)}, u32[]{:S(2)}) collective-permute-start(bf16[2,64,1536]{2,1,0:T(8,128)(2,1)} %pad_maximum_fusion.19), channel_id=1, source_target_pairs={{0,16},{8,24},{16,0},{24,8},{1,17},{9,25},{17,1},{25,9},{2,18},{10... | collective-permute-start | bytes 1179656 | tf_op jit(solution)/shard_map/ppermute | solution.py:42
  167.4 2.2 %copy-start.3 = (bf16[64,1536]{1,0:T(8,128)(2,1)S(1)}, bf16[64,1536]{1,0:T(8,128)(2,1)}, u32[]{:S(2)}) copy-start(bf16[64,1536]{1,0:T(8,128)(2,1)} %copy-done.2) | copy-start | bytes 589828
  167.4 2.3 %copy-start.5 = (bf16[64,1536]{1,0:T(8,128)(2,1)S(1)}, bf16[64,1536]{1,0:T(8,128)(2,1)}, u32[]{:S(2)}) copy-start(bf16[64,1536]{1,0:T(8,128)(2,1)} %copy-done.4) | copy-start | bytes 589828

commit v7 on v5

--- a/solution.py
+++ b/solution.py
@@ -54,22 +54,28 @@
     return value.astype(jnp.bfloat16)
 
 
-def sum_to_owner(part, grid, first):
-    second = 1 - first
-    n1, n2 = grid[first], grid[second]
-
-    def slot(i, j):
-        return (i, j) if first == 0 else (j, i)
-
-    arrived = [
+def slot_of(i, j, first):
+    return (i, j) if first == 0 else (j, i)
+
+
+def sum_first(part, grid, first):
+    n1, n2 = grid[first], grid[1 - first]
+    return [
         shift(
-            half(jnp.stack([part(slot(i, j)) for j in range(n2)])), grid, axis_step(first, -i)
+            half(jnp.stack([part(slot_of(i, j, first)) for j in range(n2)])),
+            grid,
+            axis_step(first, -i),
         )
         for i in range(1, n1)
     ]
+
+
+def sum_second(part, arrived, grid, first):
+    second = 1 - first
+    n2 = grid[second]
     sums = []
     for j in list(range(1, n2)) + [0]:
-        total = part(slot(0, j))
+        total = part(slot_of(0, j, first))
         for piece in arrived:
             total = total + piece[j].astype(jnp.float32)
         sums.append(total if j == 0 else shift(half(total), grid, axis_step(second, -j)))
@@ -129,7 +135,7 @@
         return both.reshape(-1, dp_count, tensor_count * own_rows, own_cols)
 
     (tok_cols,) = from_cores(from_chips(jnp.stack([p[:1] for p in pieces], axis=1)))
-    later = from_chips(after(jnp.stack([p[1:] for p in pieces], axis=1), tok_cols))
+    later = jnp.stack([p[1:] for p in pieces], axis=1)
     group_rows = tok_cols.shape[1]
     cut = group_rows // 2
     halves = [(0, slice(0, cut)), (1, slice(cut, group_rows))]
@@ -142,15 +148,17 @@
             rows, w_out, (((1,), (1,)), ((), ())), preferred_element_type=jnp.float32
         )
 
-    def sums(terms):
+    def parts(terms):
         return [
-            sum_to_owner(
-                lambda s, r=rows: jnp.stack([f(cols[place[s], r]) for f, cols in terms]),
-                grid,
-                first,
-            )
+            (lambda s, r=rows: jnp.stack([f(cols[place[s], r]) for f, cols in terms]), grid, first)
             for first, rows in halves
         ]
+
+    def sums_first(terms):
+        return [sum_first(*p) for p in parts(terms)]
+
+    def sums_second(terms, arrived):
+        return [sum_second(p[0], a, *p[1:]) for p, a in zip(parts(terms), arrived)]
 
     back_hi = (at_hi - jnp.arange(pod[0], dtype=jnp.int32)) % pod[0]
     back_lo = (at_lo - jnp.arange(pod[1], dtype=jnp.int32)) % pod[1]
@@ -182,19 +190,25 @@
             total = total + shift(half(near[:, i]), pod, (-i, 0), "tensor").astype(jnp.float32)
         return half(total)
 
-    pre_act = [p[0] for p in sums([(up, tok_cols)])]
+    arrived = sums_first([(up, tok_cols)])
+    arrived, later = lax.optimization_barrier((arrived, later))
+    later = from_chips(later)
+    pre_act = [p[0] for p in sums_second([(up, tok_cols)], arrived)]
     pairs = [gelu_pair(p) for p in pre_act]
     act_held = spread([a for a, _ in pairs])
     later = from_cores(after(later, pre_act))
     tan_cols, cot_cols = after(later, act_held)
     act_all = everywhere(act_held)
-    both = sums([(up, tan_cols), (back, cot_cols)])
+    terms = [(up, tan_cols), (back, cot_cols)]
+    both = sums_second(terms, sums_first(terms))
     out_near = down_cores(act_all)
     both = after(both, out_near)
     dact_held = spread([s * v[0] for (_, s), v in zip(pairs, both)])
     dact_all = everywhere(dact_held)
     back_grad = after([v[1] for v in both], dact_held)
-    grad_all = everywhere(spread([s * v for (_, s), v in zip(pairs, back_grad)]))
+    grad_held = spread([s * v for (_, s), v in zip(pairs, back_grad)])
+    dact_all, grad_held = lax.optimization_barrier((dact_all, grad_held))
+    grad_all = everywhere(grad_held)
     summed = jnp.stack([down_chips(out_near), down_chips(down_cores(dact_all))], axis=1)
     cols = jnp.stack(
         [shift(summed[place[(i, j)]], grid, (-i, -j)) for i, j in slots]

time: 160 us -> 164 us (1.025)
  waiting for transfers between devices: 70 us -> 74.8 us
  matrix products: 25.4 us -> 21.7 us
  starting transfers between devices: 48.1 us -> 50.2 us
  local copies, waits for them, and re-layouts: 5.73 us -> 7.54 us
    ppermute x42, waiting for transfers between devices: 70 us -> 74.8 us  [shift(): return lax.ppermute(value, axis, pairs)]
    dot_general x18, matrix products: 15.2 us -> 11.5 us  [dot(): return jnp.dot(a, b, preferred_element_type=jnp.float32)]
    ppermute x42, starting transfers between devices: 48.1 us -> 50.2 us  [shift(): return lax.ppermute(value, axis, pairs)]
  transfers between devices with their start and end apart: 42 -> 42, of which waited for: 24 -> 21; matrix products, arithmetic and copies ran while one was open for 20% -> 16% of each run, Pallas kernels for 0% -> 0%
where the time goes in v7:
time: 164 us; the launch traced here: 163 us
  waiting for transfers between devices  74.8 us (46%)
  starting transfers between devices  50.2 us (31%)
  matrix products  21.7 us (13%)
  other arithmetic  7.59 us (5%)
  local copies, waits for them, and re-layouts  7.54 us (5%)
    ppermute x42, waiting for transfers between devices, shift(): return lax.ppermute(value, axis, pairs)  74.8 us
    ppermute x42, starting transfers between devices, shift(): return lax.ppermute(value, axis, pairs)  50.2 us
    dot_general x18, matrix products, dot(): return jnp.dot(a, b, preferred_element_type=jnp.float32)  11.5 us
    dot_general x8, matrix products, back(): lax.dot_general(rows, w_out, (((1,), (1,)), ((), ())), preferred_element_...  6.65 us
    dot_general x1, matrix products, local(): lax.dot_general(tok_cols.reshape(dp_count * group_rows, own_cols), grad_a...  3.6 us
  transfers between devices with their start and end apart: 42, of which 21 were waited for; matrix products, arithmetic and copies ran while one was open for 16% of the time, Pallas kernels for 0%

profile of v7, /device:TPU:0, one launch (start us, length us, event | category | flops | bytes accessed | tf_op | source)
XLA Modules:
  0.0 163.3 jit_solution(11282924872763573576)
XLA Ops:
  0.7 0.9 dynamic-slice_bitcast_fusion.11
  1.7 1.5 dynamic-slice_bitcast_fusion
  3.2 4.0 %collective-permute-start.2 = (bf16[3,16,768]{2,1,0:T(8,128)(2,1)S(1)}, bf16[3,16,768]{2,1,0:T(8,128)(2,1)S(1)}, u32[]{:S(2)}, u32[]{:S(2)}) collective-permute-start(bf16[3,16,768]{2,1,0:T(8,128)(2,1)S(1)} %pad_maximum_fusion.25), channel_id=1, source_target_pairs={{0,24},{8,16},{16,8},{24,0},{1,25},{9,17},{17,9},{25,1},{2,26},{10... | collective-permute-start | bytes 221192 | tf_op jit(solution)/shard_map/ppermute | solution.py:42
  8.1 1.4 collective-permute-done.2
  9.5 0.6 copy-done.6
  10.1 1.5 collective-permute-done.1
  11.6 0.6 copy-done.2
  12.2 0.6 copy-done.4
  12.9 3.7 %collective-permute-start.5 = (bf16[1,4,16,768]{3,2,1,0:T(8,128)(2,1)S(1)}, bf16[1,4,16,768]{3,2,1,0:T(8,128)(2,1)S(1)}, u32[]{:S(2)}, u32[]{:S(2)}) collective-permute-start(bf16[1,4,16,768]{3,2,1,0:T(8,128)(2,1)S(1)} %get-tuple-element.76), channel_id=1, source_target_pairs={{0,6},{1,7},{2,0},{3,1},{4,2},{5,3},{6,4},{7,5},{8,14},{9,15},{10,... | collective-permute-start | bytes 294920 | tf_op jit(solution)/shard_map/ppermute | solution.py:42
  16.5 1.0 collective-permute-start.3
  17.6 1.3 fusion.89
  18.9 0.9 collective-permute-done.5
  19.8 5.1 %collective-permute-done.4 = bf16[1,4,16,768]{3,2,1,0:T(8,128)(2,1)S(1)} collective-permute-done((bf16[1,4,16,768]{3,2,1,0:T(8,128)(2,1)S(1)}, bf16[1,4,16,768]{3,2,1,0:T(8,128)(2,1)S(1)}, u32[]{:S(2)}, u32[]{:S(2)}) %collective-permute-start.4) | collective-permute-done | bytes 98336 | tf_op jit(solution)/shard_map/ppermute | solution.py:42
  25.0 0.6 slice_compare_fusion
  25.9 0.8 maximum_bitcast_fusion.12
  26.6 0.8 slice_bitcast_fusion.82
  29.7 1.5 collective-permute-start.7
  31.9 9.4 %collective-permute-done.7 = bf16[2,1,64,1536]{3,2,1,0:T(8,128)(2,1)S(1)} collective-permute-done((bf16[2,1,64,1536]{3,2,1,0:T(8,128)(2,1)S(1)}, bf16[2,1,64,1536]{3,2,1,0:T(8,128)(2,1)S(1)}, u32[]{:S(2)}, u32[]{:S(2)}) %collective-permute-start.7) | collective-permute-done | bytes 393248 | tf_op jit(solution)/shard_map/ppermute | solution.py:42
  41.3 1.3 collective-permute-done.8
  42.6 1.8 %collective-permute-start.21 = (bf16[2,4,16,768]{3,2,0,1:T(8,128)(2,1)S(1)}, bf16[2,4,16,768]{3,2,0,1:T(8,128)(2,1)S(1)}, u32[]{:S(2)}, u32[]{:S(2)}) collective-permute-start(bf16[2,4,16,768]{3,2,0,1:T(8,128)(2,1)S(1)} %pad_maximum_fusion.20), channel_id=1, source_target_pairs={{0,6},{1,7},{2,0},{3,1},{4,2},{5,3},{6,4},{7,5},{8,14},{9,15},{10,... | collective-permute-start | bytes 589832 | tf_op jit(solution)/shard_map/ppermute | solution.py:42
  44.7 2.0 %collective-permute-start.19 = (bf16[2,4,16,768]{3,2,0,1:T(8,128)(2,1)S(1)}, bf16[2,4,16,768]{3,2,0,1:T(8,128)(2,1)S(1)}, u32[]{:S(2)}, u32[]{:S(2)}) collective-permute-start(bf16[2,4,16,768]{3,2,0,1:T(8,128)(2,1)S(1)} %pad_maximum_fusion.20), channel_id=1, source_target_pairs={{0,2},{1,3},{2,4},{3,5},{4,6},{5,7},{6,0},{7,1},{8,10},{9,11},{10,... | collective-permute-start | bytes 589832 | tf_op jit(solution)/shard_map/ppermute | solution.py:42
  48.2 1.8 %collective-permute-start.9 = (bf16[1,64,1536]{2,1,0:T(8,128)(2,1)S(1)}, bf16[1,64,1536]{2,1,0:T(8,128)(2,1)S(1)}, u32[]{:S(2)}, u32[]{:S(2)}) collective-permute-start(bf16[1,64,1536]{2,1,0:T(8,128)(2,1)S(1)} %fusion.21), channel_id=1, source_target_pairs={{0,8},{8,0},{16,24},{24,16},{1,9},{9,1},{17,25},{25,17},{2,10},{10... | collective-permute-start | bytes 589832 | tf_op jit(solution)/shard_map/ppermute | solution.py:42
  49.9 3.1 %collective-permute-done.10 = bf16[1,64,1536]{2,1,0:T(8,128)(2,1)S(1)} collective-permute-done((bf16[1,64,1536]{2,1,0:T(8,128)(2,1)S(1)}, bf16[1,64,1536]{2,1,0:T(8,128)(2,1)S(1)}, u32[]{:S(2)}, u32[]{:S(2)}) %collective-permute-start.10) | collective-permute-done | bytes 196640 | tf_op jit(solution)/shard_map/ppermute | solution.py:42
  54.7 1.8 %collective-permute-start.11 = (bf16[64,1536]{1,0:T(8,128)(2,1)S(1)}, bf16[64,1536]{1,0:T(8,128)(2,1)S(1)}, u32[]{:S(2)}, u32[]{:S(2)}) collective-permute-start(bf16[64,1536]{1,0:T(8,128)(2,1)S(1)} %get-tuple-element.85), channel_id=1, source_target_pairs={{0,8},{8,0},{16,24},{24,16},{1,9},{9,1},{17,25},{25,17},{2,10},{10... | collective-permute-start | bytes 589832 | tf_op jit(solution)/shard_map/ppermute | solution.py:42
  56.7 5.1 %collective-permute-done.20 = bf16[2,4,16,768]{3,2,0,1:T(8,128)(2,1)S(1)} collective-permute-done((bf16[2,4,16,768]{3,2,0,1:T(8,128)(2,1)S(1)}, bf16[2,4,16,768]{3,2,0,1:T(8,128)(2,1)S(1)}, u32[]{:S(2)}, u32[]{:S(2)}) %collective-permute-start.20) | collective-permute-done | bytes 196640 | tf_op jit(solution)/shard_map/ppermute | solution.py:42
  62.1 0.6 collective-permute-start.13
  62.8 1.5 collective-permute-start.14
  64.3 9.3 %collective-permute-done.13 = bf16[2,64,1536]{2,1,0:T(8,128)(2,1)S(1)} collective-permute-done((bf16[2,64,1536]{2,1,0:T(8,128)(2,1)S(1)}, bf16[2,64,1536]{2,1,0:T(8,128)(2,1)S(1)}, u32[]{:S(2)}, u32[]{:S(2)}) %collective-permute-start.13) | collective-permute-done | bytes 393248 | tf_op jit(solution)/shard_map/ppermute | solution.py:42
  74.2 1.4 fusion
  76.2 0.8 convolution_bitcast_fusion.6
  77.0 0.8 convolution_bitcast_fusion.4
  78.9 0.8 fusion.15
  80.3 0.8 fusion.13
  81.7 0.8 convolution_bitcast_fusion.2
  82.5 0.8 fusion.19
  83.9 0.8 fusion.17
  85.4 1.5 collective-permute-start.23
  88.3 0.8 convolution_bitcast_fusion
  89.8 2.0 %collective-permute-start.17 = (bf16[4,16,768]{2,1,0:T(8,128)(2,1)S(1)}, bf16[4,16,768]{2,1,0:T(8,128)(2,1)S(1)}, u32[]{:S(2)}, u32[]{:S(2)}) collective-permute-start(bf16[4,16,768]{2,1,0:T(8,128)(2,1)S(1)} %get-tuple-element.47), channel_id=1, source_target_pairs={{0,4},{1,5},{2,6},{3,7},{4,0},{5,1},{6,2},{7,3},{8,12},{9,13},{10,... | collective-permute-start | bytes 294920 | tf_op jit(solution)/shard_map/ppermute | solution.py:42
  91.8 2.8 %collective-permute-start.16 = (bf16[4,16,768]{2,1,0:T(8,128)(2,1)S(1)}, bf16[4,16,768]{2,1,0:T(8,128)(2,1)S(1)}, u32[]{:S(2)}, u32[]{:S(2)}) collective-permute-start(bf16[4,16,768]{2,1,0:T(8,128)(2,1)S(1)} %get-tuple-element.45), channel_id=1, source_target_pairs={{0,6},{1,7},{2,0},{3,1},{4,2},{5,3},{6,4},{7,5},{8,14},{9,15},{10,... | collective-permute-start | bytes 294920 | tf_op jit(solution)/shard_map/ppermute | solution.py:42
  95.1 1.7 %collective-permute-done.18 = bf16[4,16,768]{2,1,0:T(8,128)(2,1)S(1)} collective-permute-done((bf16[4,16,768]{2,1,0:T(8,128)(2,1)S(1)}, bf16[4,16,768]{2,1,0:T(8,128)(2,1)S(1)}, u32[]{:S(2)}, u32[]{:S(2)}) %collective-permute-start.18) | collective-permute-done | bytes 98336 | tf_op jit(solution)/shard_map/ppermute | solution.py:42
  96.8 3.3 %collective-permute-done.17 = bf16[4,16,768]{2,1,0:T(8,128)(2,1)S(1)} collective-permute-done((bf16[4,16,768]{2,1,0:T(8,128)(2,1)S(1)}, bf16[4,16,768]{2,1,0:T(8,128)(2,1)S(1)}, u32[]{:S(2)}, u32[]{:S(2)}) %collective-permute-start.17) | collective-permute-done | bytes 98336 | tf_op jit(solution)/shard_map/ppermute | solution.py:42
  100.1 5.3 %collective-permute-done.23 = bf16[2,2,64,1536]{3,2,1,0:T(8,128)(2,1)S(1)} collective-permute-done((bf16[2,2,64,1536]{3,2,1,0:T(8,128)(2,1)S(1)}, bf16[2,2,64,1536]{3,2,1,0:T(8,128)(2,1)S(1)}, u32[]{:S(2)}, u32[]{:S(2)}) %collective-permute-start.23) | collective-permute-done | bytes 786464 | tf_op jit(solution)/shard_map/ppermute | solution.py:42
  105.5 1.6 collective-permute-start.24
  107.7 8.6 %collective-permute-done.24 = bf16[2,64,1536]{2,1,0:T(8,128)(2,1)S(1)} collective-permute-done((bf16[2,64,1536]{2,1,0:T(8,128)(2,1)S(1)}, bf16[2,64,1536]{2,1,0:T(8,128)(2,1)S(1)}, u32[]{:S(2)}, u32[]{:S(2)}) %collective-permute-start.24) | collective-permute-done | bytes 393248 | tf_op jit(solution)/shard_map/ppermute | solution.py:42
  116.4 1.2 collective-permute-done.26
  119.5 1.5 collective-permute-start.27
  121.0 3.6 %collective-permute-done.28 = bf16[64,1536]{1,0:T(8,128)(2,1)S(1)} collective-permute-done((bf16[64,1536]{1,0:T(8,128)(2,1)S(1)}, bf16[64,1536]{1,0:T(8,128)(2,1)S(1)}, u32[]{:S(2)}, u32[]{:S(2)}) %collective-permute-start.28) | collective-permute-done | bytes 196640 | tf_op jit(solution)/shard_map/ppermute | solution.py:42
  125.6 2.6 %collective-permute-start.30 = (bf16[2,64,1536]{2,1,0:T(8,128)(2,1)S(1)}, bf16[2,64,1536]{2,1,0:T(8,128)(2,1)S(1)}, u32[]{:S(2)}, u32[]{:S(2)}) collective-permute-start(bf16[2,64,1536]{2,1,0:T(8,128)(2,1)S(1)} %pad_maximum_fusion.17), channel_id=1, source_target_pairs={{0,16},{8,24},{16,0},{24,8},{1,17},{9,25},{17,1},{25,9},{2,18},{10... | collective-permute-start | bytes 1179656 | tf_op jit(solution)/shard_map/ppermute | solution.py:42
  128.9 2.0 %collective-permute-start.32 = (bf16[64,1536]{1,0:T(8,128)(2,1)S(1)}, bf16[64,1536]{1,0:T(8,128)(2,1)S(1)}, u32[]{:S(2)}, u32[]{:S(2)}) collective-permute-start(bf16[64,1536]{1,0:T(8,128)(2,1)S(1)} %select_convert_fusion), channel_id=1, source_target_pairs={{0,16},{8,24},{16,0},{24,8},{1,17},{9,25},{17,1},{25,9},{2,18},{10... | collective-permute-start | bytes 589832 | tf_op jit(solution)/shard_map/ppermute | solution.py:42
  130.9 6.9 %collective-permute-done.31 = bf16[64,1536]{1,0:T(8,128)(2,1)S(1)} collective-permute-done((bf16[64,1536]{1,0:T(8,128)(2,1)S(1)}, bf16[64,1536]{1,0:T(8,128)(2,1)S(1)}, u32[]{:S(2)}, u32[]{:S(2)}) %collective-permute-start.31) | collective-permute-done | bytes 196640 | tf_op jit(solution)/shard_map/ppermute | solution.py:42
  138.3 1.6 collective-permute-start.40
  139.9 1.4 fusion.2
  141.4 0.6 collective-permute-start.41
  142.1 1.0 collective-permute-done.33
  143.8 2.0 %collective-permute-start.35 = (bf16[4,16,768]{2,1,0:T(8,128)(2,1)S(1)}, bf16[4,16,768]{2,1,0:T(8,128)(2,1)S(1)}, u32[]{:S(2)}, u32[]{:S(2)}) collective-permute-start(bf16[4,16,768]{2,1,0:T(8,128)(2,1)S(1)} %get-tuple-element.50), channel_id=1, source_target_pairs={{0,4},{1,5},{2,6},{3,7},{4,0},{5,1},{6,2},{7,3},{8,12},{9,13},{10,... | collective-permute-start | bytes 294920 | tf_op jit(solution)/shard_map/ppermute | solution.py:42
  145.8 2.8 %collective-permute-start.34 = (bf16[4,16,768]{2,1,0:T(8,128)(2,1)S(1)}, bf16[4,16,768]{2,1,0:T(8,128)(2,1)S(1)}, u32[]{:S(2)}, u32[]{:S(2)}) collective-permute-start(bf16[4,16,768]{2,1,0:T(8,128)(2,1)S(1)} %get-tuple-element.48), channel_id=1, source_target_pairs={{0,6},{1,7},{2,0},{3,1},{4,2},{5,3},{6,4},{7,5},{8,14},{9,15},{10,... | collective-permute-start | bytes 294920 | tf_op jit(solution)/shard_map/ppermute | solution.py:42
  148.7 4.3 %collective-permute-done.41 = bf16[2,64,1536]{2,1,0:T(8,128)(2,1)S(1)} collective-permute-done((bf16[2,64,1536]{2,1,0:T(8,128)(2,1)S(1)}, bf16[2,64,1536]{2,1,0:T(8,128)(2,1)S(1)}, u32[]{:S(2)}, u32[]{:S(2)}) %collective-permute-start.41) | collective-permute-done | bytes 393248 | tf_op jit(solution)/shard_map/ppermute | solution.py:42
  153.3 1.0 collective-permute-done.35
  154.4 1.5 collective-permute-start.39
  156.4 1.5 collective-permute-start.37
  157.9 3.6 %fusion.100 = f32[768,1536]{1,0:T(8,128)} fusion(bf16[512,768]{1,0:T(8,128)(2,1)S(1)} %bitcast.452, bf16[512,1536]{1,0:T(8,128)(2,1)S(1)} %bitcast.453), kind=kOutput, calls=%fused_computation.283 | convolution fusion | flops 1207959552 | bytes 7077888 | tf_op jit(solution)/shard_map/dot_general | solution.py:218
  161.9 0.7 unstack.29
  162.6 0.7 unstack.31
  (154 shorter events, 21.7 us)
Async XLA Ops:
  0.6 26.9 %copy-start = (bf16[768,1536]{1,0:T(8,128)(2,1)S(1)}, bf16[768,1536]{1,0:T(8,128)(2,1)}, u32[]{:S(2)}) copy-start(bf16[768,1536]{1,0:T(8,128)(2,1)} %param.10) | copy-start | bytes 7077892
  3.2 6.3 %collective-permute-start.2 = (bf16[3,16,768]{2,1,0:T(8,128)(2,1)S(1)}, bf16[3,16,768]{2,1,0:T(8,128)(2,1)S(1)}, u32[]{:S(2)}, u32[]{:S(2)}) collective-permute-start(bf16[3,16,768]{2,1,0:T(8,128)(2,1)S(1)} %pad_maximum_fusion.25), channel_id=1, source_target_pairs={{0,24},{8,16},{16,8},{24,0},{1,25},{9,17},{17,9},{25,1},{2,26},{10... | collective-permute-start | bytes 221192 | tf_op jit(solution)/shard_map/ppermute | solution.py:42
  7.2 4.4 %collective-permute-start.1 = (bf16[3,16,768]{2,1,0:T(8,128)(2,1)S(1)}, bf16[3,16,768]{2,1,0:T(8,128)(2,1)S(1)}, u32[]{:S(2)}, u32[]{:S(2)}) collective-permute-start(bf16[3,16,768]{2,1,0:T(8,128)(2,1)S(1)} %pad_maximum_fusion.24), channel_id=1, source_target_pairs={{0,16},{8,24},{16,0},{24,8},{1,17},{9,25},{17,1},{25,9},{2,18},{10... | collective-permute-start | bytes 221192 | tf_op jit(solution)/shard_map/ppermute | solution.py:42
  7.8 4.5 %collective-permute-start = (bf16[3,16,768]{2,1,0:T(8,128)(2,1)S(1)}, bf16[3,16,768]{2,1,0:T(8,128)(2,1)S(1)}, u32[]{:S(2)}, u32[]{:S(2)}) collective-permute-start(bf16[3,16,768]{2,1,0:T(8,128)(2,1)S(1)} %pad_maximum_fusion.23), channel_id=1, source_target_pairs={{0,8},{8,0},{16,24},{24,16},{1,9},{9,1},{17,25},{25,17},{2,10},{10... | collective-permute-start | bytes 221192 | tf_op jit(solution)/shard_map/ppermute | solution.py:42
  9.5 0.6 copy-start.6
  11.6 0.6 copy-start.2
  12.2 0.6 copy-start.4
  12.9 6.9 %collective-permute-start.5 = (bf16[1,4,16,768]{3,2,1,0:T(8,128)(2,1)S(1)}, bf16[1,4,16,768]{3,2,1,0:T(8,128)(2,1)S(1)}, u32[]{:S(2)}, u32[]{:S(2)}) collective-permute-start(bf16[1,4,16,768]{3,2,1,0:T(8,128)(2,1)S(1)} %get-tuple-element.76), channel_id=1, source_target_pairs={{0,6},{1,7},{2,0},{3,1},{4,2},{5,3},{6,4},{7,5},{8,14},{9,15},{10,... | collective-permute-start | bytes 294920 | tf_op jit(solution)/shard_map/ppermute | solution.py:42
  16.5 8.3 %collective-permute-start.4 = (bf16[1,4,16,768]{3,2,1,0:T(8,128)(2,1)S(1)}, bf16[1,4,16,768]{3,2,1,0:T(8,128)(2,1)S(1)}, u32[]{:S(2)}, u32[]{:S(2)}) collective-permute-start(bf16[1,4,16,768]{3,2,1,0:T(8,128)(2,1)S(1)} %get-tuple-element.76), channel_id=1, source_target_pairs={{0,4},{1,5},{2,6},{3,7},{4,0},{5,1},{6,2},{7,3},{8,12},{9,13},{10,... | collective-permute-start | bytes 294920 | tf_op jit(solution)/shard_map/ppermute | solution.py:42
  16.5 8.3 %collective-permute-start.3 = (bf16[1,4,16,768]{3,2,1,0:T(8,128)(2,1)S(1)}, bf16[1,4,16,768]{3,2,1,0:T(8,128)(2,1)S(1)}, u32[]{:S(2)}, u32[]{:S(2)}) collective-permute-start(bf16[1,4,16,768]{3,2,1,0:T(8,128)(2,1)S(1)} %get-tuple-element.76), channel_id=1, source_target_pairs={{0,2},{1,3},{2,4},{3,5},{4,6},{5,7},{6,0},{7,1},{8,10},{9,11},{10,... | collective-permute-start | bytes 294920 | tf_op jit(solution)/shard_map/ppermute | solution.py:42
  25.0 2.5 %collective-permute-start.6 = (bf16[1,4,4,16,768]{4,3,2,1,0:T(8,128)(2,1)S(1)}, bf16[1,4,4,16,768]{4,3,2,1,0:T(8,128)(2,1)S(1)}, u32[]{:S(2)}, u32[]{:S(2)}) collective-permute-start(bf16[1,4,4,16,768]{4,3,2,1,0:T(8,128)(2,1)S(1)} %get-tuple-element.60), channel_id=1, source_target_pairs={{0,1},{1,0},{2,3},{3,2},{4,5},{5,4},{6,7},{7,6},{8,9},{9,8},{10,11... | collective-permute-start | bytes 1179656 | tf_op jit(solution)/shard_map/ppermute | solution.py:42
  29.1 2.7 %copy-start.3 = (bf16[3,16,768]{2,1,0:T(8,128)(2,1)S(1)}, bf16[3,16,768]{2,1,0:T(8,128)(2,1)}, u32[]{:S(2)}) copy-start(bf16[3,16,768]{2,1,0:T(8,128)(2,1)} %copy-done.2) | copy-start | bytes 221188
  29.1 2.7 %copy-start.5 = (bf16[3,16,768]{2,1,0:T(8,128)(2,1)S(1)}, bf16[3,16,768]{2,1,0:T(8,128)(2,1)}, u32[]{:S(2)}) copy-start(bf16[3,16,768]{2,1,0:T(8,128)(2,1)} %copy-done.4) | copy-start | bytes 221188
  29.7 11.6 %collective-permute-start.7 = (bf16[2,1,64,1536]{3,2,1,0:T(8,128)(2,1)S(1)}, bf16[2,1,64,1536]{3,2,1,0:T(8,128)(2,1)S(1)}, u32[]{:S(2)}, u32[]{:S(2)}) collective-permute-start(bf16[2,1,64,1536]{3,2,1,0:T(8,128)(2,1)S(1)} %pad_maximum_fusion.8), channel_id=1, source_target_pairs={{0,16},{8,24},{16,0},{24,8},{1,17},{9,25},{17,1},{25,9},{2,18},{10... | collective-permute-start | bytes 1179656 | tf_op jit(solution)/shard_map/ppermute | solution.py:42
  31.3 11.3 %collective-permute-start.8 = (bf16[2,1,64,1536]{3,2,1,0:T(8,128)(2,1)S(1)}, bf16[2,1,64,1536]{3,2,1,0:T(8,128)(2,1)S(1)}, u32[]{:S(2)}, u32[]{:S(2)}) collective-permute-start(bf16[2,1,64,1536]{3,2,1,0:T(8,128)(2,1)S(1)} %pad_maximum_fusion.9), channel_id=1, source_target_pairs={{0,8},{8,0},{16,24},{24,16},{1,9},{9,1},{17,25},{25,17},{2,10},{10... | collective-permute-start | bytes 1179656 | tf_op jit(solution)/shard_map/ppermute | solution.py:42
  42.6 14.0 %collective-permute-start.21 = (bf16[2,4,16,768]{3,2,0,1:T(8,128)(2,1)S(1)}, bf16[2,4,16,768]{3,2,0,1:T(8,128)(2,1)S(1)}, u32[]{:S(2)}, u32[]{:S(2)}) collective-permute-start(bf16[2,4,16,768]{3,2,0,1:T(8,128)(2,1)S(1)} %pad_maximum_fusion.20), channel_id=1, source_target_pairs={{0,6},{1,7},{2,0},{3,1},{4,2},{5,3},{6,4},{7,5},{8,14},{9,15},{10,... | collective-permute-start | bytes 589832 | tf_op jit(solution)/shard_map/ppermute | solution.py:42
  44.4 17.4 %collective-permute-start.20 = (bf16[2,4,16,768]{3,2,0,1:T(8,128)(2,1)S(1)}, bf16[2,4,16,768]{3,2,0,1:T(8,128)(2,1)S(1)}, u32[]{:S(2)}, u32[]{:S(2)}) collective-permute-start(bf16[2,4,16,768]{3,2,0,1:T(8,128)(2,1)S(1)} %pad_maximum_fusion.20), channel_id=1, source_target_pairs={{0,4},{1,5},{2,6},{3,7},{4,0},{5,1},{6,2},{7,3},{8,12},{9,13},{10,... | collective-permute-start | bytes 589832 | tf_op jit(solution)/shard_map/ppermute | solution.py:42
  44.7 17.1 %collective-permute-start.19 = (bf16[2,4,16,768]{3,2,0,1:T(8,128)(2,1)S(1)}, bf16[2,4,16,768]{3,2,0,1:T(8,128)(2,1)S(1)}, u32[]{:S(2)}, u32[]{:S(2)}) collective-permute-start(bf16[2,4,16,768]{3,2,0,1:T(8,128)(2,1)S(1)} %pad_maximum_fusion.20), channel_id=1, source_target_pairs={{0,2},{1,3},{2,4},{3,5},{4,6},{5,7},{6,0},{7,1},{8,10},{9,11},{10,... | collective-permute-start | bytes 589832 | tf_op jit(solution)/shard_map/ppermute | solution.py:42
  47.3 5.7 %collective-permute-start.10 = (bf16[1,64,1536]{2,1,0:T(8,128)(2,1)S(1)}, bf16[1,64,1536]{2,1,0:T(8,128)(2,1)S(1)}, u32[]{:S(2)}, u32[]{:S(2)}) collective-permute-start(bf16[1,64,1536]{2,1,0:T(8,128)(2,1)S(1)} %fusion.20), channel_id=1, source_target_pairs={{0,16},{8,24},{16,0},{24,8},{1,17},{9,25},{17,1},{25,9},{2,18},{10... | collective-permute-start | bytes 589832 | tf_op jit(solution)/shard_map/ppermute | solution.py:42
  48.2 6.0 %collective-permute-start.9 = (bf16[1,64,1536]{2,1,0:T(8,128)(2,1)S(1)}, bf16[1,64,1536]{2,1,0:T(8,128)(2,1)S(1)}, u32[]{:S(2)}, u32[]{:S(2)}) collective-permute-start(bf16[1,64,1536]{2,1,0:T(8,128)(2,1)S(1)} %fusion.21), channel_id=1, source_target_pairs={{0,8},{8,0},{16,24},{24,16},{1,9},{9,1},{17,25},{25,17},{2,10},{10... | collective-permute-start | bytes 589832 | tf_op jit(solution)/shard_map/ppermute | solution.py:42
  53.6 8.4 %collective-permute-start.12 = (bf16[64,1536]{1,0:T(8,128)(2,1)S(1)}, bf16[64,1536]{1,0:T(8,128)(2,1)S(1)}, u32[]{:S(2)}, u32[]{:S(2)}) collective-permute-start(bf16[64,1536]{1,0:T(8,128)(2,1)S(1)} %get-tuple-element.83), channel_id=1, source_target_pairs={{0,16},{8,24},{16,0},{24,8},{1,17},{9,25},{17,1},{25,9},{2,18},{10... | collective-permute-start | bytes 589832 | tf_op jit(solution)/shard_map/ppermute | solution.py:42
  54.7 8.0 %collective-permute-start.11 = (bf16[64,1536]{1,0:T(8,128)(2,1)S(1)}, bf16[64,1536]{1,0:T(8,128)(2,1)S(1)}, u32[]{:S(2)}, u32[]{:S(2)}) collective-permute-start(bf16[64,1536]{1,0:T(8,128)(2,1)S(1)} %get-tuple-element.85), channel_id=1, source_target_pairs={{0,8},{8,0},{16,24},{24,16},{1,9},{9,1},{17,25},{25,17},{2,10},{10... | collective-permute-start | bytes 589832 | tf_op jit(solution)/shard_map/ppermute | solution.py:42
  61.9 13.8 %collective-permute-start.22 = (bf16[2,4,4,16,768]{4,3,0,1,2:T(8,128)(2,1)S(1)}, bf16[2,4,4,16,768]{4,3,0,1,2:T(8,128)(2,1)S(1)}, u32[]{:S(2)}, u32[]{:S(2)}) collective-permute-start(bf16[2,4,4,16,768]{4,3,0,1,2:T(8,128)(2,1)S(1)} %pad_maximum_fusion.4), channel_id=1, source_target_pairs={{0,1},{1,0},{2,3},{3,2},{4,5},{5,4},{6,7},{7,6},{8,9},{9,8},{10,11... | collective-permute-start | bytes 2359304 | tf_op jit(solution)/shard_map/ppermute | solution.py:42
  62.1 11.6 %collective-permute-start.13 = (bf16[2,64,1536]{2,1,0:T(8,128)(2,1)S(1)}, bf16[2,64,1536]{2,1,0:T(8,128)(2,1)S(1)}, u32[]{:S(2)}, u32[]{:S(2)}) collective-permute-start(bf16[2,64,1536]{2,1,0:T(8,128)(2,1)S(1)} %pad_maximum_fusion.11), channel_id=1, source_target_pairs={{0,8},{8,0},{16,24},{24,16},{1,9},{9,1},{17,25},{25,17},{2,10},{10... | collective-permute-start | bytes 1179656 | tf_op jit(solution)/shard_map/ppermute | solution.py:42
  62.7 11.5 %copy-start.1 = (bf16[1536,768]{1,0:T(8,128)(2,1)S(1)}, bf16[1536,768]{1,0:T(8,128)(2,1)}, u32[]{:S(2)}) copy-start(bf16[1536,768]{1,0:T(8,128)(2,1)} %param.11) | copy-start | bytes 7077892
  62.8 11.3 %collective-permute-start.14 = (bf16[2,64,1536]{2,1,0:T(8,128)(2,1)S(1)}, bf16[2,64,1536]{2,1,0:T(8,128)(2,1)S(1)}, u32[]{:S(2)}, u32[]{:S(2)}) collective-permute-start(bf16[2,64,1536]{2,1,0:T(8,128)(2,1)S(1)} %pad_maximum_fusion.13), channel_id=1, source_target_pairs={{0,16},{8,24},{16,0},{24,8},{1,17},{9,25},{17,1},{25,9},{2,18},{10... | collective-permute-start | bytes 1179656 | tf_op jit(solution)/shard_map/ppermute | solution.py:42
  75.6 13.5 %collective-permute-start.15 = (bf16[4,4,16,768]{3,2,1,0:T(8,128)(2,1)S(1)}, bf16[4,4,16,768]{3,2,1,0:T(8,128)(2,1)S(1)}, u32[]{:S(2)}, u32[]{:S(2)}) collective-permute-start(bf16[4,4,16,768]{3,2,1,0:T(8,128)(2,1)S(1)} %fusion.62), channel_id=1, source_target_pairs={{0,1},{1,0},{2,3},{3,2},{4,5},{5,4},{6,7},{7,6},{8,9},{9,8},{10,11... | collective-permute-start | bytes 1179656 | tf_op jit(solution)/shard_map/ppermute | solution.py:42
  85.4 20.0 %collective-permute-start.23 = (bf16[2,2,64,1536]{3,2,1,0:T(8,128)(2,1)S(1)}, bf16[2,2,64,1536]{3,2,1,0:T(8,128)(2,1)S(1)}, u32[]{:S(2)}, u32[]{:S(2)}) collective-permute-start(bf16[2,2,64,1536]{3,2,1,0:T(8,128)(2,1)S(1)} %pad_maximum_fusion.5), channel_id=1, source_target_pairs={{0,16},{8,24},{16,0},{24,8},{1,17},{9,25},{17,1},{25,9},{2,18},{10... | collective-permute-start | bytes 2359304 | tf_op jit(solution)/shard_map/ppermute | solution.py:42
  87.2 19.9 %collective-permute-start.25 = (bf16[2,2,64,1536]{3,2,1,0:T(8,128)(2,1)S(1)}, bf16[2,2,64,1536]{3,2,1,0:T(8,128)(2,1)S(1)}, u32[]{:S(2)}, u32[]{:S(2)}) collective-permute-start(bf16[2,2,64,1536]{3,2,1,0:T(8,128)(2,1)S(1)} %pad_maximum_fusion.6), channel_id=1, source_target_pairs={{0,8},{8,0},{16,24},{24,16},{1,9},{9,1},{17,25},{25,17},{2,10},{10... | collective-permute-start | bytes 2359304 | tf_op jit(solution)/shard_map/ppermute | solution.py:42
  89.3 7.5 %collective-permute-start.18 = (bf16[4,16,768]{2,1,0:T(8,128)(2,1)S(1)}, bf16[4,16,768]{2,1,0:T(8,128)(2,1)S(1)}, u32[]{:S(2)}, u32[]{:S(2)}) collective-permute-start(bf16[4,16,768]{2,1,0:T(8,128)(2,1)S(1)} %get-tuple-element.46), channel_id=1, source_target_pairs={{0,2},{1,3},{2,4},{3,5},{4,6},{5,7},{6,0},{7,1},{8,10},{9,11},{10,... | collective-permute-start | bytes 294920 | tf_op jit(solution)/shard_map/ppermute | solution.py:42
  89.8 10.3 %collective-permute-start.17 = (bf16[4,16,768]{2,1,0:T(8,128)(2,1)S(1)}, bf16[4,16,768]{2,1,0:T(8,128)(2,1)S(1)}, u32[]{:S(2)}, u32[]{:S(2)}) collective-permute-start(bf16[4,16,768]{2,1,0:T(8,128)(2,1)S(1)} %get-tuple-element.47), channel_id=1, source_target_pairs={{0,4},{1,5},{2,6},{3,7},{4,0},{5,1},{6,2},{7,3},{8,12},{9,13},{10,... | collective-permute-start | bytes 294920 | tf_op jit(solution)/shard_map/ppermute | solution.py:42
  91.8 8.3 %collective-permute-start.16 = (bf16[4,16,768]{2,1,0:T(8,128)(2,1)S(1)}, bf16[4,16,768]{2,1,0:T(8,128)(2,1)S(1)}, u32[]{:S(2)}, u32[]{:S(2)}) collective-permute-start(bf16[4,16,768]{2,1,0:T(8,128)(2,1)S(1)} %get-tuple-element.45), channel_id=1, source_target_pairs={{0,6},{1,7},{2,0},{3,1},{4,2},{5,3},{6,4},{7,5},{8,14},{9,15},{10,... | collective-permute-start | bytes 294920 | tf_op jit(solution)/shard_map/ppermute | solution.py:42
  105.5 10.8 %collective-permute-start.24 = (bf16[2,64,1536]{2,1,0:T(8,128)(2,1)S(1)}, bf16[2,64,1536]{2,1,0:T(8,128)(2,1)S(1)}, u32[]{:S(2)}, u32[]{:S(2)}) collective-permute-start(bf16[2,64,1536]{2,1,0:T(8,128)(2,1)S(1)} %fusion.33), channel_id=1, source_target_pairs={{0,8},{8,0},{16,24},{24,16},{1,9},{9,1},{17,25},{25,17},{2,10},{10... | collective-permute-start | bytes 1179656 | tf_op jit(solution)/shard_map/ppermute | solution.py:42
  107.2 10.5 %collective-permute-start.26 = (bf16[2,64,1536]{2,1,0:T(8,128)(2,1)S(1)}, bf16[2,64,1536]{2,1,0:T(8,128)(2,1)S(1)}, u32[]{:S(2)}, u32[]{:S(2)}) collective-permute-start(bf16[2,64,1536]{2,1,0:T(8,128)(2,1)S(1)} %fusion.35), channel_id=1, source_target_pairs={{0,16},{8,24},{16,0},{24,8},{1,17},{9,25},{17,1},{25,9},{2,18},{10... | collective-permute-start | bytes 1179656 | tf_op jit(solution)/shard_map/ppermute | solution.py:42
  118.9 5.7 %collective-permute-start.28 = (bf16[64,1536]{1,0:T(8,128)(2,1)S(1)}, bf16[64,1536]{1,0:T(8,128)(2,1)S(1)}, u32[]{:S(2)}, u32[]{:S(2)}) collective-permute-start(bf16[64,1536]{1,0:T(8,128)(2,1)S(1)} %fusion.65), channel_id=1, source_target_pairs={{0,16},{8,24},{16,0},{24,8},{1,17},{9,25},{17,1},{25,9},{2,18},{10... | collective-permute-start | bytes 589832 | tf_op jit(solution)/shard_map/ppermute | solution.py:42
  119.5 6.1 %collective-permute-start.27 = (bf16[64,1536]{1,0:T(8,128)(2,1)S(1)}, bf16[64,1536]{1,0:T(8,128)(2,1)S(1)}, u32[]{:S(2)}, u32[]{:S(2)}) collective-permute-start(bf16[64,1536]{1,0:T(8,128)(2,1)S(1)} %fusion.67), channel_id=1, source_target_pairs={{0,8},{8,0},{16,24},{24,16},{1,9},{9,1},{17,25},{25,17},{2,10},{10... | collective-permute-start | bytes 589832 | tf_op jit(solution)/shard_map/ppermute | solution.py:42
  124.7 13.2 %collective-permute-start.29 = (bf16[2,64,1536]{2,1,0:T(8,128)(2,1)S(1)}, bf16[2,64,1536]{2,1,0:T(8,128)(2,1)S(1)}, u32[]{:S(2)}, u32[]{:S(2)}) collective-permute-start(bf16[2,64,1536]{2,1,0:T(8,128)(2,1)S(1)} %pad_maximum_fusion.16), channel_id=1, source_target_pairs={{0,8},{8,0},{16,24},{24,16},{1,9},{9,1},{17,25},{25,17},{2,10},{10... | collective-permute-start | bytes 1179656 | tf_op jit(solution)/shard_map/ppermute | solution.py:42
  125.6 12.3 %collective-permute-start.30 = (bf16[2,64,1536]{2,1,0:T(8,128)(2,1)S(1)}, bf16[2,64,1536]{2,1,0:T(8,128)(2,1)S(1)}, u32[]{:S(2)}, u32[]{:S(2)}) collective-permute-start(bf16[2,64,1536]{2,1,0:T(8,128)(2,1)S(1)} %pad_maximum_fusion.17), channel_id=1, source_target_pairs={{0,16},{8,24},{16,0},{24,8},{1,17},{9,25},{17,1},{25,9},{2,18},{10... | collective-permute-start | bytes 1179656 | tf_op jit(solution)/shard_map/ppermute | solution.py:42
  128.5 9.3 %collective-permute-start.31 = (bf16[64,1536]{1,0:T(8,128)(2,1)S(1)}, bf16[64,1536]{1,0:T(8,128)(2,1)S(1)}, u32[]{:S(2)}, u32[]{:S(2)}) collective-permute-start(bf16[64,1536]{1,0:T(8,128)(2,1)S(1)} %select_convert_fusion.1), channel_id=1, source_target_pairs={{0,8},{8,0},{16,24},{24,16},{1,9},{9,1},{17,25},{25,17},{2,10},{10... | collective-permute-start | bytes 589832 | tf_op jit(solution)/shard_map/ppermute | solution.py:42
  128.9 9.0 %collective-permute-start.32 = (bf16[64,1536]{1,0:T(8,128)(2,1)S(1)}, bf16[64,1536]{1,0:T(8,128)(2,1)S(1)}, u32[]{:S(2)}, u32[]{:S(2)}) collective-permute-start(bf16[64,1536]{1,0:T(8,128)(2,1)S(1)} %select_convert_fusion), channel_id=1, source_target_pairs={{0,16},{8,24},{16,0},{24,8},{1,17},{9,25},{17,1},{25,9},{2,18},{10... | collective-permute-start | bytes 589832 | tf_op jit(solution)/shard_map/ppermute | solution.py:42
  138.3 10.3 %collective-permute-start.40 = (bf16[2,64,1536]{2,1,0:T(8,128)(2,1)S(1)}, bf16[2,64,1536]{2,1,0:T(8,128)(2,1)S(1)}, u32[]{:S(2)}, u32[]{:S(2)}) collective-permute-start(bf16[2,64,1536]{2,1,0:T(8,128)(2,1)S(1)} %pad_maximum_fusion.19), channel_id=1, source_target_pairs={{0,8},{8,0},{16,24},{24,16},{1,9},{9,1},{17,25},{25,17},{2,10},{10... | collective-permute-start | bytes 1179656 | tf_op jit(solution)/shard_map/ppermute | solution.py:42
  141.3 1.8 %collective-permute-start.33 = (bf16[4,4,16,768]{3,2,0,1:T(8,128)(2,1)S(1)}, bf16[4,4,16,768]{3,2,0,1:T(8,128)(2,1)S(1)}, u32[]{:S(2)}, u32[]{:S(2)}) collective-permute-start(bf16[4,4,16,768]{3,2,0,1:T(8,128)(2,1)S(1)} %fusion.63), channel_id=1, source_target_pairs={{0,1},{1,0},{2,3},{3,2},{4,5},{5,4},{6,7},{7,6},{8,9},{9,8},{10,11... | collective-permute-start | bytes 1179656 | tf_op jit(solution)/shard_map/ppermute | solution.py:42
  141.4 11.5 %collective-permute-start.41 = (bf16[2,64,1536]{2,1,0:T(8,128)(2,1)S(1)}, bf16[2,64,1536]{2,1,0:T(8,128)(2,1)S(1)}, u32[]{:S(2)}, u32[]{:S(2)}) collective-permute-start(bf16[2,64,1536]{2,1,0:T(8,128)(2,1)S(1)} %pad_maximum_fusion.18), channel_id=1, source_target_pairs={{0,16},{8,24},{16,0},{24,8},{1,17},{9,25},{17,1},{25,9},{2,18},{10... | collective-permute-start | bytes 1179656 | tf_op jit(solution)/shard_map/ppermute | solution.py:42
  143.3 10.0 %collective-permute-start.36 = (bf16[4,16,768]{2,1,0:T(8,128)(2,1)S(1)}, bf16[4,16,768]{2,1,0:T(8,128)(2,1)S(1)}, u32[]{:S(2)}, u32[]{:S(2)}) collective-permute-start(bf16[4,16,768]{2,1,0:T(8,128)(2,1)S(1)} %get-tuple-element.49), channel_id=1, source_target_pairs={{0,2},{1,3},{2,4},{3,5},{4,6},{5,7},{6,0},{7,1},{8,10},{9,11},{10,... | collective-permute-start | bytes 294920 | tf_op jit(solution)/shard_map/ppermute | solution.py:42
  143.8 10.5 %collective-permute-start.35 = (bf16[4,16,768]{2,1,0:T(8,128)(2,1)S(1)}, bf16[4,16,768]{2,1,0:T(8,128)(2,1)S(1)}, u32[]{:S(2)}, u32[]{:S(2)}) collective-permute-start(bf16[4,16,768]{2,1,0:T(8,128)(2,1)S(1)} %get-tuple-element.50), channel_id=1, source_target_pairs={{0,4},{1,5},{2,6},{3,7},{4,0},{5,1},{6,2},{7,3},{8,12},{9,13},{10,... | collective-permute-start | bytes 294920 | tf_op jit(solution)/shard_map/ppermute | solution.py:42
  145.8 8.5 %collective-permute-start.34 = (bf16[4,16,768]{2,1,0:T(8,128)(2,1)S(1)}, bf16[4,16,768]{2,1,0:T(8,128)(2,1)S(1)}, u32[]{:S(2)}, u32[]{:S(2)}) collective-permute-start(bf16[4,16,768]{2,1,0:T(8,128)(2,1)S(1)} %get-tuple-element.48), channel_id=1, source_target_pairs={{0,6},{1,7},{2,0},{3,1},{4,2},{5,3},{6,4},{7,5},{8,14},{9,15},{10,... | collective-permute-start | bytes 294920 | tf_op jit(solution)/shard_map/ppermute | solution.py:42
  154.4 7.2 %collective-permute-start.39 = (bf16[2,16,768]{2,1,0:T(8,128)(2,1)S(1)}, bf16[2,16,768]{2,1,0:T(8,128)(2,1)S(1)}, u32[]{:S(2)}, u32[]{:S(2)}) collective-permute-start(bf16[2,16,768]{2,1,0:T(8,128)(2,1)S(1)} %get-tuple-element.65), channel_id=1, source_target_pairs={{0,24},{8,16},{16,8},{24,0},{1,25},{9,17},{17,9},{25,1},{2,26},{10... | collective-permute-start | bytes 147464 | tf_op jit(solution)/shard_map/ppermute | solution.py:42
  155.9 5.6 %collective-permute-start.38 = (bf16[2,16,768]{2,1,0:T(8,128)(2,1)S(1)}, bf16[2,16,768]{2,1,0:T(8,128)(2,1)S(1)}, u32[]{:S(2)}, u32[]{:S(2)}) collective-permute-start(bf16[2,16,768]{2,1,0:T(8,128)(2,1)S(1)} %get-tuple-element.66), channel_id=1, source_target_pairs={{0,16},{8,24},{16,0},{24,8},{1,17},{9,25},{17,1},{25,9},{2,18},{10... | collective-permute-start | bytes 147464 | tf_op jit(solution)/shard_map/ppermute | solution.py:42
  156.4 5.1 %collective-permute-start.37 = (bf16[2,16,768]{2,1,0:T(8,128)(2,1)S(1)}, bf16[2,16,768]{2,1,0:T(8,128)(2,1)S(1)}, u32[]{:S(2)}, u32[]{:S(2)}) collective-permute-start(bf16[2,16,768]{2,1,0:T(8,128)(2,1)S(1)} %get-tuple-element.64), channel_id=1, source_target_pairs={{0,8},{8,0},{16,24},{24,16},{1,9},{9,1},{17,25},{25,17},{2,10},{10... | collective-permute-start | bytes 147464 | tf_op jit(solution)/shard_map/ppermute | solution.py:42

commit v8 on v5

--- a/solution.py
+++ b/solution.py
@@ -143,9 +143,13 @@
         )
 
     def sums(terms):
+        whole = [
+            f(cols.reshape(dp_count * group_rows, own_cols)).reshape(dp_count, group_rows, -1)
+            for f, cols in terms
+        ]
         return [
             sum_to_owner(
-                lambda s, r=rows: jnp.stack([f(cols[place[s], r]) for f, cols in terms]),
+                lambda s, r=rows: jnp.stack([w[place[s], r] for w in whole]),
                 grid,
                 first,
             )

time: 160 us -> 163 us (1.019)
  matrix products: 25.4 us -> 10.6 us
  waiting for transfers between devices: 70 us -> 79 us
  starting transfers between devices: 48.1 us -> 54.2 us
  other arithmetic: 9.15 us -> 12.3 us
    dot_general x18 -> x4, matrix products: 15.2 us -> 5.54 us  [dot(): return jnp.dot(a, b, preferred_element_type=jnp.float32)]
    ppermute x42, waiting for transfers between devices: 70 us -> 79 us  [shift(): return lax.ppermute(value, axis, pairs)]
    ppermute x42, starting transfers between devices: 48.1 us -> 54.2 us  [shift(): return lax.ppermute(value, axis, pairs)]
    dot_general x8 -> x1, matrix products: 6.66 us -> 1.41 us  [back(): lax.dot_general(rows, w_out, (((1,), (1,)), ((), ())), preferred_element_...]
    convert_element_type x8 -> x11, other arithmetic: 1.53 us -> 4.89 us  [half(): return value.astype(jnp.bfloat16)]
  transfers between devices with their start and end apart: 42 -> 42, of which waited for: 24 -> 27; matrix products, arithmetic and copies ran while one was open for 20% -> 13% of each run, Pallas kernels for 0% -> 0%
where the time goes in v8:
time: 163 us; the launch traced here: 162 us
  waiting for transfers between devices  79 us (48%)
  starting transfers between devices  54.2 us (33%)
  other arithmetic  12.3 us (8%)
  matrix products  10.6 us (7%)
  local copies, waits for them, and re-layouts  4.82 us (3%)
    ppermute x42, waiting for transfers between devices, shift(): return lax.ppermute(value, axis, pairs)  79 us
    ppermute x42, starting transfers between devices, shift(): return lax.ppermute(value, axis, pairs)  54.2 us
    dot_general x4, matrix products, dot(): return jnp.dot(a, b, preferred_element_type=jnp.float32)  5.54 us
    convert_element_type x11, other arithmetic, half(): return value.astype(jnp.bfloat16)  4.89 us
    dot_general x1, matrix products, local(): lax.dot_general(tok_cols.reshape(dp_count * group_rows, own_cols), grad_a...  3.6 us
  transfers between devices with their start and end apart: 42, of which 27 were waited for; matrix products, arithmetic and copies ran while one was open for 13% of the time, Pallas kernels for 0%

profile of v8, /device:TPU:0, one launch (start us, length us, event | category | flops | bytes accessed | tf_op | source)
XLA Modules:
  0.0 162.2 jit_solution(16366379183208595371)
XLA Ops:
  0.7 0.9 dynamic-slice_bitcast_fusion.11
  1.7 0.9 dynamic-slice_bitcast_fusion
  2.6 4.0 %collective-permute-start.2 = (bf16[3,16,768]{2,1,0:T(8,128)(2,1)S(1)}, bf16[3,16,768]{2,1,0:T(8,128)(2,1)S(1)}, u32[]{:S(2)}, u32[]{:S(2)}) collective-permute-start(bf16[3,16,768]{2,1,0:T(8,128)(2,1)S(1)} %pad_maximum_fusion.29), channel_id=1, source_target_pairs={{0,24},{8,16},{16,8},{24,0},{1,25},{9,17},{17,9},{25,1},{2,26},{10... | collective-permute-start | bytes 221192 | tf_op jit(solution)/shard_map/ppermute | solution.py:42
  7.5 1.6 collective-permute-done.2
  9.1 1.9 %collective-permute-done = bf16[3,16,768]{2,1,0:T(8,128)(2,1)S(1)} collective-permute-done((bf16[3,16,768]{2,1,0:T(8,128)(2,1)S(1)}, bf16[3,16,768]{2,1,0:T(8,128)(2,1)S(1)}, u32[]{:S(2)}, u32[]{:S(2)}) %collective-permute-start) | collective-permute-done | bytes 73760 | tf_op jit(solution)/shard_map/ppermute | solution.py:42
  11.6 2.7 %collective-permute-start.4 = (bf16[1,4,16,768]{3,2,1,0:T(8,128)(2,1)S(1)}, bf16[1,4,16,768]{3,2,1,0:T(8,128)(2,1)S(1)}, u32[]{:S(2)}, u32[]{:S(2)}) collective-permute-start(bf16[1,4,16,768]{3,2,1,0:T(8,128)(2,1)S(1)} %get-tuple-element.75), channel_id=1, source_target_pairs={{0,4},{1,5},{2,6},{3,7},{4,0},{5,1},{6,2},{7,3},{8,12},{9,13},{10,... | collective-permute-start | bytes 294920 | tf_op jit(solution)/shard_map/ppermute | solution.py:42
  14.3 1.6 collective-permute-start.3
  15.9 2.2 %collective-permute-start.5 = (bf16[1,4,16,768]{3,2,1,0:T(8,128)(2,1)S(1)}, bf16[1,4,16,768]{3,2,1,0:T(8,128)(2,1)S(1)}, u32[]{:S(2)}, u32[]{:S(2)}) collective-permute-start(bf16[1,4,16,768]{3,2,1,0:T(8,128)(2,1)S(1)} %get-tuple-element.75), channel_id=1, source_target_pairs={{0,6},{1,7},{2,0},{3,1},{4,2},{5,3},{6,4},{7,5},{8,14},{9,15},{10,... | collective-permute-start | bytes 294920 | tf_op jit(solution)/shard_map/ppermute | solution.py:42
  18.1 2.3 %collective-permute-done.4 = bf16[1,4,16,768]{3,2,1,0:T(8,128)(2,1)S(1)} collective-permute-done((bf16[1,4,16,768]{3,2,1,0:T(8,128)(2,1)S(1)}, bf16[1,4,16,768]{3,2,1,0:T(8,128)(2,1)S(1)}, u32[]{:S(2)}, u32[]{:S(2)}) %collective-permute-start.4) | collective-permute-done | bytes 98336 | tf_op jit(solution)/shard_map/ppermute | solution.py:42
  20.4 1.1 collective-permute-done.3
  22.1 3.1 %collective-permute-start.21 = (bf16[2,4,16,768]{3,2,0,1:T(8,128)(2,1)S(1)}, bf16[2,4,16,768]{3,2,0,1:T(8,128)(2,1)S(1)}, u32[]{:S(2)}, u32[]{:S(2)}) collective-permute-start(bf16[2,4,16,768]{3,2,0,1:T(8,128)(2,1)S(1)} %pad_maximum_fusion.24), channel_id=1, source_target_pairs={{0,6},{1,7},{2,0},{3,1},{4,2},{5,3},{6,4},{7,5},{8,14},{9,15},{10,... | collective-permute-start | bytes 589832 | tf_op jit(solution)/shard_map/ppermute | solution.py:42
  25.4 1.9 %collective-permute-start.19 = (bf16[2,4,16,768]{3,2,0,1:T(8,128)(2,1)S(1)}, bf16[2,4,16,768]{3,2,0,1:T(8,128)(2,1)S(1)}, u32[]{:S(2)}, u32[]{:S(2)}) collective-permute-start(bf16[2,4,16,768]{3,2,0,1:T(8,128)(2,1)S(1)} %pad_maximum_fusion.24), channel_id=1, source_target_pairs={{0,2},{1,3},{2,4},{3,5},{4,6},{5,7},{6,0},{7,1},{8,10},{9,11},{10,... | collective-permute-start | bytes 589832 | tf_op jit(solution)/shard_map/ppermute | solution.py:42
  27.4 1.4 fusion.102
  29.0 1.6 %collective-permute-start.9 = (bf16[2,1,64,1536]{3,2,1,0:T(8,128)(2,1)S(1)}, bf16[2,1,64,1536]{3,2,1,0:T(8,128)(2,1)S(1)}, u32[]{:S(2)}, u32[]{:S(2)}) collective-permute-start(bf16[2,1,64,1536]{3,2,1,0:T(8,128)(2,1)S(1)} %pad_maximum_fusion.9), channel_id=1, source_target_pairs={{0,8},{8,0},{16,24},{24,16},{1,9},{9,1},{17,25},{25,17},{2,10},{10... | collective-permute-start | bytes 1179656 | tf_op jit(solution)/shard_map/ppermute | solution.py:42
  31.3 12.3 %collective-permute-done.20 = bf16[2,4,16,768]{3,2,0,1:T(8,128)(2,1)S(1)} collective-permute-done((bf16[2,4,16,768]{3,2,0,1:T(8,128)(2,1)S(1)}, bf16[2,4,16,768]{3,2,0,1:T(8,128)(2,1)S(1)}, u32[]{:S(2)}, u32[]{:S(2)}) %collective-permute-start.20) | collective-permute-done | bytes 196640 | tf_op jit(solution)/shard_map/ppermute | solution.py:42
  43.5 1.0 pad_maximum_fusion.4
  44.6 0.8 pad_maximum_fusion.8
  45.3 0.8 collective-permute-start.7
  46.1 0.8 fusion.56
  47.0 1.2 collective-permute-start.10
  49.0 1.5 pad_maximum_fusion
  50.8 6.7 %collective-permute-done.7 = bf16[2,1,64,1536]{3,2,1,0:T(8,128)(2,1)S(1)} collective-permute-done((bf16[2,1,64,1536]{3,2,1,0:T(8,128)(2,1)}, bf16[2,1,64,1536]{3,2,1,0:T(8,128)(2,1)S(1)}, u32[]{:S(2)}, u32[]{:S(2)}) %collective-permute-start.7) | collective-permute-done | bytes 393248 | tf_op jit(solution)/shard_map/ppermute | solution.py:42
  57.5 3.9 %collective-permute-done.10 = bf16[1,64,1536]{2,1,0:T(8,128)(2,1)} collective-permute-done((bf16[1,64,1536]{2,1,0:T(8,128)(2,1)}, bf16[1,64,1536]{2,1,0:T(8,128)(2,1)}, u32[]{:S(2)}, u32[]{:S(2)}) %collective-permute-start.10) | collective-permute-done | bytes 196640 | tf_op jit(solution)/shard_map/ppermute | solution.py:42
  61.4 1.4 select_convert_fusion.3
  62.8 1.6 %collective-permute-start.8 = (bf16[1,64,1536]{2,1,0:T(8,128)(2,1)S(1)}, bf16[1,64,1536]{2,1,0:T(8,128)(2,1)S(1)}, u32[]{:S(2)}, u32[]{:S(2)}) collective-permute-start(bf16[1,64,1536]{2,1,0:T(8,128)(2,1)S(1)} %get-tuple-element.31), channel_id=1, source_target_pairs={{0,8},{8,0},{16,24},{24,16},{1,9},{9,1},{17,25},{25,17},{2,10},{10... | collective-permute-start | bytes 589832 | tf_op jit(solution)/shard_map/ppermute | solution.py:42
  65.2 4.2 %collective-permute-done.8 = bf16[1,64,1536]{2,1,0:T(8,128)(2,1)S(1)} collective-permute-done((bf16[1,64,1536]{2,1,0:T(8,128)(2,1)S(1)}, bf16[1,64,1536]{2,1,0:T(8,128)(2,1)S(1)}, u32[]{:S(2)}, u32[]{:S(2)}) %collective-permute-start.8) | collective-permute-done | bytes 196640 | tf_op jit(solution)/shard_map/ppermute | solution.py:42
  69.4 1.2 select_convert_fusion.2
  70.8 1.6 %collective-permute-start.11 = (bf16[64,1536]{1,0:T(8,128)(2,1)S(1)}, bf16[64,1536]{1,0:T(8,128)(2,1)S(1)}, u32[]{:S(2)}, u32[]{:S(2)}) collective-permute-start(bf16[64,1536]{1,0:T(8,128)(2,1)S(1)} %select_convert_fusion.5), channel_id=1, source_target_pairs={{0,8},{8,0},{16,24},{24,16},{1,9},{9,1},{17,25},{25,17},{2,10},{10... | collective-permute-start | bytes 589832 | tf_op jit(solution)/shard_map/ppermute | solution.py:42
  73.0 5.7 %collective-permute-done.11 = bf16[64,1536]{1,0:T(8,128)(2,1)S(1)} collective-permute-done((bf16[64,1536]{1,0:T(8,128)(2,1)S(1)}, bf16[64,1536]{1,0:T(8,128)(2,1)S(1)}, u32[]{:S(2)}, u32[]{:S(2)}) %collective-permute-start.11) | collective-permute-done | bytes 196640 | tf_op jit(solution)/shard_map/ppermute | solution.py:42
  78.7 0.9 collective-permute-start.14
  79.6 1.4 fusion.104
  81.2 1.4 fusion.103
  83.0 1.3 collective-permute-start.23
  84.4 1.6 %collective-permute-start.25 = (bf16[2,2,64,1536]{3,2,1,0:T(8,128)(2,1)S(1)}, bf16[2,2,64,1536]{3,2,1,0:T(8,128)(2,1)S(1)}, u32[]{:S(2)}, u32[]{:S(2)}) collective-permute-start(bf16[2,2,64,1536]{3,2,1,0:T(8,128)(2,1)S(1)} %pad_maximum_fusion.6), channel_id=1, source_target_pairs={{0,8},{8,0},{16,24},{24,16},{1,9},{9,1},{17,25},{25,17},{2,10},{10... | collective-permute-start | bytes 2359304 | tf_op jit(solution)/shard_map/ppermute | solution.py:42
  86.2 0.9 collective-permute-done.13
  87.2 3.7 %collective-permute-done.14 = bf16[2,64,1536]{2,1,0:T(8,128)(2,1)S(1)} collective-permute-done((bf16[2,64,1536]{2,1,0:T(8,128)(2,1)S(1)}, bf16[2,64,1536]{2,1,0:T(8,128)(2,1)S(1)}, u32[]{:S(2)}, u32[]{:S(2)}) %collective-permute-start.14) | collective-permute-done | bytes 393248 | tf_op jit(solution)/shard_map/ppermute | solution.py:42
  90.9 1.4 fusion
  92.6 1.6 collective-permute-done.15
  94.4 2.0 %collective-permute-start.18 = (bf16[4,16,768]{2,1,0:T(8,128)(2,1)S(1)}, bf16[4,16,768]{2,1,0:T(8,128)(2,1)S(1)}, u32[]{:S(2)}, u32[]{:S(2)}) collective-permute-start(bf16[4,16,768]{2,1,0:T(8,128)(2,1)S(1)} %get-tuple-element.53), channel_id=1, source_target_pairs={{0,2},{1,3},{2,4},{3,5},{4,6},{5,7},{6,0},{7,1},{8,10},{9,11},{10,... | collective-permute-start | bytes 294920 | tf_op jit(solution)/shard_map/ppermute | solution.py:42
  96.4 2.5 %collective-permute-start.17 = (bf16[4,16,768]{2,1,0:T(8,128)(2,1)S(1)}, bf16[4,16,768]{2,1,0:T(8,128)(2,1)S(1)}, u32[]{:S(2)}, u32[]{:S(2)}) collective-permute-start(bf16[4,16,768]{2,1,0:T(8,128)(2,1)S(1)} %get-tuple-element.54), channel_id=1, source_target_pairs={{0,4},{1,5},{2,6},{3,7},{4,0},{5,1},{6,2},{7,3},{8,12},{9,13},{10,... | collective-permute-start | bytes 294920 | tf_op jit(solution)/shard_map/ppermute | solution.py:42
  98.9 2.9 %collective-permute-done.25 = bf16[2,2,64,1536]{3,2,1,0:T(8,128)(2,1)S(1)} collective-permute-done((bf16[2,2,64,1536]{3,2,1,0:T(8,128)(2,1)S(1)}, bf16[2,2,64,1536]{3,2,1,0:T(8,128)(2,1)S(1)}, u32[]{:S(2)}, u32[]{:S(2)}) %collective-permute-start.25) | collective-permute-done | bytes 786464 | tf_op jit(solution)/shard_map/ppermute | solution.py:42
  101.8 0.9 collective-permute-start.26
  103.0 1.6 %collective-permute-start.24 = (bf16[2,64,1536]{2,1,0:T(8,128)(2,1)S(1)}, bf16[2,64,1536]{2,1,0:T(8,128)(2,1)S(1)}, u32[]{:S(2)}, u32[]{:S(2)}) collective-permute-start(bf16[2,64,1536]{2,1,0:T(8,128)(2,1)S(1)} %fusion.21), channel_id=1, source_target_pairs={{0,8},{8,0},{16,24},{24,16},{1,9},{9,1},{17,25},{25,17},{2,10},{10... | collective-permute-start | bytes 1179656 | tf_op jit(solution)/shard_map/ppermute | solution.py:42
  104.6 1.7 %collective-permute-done.17 = bf16[4,16,768]{2,1,0:T(8,128)(2,1)S(1)} collective-permute-done((bf16[4,16,768]{2,1,0:T(8,128)(2,1)S(1)}, bf16[4,16,768]{2,1,0:T(8,128)(2,1)S(1)}, u32[]{:S(2)}, u32[]{:S(2)}) %collective-permute-start.17) | collective-permute-done | bytes 98336 | tf_op jit(solution)/shard_map/ppermute | solution.py:42
  106.3 4.3 %collective-permute-done.26 = bf16[2,64,1536]{2,1,0:T(8,128)(2,1)S(1)} collective-permute-done((bf16[2,64,1536]{2,1,0:T(8,128)(2,1)S(1)}, bf16[2,64,1536]{2,1,0:T(8,128)(2,1)S(1)}, u32[]{:S(2)}, u32[]{:S(2)}) %collective-permute-start.26) | collective-permute-done | bytes 393248 | tf_op jit(solution)/shard_map/ppermute | solution.py:42
  112.0 1.3 collective-permute-start.28
  113.3 1.8 %collective-permute-start.27 = (bf16[64,1536]{1,0:T(8,128)(2,1)S(1)}, bf16[64,1536]{1,0:T(8,128)(2,1)S(1)}, u32[]{:S(2)}, u32[]{:S(2)}) collective-permute-start(bf16[64,1536]{1,0:T(8,128)(2,1)S(1)} %fusion.63), channel_id=1, source_target_pairs={{0,8},{8,0},{16,24},{24,16},{1,9},{9,1},{17,25},{25,17},{2,10},{10... | collective-permute-start | bytes 589832 | tf_op jit(solution)/shard_map/ppermute | solution.py:42
  115.2 5.2 %collective-permute-done.27 = bf16[64,1536]{1,0:T(8,128)(2,1)S(1)} collective-permute-done((bf16[64,1536]{1,0:T(8,128)(2,1)S(1)}, bf16[64,1536]{1,0:T(8,128)(2,1)S(1)}, u32[]{:S(2)}, u32[]{:S(2)}) %collective-permute-start.27) | collective-permute-done | bytes 196640 | tf_op jit(solution)/shard_map/ppermute | solution.py:42
  120.9 1.9 %collective-permute-start.29 = (bf16[2,64,1536]{2,1,0:T(8,128)(2,1)S(1)}, bf16[2,64,1536]{2,1,0:T(8,128)(2,1)S(1)}, u32[]{:S(2)}, u32[]{:S(2)}) collective-permute-start(bf16[2,64,1536]{2,1,0:T(8,128)(2,1)S(1)} %pad_maximum_fusion.17), channel_id=1, source_target_pairs={{0,8},{8,0},{16,24},{24,16},{1,9},{9,1},{17,25},{25,17},{2,10},{10... | collective-permute-start | bytes 1179656 | tf_op jit(solution)/shard_map/ppermute | solution.py:42
  123.6 1.9 %collective-permute-start.39 = (bf16[64,1536]{1,0:T(8,128)(2,1)S(1)}, bf16[64,1536]{1,0:T(8,128)(2,1)S(1)}, u32[]{:S(2)}, u32[]{:S(2)}) collective-permute-start(bf16[64,1536]{1,0:T(8,128)(2,1)S(1)} %select_convert_fusion), channel_id=1, source_target_pairs={{0,16},{8,24},{16,0},{24,8},{1,17},{9,25},{17,1},{25,9},{2,18},{10... | collective-permute-start | bytes 589832 | tf_op jit(solution)/shard_map/ppermute | solution.py:42
  125.5 8.6 %collective-permute-done.38 = bf16[64,1536]{1,0:T(8,128)(2,1)S(1)} collective-permute-done((bf16[64,1536]{1,0:T(8,128)(2,1)S(1)}, bf16[64,1536]{1,0:T(8,128)(2,1)S(1)}, u32[]{:S(2)}, u32[]{:S(2)}) %collective-permute-start.38) | collective-permute-done | bytes 196640 | tf_op jit(solution)/shard_map/ppermute | solution.py:42
  134.6 2.4 %collective-permute-start.40 = (bf16[2,64,1536]{2,1,0:T(8,128)(2,1)S(1)}, bf16[2,64,1536]{2,1,0:T(8,128)(2,1)S(1)}, u32[]{:S(2)}, u32[]{:S(2)}) collective-permute-start(bf16[2,64,1536]{2,1,0:T(8,128)(2,1)S(1)} %pad_maximum_fusion.22), channel_id=1, source_target_pairs={{0,8},{8,0},{16,24},{24,16},{1,9},{9,1},{17,25},{25,17},{2,10},{10... | collective-permute-start | bytes 1179656 | tf_op jit(solution)/shard_map/ppermute | solution.py:42
  137.2 1.4 fusion.4
  138.7 3.3 %collective-permute-done.41 = bf16[2,64,1536]{2,1,0:T(8,128)(2,1)S(1)} collective-permute-done((bf16[2,64,1536]{2,1,0:T(8,128)(2,1)S(1)}, bf16[2,64,1536]{2,1,0:T(8,128)(2,1)S(1)}, u32[]{:S(2)}, u32[]{:S(2)}) %collective-permute-start.41) | collective-permute-done | bytes 393248 | tf_op jit(solution)/shard_map/ppermute | solution.py:42
  142.0 0.7 collective-permute-done.40
  143.1 2.0 %collective-permute-start.34 = (bf16[4,16,768]{2,1,0:T(8,128)(2,1)S(1)}, bf16[4,16,768]{2,1,0:T(8,128)(2,1)S(1)}, u32[]{:S(2)}, u32[]{:S(2)}) collective-permute-start(bf16[4,16,768]{2,1,0:T(8,128)(2,1)S(1)} %get-tuple-element.56), channel_id=1, source_target_pairs={{0,2},{1,3},{2,4},{3,5},{4,6},{5,7},{6,0},{7,1},{8,10},{9,11},{10,... | collective-permute-start | bytes 294920 | tf_op jit(solution)/shard_map/ppermute | solution.py:42
  145.1 2.7 %collective-permute-start.33 = (bf16[4,16,768]{2,1,0:T(8,128)(2,1)S(1)}, bf16[4,16,768]{2,1,0:T(8,128)(2,1)S(1)}, u32[]{:S(2)}, u32[]{:S(2)}) collective-permute-start(bf16[4,16,768]{2,1,0:T(8,128)(2,1)S(1)} %get-tuple-element.57), channel_id=1, source_target_pairs={{0,4},{1,5},{2,6},{3,7},{4,0},{5,1},{6,2},{7,3},{8,12},{9,13},{10,... | collective-permute-start | bytes 294920 | tf_op jit(solution)/shard_map/ppermute | solution.py:42
  148.0 0.7 collective-permute-done.32
  148.7 2.3 %collective-permute-done.34 = bf16[4,16,768]{2,1,0:T(8,128)(2,1)S(1)} collective-permute-done((bf16[4,16,768]{2,1,0:T(8,128)(2,1)S(1)}, bf16[4,16,768]{2,1,0:T(8,128)(2,1)S(1)}, u32[]{:S(2)}, u32[]{:S(2)}) %collective-permute-start.34) | collective-permute-done | bytes 98336 | tf_op jit(solution)/shard_map/ppermute | solution.py:42
  151.0 2.1 %collective-permute-done.33 = bf16[4,16,768]{2,1,0:T(8,128)(2,1)S(1)} collective-permute-done((bf16[4,16,768]{2,1,0:T(8,128)(2,1)S(1)}, bf16[4,16,768]{2,1,0:T(8,128)(2,1)S(1)}, u32[]{:S(2)}, u32[]{:S(2)}) %collective-permute-start.33) | collective-permute-done | bytes 98336 | tf_op jit(solution)/shard_map/ppermute | solution.py:42
  153.2 1.7 %collective-permute-start.35 = (bf16[2,16,768]{2,1,0:T(8,128)(2,1)S(1)}, bf16[2,16,768]{2,1,0:T(8,128)(2,1)S(1)}, u32[]{:S(2)}, u32[]{:S(2)}) collective-permute-start(bf16[2,16,768]{2,1,0:T(8,128)(2,1)S(1)} %get-tuple-element.71), channel_id=1, source_target_pairs={{0,8},{8,0},{16,24},{24,16},{1,9},{9,1},{17,25},{25,17},{2,10},{10... | collective-permute-start | bytes 147464 | tf_op jit(solution)/shard_map/ppermute | solution.py:42
  154.9 1.1 collective-permute-start.37
  156.0 0.8 collective-permute-start.36
  156.7 3.6 %fusion.105 = f32[768,1536]{1,0:T(8,128)} fusion(bf16[512,768]{1,0:T(8,128)(2,1)S(1)} %bitcast.315, bf16[512,1536]{1,0:T(8,128)(2,1)S(1)} %bitcast.316), kind=kOutput, calls=%fused_computation.242 | convolution fusion | flops 1207959552 | bytes 7077888 | tf_op jit(solution)/shard_map/dot_general | solution.py:208
  (139 shorter events, 13.4 us)
Async XLA Ops:
  0.6 26.8 %copy-start = (bf16[768,1536]{1,0:T(8,128)(2,1)S(1)}, bf16[768,1536]{1,0:T(8,128)(2,1)}, u32[]{:S(2)}) copy-start(bf16[768,1536]{1,0:T(8,128)(2,1)} %param.10) | copy-start | bytes 7077892
  2.6 6.5 %collective-permute-start.2 = (bf16[3,16,768]{2,1,0:T(8,128)(2,1)S(1)}, bf16[3,16,768]{2,1,0:T(8,128)(2,1)S(1)}, u32[]{:S(2)}, u32[]{:S(2)}) collective-permute-start(bf16[3,16,768]{2,1,0:T(8,128)(2,1)S(1)} %pad_maximum_fusion.29), channel_id=1, source_target_pairs={{0,24},{8,16},{16,8},{24,0},{1,25},{9,17},{17,9},{25,1},{2,26},{10... | collective-permute-start | bytes 221192 | tf_op jit(solution)/shard_map/ppermute | solution.py:42
  6.6 4.4 %collective-permute-start = (bf16[3,16,768]{2,1,0:T(8,128)(2,1)S(1)}, bf16[3,16,768]{2,1,0:T(8,128)(2,1)S(1)}, u32[]{:S(2)}, u32[]{:S(2)}) collective-permute-start(bf16[3,16,768]{2,1,0:T(8,128)(2,1)S(1)} %pad_maximum_fusion.27), channel_id=1, source_target_pairs={{0,8},{8,0},{16,24},{24,16},{1,9},{9,1},{17,25},{25,17},{2,10},{10... | collective-permute-start | bytes 221192 | tf_op jit(solution)/shard_map/ppermute | solution.py:42
  7.2 4.4 %collective-permute-start.1 = (bf16[3,16,768]{2,1,0:T(8,128)(2,1)S(1)}, bf16[3,16,768]{2,1,0:T(8,128)(2,1)S(1)}, u32[]{:S(2)}, u32[]{:S(2)}) collective-permute-start(bf16[3,16,768]{2,1,0:T(8,128)(2,1)S(1)} %pad_maximum_fusion.28), channel_id=1, source_target_pairs={{0,16},{8,24},{16,0},{24,8},{1,17},{9,25},{17,1},{25,9},{2,18},{10... | collective-permute-start | bytes 221192 | tf_op jit(solution)/shard_map/ppermute | solution.py:42
  11.6 8.8 %collective-permute-start.4 = (bf16[1,4,16,768]{3,2,1,0:T(8,128)(2,1)S(1)}, bf16[1,4,16,768]{3,2,1,0:T(8,128)(2,1)S(1)}, u32[]{:S(2)}, u32[]{:S(2)}) collective-permute-start(bf16[1,4,16,768]{3,2,1,0:T(8,128)(2,1)S(1)} %get-tuple-element.75), channel_id=1, source_target_pairs={{0,4},{1,5},{2,6},{3,7},{4,0},{5,1},{6,2},{7,3},{8,12},{9,13},{10,... | collective-permute-start | bytes 294920 | tf_op jit(solution)/shard_map/ppermute | solution.py:42
  14.3 7.2 %collective-permute-start.3 = (bf16[1,4,16,768]{3,2,1,0:T(8,128)(2,1)S(1)}, bf16[1,4,16,768]{3,2,1,0:T(8,128)(2,1)S(1)}, u32[]{:S(2)}, u32[]{:S(2)}) collective-permute-start(bf16[1,4,16,768]{3,2,1,0:T(8,128)(2,1)S(1)} %get-tuple-element.75), channel_id=1, source_target_pairs={{0,2},{1,3},{2,4},{3,5},{4,6},{5,7},{6,0},{7,1},{8,10},{9,11},{10,... | collective-permute-start | bytes 294920 | tf_op jit(solution)/shard_map/ppermute | solution.py:42
  15.9 6.0 %collective-permute-start.5 = (bf16[1,4,16,768]{3,2,1,0:T(8,128)(2,1)S(1)}, bf16[1,4,16,768]{3,2,1,0:T(8,128)(2,1)S(1)}, u32[]{:S(2)}, u32[]{:S(2)}) collective-permute-start(bf16[1,4,16,768]{3,2,1,0:T(8,128)(2,1)S(1)} %get-tuple-element.75), channel_id=1, source_target_pairs={{0,6},{1,7},{2,0},{3,1},{4,2},{5,3},{6,4},{7,5},{8,14},{9,15},{10,... | collective-permute-start | bytes 294920 | tf_op jit(solution)/shard_map/ppermute | solution.py:42
  21.9 5.4 %collective-permute-start.6 = (bf16[1,4,4,16,768]{4,3,2,1,0:T(8,128)(2,1)S(1)}, bf16[1,4,4,16,768]{4,3,2,1,0:T(8,128)(2,1)S(1)}, u32[]{:S(2)}, u32[]{:S(2)}) collective-permute-start(bf16[1,4,4,16,768]{4,3,2,1,0:T(8,128)(2,1)S(1)} %get-tuple-element.67), channel_id=1, source_target_pairs={{0,1},{1,0},{2,3},{3,2},{4,5},{5,4},{6,7},{7,6},{8,9},{9,8},{10,11... | collective-permute-start | bytes 1179656 | tf_op jit(solution)/shard_map/ppermute | solution.py:42
  22.1 9.2 %collective-permute-start.21 = (bf16[2,4,16,768]{3,2,0,1:T(8,128)(2,1)S(1)}, bf16[2,4,16,768]{3,2,0,1:T(8,128)(2,1)S(1)}, u32[]{:S(2)}, u32[]{:S(2)}) collective-permute-start(bf16[2,4,16,768]{3,2,0,1:T(8,128)(2,1)S(1)} %pad_maximum_fusion.24), channel_id=1, source_target_pairs={{0,6},{1,7},{2,0},{3,1},{4,2},{5,3},{6,4},{7,5},{8,14},{9,15},{10,... | collective-permute-start | bytes 589832 | tf_op jit(solution)/shard_map/ppermute | solution.py:42
  25.2 18.3 %collective-permute-start.20 = (bf16[2,4,16,768]{3,2,0,1:T(8,128)(2,1)S(1)}, bf16[2,4,16,768]{3,2,0,1:T(8,128)(2,1)S(1)}, u32[]{:S(2)}, u32[]{:S(2)}) collective-permute-start(bf16[2,4,16,768]{3,2,0,1:T(8,128)(2,1)S(1)} %pad_maximum_fusion.24), channel_id=1, source_target_pairs={{0,4},{1,5},{2,6},{3,7},{4,0},{5,1},{6,2},{7,3},{8,12},{9,13},{10,... | collective-permute-start | bytes 589832 | tf_op jit(solution)/shard_map/ppermute | solution.py:42
  25.4 18.1 %collective-permute-start.19 = (bf16[2,4,16,768]{3,2,0,1:T(8,128)(2,1)S(1)}, bf16[2,4,16,768]{3,2,0,1:T(8,128)(2,1)S(1)}, u32[]{:S(2)}, u32[]{:S(2)}) collective-permute-start(bf16[2,4,16,768]{3,2,0,1:T(8,128)(2,1)S(1)} %pad_maximum_fusion.24), channel_id=1, source_target_pairs={{0,2},{1,3},{2,4},{3,5},{4,6},{5,7},{6,0},{7,1},{8,10},{9,11},{10,... | collective-permute-start | bytes 589832 | tf_op jit(solution)/shard_map/ppermute | solution.py:42
  28.8 17.3 %copy-start.2 = (f32[4,128,1536]{2,1,0:T(8,128)}, f32[4,128,1536]{2,1,0:T(8,128)S(1)}, u32[]{:S(2)}) copy-start(f32[4,128,1536]{2,1,0:T(8,128)S(1)} %get-tuple-element.91) | copy-start | bytes 9437188
  28.9 1.8 %copy-start.6 = (s32[16]{0:T(128)S(1)}, s32[16]{0:T(128)}, u32[]{:S(2)}) copy-start(s32[16]{0:T(128)} %param.12) | copy-start | bytes 196
  28.9 1.8 %copy-start.7 = (s32[16]{0:T(128)S(1)}, s32[16]{0:T(128)}, u32[]{:S(2)}) copy-start(s32[16]{0:T(128)} %param.13) | copy-start | bytes 196
  29.0 17.1 %collective-permute-start.9 = (bf16[2,1,64,1536]{3,2,1,0:T(8,128)(2,1)S(1)}, bf16[2,1,64,1536]{3,2,1,0:T(8,128)(2,1)S(1)}, u32[]{:S(2)}, u32[]{:S(2)}) collective-permute-start(bf16[2,1,64,1536]{3,2,1,0:T(8,128)(2,1)S(1)} %pad_maximum_fusion.9), channel_id=1, source_target_pairs={{0,8},{8,0},{16,24},{24,16},{1,9},{9,1},{17,25},{25,17},{2,10},{10... | collective-permute-start | bytes 1179656 | tf_op jit(solution)/shard_map/ppermute | solution.py:42
  44.6 4.5 %collective-permute-start.22 = (bf16[2,4,4,16,768]{4,3,0,1,2:T(8,128)(2,1)}, bf16[2,4,4,16,768]{4,3,0,1,2:T(8,128)(2,1)}, u32[]{:S(2)}, u32[]{:S(2)}) collective-permute-start(bf16[2,4,4,16,768]{4,3,0,1,2:T(8,128)(2,1)} %pad_maximum_fusion.4), channel_id=1, source_target_pairs={{0,1},{1,0},{2,3},{3,2},{4,5},{5,4},{6,7},{7,6},{8,9},{9,8},{10,11... | collective-permute-start | bytes 2359304 | tf_op jit(solution)/shard_map/ppermute | solution.py:42
  45.3 12.1 %collective-permute-start.7 = (bf16[2,1,64,1536]{3,2,1,0:T(8,128)(2,1)}, bf16[2,1,64,1536]{3,2,1,0:T(8,128)(2,1)S(1)}, u32[]{:S(2)}, u32[]{:S(2)}) collective-permute-start(bf16[2,1,64,1536]{3,2,1,0:T(8,128)(2,1)} %pad_maximum_fusion.8), channel_id=1, source_target_pairs={{0,16},{8,24},{16,0},{24,8},{1,17},{9,25},{17,1},{25,9},{2,18},{10... | collective-permute-start | bytes 1179656 | tf_op jit(solution)/shard_map/ppermute | solution.py:42
  46.1 0.8 copy-start.4
  47.0 14.4 %collective-permute-start.10 = (bf16[1,64,1536]{2,1,0:T(8,128)(2,1)}, bf16[1,64,1536]{2,1,0:T(8,128)(2,1)}, u32[]{:S(2)}, u32[]{:S(2)}) collective-permute-start(bf16[1,64,1536]{2,1,0:T(8,128)(2,1)} %fusion.56), channel_id=1, source_target_pairs={{0,16},{8,24},{16,0},{24,8},{1,17},{9,25},{17,1},{25,9},{2,18},{10... | collective-permute-start | bytes 589832 | tf_op jit(solution)/shard_map/ppermute | solution.py:42
  50.6 10.8 %copy-start.5 = (bf16[2,1,64,1536]{3,2,1,0:T(8,128)(2,1)S(1)}, bf16[2,1,64,1536]{3,2,1,0:T(8,128)(2,1)}, u32[]{:S(2)}) copy-start(bf16[2,1,64,1536]{3,2,1,0:T(8,128)(2,1)} %copy-done.4) | copy-start | bytes 1179652
  62.8 6.6 %collective-permute-start.8 = (bf16[1,64,1536]{2,1,0:T(8,128)(2,1)S(1)}, bf16[1,64,1536]{2,1,0:T(8,128)(2,1)S(1)}, u32[]{:S(2)}, u32[]{:S(2)}) collective-permute-start(bf16[1,64,1536]{2,1,0:T(8,128)(2,1)S(1)} %get-tuple-element.31), channel_id=1, source_target_pairs={{0,8},{8,0},{16,24},{24,16},{1,9},{9,1},{17,25},{25,17},{2,10},{10... | collective-permute-start | bytes 589832 | tf_op jit(solution)/shard_map/ppermute | solution.py:42
  64.6 7.8 %collective-permute-start.12 = (bf16[64,1536]{1,0:T(8,128)(2,1)S(1)}, bf16[64,1536]{1,0:T(8,128)(2,1)S(1)}, u32[]{:S(2)}, u32[]{:S(2)}) collective-permute-start(bf16[64,1536]{1,0:T(8,128)(2,1)S(1)} %select_convert_fusion.4), channel_id=1, source_target_pairs={{0,16},{8,24},{16,0},{24,8},{1,17},{9,25},{17,1},{25,9},{2,18},{10... | collective-permute-start | bytes 589832 | tf_op jit(solution)/shard_map/ppermute | solution.py:42
  70.8 7.9 %collective-permute-start.11 = (bf16[64,1536]{1,0:T(8,128)(2,1)S(1)}, bf16[64,1536]{1,0:T(8,128)(2,1)S(1)}, u32[]{:S(2)}, u32[]{:S(2)}) collective-permute-start(bf16[64,1536]{1,0:T(8,128)(2,1)S(1)} %select_convert_fusion.5), channel_id=1, source_target_pairs={{0,8},{8,0},{16,24},{24,16},{1,9},{9,1},{17,25},{25,17},{2,10},{10... | collective-permute-start | bytes 589832 | tf_op jit(solution)/shard_map/ppermute | solution.py:42
  72.5 14.6 %collective-permute-start.13 = (bf16[2,64,1536]{2,1,0:T(8,128)(2,1)S(1)}, bf16[2,64,1536]{2,1,0:T(8,128)(2,1)S(1)}, u32[]{:S(2)}, u32[]{:S(2)}) collective-permute-start(bf16[2,64,1536]{2,1,0:T(8,128)(2,1)S(1)} %pad_maximum_fusion.11), channel_id=1, source_target_pairs={{0,8},{8,0},{16,24},{24,16},{1,9},{9,1},{17,25},{25,17},{2,10},{10... | collective-permute-start | bytes 1179656 | tf_op jit(solution)/shard_map/ppermute | solution.py:42
  78.7 12.1 %collective-permute-start.14 = (bf16[2,64,1536]{2,1,0:T(8,128)(2,1)S(1)}, bf16[2,64,1536]{2,1,0:T(8,128)(2,1)S(1)}, u32[]{:S(2)}, u32[]{:S(2)}) collective-permute-start(bf16[2,64,1536]{2,1,0:T(8,128)(2,1)S(1)} %pad_maximum_fusion.13), channel_id=1, source_target_pairs={{0,16},{8,24},{16,0},{24,8},{1,17},{9,25},{17,1},{25,9},{2,18},{10... | collective-permute-start | bytes 1179656 | tf_op jit(solution)/shard_map/ppermute | solution.py:42
  79.6 1.7 %copy-start.3 = (bf16[1536,768]{1,0:T(8,128)(2,1)S(1)}, bf16[1536,768]{1,0:T(8,128)(2,1)}, u32[]{:S(2)}) copy-start(bf16[1536,768]{1,0:T(8,128)(2,1)} %param.11) | copy-start | bytes 7077892
  83.0 19.9 %collective-permute-start.23 = (bf16[2,2,64,1536]{3,2,1,0:T(8,128)(2,1)S(1)}, bf16[2,2,64,1536]{3,2,1,0:T(8,128)(2,1)S(1)}, u32[]{:S(2)}, u32[]{:S(2)}) collective-permute-start(bf16[2,2,64,1536]{3,2,1,0:T(8,128)(2,1)S(1)} %pad_maximum_fusion.5), channel_id=1, source_target_pairs={{0,16},{8,24},{16,0},{24,8},{1,17},{9,25},{17,1},{25,9},{2,18},{10... | collective-permute-start | bytes 2359304 | tf_op jit(solution)/shard_map/ppermute | solution.py:42
  84.4 17.3 %collective-permute-start.25 = (bf16[2,2,64,1536]{3,2,1,0:T(8,128)(2,1)S(1)}, bf16[2,2,64,1536]{3,2,1,0:T(8,128)(2,1)S(1)}, u32[]{:S(2)}, u32[]{:S(2)}) collective-permute-start(bf16[2,2,64,1536]{3,2,1,0:T(8,128)(2,1)S(1)} %pad_maximum_fusion.6), channel_id=1, source_target_pairs={{0,8},{8,0},{16,24},{24,16},{1,9},{9,1},{17,25},{25,17},{2,10},{10... | collective-permute-start | bytes 2359304 | tf_op jit(solution)/shard_map/ppermute | solution.py:42
  92.4 1.8 %collective-permute-start.15 = (bf16[4,4,16,768]{3,2,1,0:T(8,128)(2,1)S(1)}, bf16[4,4,16,768]{3,2,1,0:T(8,128)(2,1)S(1)}, u32[]{:S(2)}, u32[]{:S(2)}) collective-permute-start(bf16[4,4,16,768]{3,2,1,0:T(8,128)(2,1)S(1)} %fusion.54), channel_id=1, source_target_pairs={{0,1},{1,0},{2,3},{3,2},{4,5},{5,4},{6,7},{7,6},{8,9},{9,8},{10,11... | collective-permute-start | bytes 1179656 | tf_op jit(solution)/shard_map/ppermute | solution.py:42
  94.3 10.3 %collective-permute-start.16 = (bf16[4,16,768]{2,1,0:T(8,128)(2,1)S(1)}, bf16[4,16,768]{2,1,0:T(8,128)(2,1)S(1)}, u32[]{:S(2)}, u32[]{:S(2)}) collective-permute-start(bf16[4,16,768]{2,1,0:T(8,128)(2,1)S(1)} %get-tuple-element.52), channel_id=1, source_target_pairs={{0,6},{1,7},{2,0},{3,1},{4,2},{5,3},{6,4},{7,5},{8,14},{9,15},{10,... | collective-permute-start | bytes 294920 | tf_op jit(solution)/shard_map/ppermute | solution.py:42
  94.4 10.2 %collective-permute-start.18 = (bf16[4,16,768]{2,1,0:T(8,128)(2,1)S(1)}, bf16[4,16,768]{2,1,0:T(8,128)(2,1)S(1)}, u32[]{:S(2)}, u32[]{:S(2)}) collective-permute-start(bf16[4,16,768]{2,1,0:T(8,128)(2,1)S(1)} %get-tuple-element.53), channel_id=1, source_target_pairs={{0,2},{1,3},{2,4},{3,5},{4,6},{5,7},{6,0},{7,1},{8,10},{9,11},{10,... | collective-permute-start | bytes 294920 | tf_op jit(solution)/shard_map/ppermute | solution.py:42
  96.4 9.9 %collective-permute-start.17 = (bf16[4,16,768]{2,1,0:T(8,128)(2,1)S(1)}, bf16[4,16,768]{2,1,0:T(8,128)(2,1)S(1)}, u32[]{:S(2)}, u32[]{:S(2)}) collective-permute-start(bf16[4,16,768]{2,1,0:T(8,128)(2,1)S(1)} %get-tuple-element.54), channel_id=1, source_target_pairs={{0,4},{1,5},{2,6},{3,7},{4,0},{5,1},{6,2},{7,3},{8,12},{9,13},{10,... | collective-permute-start | bytes 294920 | tf_op jit(solution)/shard_map/ppermute | solution.py:42
  101.8 8.8 %collective-permute-start.26 = (bf16[2,64,1536]{2,1,0:T(8,128)(2,1)S(1)}, bf16[2,64,1536]{2,1,0:T(8,128)(2,1)S(1)}, u32[]{:S(2)}, u32[]{:S(2)}) collective-permute-start(bf16[2,64,1536]{2,1,0:T(8,128)(2,1)S(1)} %fusion.23), channel_id=1, source_target_pairs={{0,16},{8,24},{16,0},{24,8},{1,17},{9,25},{17,1},{25,9},{2,18},{10... | collective-permute-start | bytes 1179656 | tf_op jit(solution)/shard_map/ppermute | solution.py:42
  103.0 7.8 %collective-permute-start.24 = (bf16[2,64,1536]{2,1,0:T(8,128)(2,1)S(1)}, bf16[2,64,1536]{2,1,0:T(8,128)(2,1)S(1)}, u32[]{:S(2)}, u32[]{:S(2)}) collective-permute-start(bf16[2,64,1536]{2,1,0:T(8,128)(2,1)S(1)} %fusion.21), channel_id=1, source_target_pairs={{0,8},{8,0},{16,24},{24,16},{1,9},{9,1},{17,25},{25,17},{2,10},{10... | collective-permute-start | bytes 1179656 | tf_op jit(solution)/shard_map/ppermute | solution.py:42
  112.0 8.8 %collective-permute-start.28 = (bf16[64,1536]{1,0:T(8,128)(2,1)S(1)}, bf16[64,1536]{1,0:T(8,128)(2,1)S(1)}, u32[]{:S(2)}, u32[]{:S(2)}) collective-permute-start(bf16[64,1536]{1,0:T(8,128)(2,1)S(1)} %fusion.61), channel_id=1, source_target_pairs={{0,16},{8,24},{16,0},{24,8},{1,17},{9,25},{17,1},{25,9},{2,18},{10... | collective-permute-start | bytes 589832 | tf_op jit(solution)/shard_map/ppermute | solution.py:42
  113.3 7.1 %collective-permute-start.27 = (bf16[64,1536]{1,0:T(8,128)(2,1)S(1)}, bf16[64,1536]{1,0:T(8,128)(2,1)S(1)}, u32[]{:S(2)}, u32[]{:S(2)}) collective-permute-start(bf16[64,1536]{1,0:T(8,128)(2,1)S(1)} %fusion.63), channel_id=1, source_target_pairs={{0,8},{8,0},{16,24},{24,16},{1,9},{9,1},{17,25},{25,17},{2,10},{10... | collective-permute-start | bytes 589832 | tf_op jit(solution)/shard_map/ppermute | solution.py:42
  120.5 16.5 %collective-permute-start.30 = (bf16[2,64,1536]{2,1,0:T(8,128)(2,1)S(1)}, bf16[2,64,1536]{2,1,0:T(8,128)(2,1)S(1)}, u32[]{:S(2)}, u32[]{:S(2)}) collective-permute-start(bf16[2,64,1536]{2,1,0:T(8,128)(2,1)S(1)} %pad_maximum_fusion.19), channel_id=1, source_target_pairs={{0,16},{8,24},{16,0},{24,8},{1,17},{9,25},{17,1},{25,9},{2,18},{10... | collective-permute-start | bytes 1179656 | tf_op jit(solution)/shard_map/ppermute | solution.py:42
  120.9 16.1 %collective-permute-start.29 = (bf16[2,64,1536]{2,1,0:T(8,128)(2,1)S(1)}, bf16[2,64,1536]{2,1,0:T(8,128)(2,1)S(1)}, u32[]{:S(2)}, u32[]{:S(2)}) collective-permute-start(bf16[2,64,1536]{2,1,0:T(8,128)(2,1)S(1)} %pad_maximum_fusion.17), channel_id=1, source_target_pairs={{0,8},{8,0},{16,24},{24,16},{1,9},{9,1},{17,25},{25,17},{2,10},{10... | collective-permute-start | bytes 1179656 | tf_op jit(solution)/shard_map/ppermute | solution.py:42
  123.3 10.8 %collective-permute-start.38 = (bf16[64,1536]{1,0:T(8,128)(2,1)S(1)}, bf16[64,1536]{1,0:T(8,128)(2,1)S(1)}, u32[]{:S(2)}, u32[]{:S(2)}) collective-permute-start(bf16[64,1536]{1,0:T(8,128)(2,1)S(1)} %select_convert_fusion.1), channel_id=1, source_target_pairs={{0,8},{8,0},{16,24},{24,16},{1,9},{9,1},{17,25},{25,17},{2,10},{10... | collective-permute-start | bytes 589832 | tf_op jit(solution)/shard_map/ppermute | solution.py:42
  123.6 11.0 %collective-permute-start.39 = (bf16[64,1536]{1,0:T(8,128)(2,1)S(1)}, bf16[64,1536]{1,0:T(8,128)(2,1)S(1)}, u32[]{:S(2)}, u32[]{:S(2)}) collective-permute-start(bf16[64,1536]{1,0:T(8,128)(2,1)S(1)} %select_convert_fusion), channel_id=1, source_target_pairs={{0,16},{8,24},{16,0},{24,8},{1,17},{9,25},{17,1},{25,9},{2,18},{10... | collective-permute-start | bytes 589832 | tf_op jit(solution)/shard_map/ppermute | solution.py:42
  134.2 7.8 %collective-permute-start.41 = (bf16[2,64,1536]{2,1,0:T(8,128)(2,1)S(1)}, bf16[2,64,1536]{2,1,0:T(8,128)(2,1)S(1)}, u32[]{:S(2)}, u32[]{:S(2)}) collective-permute-start(bf16[2,64,1536]{2,1,0:T(8,128)(2,1)S(1)} %pad_maximum_fusion.23), channel_id=1, source_target_pairs={{0,16},{8,24},{16,0},{24,8},{1,17},{9,25},{17,1},{25,9},{2,18},{10... | collective-permute-start | bytes 1179656 | tf_op jit(solution)/shard_map/ppermute | solution.py:42
  134.6 8.1 %collective-permute-start.40 = (bf16[2,64,1536]{2,1,0:T(8,128)(2,1)S(1)}, bf16[2,64,1536]{2,1,0:T(8,128)(2,1)S(1)}, u32[]{:S(2)}, u32[]{:S(2)}) collective-permute-start(bf16[2,64,1536]{2,1,0:T(8,128)(2,1)S(1)} %pad_maximum_fusion.22), channel_id=1, source_target_pairs={{0,8},{8,0},{16,24},{24,16},{1,9},{9,1},{17,25},{25,17},{2,10},{10... | collective-permute-start | bytes 1179656 | tf_op jit(solution)/shard_map/ppermute | solution.py:42
  138.6 4.3 %collective-permute-start.31 = (bf16[4,4,16,768]{3,2,0,1:T(8,128)(2,1)S(1)}, bf16[4,4,16,768]{3,2,0,1:T(8,128)(2,1)S(1)}, u32[]{:S(2)}, u32[]{:S(2)}) collective-permute-start(bf16[4,4,16,768]{3,2,0,1:T(8,128)(2,1)S(1)} %fusion.55), channel_id=1, source_target_pairs={{0,1},{1,0},{2,3},{3,2},{4,5},{5,4},{6,7},{7,6},{8,9},{9,8},{10,11... | collective-permute-start | bytes 1179656 | tf_op jit(solution)/shard_map/ppermute | solution.py:42
  143.0 5.7 %collective-permute-start.32 = (bf16[4,16,768]{2,1,0:T(8,128)(2,1)S(1)}, bf16[4,16,768]{2,1,0:T(8,128)(2,1)S(1)}, u32[]{:S(2)}, u32[]{:S(2)}) collective-permute-start(bf16[4,16,768]{2,1,0:T(8,128)(2,1)S(1)} %get-tuple-element.55), channel_id=1, source_target_pairs={{0,6},{1,7},{2,0},{3,1},{4,2},{5,3},{6,4},{7,5},{8,14},{9,15},{10,... | collective-permute-start | bytes 294920 | tf_op jit(solution)/shard_map/ppermute | solution.py:42
  143.1 7.9 %collective-permute-start.34 = (bf16[4,16,768]{2,1,0:T(8,128)(2,1)S(1)}, bf16[4,16,768]{2,1,0:T(8,128)(2,1)S(1)}, u32[]{:S(2)}, u32[]{:S(2)}) collective-permute-start(bf16[4,16,768]{2,1,0:T(8,128)(2,1)S(1)} %get-tuple-element.56), channel_id=1, source_target_pairs={{0,2},{1,3},{2,4},{3,5},{4,6},{5,7},{6,0},{7,1},{8,10},{9,11},{10,... | collective-permute-start | bytes 294920 | tf_op jit(solution)/shard_map/ppermute | solution.py:42
  145.1 8.0 %collective-permute-start.33 = (bf16[4,16,768]{2,1,0:T(8,128)(2,1)S(1)}, bf16[4,16,768]{2,1,0:T(8,128)(2,1)S(1)}, u32[]{:S(2)}, u32[]{:S(2)}) collective-permute-start(bf16[4,16,768]{2,1,0:T(8,128)(2,1)S(1)} %get-tuple-element.57), channel_id=1, source_target_pairs={{0,4},{1,5},{2,6},{3,7},{4,0},{5,1},{6,2},{7,3},{8,12},{9,13},{10,... | collective-permute-start | bytes 294920 | tf_op jit(solution)/shard_map/ppermute | solution.py:42
  153.2 7.2 %collective-permute-start.35 = (bf16[2,16,768]{2,1,0:T(8,128)(2,1)S(1)}, bf16[2,16,768]{2,1,0:T(8,128)(2,1)S(1)}, u32[]{:S(2)}, u32[]{:S(2)}) collective-permute-start(bf16[2,16,768]{2,1,0:T(8,128)(2,1)S(1)} %get-tuple-element.71), channel_id=1, source_target_pairs={{0,8},{8,0},{16,24},{24,16},{1,9},{9,1},{17,25},{25,17},{2,10},{10... | collective-permute-start | bytes 147464 | tf_op jit(solution)/shard_map/ppermute | solution.py:42
  154.9 5.5 %collective-permute-start.37 = (bf16[2,16,768]{2,1,0:T(8,128)(2,1)S(1)}, bf16[2,16,768]{2,1,0:T(8,128)(2,1)S(1)}, u32[]{:S(2)}, u32[]{:S(2)}) collective-permute-start(bf16[2,16,768]{2,1,0:T(8,128)(2,1)S(1)} %get-tuple-element.72), channel_id=1, source_target_pairs={{0,24},{8,16},{16,8},{24,0},{1,25},{9,17},{17,9},{25,1},{2,26},{10... | collective-permute-start | bytes 147464 | tf_op jit(solution)/shard_map/ppermute | solution.py:42
  156.0 4.4 %collective-permute-start.36 = (bf16[2,16,768]{2,1,0:T(8,128)(2,1)S(1)}, bf16[2,16,768]{2,1,0:T(8,128)(2,1)S(1)}, u32[]{:S(2)}, u32[]{:S(2)}) collective-permute-start(bf16[2,16,768]{2,1,0:T(8,128)(2,1)S(1)} %get-tuple-element.73), channel_id=1, source_target_pairs={{0,16},{8,24},{16,0},{24,8},{1,17},{9,25},{17,1},{25,9},{2,18},{10... | collective-permute-start | bytes 147464 | tf_op jit(solution)/shard_map/ppermute | solution.py:42
  156.7 5.5 %copy-start.1 = (bf16[768,1536]{1,0:T(8,128)(2,1)S(1)}, bf16[768,1536]{1,0:T(8,128)(2,1)}, u32[]{:S(2)}) copy-start(bf16[768,1536]{1,0:T(8,128)(2,1)} %param.10) | copy-start | bytes 7077892

commit v9 on v5

--- a/solution.py
+++ b/solution.py
@@ -193,7 +193,7 @@
     both = after(both, out_near)
     dact_held = spread([s * v[0] for (_, s), v in zip(pairs, both)])
     dact_all = everywhere(dact_held)
-    back_grad = after([v[1] for v in both], dact_held)
+    back_grad = [v[1] for v in both]
     grad_all = everywhere(spread([s * v for (_, s), v in zip(pairs, back_grad)]))
     summed = jnp.stack([down_chips(out_near), down_chips(down_cores(dact_all))], axis=1)
     cols = jnp.stack(

time: 160 us -> 158 us (0.988)
  waiting for transfers between devices: 70 us -> 67.4 us
    ppermute x42, waiting for transfers between devices: 70 us -> 67.4 us  [shift(): return lax.ppermute(value, axis, pairs)]
  transfers between devices with their start and end apart: 42 -> 42, of which waited for: 24 -> 23; matrix products, arithmetic and copies ran while one was open for 20% -> 20% of each run, Pallas kernels for 0% -> 0%
where the time goes in v9:
time: 158 us; the launch traced here: 157 us
  waiting for transfers between devices  67.4 us (43%)
  starting transfers between devices  48.5 us (31%)
  matrix products  25.4 us (16%)
  other arithmetic  8.71 us (6%)
  local copies, waits for them, and re-layouts  5.74 us (4%)
    ppermute x42, waiting for transfers between devices, shift(): return lax.ppermute(value, axis, pairs)  67.4 us
    ppermute x42, starting transfers between devices, shift(): return lax.ppermute(value, axis, pairs)  48.5 us
    dot_general x18, matrix products, dot(): return jnp.dot(a, b, preferred_element_type=jnp.float32)  15.2 us
    dot_general x8, matrix products, back(): lax.dot_general(rows, w_out, (((1,), (1,)), ((), ())), preferred_element_...  6.66 us
    dot_general x1, matrix products, local(): lax.dot_general(tok_cols.reshape(dp_count * group_rows, own_cols), grad_a...  3.6 us
  transfers between devices with their start and end apart: 42, of which 23 were waited for; matrix products, arithmetic and copies ran while one was open for 20% of the time, Pallas kernels for 0%

profile of v9, /device:TPU:0, one launch (start us, length us, event | category | flops | bytes accessed | tf_op | source)
XLA Modules:
  0.0 157.2 jit_solution(12749173346275266450)
XLA Ops:
  0.7 0.9 dynamic-slice_bitcast_fusion.11
  1.7 0.9 dynamic-slice_bitcast_fusion
  2.6 4.0 %collective-permute-start.2 = (bf16[3,16,768]{2,1,0:T(8,128)(2,1)S(1)}, bf16[3,16,768]{2,1,0:T(8,128)(2,1)S(1)}, u32[]{:S(2)}, u32[]{:S(2)}) collective-permute-start(bf16[3,16,768]{2,1,0:T(8,128)(2,1)S(1)} %pad_maximum_fusion.29), channel_id=1, source_target_pairs={{0,24},{8,16},{16,8},{24,0},{1,25},{9,17},{17,9},{25,1},{2,26},{10... | collective-permute-start | bytes 221192 | tf_op jit(solution)/shard_map/ppermute | solution.py:42
  7.5 1.3 fusion.93
  8.9 2.1 %collective-permute-done.1 = bf16[3,16,768]{2,1,0:T(8,128)(2,1)S(1)} collective-permute-done((bf16[3,16,768]{2,1,0:T(8,128)(2,1)S(1)}, bf16[3,16,768]{2,1,0:T(8,128)(2,1)S(1)}, u32[]{:S(2)}, u32[]{:S(2)}) %collective-permute-start.1) | collective-permute-done | bytes 73760 | tf_op jit(solution)/shard_map/ppermute | solution.py:42
  11.6 3.7 %collective-permute-start.5 = (bf16[1,4,16,768]{3,2,1,0:T(8,128)(2,1)S(1)}, bf16[1,4,16,768]{3,2,1,0:T(8,128)(2,1)S(1)}, u32[]{:S(2)}, u32[]{:S(2)}) collective-permute-start(bf16[1,4,16,768]{3,2,1,0:T(8,128)(2,1)S(1)} %get-tuple-element.54), channel_id=1, source_target_pairs={{0,6},{1,7},{2,0},{3,1},{4,2},{5,3},{6,4},{7,5},{8,14},{9,15},{10,... | collective-permute-start | bytes 294920 | tf_op jit(solution)/shard_map/ppermute | solution.py:42
  15.3 1.0 collective-permute-start.3
  16.3 2.1 %collective-permute-done.5 = bf16[1,4,16,768]{3,2,1,0:T(8,128)(2,1)S(1)} collective-permute-done((bf16[1,4,16,768]{3,2,1,0:T(8,128)(2,1)S(1)}, bf16[1,4,16,768]{3,2,1,0:T(8,128)(2,1)S(1)}, u32[]{:S(2)}, u32[]{:S(2)}) %collective-permute-start.5) | collective-permute-done | bytes 98336 | tf_op jit(solution)/shard_map/ppermute | solution.py:42
  18.4 5.1 %collective-permute-done.4 = bf16[1,4,16,768]{3,2,1,0:T(8,128)(2,1)S(1)} collective-permute-done((bf16[1,4,16,768]{3,2,1,0:T(8,128)(2,1)S(1)}, bf16[1,4,16,768]{3,2,1,0:T(8,128)(2,1)S(1)}, u32[]{:S(2)}, u32[]{:S(2)}) %collective-permute-start.4) | collective-permute-done | bytes 98336 | tf_op jit(solution)/shard_map/ppermute | solution.py:42
  23.7 1.6 %collective-permute-done.6 = bf16[1,4,4,16,768]{4,3,2,1,0:T(8,128)(2,1)S(1)} collective-permute-done((bf16[1,4,4,16,768]{4,3,2,1,0:T(8,128)(2,1)S(1)}, bf16[1,4,4,16,768]{4,3,2,1,0:T(8,128)(2,1)S(1)}, u32[]{:S(2)}, u32[]{:S(2)}) %collective-permute-start.6) | collective-permute-done | bytes 393248 | tf_op jit(solution)/shard_map/ppermute | solution.py:42
  27.5 1.5 collective-permute-start.21
  29.4 1.9 %collective-permute-start.19 = (bf16[2,4,16,768]{3,2,0,1:T(8,128)(2,1)S(1)}, bf16[2,4,16,768]{3,2,0,1:T(8,128)(2,1)}, u32[]{:S(2)}, u32[]{:S(2)}) collective-permute-start(bf16[2,4,16,768]{3,2,0,1:T(8,128)(2,1)S(1)} %pad_maximum_fusion.24), channel_id=1, source_target_pairs={{0,2},{1,3},{2,4},{3,5},{4,6},{5,7},{6,0},{7,1},{8,10},{9,11},{10,... | collective-permute-start | bytes 589832 | tf_op jit(solution)/shard_map/ppermute | solution.py:42
  31.4 0.8 pad_maximum_fusion.9
  32.1 1.4 collective-permute-start.9
  33.5 0.8 pad_maximum_fusion.8
  35.8 11.5 %collective-permute-done.20 = bf16[2,4,16,768]{3,2,0,1:T(8,128)(2,1)} collective-permute-done((bf16[2,4,16,768]{3,2,0,1:T(8,128)(2,1)S(1)}, bf16[2,4,16,768]{3,2,0,1:T(8,128)(2,1)}, u32[]{:S(2)}, u32[]{:S(2)}) %collective-permute-start.20) | collective-permute-done | bytes 196640 | tf_op jit(solution)/shard_map/ppermute | solution.py:42
  47.3 1.1 pad_maximum_fusion.4
  48.5 1.5 fusion.67
  50.0 1.5 collective-permute-start.10
  51.4 1.5 fusion.66
  53.6 3.8 %collective-permute-done.10 = bf16[1,64,1536]{2,1,0:T(8,128)(2,1)S(1)} collective-permute-done((bf16[1,64,1536]{2,1,0:T(8,128)(2,1)S(1)}, bf16[1,64,1536]{2,1,0:T(8,128)(2,1)S(1)}, u32[]{:S(2)}, u32[]{:S(2)}) %collective-permute-start.10) | collective-permute-done | bytes 196640 | tf_op jit(solution)/shard_map/ppermute | solution.py:42
  57.3 1.5 select_convert_fusion.6
  58.9 1.5 collective-permute-start.12
  60.5 1.5 select_convert_fusion.7
  62.9 2.6 %collective-permute-done.12 = bf16[64,1536]{1,0:T(8,128)(2,1)S(1)} collective-permute-done((bf16[64,1536]{1,0:T(8,128)(2,1)S(1)}, bf16[64,1536]{1,0:T(8,128)(2,1)S(1)}, u32[]{:S(2)}, u32[]{:S(2)}) %collective-permute-start.12) | collective-permute-done | bytes 196640 | tf_op jit(solution)/shard_map/ppermute | solution.py:42
  65.5 1.4 collective-permute-start.13
  66.9 2.7 %collective-permute-done.11 = bf16[64,1536]{1,0:T(8,128)(2,1)S(1)} collective-permute-done((bf16[64,1536]{1,0:T(8,128)(2,1)S(1)}, bf16[64,1536]{1,0:T(8,128)(2,1)S(1)}, u32[]{:S(2)}, u32[]{:S(2)}) %collective-permute-start.11) | collective-permute-done | bytes 196640 | tf_op jit(solution)/shard_map/ppermute | solution.py:42
  70.3 1.5 copy-done.1
  71.8 0.8 convolution_bitcast_fusion.6
  72.6 0.8 convolution_bitcast_fusion.4
  73.5 0.8 fusion.11
  75.4 0.8 fusion.9
  76.8 0.8 fusion.15
  78.1 0.8 fusion.13
  79.7 2.1 %collective-permute-start.23 = (bf16[2,2,64,1536]{3,2,1,0:T(8,128)(2,1)S(1)}, bf16[2,2,64,1536]{3,2,1,0:T(8,128)(2,1)S(1)}, u32[]{:S(2)}, u32[]{:S(2)}) collective-permute-start(bf16[2,2,64,1536]{3,2,1,0:T(8,128)(2,1)S(1)} %pad_maximum_fusion.5), channel_id=1, source_target_pairs={{0,16},{8,24},{16,0},{24,8},{1,17},{9,25},{17,1},{25,9},{2,18},{10... | collective-permute-start | bytes 2359304 | tf_op jit(solution)/shard_map/ppermute | solution.py:42
  82.5 0.8 convolution_bitcast_fusion.2
  83.5 1.4 fusion
  85.6 0.8 convolution_bitcast_fusion
  87.3 2.1 %collective-permute-start.17 = (bf16[4,16,768]{2,1,0:T(8,128)(2,1)S(1)}, bf16[4,16,768]{2,1,0:T(8,128)(2,1)S(1)}, u32[]{:S(2)}, u32[]{:S(2)}) collective-permute-start(bf16[4,16,768]{2,1,0:T(8,128)(2,1)S(1)} %get-tuple-element.33), channel_id=1, source_target_pairs={{0,4},{1,5},{2,6},{3,7},{4,0},{5,1},{6,2},{7,3},{8,12},{9,13},{10,... | collective-permute-start | bytes 294920 | tf_op jit(solution)/shard_map/ppermute | solution.py:42
  89.4 2.8 %collective-permute-start.16 = (bf16[4,16,768]{2,1,0:T(8,128)(2,1)S(1)}, bf16[4,16,768]{2,1,0:T(8,128)(2,1)S(1)}, u32[]{:S(2)}, u32[]{:S(2)}) collective-permute-start(bf16[4,16,768]{2,1,0:T(8,128)(2,1)S(1)} %get-tuple-element.31), channel_id=1, source_target_pairs={{0,6},{1,7},{2,0},{3,1},{4,2},{5,3},{6,4},{7,5},{8,14},{9,15},{10,... | collective-permute-start | bytes 294920 | tf_op jit(solution)/shard_map/ppermute | solution.py:42
  92.8 1.7 %collective-permute-done.18 = bf16[4,16,768]{2,1,0:T(8,128)(2,1)S(1)} collective-permute-done((bf16[4,16,768]{2,1,0:T(8,128)(2,1)S(1)}, bf16[4,16,768]{2,1,0:T(8,128)(2,1)S(1)}, u32[]{:S(2)}, u32[]{:S(2)}) %collective-permute-start.18) | collective-permute-done | bytes 98336 | tf_op jit(solution)/shard_map/ppermute | solution.py:42
  94.5 3.4 %collective-permute-done.17 = bf16[4,16,768]{2,1,0:T(8,128)(2,1)S(1)} collective-permute-done((bf16[4,16,768]{2,1,0:T(8,128)(2,1)S(1)}, bf16[4,16,768]{2,1,0:T(8,128)(2,1)S(1)}, u32[]{:S(2)}, u32[]{:S(2)}) %collective-permute-start.17) | collective-permute-done | bytes 98336 | tf_op jit(solution)/shard_map/ppermute | solution.py:42
  98.1 2.1 %collective-permute-start.24 = (bf16[2,64,1536]{2,1,0:T(8,128)(2,1)S(1)}, bf16[2,64,1536]{2,1,0:T(8,128)(2,1)S(1)}, u32[]{:S(2)}, u32[]{:S(2)}) collective-permute-start(bf16[2,64,1536]{2,1,0:T(8,128)(2,1)S(1)} %fusion.27), channel_id=1, source_target_pairs={{0,8},{8,0},{16,24},{24,16},{1,9},{9,1},{17,25},{25,17},{2,10},{10... | collective-permute-start | bytes 1179656 | tf_op jit(solution)/shard_map/ppermute | solution.py:42
  100.4 7.4 %collective-permute-done.24 = bf16[2,64,1536]{2,1,0:T(8,128)(2,1)S(1)} collective-permute-done((bf16[2,64,1536]{2,1,0:T(8,128)(2,1)S(1)}, bf16[2,64,1536]{2,1,0:T(8,128)(2,1)S(1)}, u32[]{:S(2)}, u32[]{:S(2)}) %collective-permute-start.24) | collective-permute-done | bytes 393248 | tf_op jit(solution)/shard_map/ppermute | solution.py:42
  107.9 1.5 collective-permute-done.26
  111.1 1.7 %collective-permute-start.27 = (bf16[64,1536]{1,0:T(8,128)(2,1)S(1)}, bf16[64,1536]{1,0:T(8,128)(2,1)S(1)}, u32[]{:S(2)}, u32[]{:S(2)}) collective-permute-start(bf16[64,1536]{1,0:T(8,128)(2,1)S(1)} %get-tuple-element.22), channel_id=1, source_target_pairs={{0,8},{8,0},{16,24},{24,16},{1,9},{9,1},{17,25},{25,17},{2,10},{10... | collective-permute-start | bytes 589832 | tf_op jit(solution)/shard_map/ppermute | solution.py:42
  113.2 1.7 %collective-permute-start.38 = (bf16[64,1536]{1,0:T(8,128)(2,1)S(1)}, bf16[64,1536]{1,0:T(8,128)(2,1)S(1)}, u32[]{:S(2)}, u32[]{:S(2)}) collective-permute-start(bf16[64,1536]{1,0:T(8,128)(2,1)S(1)} %get-tuple-element.21), channel_id=1, source_target_pairs={{0,8},{8,0},{16,24},{24,16},{1,9},{9,1},{17,25},{25,17},{2,10},{10... | collective-permute-start | bytes 589832 | tf_op jit(solution)/shard_map/ppermute | solution.py:42
  115.0 3.1 %collective-permute-done.28 = bf16[64,1536]{1,0:T(8,128)(2,1)S(1)} collective-permute-done((bf16[64,1536]{1,0:T(8,128)(2,1)S(1)}, bf16[64,1536]{1,0:T(8,128)(2,1)S(1)}, u32[]{:S(2)}, u32[]{:S(2)}) %collective-permute-start.28) | collective-permute-done | bytes 196640 | tf_op jit(solution)/shard_map/ppermute | solution.py:42
  118.2 0.8 collective-permute-done.27
  119.0 1.8 %collective-permute-start.30 = (bf16[2,64,1536]{2,1,0:T(8,128)(2,1)S(1)}, bf16[2,64,1536]{2,1,0:T(8,128)(2,1)S(1)}, u32[]{:S(2)}, u32[]{:S(2)}) collective-permute-start(bf16[2,64,1536]{2,1,0:T(8,128)(2,1)S(1)} %pad_maximum_fusion.19), channel_id=1, source_target_pairs={{0,16},{8,24},{16,0},{24,8},{1,17},{9,25},{17,1},{25,9},{2,18},{10... | collective-permute-start | bytes 1179656 | tf_op jit(solution)/shard_map/ppermute | solution.py:42
  120.8 1.5 collective-permute-done.39
  122.4 0.8 collective-permute-done.38
  123.2 1.8 %collective-permute-start.41 = (bf16[2,64,1536]{2,1,0:T(8,128)(2,1)S(1)}, bf16[2,64,1536]{2,1,0:T(8,128)(2,1)S(1)}, u32[]{:S(2)}, u32[]{:S(2)}) collective-permute-start(bf16[2,64,1536]{2,1,0:T(8,128)(2,1)S(1)} %pad_maximum_fusion.23), channel_id=1, source_target_pairs={{0,16},{8,24},{16,0},{24,8},{1,17},{9,25},{17,1},{25,9},{2,18},{10... | collective-permute-start | bytes 1179656 | tf_op jit(solution)/shard_map/ppermute | solution.py:42
  125.0 6.6 %collective-permute-done.29 = bf16[2,64,1536]{2,1,0:T(8,128)(2,1)S(1)} collective-permute-done((bf16[2,64,1536]{2,1,0:T(8,128)(2,1)S(1)}, bf16[2,64,1536]{2,1,0:T(8,128)(2,1)S(1)}, u32[]{:S(2)}, u32[]{:S(2)}) %collective-permute-start.29) | collective-permute-done | bytes 393248 | tf_op jit(solution)/shard_map/ppermute | solution.py:42
  131.7 1.4 fusion.2
  133.3 2.8 %collective-permute-done.40 = bf16[2,64,1536]{2,1,0:T(8,128)(2,1)S(1)} collective-permute-done((bf16[2,64,1536]{2,1,0:T(8,128)(2,1)S(1)}, bf16[2,64,1536]{2,1,0:T(8,128)(2,1)S(1)}, u32[]{:S(2)}, u32[]{:S(2)}) %collective-permute-start.40) | collective-permute-done | bytes 393248 | tf_op jit(solution)/shard_map/ppermute | solution.py:42
  136.4 3.6 %collective-permute-start.34 = (bf16[4,16,768]{2,1,0:T(8,128)(2,1)S(1)}, bf16[4,16,768]{2,1,0:T(8,128)(2,1)S(1)}, u32[]{:S(2)}, u32[]{:S(2)}) collective-permute-start(bf16[4,16,768]{2,1,0:T(8,128)(2,1)S(1)} %get-tuple-element.35), channel_id=1, source_target_pairs={{0,2},{1,3},{2,4},{3,5},{4,6},{5,7},{6,0},{7,1},{8,10},{9,11},{10,... | collective-permute-start | bytes 294920 | tf_op jit(solution)/shard_map/ppermute | solution.py:42
  140.0 2.6 %collective-permute-start.33 = (bf16[4,16,768]{2,1,0:T(8,128)(2,1)S(1)}, bf16[4,16,768]{2,1,0:T(8,128)(2,1)S(1)}, u32[]{:S(2)}, u32[]{:S(2)}) collective-permute-start(bf16[4,16,768]{2,1,0:T(8,128)(2,1)S(1)} %get-tuple-element.36), channel_id=1, source_target_pairs={{0,4},{1,5},{2,6},{3,7},{4,0},{5,1},{6,2},{7,3},{8,12},{9,13},{10,... | collective-permute-start | bytes 294920 | tf_op jit(solution)/shard_map/ppermute | solution.py:42
  142.8 2.2 %collective-permute-done.34 = bf16[4,16,768]{2,1,0:T(8,128)(2,1)S(1)} collective-permute-done((bf16[4,16,768]{2,1,0:T(8,128)(2,1)S(1)}, bf16[4,16,768]{2,1,0:T(8,128)(2,1)S(1)}, u32[]{:S(2)}, u32[]{:S(2)}) %collective-permute-start.34) | collective-permute-done | bytes 98336 | tf_op jit(solution)/shard_map/ppermute | solution.py:42
  145.0 3.2 %collective-permute-done.33 = bf16[4,16,768]{2,1,0:T(8,128)(2,1)S(1)} collective-permute-done((bf16[4,16,768]{2,1,0:T(8,128)(2,1)S(1)}, bf16[4,16,768]{2,1,0:T(8,128)(2,1)S(1)}, u32[]{:S(2)}, u32[]{:S(2)}) %collective-permute-start.33) | collective-permute-done | bytes 98336 | tf_op jit(solution)/shard_map/ppermute | solution.py:42
  148.3 1.6 collective-permute-start.37
  149.8 1.5 collective-permute-start.36
  151.8 3.6 %fusion.104 = f32[768,1536]{1,0:T(8,128)} fusion(bf16[512,768]{1,0:T(8,128)(2,1)S(1)} %bitcast.457, bf16[512,1536]{1,0:T(8,128)(2,1)S(1)} %bitcast.458), kind=kOutput, calls=%fused_computation.287 | convolution fusion | flops 1207959552 | bytes 7077888 | tf_op jit(solution)/shard_map/dot_general | solution.py:204
  155.8 0.7 unstack.29
  (139 shorter events, 19.2 us)
Async XLA Ops:
  0.6 24.8 %copy-start = (bf16[768,1536]{1,0:T(8,128)(2,1)S(1)}, bf16[768,1536]{1,0:T(8,128)(2,1)}, u32[]{:S(2)}) copy-start(bf16[768,1536]{1,0:T(8,128)(2,1)} %param.10) | copy-start | bytes 7077892
  2.6 6.3 %collective-permute-start.2 = (bf16[3,16,768]{2,1,0:T(8,128)(2,1)S(1)}, bf16[3,16,768]{2,1,0:T(8,128)(2,1)S(1)}, u32[]{:S(2)}, u32[]{:S(2)}) collective-permute-start(bf16[3,16,768]{2,1,0:T(8,128)(2,1)S(1)} %pad_maximum_fusion.29), channel_id=1, source_target_pairs={{0,24},{8,16},{16,8},{24,0},{1,25},{9,17},{17,9},{25,1},{2,26},{10... | collective-permute-start | bytes 221192 | tf_op jit(solution)/shard_map/ppermute | solution.py:42
  6.6 4.4 %collective-permute-start.1 = (bf16[3,16,768]{2,1,0:T(8,128)(2,1)S(1)}, bf16[3,16,768]{2,1,0:T(8,128)(2,1)S(1)}, u32[]{:S(2)}, u32[]{:S(2)}) collective-permute-start(bf16[3,16,768]{2,1,0:T(8,128)(2,1)S(1)} %pad_maximum_fusion.28), channel_id=1, source_target_pairs={{0,16},{8,24},{16,0},{24,8},{1,17},{9,25},{17,1},{25,9},{2,18},{10... | collective-permute-start | bytes 221192 | tf_op jit(solution)/shard_map/ppermute | solution.py:42
  7.2 4.4 %collective-permute-start = (bf16[3,16,768]{2,1,0:T(8,128)(2,1)S(1)}, bf16[3,16,768]{2,1,0:T(8,128)(2,1)S(1)}, u32[]{:S(2)}, u32[]{:S(2)}) collective-permute-start(bf16[3,16,768]{2,1,0:T(8,128)(2,1)S(1)} %pad_maximum_fusion.27), channel_id=1, source_target_pairs={{0,8},{8,0},{16,24},{24,16},{1,9},{9,1},{17,25},{25,17},{2,10},{10... | collective-permute-start | bytes 221192 | tf_op jit(solution)/shard_map/ppermute | solution.py:42
  11.6 6.8 %collective-permute-start.5 = (bf16[1,4,16,768]{3,2,1,0:T(8,128)(2,1)S(1)}, bf16[1,4,16,768]{3,2,1,0:T(8,128)(2,1)S(1)}, u32[]{:S(2)}, u32[]{:S(2)}) collective-permute-start(bf16[1,4,16,768]{3,2,1,0:T(8,128)(2,1)S(1)} %get-tuple-element.54), channel_id=1, source_target_pairs={{0,6},{1,7},{2,0},{3,1},{4,2},{5,3},{6,4},{7,5},{8,14},{9,15},{10,... | collective-permute-start | bytes 294920 | tf_op jit(solution)/shard_map/ppermute | solution.py:42
  15.3 8.2 %collective-permute-start.4 = (bf16[1,4,16,768]{3,2,1,0:T(8,128)(2,1)S(1)}, bf16[1,4,16,768]{3,2,1,0:T(8,128)(2,1)S(1)}, u32[]{:S(2)}, u32[]{:S(2)}) collective-permute-start(bf16[1,4,16,768]{3,2,1,0:T(8,128)(2,1)S(1)} %get-tuple-element.54), channel_id=1, source_target_pairs={{0,4},{1,5},{2,6},{3,7},{4,0},{5,1},{6,2},{7,3},{8,12},{9,13},{10,... | collective-permute-start | bytes 294920 | tf_op jit(solution)/shard_map/ppermute | solution.py:42
  15.3 8.2 %collective-permute-start.3 = (bf16[1,4,16,768]{3,2,1,0:T(8,128)(2,1)S(1)}, bf16[1,4,16,768]{3,2,1,0:T(8,128)(2,1)S(1)}, u32[]{:S(2)}, u32[]{:S(2)}) collective-permute-start(bf16[1,4,16,768]{3,2,1,0:T(8,128)(2,1)S(1)} %get-tuple-element.54), channel_id=1, source_target_pairs={{0,2},{1,3},{2,4},{3,5},{4,6},{5,7},{6,0},{7,1},{8,10},{9,11},{10,... | collective-permute-start | bytes 294920 | tf_op jit(solution)/shard_map/ppermute | solution.py:42
  23.5 1.8 %collective-permute-start.6 = (bf16[1,4,4,16,768]{4,3,2,1,0:T(8,128)(2,1)S(1)}, bf16[1,4,4,16,768]{4,3,2,1,0:T(8,128)(2,1)S(1)}, u32[]{:S(2)}, u32[]{:S(2)}) collective-permute-start(bf16[1,4,4,16,768]{4,3,2,1,0:T(8,128)(2,1)S(1)} %get-tuple-element.46), channel_id=1, source_target_pairs={{0,1},{1,0},{2,3},{3,2},{4,5},{5,4},{6,7},{7,6},{8,9},{9,8},{10,11... | collective-permute-start | bytes 1179656 | tf_op jit(solution)/shard_map/ppermute | solution.py:42
  27.5 8.2 %collective-permute-start.21 = (bf16[2,4,16,768]{3,2,0,1:T(8,128)(2,1)S(1)}, bf16[2,4,16,768]{3,2,0,1:T(8,128)(2,1)S(1)}, u32[]{:S(2)}, u32[]{:S(2)}) collective-permute-start(bf16[2,4,16,768]{3,2,0,1:T(8,128)(2,1)S(1)} %pad_maximum_fusion.24), channel_id=1, source_target_pairs={{0,6},{1,7},{2,0},{3,1},{4,2},{5,3},{6,4},{7,5},{8,14},{9,15},{10,... | collective-permute-start | bytes 589832 | tf_op jit(solution)/shard_map/ppermute | solution.py:42
  29.0 18.3 %collective-permute-start.20 = (bf16[2,4,16,768]{3,2,0,1:T(8,128)(2,1)S(1)}, bf16[2,4,16,768]{3,2,0,1:T(8,128)(2,1)}, u32[]{:S(2)}, u32[]{:S(2)}) collective-permute-start(bf16[2,4,16,768]{3,2,0,1:T(8,128)(2,1)S(1)} %pad_maximum_fusion.24), channel_id=1, source_target_pairs={{0,4},{1,5},{2,6},{3,7},{4,0},{5,1},{6,2},{7,3},{8,12},{9,13},{10,... | collective-permute-start | bytes 589832 | tf_op jit(solution)/shard_map/ppermute | solution.py:42
  29.4 17.9 %collective-permute-start.19 = (bf16[2,4,16,768]{3,2,0,1:T(8,128)(2,1)S(1)}, bf16[2,4,16,768]{3,2,0,1:T(8,128)(2,1)}, u32[]{:S(2)}, u32[]{:S(2)}) collective-permute-start(bf16[2,4,16,768]{3,2,0,1:T(8,128)(2,1)S(1)} %pad_maximum_fusion.24), channel_id=1, source_target_pairs={{0,2},{1,3},{2,4},{3,5},{4,6},{5,7},{6,0},{7,1},{8,10},{9,11},{10,... | collective-permute-start | bytes 589832 | tf_op jit(solution)/shard_map/ppermute | solution.py:42
  32.1 16.3 %collective-permute-start.9 = (bf16[2,1,64,1536]{3,2,1,0:T(8,128)(2,1)}, bf16[2,1,64,1536]{3,2,1,0:T(8,128)(2,1)}, u32[]{:S(2)}, u32[]{:S(2)}) collective-permute-start(bf16[2,1,64,1536]{3,2,1,0:T(8,128)(2,1)} %pad_maximum_fusion.9), channel_id=1, source_target_pairs={{0,8},{8,0},{16,24},{24,16},{1,9},{9,1},{17,25},{25,17},{2,10},{10... | collective-permute-start | bytes 1179656 | tf_op jit(solution)/shard_map/ppermute | solution.py:42
  34.3 17.1 %collective-permute-start.7 = (bf16[2,1,64,1536]{3,2,1,0:T(8,128)(2,1)}, bf16[2,1,64,1536]{3,2,1,0:T(8,128)(2,1)}, u32[]{:S(2)}, u32[]{:S(2)}) collective-permute-start(bf16[2,1,64,1536]{3,2,1,0:T(8,128)(2,1)} %pad_maximum_fusion.8), channel_id=1, source_target_pairs={{0,16},{8,24},{16,0},{24,8},{1,17},{9,25},{17,1},{25,9},{2,18},{10... | collective-permute-start | bytes 1179656 | tf_op jit(solution)/shard_map/ppermute | solution.py:42
  48.4 21.3 %collective-permute-start.22 = (bf16[2,4,4,16,768]{4,3,0,1,2:T(8,128)(2,1)S(1)}, bf16[2,4,4,16,768]{4,3,0,1,2:T(8,128)(2,1)S(1)}, u32[]{:S(2)}, u32[]{:S(2)}) collective-permute-start(bf16[2,4,4,16,768]{4,3,0,1,2:T(8,128)(2,1)S(1)} %pad_maximum_fusion.4), channel_id=1, source_target_pairs={{0,1},{1,0},{2,3},{3,2},{4,5},{5,4},{6,7},{7,6},{8,9},{9,8},{10,11... | collective-permute-start | bytes 2359304 | tf_op jit(solution)/shard_map/ppermute | solution.py:42
  50.0 7.4 %collective-permute-start.10 = (bf16[1,64,1536]{2,1,0:T(8,128)(2,1)S(1)}, bf16[1,64,1536]{2,1,0:T(8,128)(2,1)S(1)}, u32[]{:S(2)}, u32[]{:S(2)}) collective-permute-start(bf16[1,64,1536]{2,1,0:T(8,128)(2,1)S(1)} %fusion.67), channel_id=1, source_target_pairs={{0,16},{8,24},{16,0},{24,8},{1,17},{9,25},{17,1},{25,9},{2,18},{10... | collective-permute-start | bytes 589832 | tf_op jit(solution)/shard_map/ppermute | solution.py:42
  52.9 7.6 %collective-permute-start.8 = (bf16[1,64,1536]{2,1,0:T(8,128)(2,1)S(1)}, bf16[1,64,1536]{2,1,0:T(8,128)(2,1)S(1)}, u32[]{:S(2)}, u32[]{:S(2)}) collective-permute-start(bf16[1,64,1536]{2,1,0:T(8,128)(2,1)S(1)} %fusion.66), channel_id=1, source_target_pairs={{0,8},{8,0},{16,24},{24,16},{1,9},{9,1},{17,25},{25,17},{2,10},{10... | collective-permute-start | bytes 589832 | tf_op jit(solution)/shard_map/ppermute | solution.py:42
  58.9 6.6 %collective-permute-start.12 = (bf16[64,1536]{1,0:T(8,128)(2,1)S(1)}, bf16[64,1536]{1,0:T(8,128)(2,1)S(1)}, u32[]{:S(2)}, u32[]{:S(2)}) collective-permute-start(bf16[64,1536]{1,0:T(8,128)(2,1)S(1)} %get-tuple-element.69), channel_id=1, source_target_pairs={{0,16},{8,24},{16,0},{24,8},{1,17},{9,25},{17,1},{25,9},{2,18},{10... | collective-permute-start | bytes 589832 | tf_op jit(solution)/shard_map/ppermute | solution.py:42
  62.0 7.6 %collective-permute-start.11 = (bf16[64,1536]{1,0:T(8,128)(2,1)S(1)}, bf16[64,1536]{1,0:T(8,128)(2,1)S(1)}, u32[]{:S(2)}, u32[]{:S(2)}) collective-permute-start(bf16[64,1536]{1,0:T(8,128)(2,1)S(1)} %get-tuple-element.71), channel_id=1, source_target_pairs={{0,8},{8,0},{16,24},{24,16},{1,9},{9,1},{17,25},{25,17},{2,10},{10... | collective-permute-start | bytes 589832 | tf_op jit(solution)/shard_map/ppermute | solution.py:42
  65.5 17.9 %collective-permute-start.13 = (bf16[2,64,1536]{2,1,0:T(8,128)(2,1)S(1)}, bf16[2,64,1536]{2,1,0:T(8,128)(2,1)S(1)}, u32[]{:S(2)}, u32[]{:S(2)}) collective-permute-start(bf16[2,64,1536]{2,1,0:T(8,128)(2,1)S(1)} %pad_maximum_fusion.11), channel_id=1, source_target_pairs={{0,8},{8,0},{16,24},{24,16},{1,9},{9,1},{17,25},{25,17},{2,10},{10... | collective-permute-start | bytes 1179656 | tf_op jit(solution)/shard_map/ppermute | solution.py:42
  69.7 13.7 %collective-permute-start.14 = (bf16[2,64,1536]{2,1,0:T(8,128)(2,1)S(1)}, bf16[2,64,1536]{2,1,0:T(8,128)(2,1)S(1)}, u32[]{:S(2)}, u32[]{:S(2)}) collective-permute-start(bf16[2,64,1536]{2,1,0:T(8,128)(2,1)S(1)} %pad_maximum_fusion.13), channel_id=1, source_target_pairs={{0,16},{8,24},{16,0},{24,8},{1,17},{9,25},{17,1},{25,9},{2,18},{10... | collective-permute-start | bytes 1179656 | tf_op jit(solution)/shard_map/ppermute | solution.py:42
  70.1 1.7 %copy-start.1 = (bf16[1536,768]{1,0:T(8,128)(2,1)S(1)}, bf16[1536,768]{1,0:T(8,128)(2,1)}, u32[]{:S(2)}) copy-start(bf16[1536,768]{1,0:T(8,128)(2,1)} %param.11) | copy-start | bytes 7077892
  79.7 18.4 %collective-permute-start.23 = (bf16[2,2,64,1536]{3,2,1,0:T(8,128)(2,1)S(1)}, bf16[2,2,64,1536]{3,2,1,0:T(8,128)(2,1)S(1)}, u32[]{:S(2)}, u32[]{:S(2)}) collective-permute-start(bf16[2,2,64,1536]{3,2,1,0:T(8,128)(2,1)S(1)} %pad_maximum_fusion.5), channel_id=1, source_target_pairs={{0,16},{8,24},{16,0},{24,8},{1,17},{9,25},{17,1},{25,9},{2,18},{10... | collective-permute-start | bytes 2359304 | tf_op jit(solution)/shard_map/ppermute | solution.py:42
  81.9 18.3 %collective-permute-start.25 = (bf16[2,2,64,1536]{3,2,1,0:T(8,128)(2,1)S(1)}, bf16[2,2,64,1536]{3,2,1,0:T(8,128)(2,1)S(1)}, u32[]{:S(2)}, u32[]{:S(2)}) collective-permute-start(bf16[2,2,64,1536]{3,2,1,0:T(8,128)(2,1)S(1)} %pad_maximum_fusion.6), channel_id=1, source_target_pairs={{0,8},{8,0},{16,24},{24,16},{1,9},{9,1},{17,25},{25,17},{2,10},{10... | collective-permute-start | bytes 2359304 | tf_op jit(solution)/shard_map/ppermute | solution.py:42
  85.0 1.8 %collective-permute-start.15 = (bf16[4,4,16,768]{3,2,1,0:T(8,128)(2,1)S(1)}, bf16[4,4,16,768]{3,2,1,0:T(8,128)(2,1)S(1)}, u32[]{:S(2)}, u32[]{:S(2)}) collective-permute-start(bf16[4,4,16,768]{3,2,1,0:T(8,128)(2,1)S(1)} %fusion.50), channel_id=1, source_target_pairs={{0,1},{1,0},{2,3},{3,2},{4,5},{5,4},{6,7},{7,6},{8,9},{9,8},{10,11... | collective-permute-start | bytes 1179656 | tf_op jit(solution)/shard_map/ppermute | solution.py:42
  86.9 7.6 %collective-permute-start.18 = (bf16[4,16,768]{2,1,0:T(8,128)(2,1)S(1)}, bf16[4,16,768]{2,1,0:T(8,128)(2,1)S(1)}, u32[]{:S(2)}, u32[]{:S(2)}) collective-permute-start(bf16[4,16,768]{2,1,0:T(8,128)(2,1)S(1)} %get-tuple-element.32), channel_id=1, source_target_pairs={{0,2},{1,3},{2,4},{3,5},{4,6},{5,7},{6,0},{7,1},{8,10},{9,11},{10,... | collective-permute-start | bytes 294920 | tf_op jit(solution)/shard_map/ppermute | solution.py:42
  87.3 10.6 %collective-permute-start.17 = (bf16[4,16,768]{2,1,0:T(8,128)(2,1)S(1)}, bf16[4,16,768]{2,1,0:T(8,128)(2,1)S(1)}, u32[]{:S(2)}, u32[]{:S(2)}) collective-permute-start(bf16[4,16,768]{2,1,0:T(8,128)(2,1)S(1)} %get-tuple-element.33), channel_id=1, source_target_pairs={{0,4},{1,5},{2,6},{3,7},{4,0},{5,1},{6,2},{7,3},{8,12},{9,13},{10,... | collective-permute-start | bytes 294920 | tf_op jit(solution)/shard_map/ppermute | solution.py:42
  89.4 8.5 %collective-permute-start.16 = (bf16[4,16,768]{2,1,0:T(8,128)(2,1)S(1)}, bf16[4,16,768]{2,1,0:T(8,128)(2,1)S(1)}, u32[]{:S(2)}, u32[]{:S(2)}) collective-permute-start(bf16[4,16,768]{2,1,0:T(8,128)(2,1)S(1)} %get-tuple-element.31), channel_id=1, source_target_pairs={{0,6},{1,7},{2,0},{3,1},{4,2},{5,3},{6,4},{7,5},{8,14},{9,15},{10,... | collective-permute-start | bytes 294920 | tf_op jit(solution)/shard_map/ppermute | solution.py:42
  98.1 9.6 %collective-permute-start.24 = (bf16[2,64,1536]{2,1,0:T(8,128)(2,1)S(1)}, bf16[2,64,1536]{2,1,0:T(8,128)(2,1)S(1)}, u32[]{:S(2)}, u32[]{:S(2)}) collective-permute-start(bf16[2,64,1536]{2,1,0:T(8,128)(2,1)S(1)} %fusion.27), channel_id=1, source_target_pairs={{0,8},{8,0},{16,24},{24,16},{1,9},{9,1},{17,25},{25,17},{2,10},{10... | collective-permute-start | bytes 1179656 | tf_op jit(solution)/shard_map/ppermute | solution.py:42
  100.3 9.1 %collective-permute-start.26 = (bf16[2,64,1536]{2,1,0:T(8,128)(2,1)S(1)}, bf16[2,64,1536]{2,1,0:T(8,128)(2,1)S(1)}, u32[]{:S(2)}, u32[]{:S(2)}) collective-permute-start(bf16[2,64,1536]{2,1,0:T(8,128)(2,1)S(1)} %fusion.29), channel_id=1, source_target_pairs={{0,16},{8,24},{16,0},{24,8},{1,17},{9,25},{17,1},{25,9},{2,18},{10... | collective-permute-start | bytes 1179656 | tf_op jit(solution)/shard_map/ppermute | solution.py:42
  110.7 7.3 %collective-permute-start.28 = (bf16[64,1536]{1,0:T(8,128)(2,1)S(1)}, bf16[64,1536]{1,0:T(8,128)(2,1)S(1)}, u32[]{:S(2)}, u32[]{:S(2)}) collective-permute-start(bf16[64,1536]{1,0:T(8,128)(2,1)S(1)} %get-tuple-element.26), channel_id=1, source_target_pairs={{0,16},{8,24},{16,0},{24,8},{1,17},{9,25},{17,1},{25,9},{2,18},{10... | collective-permute-start | bytes 589832 | tf_op jit(solution)/shard_map/ppermute | solution.py:42
  111.1 7.8 %collective-permute-start.27 = (bf16[64,1536]{1,0:T(8,128)(2,1)S(1)}, bf16[64,1536]{1,0:T(8,128)(2,1)S(1)}, u32[]{:S(2)}, u32[]{:S(2)}) collective-permute-start(bf16[64,1536]{1,0:T(8,128)(2,1)S(1)} %get-tuple-element.22), channel_id=1, source_target_pairs={{0,8},{8,0},{16,24},{24,16},{1,9},{9,1},{17,25},{25,17},{2,10},{10... | collective-permute-start | bytes 589832 | tf_op jit(solution)/shard_map/ppermute | solution.py:42
  112.8 9.4 %collective-permute-start.39 = (bf16[64,1536]{1,0:T(8,128)(2,1)S(1)}, bf16[64,1536]{1,0:T(8,128)(2,1)S(1)}, u32[]{:S(2)}, u32[]{:S(2)}) collective-permute-start(bf16[64,1536]{1,0:T(8,128)(2,1)S(1)} %get-tuple-element.25), channel_id=1, source_target_pairs={{0,16},{8,24},{16,0},{24,8},{1,17},{9,25},{17,1},{25,9},{2,18},{10... | collective-permute-start | bytes 589832 | tf_op jit(solution)/shard_map/ppermute | solution.py:42
  113.2 9.9 %collective-permute-start.38 = (bf16[64,1536]{1,0:T(8,128)(2,1)S(1)}, bf16[64,1536]{1,0:T(8,128)(2,1)S(1)}, u32[]{:S(2)}, u32[]{:S(2)}) collective-permute-start(bf16[64,1536]{1,0:T(8,128)(2,1)S(1)} %get-tuple-element.21), channel_id=1, source_target_pairs={{0,8},{8,0},{16,24},{24,16},{1,9},{9,1},{17,25},{25,17},{2,10},{10... | collective-permute-start | bytes 589832 | tf_op jit(solution)/shard_map/ppermute | solution.py:42
  118.1 13.5 %collective-permute-start.29 = (bf16[2,64,1536]{2,1,0:T(8,128)(2,1)S(1)}, bf16[2,64,1536]{2,1,0:T(8,128)(2,1)S(1)}, u32[]{:S(2)}, u32[]{:S(2)}) collective-permute-start(bf16[2,64,1536]{2,1,0:T(8,128)(2,1)S(1)} %pad_maximum_fusion.17), channel_id=1, source_target_pairs={{0,8},{8,0},{16,24},{24,16},{1,9},{9,1},{17,25},{25,17},{2,10},{10... | collective-permute-start | bytes 1179656 | tf_op jit(solution)/shard_map/ppermute | solution.py:42
  119.0 12.6 %collective-permute-start.30 = (bf16[2,64,1536]{2,1,0:T(8,128)(2,1)S(1)}, bf16[2,64,1536]{2,1,0:T(8,128)(2,1)S(1)}, u32[]{:S(2)}, u32[]{:S(2)}) collective-permute-start(bf16[2,64,1536]{2,1,0:T(8,128)(2,1)S(1)} %pad_maximum_fusion.19), channel_id=1, source_target_pairs={{0,16},{8,24},{16,0},{24,8},{1,17},{9,25},{17,1},{25,9},{2,18},{10... | collective-permute-start | bytes 1179656 | tf_op jit(solution)/shard_map/ppermute | solution.py:42
  122.3 13.7 %collective-permute-start.40 = (bf16[2,64,1536]{2,1,0:T(8,128)(2,1)S(1)}, bf16[2,64,1536]{2,1,0:T(8,128)(2,1)S(1)}, u32[]{:S(2)}, u32[]{:S(2)}) collective-permute-start(bf16[2,64,1536]{2,1,0:T(8,128)(2,1)S(1)} %pad_maximum_fusion.22), channel_id=1, source_target_pairs={{0,8},{8,0},{16,24},{24,16},{1,9},{9,1},{17,25},{25,17},{2,10},{10... | collective-permute-start | bytes 1179656 | tf_op jit(solution)/shard_map/ppermute | solution.py:42
  123.2 12.9 %collective-permute-start.41 = (bf16[2,64,1536]{2,1,0:T(8,128)(2,1)S(1)}, bf16[2,64,1536]{2,1,0:T(8,128)(2,1)S(1)}, u32[]{:S(2)}, u32[]{:S(2)}) collective-permute-start(bf16[2,64,1536]{2,1,0:T(8,128)(2,1)S(1)} %pad_maximum_fusion.23), channel_id=1, source_target_pairs={{0,16},{8,24},{16,0},{24,8},{1,17},{9,25},{17,1},{25,9},{2,18},{10... | collective-permute-start | bytes 1179656 | tf_op jit(solution)/shard_map/ppermute | solution.py:42
  133.2 3.0 %collective-permute-start.31 = (bf16[4,4,16,768]{3,2,0,1:T(8,128)(2,1)S(1)}, bf16[4,4,16,768]{3,2,0,1:T(8,128)(2,1)S(1)}, u32[]{:S(2)}, u32[]{:S(2)}) collective-permute-start(bf16[4,4,16,768]{3,2,0,1:T(8,128)(2,1)S(1)} %fusion.51), channel_id=1, source_target_pairs={{0,1},{1,0},{2,3},{3,2},{4,5},{5,4},{6,7},{7,6},{8,9},{9,8},{10,11... | collective-permute-start | bytes 1179656 | tf_op jit(solution)/shard_map/ppermute | solution.py:42
  136.4 8.6 %collective-permute-start.34 = (bf16[4,16,768]{2,1,0:T(8,128)(2,1)S(1)}, bf16[4,16,768]{2,1,0:T(8,128)(2,1)S(1)}, u32[]{:S(2)}, u32[]{:S(2)}) collective-permute-start(bf16[4,16,768]{2,1,0:T(8,128)(2,1)S(1)} %get-tuple-element.35), channel_id=1, source_target_pairs={{0,2},{1,3},{2,4},{3,5},{4,6},{5,7},{6,0},{7,1},{8,10},{9,11},{10,... | collective-permute-start | bytes 294920 | tf_op jit(solution)/shard_map/ppermute | solution.py:42
  140.0 8.2 %collective-permute-start.33 = (bf16[4,16,768]{2,1,0:T(8,128)(2,1)S(1)}, bf16[4,16,768]{2,1,0:T(8,128)(2,1)S(1)}, u32[]{:S(2)}, u32[]{:S(2)}) collective-permute-start(bf16[4,16,768]{2,1,0:T(8,128)(2,1)S(1)} %get-tuple-element.36), channel_id=1, source_target_pairs={{0,4},{1,5},{2,6},{3,7},{4,0},{5,1},{6,2},{7,3},{8,12},{9,13},{10,... | collective-permute-start | bytes 294920 | tf_op jit(solution)/shard_map/ppermute | solution.py:42
  142.6 5.6 %collective-permute-start.32 = (bf16[4,16,768]{2,1,0:T(8,128)(2,1)S(1)}, bf16[4,16,768]{2,1,0:T(8,128)(2,1)S(1)}, u32[]{:S(2)}, u32[]{:S(2)}) collective-permute-start(bf16[4,16,768]{2,1,0:T(8,128)(2,1)S(1)} %get-tuple-element.34), channel_id=1, source_target_pairs={{0,6},{1,7},{2,0},{3,1},{4,2},{5,3},{6,4},{7,5},{8,14},{9,15},{10,... | collective-permute-start | bytes 294920 | tf_op jit(solution)/shard_map/ppermute | solution.py:42
  148.3 7.2 %collective-permute-start.37 = (bf16[2,16,768]{2,1,0:T(8,128)(2,1)S(1)}, bf16[2,16,768]{2,1,0:T(8,128)(2,1)S(1)}, u32[]{:S(2)}, u32[]{:S(2)}) collective-permute-start(bf16[2,16,768]{2,1,0:T(8,128)(2,1)S(1)} %get-tuple-element.51), channel_id=1, source_target_pairs={{0,24},{8,16},{16,8},{24,0},{1,25},{9,17},{17,9},{25,1},{2,26},{10... | collective-permute-start | bytes 147464 | tf_op jit(solution)/shard_map/ppermute | solution.py:42
  149.8 5.6 %collective-permute-start.36 = (bf16[2,16,768]{2,1,0:T(8,128)(2,1)S(1)}, bf16[2,16,768]{2,1,0:T(8,128)(2,1)S(1)}, u32[]{:S(2)}, u32[]{:S(2)}) collective-permute-start(bf16[2,16,768]{2,1,0:T(8,128)(2,1)S(1)} %get-tuple-element.52), channel_id=1, source_target_pairs={{0,16},{8,24},{16,0},{24,8},{1,17},{9,25},{17,1},{25,9},{2,18},{10... | collective-permute-start | bytes 147464 | tf_op jit(solution)/shard_map/ppermute | solution.py:42
  151.4 4.1 %collective-permute-start.35 = (bf16[2,16,768]{2,1,0:T(8,128)(2,1)S(1)}, bf16[2,16,768]{2,1,0:T(8,128)(2,1)S(1)}, u32[]{:S(2)}, u32[]{:S(2)}) collective-permute-start(bf16[2,16,768]{2,1,0:T(8,128)(2,1)S(1)} %get-tuple-element.50), channel_id=1, source_target_pairs={{0,8},{8,0},{16,24},{24,16},{1,9},{9,1},{17,25},{25,17},{2,10},{10... | collective-permute-start | bytes 147464 | tf_op jit(solution)/shard_map/ppermute | solution.py:42
